TPU v7x, 32 devices: a whole 2x2x4 slice. The times are simulated.
32 devices in a mesh: groups: 2 (over x), row: 8 (over z, y), col: 2 (over core).
Axes of the slice: x: 2, y: 2, z: 4, core: 2. Of those that a mesh axis runs over, the one named last changes fastest.
Arguments:
- affinity: bfloat16 [4096, 2, 1024], P(('groups', 'col'), None, 'row'), parts along dimension 0, may hold values from 0 to 64, as said below
- block_live: int32 [32, 2, 8], P(('groups', 'col'), None, 'row'), parts along dimension 0, may hold values from 0 to 1, as said below
- labels: bfloat16 [4096, 256], P(('groups', 'col', 'row')), parts along dimension 0, may hold values from 0 to 1
- seed_class: int32 [4096], P(('groups', 'col', 'row')), parts along dimension 0, may hold values from 0 to 149
- seed_mask: int32 [4096], P(('groups', 'col', 'row')), parts along dimension 0, may hold values 0 or 1
Outputs:
- propagated: bfloat16 [4096, 256], P(('groups', 'col', 'row')), parts along dimension 0
There are 2 independent parts, one for each index of `groups`. A program takes and returns all parts, laid end to end along the dimension named above; each array names one. Nothing has to cross between parts.
Inputs may be any that keep to these rules, and one draw needn't show every extreme that they name: `affinity`: positive affinities. `block_live`: 1 where the 128 x 128 block of affinities is stored, 0 where it is absent.
All inputs are finite; a program needn't handle non-finite values. No bound on the sum of `seed_mask` on one device may be relied on, other than what follows from the above.
Results may differ from a plain program's by a relative error of at most 0.0036.
Values may be sent and summed in bfloat16 or wider, within the bound.
No kernel may reach another device: no remote copies, remote signals or barrier semaphores. Data moves between devices by JAX's collectives and lax.ppermute only.
A program may use at most 128 MiB of HBM per device.

v0:
```python
import jax
import jax.numpy as jnp
from jax import lax
from jax.sharding import PartitionSpec as P

ITERS = 2


carry_weight = 0.8


def masked_tile(affinity, block_live):
    stripe, sides, width = affinity.shape
    block = stripe // block_live.shape[0]
    shaped = affinity.reshape(stripe // block, block, sides, width // block, block)
    keep = block_live[:, None, :, :, None] == 1
    return jnp.where(keep, shaped, jnp.zeros_like(shaped)).reshape(stripe, sides * width)


def narrow_spread(matrices, current):
    panels = lax.all_gather(current, "col", axis=0, tiled=True)
    classes = current.shape[1]
    total = jnp.zeros((current.shape[0] * lax.axis_size("row"), classes), jnp.float32)
    for matrix in matrices:
        total = total + jnp.dot(matrix, panels, preferred_element_type=jnp.float32)
    return lax.psum_scatter(total, "row", scatter_dimension=0, tiled=True)


def row_degree(matrices):
    totals = jnp.zeros((matrices[0].shape[0],), jnp.float32)
    for matrix in matrices:
        totals = totals + jnp.sum(matrix, axis=1, dtype=jnp.float32)
    return lax.psum_scatter(totals, "row", scatter_dimension=0, tiled=True)


def on_device(affinity, block_live, labels, seed_class, seed_mask):
    stored = masked_tile(affinity, block_live)
    width = labels.shape[0]
    stripe = stored.shape[0]
    sides = stored.shape[1] // width
    shaped = stored.reshape(stripe // width, width, sides, width)
    arrived = lax.all_to_all(
        lax.all_to_all(shaped, "row", split_axis=0, concat_axis=0, tiled=True),
        "col",
        split_axis=2,
        concat_axis=2,
        tiled=True,
    )
    mirrored = arrived.transpose(0, 3, 2, 1).reshape(stored.shape)
    matrices = (stored, mirrored)
    sums = row_degree(matrices)
    degree = 1.0 + 0.5 * sums
    classes = labels.shape[1]
    slots = lax.broadcasted_iota(jnp.int32, (width, classes), 1)
    is_seed = (seed_class[:, None] == slots) & (seed_mask[:, None] == 1)
    seed_rows = jnp.where(is_seed, 1.0, 0.0).astype(jnp.float32)
    current = labels
    for step in range(ITERS):
        spread = narrow_spread(matrices, current)
        mixed = carry_weight * (0.5 * spread + current.astype(jnp.float32)) / degree[:, None]
        current = (mixed + (1.0 - carry_weight) * seed_rows).astype(jnp.bfloat16)
    return current


def solution(mesh):
    return jax.shard_map(
        on_device,
        mesh=mesh,
        in_specs=(
            P(("groups", "col"), None, "row"),
            P(("groups", "col"), None, "row"),
            P(("groups", "col", "row"), None),
            P(("groups", "col", "row")),
            P(("groups", "col", "row")),
        ),
        out_specs=P(("groups", "col", "row"), None),
        check_vma=False,
    )
```

profile of v0, /device:TPU:0, one launch (start us, length us, event | category | flops | bytes accessed | tf_op | source)
XLA Modules:
  0.0 176.4 jit_solution(12237544475492908366)
XLA Ops:
  6.5 0.7 broadcast_compare_fusion
  7.2 1.1 copy.22
  8.3 0.1 broadcast_select_fusion.1
  8.5 0.8 copy.23
  9.3 0.0 copy-start
  9.3 7.4 %all-to-all-start = ((bf16[8,128,2,128]{3,1,2,0:T(8,128)(2,1)}), bf16[8,128,2,128]{3,1,2,0:T(8,128)(2,1)S(1)}, u32[]{:S(2)}, u32[]{:S(2)}) async-start(bf16[8,128,2,128]{3,1,2,0:T(8,128)(2,1)} %copy.23), calls=%async_computation | async-start | bytes 1048576 | tf_op jit(solution)/shard_map/all_to_all | solution.py:43
  16.7 0.0 copy-start.1
  16.7 0.0 reduce-scatter.3.cloned.1.call-start
  16.8 0.0 copy-done
  16.8 0.4 copy.21
  17.2 0.3 copy-done.1
  17.5 1.9 %all_gather.6 = bf16[256,256]{1,0:T(8,128)(2,1)S(1)} all-gather(bf16[128,256]{1,0:T(8,128)(2,1)S(1)} %copy-done.1), channel_id=1, replica_groups=mesh['groups'=2,'row'=8,'col'=2] {'col'}, dimensions={0}, use_global_device_ids=true | all-gather | bytes 196608 | tf_op jit(solution)/shard_map/all_gather | solution.py:21
  19.4 0.1 broadcast_in_dim.38
  19.6 0.2 bitcast_select_fusion
  19.8 0.4 fusion.6
  20.1 11.1 %all-to-all-done = bf16[8,128,2,128]{3,1,2,0:T(8,128)(2,1)S(1)} async-done(((bf16[8,128,2,128]{3,1,2,0:T(8,128)(2,1)}), bf16[8,128,2,128]{3,1,2,0:T(8,128)(2,1)S(1)}, u32[]{:S(2)}, u32[]{:S(2)}) %all-to-all-start) | async-done | bytes 524320 | tf_op jit(solution)/shard_map/all_to_all | solution.py:43
  31.2 4.2 %all_to_all.10 = bf16[8,128,2,128]{3,1,0,2:T(8,128)(2,1)S(1)} all-to-all(bf16[8,128,2,128]{3,1,0,2:T(8,128)(2,1)S(1)} %copy.24), channel_id=1, replica_groups=mesh['groups'=2,'row'=8,'col'=2] {'col'}, dimensions={2} | all-to-all | bytes 1048576 | tf_op jit(solution)/shard_map/all_to_all | solution.py:42
  35.4 0.3 copy.25
  35.7 1.3 convolution_add_fusion.1
  37.1 0.0 reduce-scatter.3.cloned.1.call-update
  37.1 0.0 reduce-scatter.5.cloned.1.call-start
  37.2 0.1 copy.26
  37.3 0.0 copy-start.4
  37.3 0.7 copy-done.4
  37.9 0.6 dynamic-slice
  38.5 0.0 copy-start.3
  39.2 0.0 copy-done.3
  39.2 15.0 %convert_reduce_fusion.1 = f32[1024]{0:T(1024)S(1)} fusion(bf16[1024,2,128]{2,1,0:T(2,128)(2,1)S(1)} %copy-done, pred[1024,2]{1,0:T(8,128)(4,1)S(1)} %bitcast.38), kind=kLoop, calls=%fused_computation.3 | loop fusion | flops 785408 | bytes 530432 | tf_op jit(solution)/shard_map/reduce_sum | solution.py:32
  54.2 0.1 convert_reduce_fusion
  54.3 19.6 %all-reduce = f32[1024]{0:T(1024)S(1)} all-reduce(f32[1024]{0:T(1024)S(1)} %bitcast_add_fusion), channel_id=3, replica_groups=mesh['groups'=2,'row'=8,'col'=2] {'row'}, use_global_device_ids=true, to_apply=%region_3.4.clone | all-reduce | flops 1024 | bytes 8192
  73.9 0.0 copy-start.2
  73.9 0.1 fusion.5
  73.9 26.3 %reduce-scatter.3.cloned.1.call-done = f32[128,256]{1,0:T(8,128)} async-done(((f32[1024,256]{1,0:T(8,128)}), f32[128,256]{1,0:T(8,128)}) %reduce-scatter.3.cloned.1.call-update) | async-done | bytes 131088 | tf_op jit(solution)/shard_map/reduce_scatter | solution.py:26
  100.2 0.0 copy-done.2
  100.2 1.0 add_convert_fusion.1
  101.2 1.9 %all_gather.7 = bf16[256,256]{1,0:T(8,128)(2,1)S(1)} all-gather(bf16[128,256]{1,0:T(8,128)(2,1)S(1)} %add_convert_fusion.1), channel_id=1, replica_groups=mesh['groups'=2,'row'=8,'col'=2] {'col'}, dimensions={0}, use_global_device_ids=true | all-gather | bytes 196608 | tf_op jit(solution)/shard_map/all_gather | solution.py:21
  103.1 0.4 fusion.7
  103.5 1.3 convolution_add_fusion
  104.8 0.0 reduce-scatter.5.cloned.1.call-update
  104.9 63.0 %reduce-scatter.5.cloned.1.call-done = f32[128,256]{1,0:T(8,128)} async-done(((f32[1024,256]{1,0:T(8,128)}), f32[128,256]{1,0:T(8,128)}) %reduce-scatter.5.cloned.1.call-update) | async-done | bytes 131088 | tf_op jit(solution)/shard_map/reduce_scatter | solution.py:26
  167.9 1.7 add_convert_fusion
  (5 shorter events, 0.1 us)
Async XLA Ops:
  9.3 7.5 %copy-start = (bf16[1024,2,128]{2,1,0:T(2,128)(2,1)S(1)}, bf16[1024,2,128]{2,1,0:T(2,128)(2,1)}, u32[]{:S(2)}) copy-start(bf16[1024,2,128]{2,1,0:T(2,128)(2,1)} %param.5) | copy-start | bytes 1572868
  9.3 21.9 %all-to-all-start = ((bf16[8,128,2,128]{3,1,2,0:T(8,128)(2,1)}), bf16[8,128,2,128]{3,1,2,0:T(8,128)(2,1)S(1)}, u32[]{:S(2)}, u32[]{:S(2)}) async-start(bf16[8,128,2,128]{3,1,2,0:T(8,128)(2,1)} %copy.23), calls=%async_computation | async-start | bytes 1048576 | tf_op jit(solution)/shard_map/all_to_all | solution.py:43
  16.7 0.8 copy-start.1
  16.7 83.5 %reduce-scatter.3.cloned.1.call-start = ((), (), s32[]{:S(2)}) async-start(), calls=%async_computation.4 | async-start | bytes 1179648 | tf_op jit(solution)/shard_map/reduce_scatter | solution.py:26
  37.1 130.8 %reduce-scatter.5.cloned.1.call-start = ((), (), s32[]{:S(2)}) async-start(), calls=%async_computation.5 | async-start | bytes 1179648 | tf_op jit(solution)/shard_map/reduce_scatter | solution.py:26
  37.3 0.7 copy-start.4
  38.5 0.7 copy-start.3
  73.9 26.3 %copy-start.2 = (s32[128]{0:T(128)S(1)}, s32[128]{0:T(128)}, u32[]{:S(2)}) copy-start(s32[128]{0:T(128)} %param.8) | copy-start | bytes 1540
Sparse Core Ops, SparseCore 0:
  37.2 62.9 reduce-scatter.2
  105.0 62.8 reduce-scatter.4
where the time goes:
time: 177 us; the launch traced here: 176 us
  waiting for transfers between devices  100 us (56%)
  blocking collectives  27.5 us (16%)
  other arithmetic  18.8 us (11%)
  between operations  14.2 us (8%)
  starting transfers between devices  7.5 us (4%)
  local copies, waits for them, and re-layouts  4.63 us (3%)
  matrix products  3.39 us (2%)
    reduce_scatter x2, waiting for transfers between devices, narrow_spread(): return lax.psum_scatter(total, 'row', scatter_dimension=0, tiled=True)  89.3 us
    unnamed x1, blocking collectives  19.6 us
    reduce_sum x2, other arithmetic, row_degree(): totals = totals + jnp.sum(matrix, axis=1, dtype=jnp.float32)  15 us
    all_to_all x1, waiting for transfers between devices, on_device(): lax.all_to_all(shaped, 'row', split_axis=0, concat_axis=0, tiled=True)  11.1 us
    all_to_all x1, starting transfers between devices, on_device(): lax.all_to_all(shaped, 'row', split_axis=0, concat_axis=0, tiled=True)  7.41 us
    all_to_all x1, blocking collectives, on_device(): lax.all_to_all(lax.all_to_all(shaped, 'row', split_axis=0, concat_axis=0,...  4.15 us
    all_gather x2, blocking collectives, narrow_spread(): panels = lax.all_gather(current, 'col', axis=0, tiled=True)  3.79 us
  transfers between devices with their start and end apart: 3, of which 3 were waited for; matrix products, arithmetic and copies ran while one was open for 10% of the time, Pallas kernels for 0%

commit v1 on v0

v1 whole, which is shorter than its diff:
```python
import jax
import jax.numpy as jnp
from jax import lax
from jax.experimental import pallas as pl
from jax.experimental.pallas import tpu as pltpu
from jax.sharding import PartitionSpec as P

ITERS = 2
CARRY = 0.8
LANES = 128


def gather_rows(own):
    count = lax.axis_size("row")
    pieces = [own]
    for k in range(1, count):
        pieces.append(lax.ppermute(own, "row", [(i, i ^ k) for i in range(count)]))
    return pieces


def swap_cores(value):
    return lax.ppermute(value, "col", [(0, 1), (1, 0)])


def spread_kernel(with_degree, row_ref, here_ref, there_ref, *refs):
    pieces, (keep_ref, give_ref, gathered) = refs[:-3], refs[-3:]
    row, col = row_ref[0], row_ref[1]
    count = len(pieces)
    width, classes = pieces[0].shape
    for k, piece in enumerate(pieces):
        gathered[lax.bitwise_xor(row, k), :, :classes] = piece[...]
    if with_degree:
        gathered[:, :, classes:] = jnp.ones((count, width, LANES), jnp.bfloat16)
    columns = keep_ref.shape[1]

    def side(s):
        def step(r, total):
            values = gathered[r]
            total += lax.dot_general(
                here_ref[r, s], values, (((0,), (0,)), ((), ())), preferred_element_type=jnp.float32
            )
            return total + jnp.dot(there_ref[r, s], values, preferred_element_type=jnp.float32)

        return lax.fori_loop(0, count, step, jnp.zeros((width, columns), jnp.float32), unroll=min(count, 8))

    keep_ref[...] = side(col)
    give_ref[...] = side(1 - col)


def spread_parts(position, here, there, pieces, with_degree):
    width, classes = pieces[0].shape
    columns = classes + (LANES if with_degree else 0)
    count = len(pieces)
    vmem = pl.BlockSpec(memory_space=pltpu.VMEM)
    return pl.pallas_call(
        lambda *refs: spread_kernel(with_degree, *refs),
        out_shape=[jax.ShapeDtypeStruct((width, columns), jnp.float32)] * 2,
        in_specs=[pl.BlockSpec(memory_space=pltpu.SMEM)] + [vmem] * (2 + count),
        out_specs=[vmem, vmem],
        scratch_shapes=[pltpu.VMEM((count, width, columns), jnp.bfloat16)],
        compiler_params=pltpu.CompilerParams(vmem_limit_bytes=40 * 1024 * 1024),
        cost_estimate=pl.CostEstimate(
            flops=8 * count * width * width * columns, bytes_accessed=2 * here.size * 2, transcendentals=0
        ),
    )(position, here, there, *pieces)


def on_device(affinity, block_live, labels, seed_class, seed_mask):
    stripe, sides, width = affinity.shape
    count = stripe // width
    classes = labels.shape[1]
    shaped = affinity.reshape(count, width, sides, width)
    keep = block_live[:, None, :, :] == 1
    stored = jnp.where(keep, shaped, jnp.zeros_like(shaped)).transpose(0, 2, 1, 3)
    mirror = lax.all_to_all(
        stored.reshape(count * sides, width, width), ("row", "col"), split_axis=0, concat_axis=0, tiled=True
    ).reshape(stored.shape)

    slots = lax.broadcasted_iota(jnp.int32, (width, classes), 1)
    is_seed = (seed_class[:, None] == slots) & (seed_mask[:, None] == 1)
    seed_rows = jnp.where(is_seed, 1.0, 0.0).astype(jnp.float32)
    position = jnp.stack([lax.axis_index("row"), lax.axis_index("col")]).astype(jnp.int32)

    current = labels
    degree = None
    for step in range(ITERS):
        pieces = gather_rows(current)
        kept, given = spread_parts(position, stored, mirror, pieces, step == 0)
        spread = kept + swap_cores(given)
        if step == 0:
            degree = 1.0 + 0.5 * spread[:, classes : classes + 1]
            spread = spread[:, :classes]
        mixed = CARRY * (0.5 * spread + current.astype(jnp.float32)) / degree
        current = (mixed + (1.0 - CARRY) * seed_rows).astype(jnp.bfloat16)
    return current


def solution(mesh):
    return jax.shard_map(
        on_device,
        mesh=mesh,
        in_specs=(
            P(("groups", "col"), None, "row"),
            P(("groups", "col"), None, "row"),
            P(("groups", "col", "row"), None),
            P(("groups", "col", "row")),
            P(("groups", "col", "row")),
        ),
        out_specs=P(("groups", "col", "row"), None),
        check_vma=False,
    )
```

time: 177 us -> 59.3 us (0.34)
  waiting for transfers between devices: 100 us -> 16.1 us
  blocking collectives: 27.5 us -> 0 us
  starting transfers between devices: 7.5 us -> 35 us
  other arithmetic: 18.8 us -> 3.84 us
  between operations: 14.2 us -> 0.12 us
  local copies, waits for them, and re-layouts: 4.63 us -> 1.22 us
  matrix products: 3.39 us -> 0 us
  Pallas kernels: 0 us -> 2.82 us
    reduce_scatter x2 -> x0, waiting for transfers between devices: 89.3 us -> none  [narrow_spread(): return lax.psum_scatter(total, 'row', scatter_dimension=0, tiled=True)]
    ppermute x0 -> x16, starting transfers between devices: none -> 27.4 us  [the longest x14 27.3 us: gather_rows(): pieces.append(lax.ppermute(own, 'row', [(i, i ^ k) for i in range(count)]))]
    unnamed x1 -> x0, blocking collectives: 19.6 us -> none
    ppermute x0 -> x16, waiting for transfers between devices: none -> 16.1 us  [the longest x14 13.9 us: gather_rows(): pieces.append(lax.ppermute(own, 'row', [(i, i ^ k) for i in range(count)]))]
    reduce_sum x2 -> x0, other arithmetic: 15 us -> none  [row_degree(): totals = totals + jnp.sum(matrix, axis=1, dtype=jnp.float32)]
    all_to_all x1, waiting for transfers between devices: 11.1 us -> 0.01 us  [on_device(): lax.all_to_all(stored.reshape(count * sides, width, width), ('row', 'col'...]
    all_to_all x1 -> x0, blocking collectives: 4.15 us -> none  [on_device(): lax.all_to_all(lax.all_to_all(shaped, 'row', split_axis=0, concat_axis=0,...]
    all_gather x2 -> x0, blocking collectives: 3.79 us -> none  [narrow_spread(): panels = lax.all_gather(current, 'col', axis=0, tiled=True)]
  transfers between devices with their start and end apart: 3 -> 17, of which waited for: 3 -> 8; matrix products, arithmetic and copies ran while one was open for 10% -> 0% of each run, Pallas kernels for 0% -> 0%
where the time goes in v1:
time: 59.3 us; the launch traced here: 59 us
  starting transfers between devices  35 us (59%)
  waiting for transfers between devices  16.1 us (27%)
  other arithmetic  3.84 us (6%)
  Pallas kernels  2.82 us (5%)
  local copies, waits for them, and re-layouts  1.22 us (2%)
    ppermute x14, starting transfers between devices, gather_rows(): pieces.append(lax.ppermute(own, 'row', [(i, i ^ k) for i in range(count)]))  27.3 us
    ppermute x14, waiting for transfers between devices, gather_rows(): pieces.append(lax.ppermute(own, 'row', [(i, i ^ k) for i in range(count)]))  13.9 us
    all_to_all x1, starting transfers between devices, on_device(): lax.all_to_all(stored.reshape(count * sides, width, width), ('row', 'col'...  7.52 us
    pallas_call x2, Pallas kernels, spread_parts(): pl.pallas_call(lambda *refs: spread_kernel(with_degree, *refs), out_shape...  2.82 us
    ppermute x2, waiting for transfers between devices, swap_cores(): return lax.ppermute(value, 'col', [(0, 1), (1, 0)])  2.19 us
    select_n x1, other arithmetic, on_device(): jnp.where(keep, shaped, jnp.zeros_like(shaped)).transpose(0, 2, 1, 3)  1.95 us
  transfers between devices with their start and end apart: 17, of which 8 were waited for; matrix products, arithmetic and copies ran while one was open for 0% of the time, Pallas kernels for 0%

profile of v1, /device:TPU:0, one launch (start us, length us, event | category | flops | bytes accessed | tf_op | source)
XLA Modules:
  0.0 59.0 jit_solution(15260832682971618372)
XLA Ops:
  0.0 0.7 %broadcast_compare_fusion = pred[8,2,1]{0,2,1:T(4,128)(4,1)S(1)} fusion(s32[8,2,1]{0,2,1:T(1,128)} %param.6), kind=kLoop, calls=%fused_computation.15 | loop fusion | flops 16 | bytes 80 | tf_op jit(solution)/shard_map/eq | solution.py:73
  0.7 0.1 copy.10
  0.8 2.0 %copy_select_fusion = bf16[8,128,2,128]{3,1,2,0:T(8,128)(2,1)} fusion(bf16[8,128,2,128]{3,2,1,0:T(2,128)(2,1)} %bitcast.11, pred[8,2]{1,0:T(8,128)(4,1)S(1)} %bitcast.13), kind=kLoop, calls=%fused_computation | loop fusion | flops 262144 | bytes 1048592 | tf_op jit(solution)/shard_map/jit(_where)/select_n | solution.py:74
  2.7 0.0 copy-start
  2.7 0.0 copy-start.1
  2.7 7.5 %all-to-all-start = ((bf16[16,128,128]{2,1,0:T(8,128)(2,1)}), bf16[16,128,128]{2,1,0:T(8,128)(2,1)S(1)}, u32[]{:S(2)}, u32[]{:S(2)}) async-start(bf16[16,128,128]{2,1,0:T(8,128)(2,1)} %bitcast.5), calls=%async_computation | async-start | bytes 1048576 | tf_op jit(solution)/shard_map/all_to_all | solution.py:75
  10.3 0.0 copy-done
  10.3 2.0 %collective-permute-start = (bf16[128,256]{1,0:T(8,128)(2,1)S(1)}, bf16[128,256]{1,0:T(8,128)(2,1)S(1)}, u32[]{:S(2)}, u32[]{:S(2)}) collective-permute-start(bf16[128,256]{1,0:T(8,128)(2,1)S(1)} %copy-done), channel_id=1, source_target_pairs={{0,2},{2,0},{4,6},{6,4},{8,10},{10,8},{12,14},{14,12},{1,3},{3,1},... | collective-permute-start | bytes 196616 | tf_op jit(solution)/shard_map/ppermute | solution.py:17
  12.3 1.5 %collective-permute-start.1 = (bf16[128,256]{1,0:T(8,128)(2,1)S(1)}, bf16[128,256]{1,0:T(8,128)(2,1)S(1)}, u32[]{:S(2)}, u32[]{:S(2)}) collective-permute-start(bf16[128,256]{1,0:T(8,128)(2,1)S(1)} %copy-done), channel_id=1, source_target_pairs={{0,4},{2,6},{4,0},{6,2},{8,12},{10,14},{12,8},{14,10},{1,5},{3,7},... | collective-permute-start | bytes 196616 | tf_op jit(solution)/shard_map/ppermute | solution.py:17
  13.7 0.1 collective-permute-start.2
  13.8 2.8 %collective-permute-start.3 = (bf16[128,256]{1,0:T(8,128)(2,1)S(1)}, bf16[128,256]{1,0:T(8,128)(2,1)S(1)}, u32[]{:S(2)}, u32[]{:S(2)}) collective-permute-start(bf16[128,256]{1,0:T(8,128)(2,1)S(1)} %copy-done), channel_id=1, source_target_pairs={{0,8},{2,10},{4,12},{6,14},{8,0},{10,2},{12,4},{14,6},{1,9},{3,11}... | collective-permute-start | bytes 196616 | tf_op jit(solution)/shard_map/ppermute | solution.py:17
  16.7 1.5 %collective-permute-start.4 = (bf16[128,256]{1,0:T(8,128)(2,1)S(1)}, bf16[128,256]{1,0:T(8,128)(2,1)S(1)}, u32[]{:S(2)}, u32[]{:S(2)}) collective-permute-start(bf16[128,256]{1,0:T(8,128)(2,1)S(1)} %copy-done), channel_id=1, source_target_pairs={{0,10},{2,8},{4,14},{6,12},{8,2},{10,0},{12,6},{14,4},{1,11},{3,9}... | collective-permute-start | bytes 196616 | tf_op jit(solution)/shard_map/ppermute | solution.py:17
  18.1 0.0 copy-done.1
  18.1 0.1 fusion.8.refs_1_
  18.2 0.0 collective-permute-done.refs_4_
  18.2 3.8 %collective-permute-start.5 = (bf16[128,256]{1,0:T(8,128)(2,1)S(1)}, bf16[128,256]{1,0:T(8,128)(2,1)S(1)}, u32[]{:S(2)}, u32[]{:S(2)}) collective-permute-start(bf16[128,256]{1,0:T(8,128)(2,1)S(1)} %copy-done), channel_id=1, source_target_pairs={{0,12},{2,14},{4,8},{6,10},{8,4},{10,6},{12,0},{14,2},{1,13},{3,15... | collective-permute-start | bytes 196616 | tf_op jit(solution)/shard_map/ppermute | solution.py:17
  22.1 0.4 collective-permute-done.1.refs_5_
  22.5 3.6 %collective-permute-start.6 = (bf16[128,256]{1,0:T(8,128)(2,1)S(1)}, bf16[128,256]{1,0:T(8,128)(2,1)S(1)}, u32[]{:S(2)}, u32[]{:S(2)}) collective-permute-start(bf16[128,256]{1,0:T(8,128)(2,1)S(1)} %copy-done), channel_id=1, source_target_pairs={{0,14},{2,12},{4,10},{6,8},{8,6},{10,4},{12,2},{14,0},{1,15},{3,13... | collective-permute-start | bytes 196616 | tf_op jit(solution)/shard_map/ppermute | solution.py:17
  26.1 0.1 pad_add_fusion.refs_0_
  26.1 0.0 collective-permute-done.2.refs_6_
  26.1 6.9 %collective-permute-done.3.refs_7_ = bf16[128,256]{1,0:T(8,128)(2,1)S(1)} collective-permute-done((bf16[128,256]{1,0:T(8,128)(2,1)S(1)}, bf16[128,256]{1,0:T(8,128)(2,1)S(1)}, u32[]{:S(2)}, u32[]{:S(2)}) %collective-permute-start.3) | collective-permute-done | bytes 65568 | tf_op jit(solution)/shard_map/ppermute | solution.py:17
  33.0 2.3 %collective-permute-done.4.refs_8_ = bf16[128,256]{1,0:T(8,128)(2,1)S(1)} collective-permute-done((bf16[128,256]{1,0:T(8,128)(2,1)S(1)}, bf16[128,256]{1,0:T(8,128)(2,1)S(1)}, u32[]{:S(2)}, u32[]{:S(2)}) %collective-permute-start.4) | collective-permute-done | bytes 65568 | tf_op jit(solution)/shard_map/ppermute | solution.py:17
  35.3 0.0 collective-permute-done.5.refs_9_
  35.3 0.0 collective-permute-done.6.refs_10_
  35.4 0.0 all-to-all-done
  35.4 1.6 %shard_map.55 = (f32[128,384]{1,0:T(8,128)S(1)}, f32[128,384]{1,0:T(8,128)S(1)}) custom-call(s32[2]{0:T(128)S(1)} %pad_add_fusion.refs_0_, bf16[8,2,128,128]{3,2,1,0:T(8,128)(2,1)S(1)} %fusion.8.refs_1_, bf16[8,2,128,128]{3,2,1,0:T(8,128)(2,1)S(1)} %bitcast.9, bf16[128,256]{1,0:T(8,128)(2,1)S(1)} %copy-done, ...), custom_call_target="tpu_custom_call" | custom-call | flops 402653184 | bytes 1048576 | tf_op jit(solution)/shard_map/pallas_call | solution.py:55
  36.9 0.0 copy-start.3
  36.9 0.1 collective-permute-start.7
  37.0 0.6 copy-done.3
  37.6 0.9 %collective-permute-done.7 = f32[128,384]{1,0:T(8,128)S(1)} collective-permute-done((f32[128,384]{1,0:T(8,128)S(1)}, f32[128,384]{1,0:T(8,128)S(1)}, u32[]{:S(2)}, u32[]{:S(2)}) %collective-permute-start.7) | collective-permute-done | bytes 196640 | tf_op jit(solution)/shard_map/ppermute | solution.py:22
  38.5 0.0 copy-start.2
  38.5 0.1 fusion.7
  38.6 0.5 copy-done.2
  39.1 0.1 fusion.4.refs_3_
  39.3 3.0 %collective-permute-start.10 = (bf16[128,256]{1,0:T(8,128)(2,1)S(1)}, bf16[128,256]{1,0:T(8,128)(2,1)S(1)}, u32[]{:S(2)}, u32[]{:S(2)}) collective-permute-start(bf16[128,256]{1,0:T(8,128)(2,1)S(1)} %fusion.4.refs_3_), channel_id=1, source_target_pairs={{0,6},{2,4},{4,2},{6,0},{8,14},{10,12},{12,10},{14,8},{1,7},{3,5},... | collective-permute-start | bytes 196616 | tf_op jit(solution)/shard_map/ppermute | solution.py:17
  42.2 0.1 collective-permute-start.11
  42.3 3.8 %collective-permute-start.12 = (bf16[128,256]{1,0:T(8,128)(2,1)S(1)}, bf16[128,256]{1,0:T(8,128)(2,1)S(1)}, u32[]{:S(2)}, u32[]{:S(2)}) collective-permute-start(bf16[128,256]{1,0:T(8,128)(2,1)S(1)} %fusion.4.refs_3_), channel_id=1, source_target_pairs={{0,10},{2,8},{4,14},{6,12},{8,2},{10,0},{12,6},{14,4},{1,11},{3,9}... | collective-permute-start | bytes 196616 | tf_op jit(solution)/shard_map/ppermute | solution.py:17
  46.0 1.4 %collective-permute-start.13 = (bf16[128,256]{1,0:T(8,128)(2,1)S(1)}, bf16[128,256]{1,0:T(8,128)(2,1)S(1)}, u32[]{:S(2)}, u32[]{:S(2)}) collective-permute-start(bf16[128,256]{1,0:T(8,128)(2,1)S(1)} %fusion.4.refs_3_), channel_id=1, source_target_pairs={{0,12},{2,14},{4,8},{6,10},{8,4},{10,6},{12,0},{14,2},{1,13},{3,15... | collective-permute-start | bytes 196616 | tf_op jit(solution)/shard_map/ppermute | solution.py:17
  47.5 2.4 %collective-permute-start.14 = (bf16[128,256]{1,0:T(8,128)(2,1)S(1)}, bf16[128,256]{1,0:T(8,128)(2,1)S(1)}, u32[]{:S(2)}, u32[]{:S(2)}) collective-permute-start(bf16[128,256]{1,0:T(8,128)(2,1)S(1)} %fusion.4.refs_3_), channel_id=1, source_target_pairs={{0,14},{2,12},{4,10},{6,8},{8,6},{10,4},{12,2},{14,0},{1,15},{3,13... | collective-permute-start | bytes 196616 | tf_op jit(solution)/shard_map/ppermute | solution.py:17
  49.9 0.0 collective-permute-done.10.refs_6_
  49.9 1.5 %collective-permute-start.8 = (bf16[128,256]{1,0:T(8,128)(2,1)S(1)}, bf16[128,256]{1,0:T(8,128)(2,1)S(1)}, u32[]{:S(2)}, u32[]{:S(2)}) collective-permute-start(bf16[128,256]{1,0:T(8,128)(2,1)S(1)} %fusion.4.refs_3_), channel_id=1, source_target_pairs={{0,2},{2,0},{4,6},{6,4},{8,10},{10,8},{12,14},{14,12},{1,3},{3,1},... | collective-permute-start | bytes 196616 | tf_op jit(solution)/shard_map/ppermute | solution.py:17
  51.3 0.0 collective-permute-done.11.refs_7_
  51.3 0.0 collective-permute-start.9
  51.3 3.9 %collective-permute-done.12.refs_8_ = bf16[128,256]{1,0:T(8,128)(2,1)S(1)} collective-permute-done((bf16[128,256]{1,0:T(8,128)(2,1)S(1)}, bf16[128,256]{1,0:T(8,128)(2,1)S(1)}, u32[]{:S(2)}, u32[]{:S(2)}) %collective-permute-start.12) | collective-permute-done | bytes 65568 | tf_op jit(solution)/shard_map/ppermute | solution.py:17
  55.2 0.0 collective-permute-done.13.refs_9_
  55.2 0.0 collective-permute-done.14.refs_10_
  55.2 0.2 collective-permute-done.8.refs_4_
  55.4 0.2 collective-permute-done.9.refs_5_
  55.6 1.3 %shard_map.56 = (f32[128,256]{1,0:T(8,128)S(1)}, f32[128,256]{1,0:T(8,128)S(1)}) custom-call(s32[2]{0:T(128)S(1)} %pad_add_fusion.refs_0_, bf16[8,2,128,128]{3,2,1,0:T(8,128)(2,1)S(1)} %fusion.8.refs_1_, bf16[8,2,128,128]{3,2,1,0:T(8,128)(2,1)S(1)} %bitcast.10, bf16[128,256]{1,0:T(8,128)(2,1)S(1)} %fusion.4.refs_3_, ...), custom_call_target="tpu_custom_call" | custom-call | flops 268435456 | bytes 1048576 | tf_op jit(solution)/shard_map/pallas_call | solution.py:55
  56.9 0.1 collective-permute-start.15
  57.0 1.3 %collective-permute-done.15 = f32[128,256]{1,0:T(8,128)S(1)} collective-permute-done((f32[128,256]{1,0:T(8,128)S(1)}, f32[128,256]{1,0:T(8,128)S(1)}, u32[]{:S(2)}, u32[]{:S(2)}) %collective-permute-start.15) | collective-permute-done | bytes 131104 | tf_op jit(solution)/shard_map/ppermute | solution.py:22
  58.3 0.8 %add_convert_fusion = bf16[128,256]{1,0:T(8,128)(2,1)} fusion(bf16[128,256]{1,0:T(8,128)(2,1)S(1)} %fusion.4.refs_3_, f32[128,256]{1,0:T(8,128)S(1)} %get-tuple-element.11, f32[128,256]{1,0:T(8,128)S(1)} %collective-permute-done.15, s32[128]{0:T(128)S(1)} %copy-done.2, f32[128]{0:T(128)S(1)} %fusion.7, pred[128]{0:T(512)(128)(4,1)S(1)} %broadcast_compare_fusion.1), kind=kLoop, calls=%fused_computation.6 | loop fusion | flops 393216 | bytes 394368 | tf_op jit(solution)/shard_map/convert_element_type | solution.py:94
  (2 shorter events, 0.0 us)
Async XLA Ops:
  2.7 7.5 %copy-start = (bf16[128,256]{1,0:T(8,128)(2,1)S(1)}, bf16[128,256]{1,0:T(8,128)(2,1)}, u32[]{:S(2)}) copy-start(bf16[128,256]{1,0:T(8,128)(2,1)} %refs_3_.1) | copy-start | bytes 196612
  2.7 15.4 %copy-start.1 = (bf16[1024,2,128]{2,1,0:T(2,128)(2,1)S(1)}, bf16[1024,2,128]{2,1,0:T(2,128)(2,1)}, u32[]{:S(2)}) copy-start(bf16[1024,2,128]{2,1,0:T(2,128)(2,1)} %param.5) | copy-start | bytes 1572868
  2.7 32.6 %all-to-all-start = ((bf16[16,128,128]{2,1,0:T(8,128)(2,1)}), bf16[16,128,128]{2,1,0:T(8,128)(2,1)S(1)}, u32[]{:S(2)}, u32[]{:S(2)}) async-start(bf16[16,128,128]{2,1,0:T(8,128)(2,1)} %bitcast.5), calls=%async_computation | async-start | bytes 1048576 | tf_op jit(solution)/shard_map/all_to_all | solution.py:75
  10.3 8.0 %collective-permute-start = (bf16[128,256]{1,0:T(8,128)(2,1)S(1)}, bf16[128,256]{1,0:T(8,128)(2,1)S(1)}, u32[]{:S(2)}, u32[]{:S(2)}) collective-permute-start(bf16[128,256]{1,0:T(8,128)(2,1)S(1)} %copy-done), channel_id=1, source_target_pairs={{0,2},{2,0},{4,6},{6,4},{8,10},{10,8},{12,14},{14,12},{1,3},{3,1},... | collective-permute-start | bytes 196616 | tf_op jit(solution)/shard_map/ppermute | solution.py:17
  12.3 10.2 %collective-permute-start.1 = (bf16[128,256]{1,0:T(8,128)(2,1)S(1)}, bf16[128,256]{1,0:T(8,128)(2,1)S(1)}, u32[]{:S(2)}, u32[]{:S(2)}) collective-permute-start(bf16[128,256]{1,0:T(8,128)(2,1)S(1)} %copy-done), channel_id=1, source_target_pairs={{0,4},{2,6},{4,0},{6,2},{8,12},{10,14},{12,8},{14,10},{1,5},{3,7},... | collective-permute-start | bytes 196616 | tf_op jit(solution)/shard_map/ppermute | solution.py:17
  13.7 12.4 %collective-permute-start.2 = (bf16[128,256]{1,0:T(8,128)(2,1)S(1)}, bf16[128,256]{1,0:T(8,128)(2,1)S(1)}, u32[]{:S(2)}, u32[]{:S(2)}) collective-permute-start(bf16[128,256]{1,0:T(8,128)(2,1)S(1)} %copy-done), channel_id=1, source_target_pairs={{0,6},{2,4},{4,2},{6,0},{8,14},{10,12},{12,10},{14,8},{1,7},{3,5},... | collective-permute-start | bytes 196616 | tf_op jit(solution)/shard_map/ppermute | solution.py:17
  13.8 19.2 %collective-permute-start.3 = (bf16[128,256]{1,0:T(8,128)(2,1)S(1)}, bf16[128,256]{1,0:T(8,128)(2,1)S(1)}, u32[]{:S(2)}, u32[]{:S(2)}) collective-permute-start(bf16[128,256]{1,0:T(8,128)(2,1)S(1)} %copy-done), channel_id=1, source_target_pairs={{0,8},{2,10},{4,12},{6,14},{8,0},{10,2},{12,4},{14,6},{1,9},{3,11}... | collective-permute-start | bytes 196616 | tf_op jit(solution)/shard_map/ppermute | solution.py:17
  16.7 18.7 %collective-permute-start.4 = (bf16[128,256]{1,0:T(8,128)(2,1)S(1)}, bf16[128,256]{1,0:T(8,128)(2,1)S(1)}, u32[]{:S(2)}, u32[]{:S(2)}) collective-permute-start(bf16[128,256]{1,0:T(8,128)(2,1)S(1)} %copy-done), channel_id=1, source_target_pairs={{0,10},{2,8},{4,14},{6,12},{8,2},{10,0},{12,6},{14,4},{1,11},{3,9}... | collective-permute-start | bytes 196616 | tf_op jit(solution)/shard_map/ppermute | solution.py:17
  18.2 17.1 %collective-permute-start.5 = (bf16[128,256]{1,0:T(8,128)(2,1)S(1)}, bf16[128,256]{1,0:T(8,128)(2,1)S(1)}, u32[]{:S(2)}, u32[]{:S(2)}) collective-permute-start(bf16[128,256]{1,0:T(8,128)(2,1)S(1)} %copy-done), channel_id=1, source_target_pairs={{0,12},{2,14},{4,8},{6,10},{8,4},{10,6},{12,0},{14,2},{1,13},{3,15... | collective-permute-start | bytes 196616 | tf_op jit(solution)/shard_map/ppermute | solution.py:17
  22.5 12.9 %collective-permute-start.6 = (bf16[128,256]{1,0:T(8,128)(2,1)S(1)}, bf16[128,256]{1,0:T(8,128)(2,1)S(1)}, u32[]{:S(2)}, u32[]{:S(2)}) collective-permute-start(bf16[128,256]{1,0:T(8,128)(2,1)S(1)} %copy-done), channel_id=1, source_target_pairs={{0,14},{2,12},{4,10},{6,8},{8,6},{10,4},{12,2},{14,0},{1,15},{3,13... | collective-permute-start | bytes 196616 | tf_op jit(solution)/shard_map/ppermute | solution.py:17
  36.9 0.7 %copy-start.3 = (s32[128]{0:T(128)S(1)}, s32[128]{0:T(128)}, u32[]{:S(2)}) copy-start(s32[128]{0:T(128)} %param.9) | copy-start | bytes 1540
  36.9 1.5 %collective-permute-start.7 = (f32[128,384]{1,0:T(8,128)S(1)}, f32[128,384]{1,0:T(8,128)S(1)}, u32[]{:S(2)}, u32[]{:S(2)}) collective-permute-start(f32[128,384]{1,0:T(8,128)S(1)} %get-tuple-element.10), channel_id=1, source_target_pairs={{0,1},{1,0},{2,3},{3,2},{4,5},{5,4},{6,7},{7,6},{8,9},{9,8},{10,11... | collective-permute-start | bytes 589832 | tf_op jit(solution)/shard_map/ppermute | solution.py:22
  38.5 0.7 %copy-start.2 = (s32[128]{0:T(128)S(1)}, s32[128]{0:T(128)}, u32[]{:S(2)}) copy-start(s32[128]{0:T(128)} %param.8) | copy-start | bytes 1540
  39.3 10.6 %collective-permute-start.10 = (bf16[128,256]{1,0:T(8,128)(2,1)S(1)}, bf16[128,256]{1,0:T(8,128)(2,1)S(1)}, u32[]{:S(2)}, u32[]{:S(2)}) collective-permute-start(bf16[128,256]{1,0:T(8,128)(2,1)S(1)} %fusion.4.refs_3_), channel_id=1, source_target_pairs={{0,6},{2,4},{4,2},{6,0},{8,14},{10,12},{12,10},{14,8},{1,7},{3,5},... | collective-permute-start | bytes 196616 | tf_op jit(solution)/shard_map/ppermute | solution.py:17
  42.2 9.1 %collective-permute-start.11 = (bf16[128,256]{1,0:T(8,128)(2,1)S(1)}, bf16[128,256]{1,0:T(8,128)(2,1)S(1)}, u32[]{:S(2)}, u32[]{:S(2)}) collective-permute-start(bf16[128,256]{1,0:T(8,128)(2,1)S(1)} %fusion.4.refs_3_), channel_id=1, source_target_pairs={{0,8},{2,10},{4,12},{6,14},{8,0},{10,2},{12,4},{14,6},{1,9},{3,11}... | collective-permute-start | bytes 196616 | tf_op jit(solution)/shard_map/ppermute | solution.py:17
  42.3 12.9 %collective-permute-start.12 = (bf16[128,256]{1,0:T(8,128)(2,1)S(1)}, bf16[128,256]{1,0:T(8,128)(2,1)S(1)}, u32[]{:S(2)}, u32[]{:S(2)}) collective-permute-start(bf16[128,256]{1,0:T(8,128)(2,1)S(1)} %fusion.4.refs_3_), channel_id=1, source_target_pairs={{0,10},{2,8},{4,14},{6,12},{8,2},{10,0},{12,6},{14,4},{1,11},{3,9}... | collective-permute-start | bytes 196616 | tf_op jit(solution)/shard_map/ppermute | solution.py:17
  46.0 9.2 %collective-permute-start.13 = (bf16[128,256]{1,0:T(8,128)(2,1)S(1)}, bf16[128,256]{1,0:T(8,128)(2,1)S(1)}, u32[]{:S(2)}, u32[]{:S(2)}) collective-permute-start(bf16[128,256]{1,0:T(8,128)(2,1)S(1)} %fusion.4.refs_3_), channel_id=1, source_target_pairs={{0,12},{2,14},{4,8},{6,10},{8,4},{10,6},{12,0},{14,2},{1,13},{3,15... | collective-permute-start | bytes 196616 | tf_op jit(solution)/shard_map/ppermute | solution.py:17
  47.5 7.7 %collective-permute-start.14 = (bf16[128,256]{1,0:T(8,128)(2,1)S(1)}, bf16[128,256]{1,0:T(8,128)(2,1)S(1)}, u32[]{:S(2)}, u32[]{:S(2)}) collective-permute-start(bf16[128,256]{1,0:T(8,128)(2,1)S(1)} %fusion.4.refs_3_), channel_id=1, source_target_pairs={{0,14},{2,12},{4,10},{6,8},{8,6},{10,4},{12,2},{14,0},{1,15},{3,13... | collective-permute-start | bytes 196616 | tf_op jit(solution)/shard_map/ppermute | solution.py:17
  49.9 5.5 %collective-permute-start.8 = (bf16[128,256]{1,0:T(8,128)(2,1)S(1)}, bf16[128,256]{1,0:T(8,128)(2,1)S(1)}, u32[]{:S(2)}, u32[]{:S(2)}) collective-permute-start(bf16[128,256]{1,0:T(8,128)(2,1)S(1)} %fusion.4.refs_3_), channel_id=1, source_target_pairs={{0,2},{2,0},{4,6},{6,4},{8,10},{10,8},{12,14},{14,12},{1,3},{3,1},... | collective-permute-start | bytes 196616 | tf_op jit(solution)/shard_map/ppermute | solution.py:17
  51.3 4.3 %collective-permute-start.9 = (bf16[128,256]{1,0:T(8,128)(2,1)S(1)}, bf16[128,256]{1,0:T(8,128)(2,1)S(1)}, u32[]{:S(2)}, u32[]{:S(2)}) collective-permute-start(bf16[128,256]{1,0:T(8,128)(2,1)S(1)} %fusion.4.refs_3_), channel_id=1, source_target_pairs={{0,4},{2,6},{4,0},{6,2},{8,12},{10,14},{12,8},{14,10},{1,5},{3,7},... | collective-permute-start | bytes 196616 | tf_op jit(solution)/shard_map/ppermute | solution.py:17
  56.9 1.4 %collective-permute-start.15 = (f32[128,256]{1,0:T(8,128)S(1)}, f32[128,256]{1,0:T(8,128)S(1)}, u32[]{:S(2)}, u32[]{:S(2)}) collective-permute-start(f32[128,256]{1,0:T(8,128)S(1)} %get-tuple-element.12), channel_id=1, source_target_pairs={{0,1},{1,0},{2,3},{3,2},{4,5},{5,4},{6,7},{7,6},{8,9},{9,8},{10,11... | collective-permute-start | bytes 393224 | tf_op jit(solution)/shard_map/ppermute | solution.py:22

commit v2 on v1

v2 whole, which is shorter than its diff:
```python
import jax
import jax.numpy as jnp
from jax import lax
from jax.experimental import pallas as pl
from jax.experimental.pallas import tpu as pltpu
from jax.sharding import PartitionSpec as P

ITERS = 2
CARRY = 0.8
LANES = 128


def gather_rows(own):
    return lax.all_gather(own, "row", axis=0, tiled=False)


def swap_cores(value):
    return lax.ppermute(value, "col", [(0, 1), (1, 0)])


def spread_kernel(with_degree, col_ref, here_ref, there_ref, values_ref, keep_ref, give_ref):
    col = col_ref[0]
    count, width, classes = values_ref.shape

    def side(s):
        def step(r, totals):
            mirrored = there_ref[r, s]
            total, sums = totals
            values = values_ref[r]
            total += lax.dot_general(
                here_ref[r, s], values, (((0,), (0,)), ((), ())), preferred_element_type=jnp.float32
            )
            total += jnp.dot(mirrored, values, preferred_element_type=jnp.float32)
            if with_degree:
                ones = jnp.ones((width, LANES), jnp.bfloat16)
                sums += lax.dot_general(
                    here_ref[r, s], ones, (((0,), (0,)), ((), ())), preferred_element_type=jnp.float32
                )
                sums += jnp.dot(mirrored, ones, preferred_element_type=jnp.float32)
            return total, sums

        zeros = jnp.zeros((width, classes), jnp.float32), jnp.zeros((width, LANES), jnp.float32)
        return lax.fori_loop(0, count, step, zeros, unroll=min(count, 8))

    for ref, s in ((keep_ref, col), (give_ref, 1 - col)):
        total, sums = side(s)
        ref[:, :classes] = total
        if with_degree:
            ref[:, classes:] = sums


def spread_parts(position, here, there, values, with_degree):
    count, width, classes = values.shape
    columns = classes + (LANES if with_degree else 0)
    vmem = pl.BlockSpec(memory_space=pltpu.VMEM)
    return pl.pallas_call(
        lambda *refs: spread_kernel(with_degree, *refs),
        out_shape=[jax.ShapeDtypeStruct((width, columns), jnp.float32)] * 2,
        in_specs=[pl.BlockSpec(memory_space=pltpu.SMEM)] + [vmem] * 3,
        out_specs=[vmem, vmem],
        compiler_params=pltpu.CompilerParams(vmem_limit_bytes=40 * 1024 * 1024),
        cost_estimate=pl.CostEstimate(
            flops=8 * count * width * width * columns, bytes_accessed=2 * here.size * 2, transcendentals=0
        ),
    )(position, here, there, values)


def on_device(affinity, block_live, labels, seed_class, seed_mask):
    stripe, sides, width = affinity.shape
    count = stripe // width
    classes = labels.shape[1]
    shaped = affinity.reshape(count, width, sides, width)
    keep = block_live[:, None, :, :] == 1
    stored = jnp.where(keep, shaped, jnp.zeros_like(shaped)).transpose(0, 2, 1, 3)
    mirror = lax.all_to_all(
        stored.reshape(count * sides, width, width), ("row", "col"), split_axis=0, concat_axis=0, tiled=True
    ).reshape(stored.shape)

    slots = lax.broadcasted_iota(jnp.int32, (width, classes), 1)
    is_seed = (seed_class[:, None] == slots) & (seed_mask[:, None] == 1)
    seed_rows = jnp.where(is_seed, 1.0, 0.0).astype(jnp.float32)
    position = lax.axis_index("col").astype(jnp.int32).reshape(1)

    current = labels
    degree = None
    for step in range(ITERS):
        values = gather_rows(current)
        kept, given = spread_parts(position, stored, mirror, values, step == 0)
        spread = kept + swap_cores(given)
        if step == 0:
            degree = 1.0 + 0.5 * spread[:, classes : classes + 1]
            spread = spread[:, :classes]
        mixed = CARRY * (0.5 * spread + current.astype(jnp.float32)) / degree
        current = (mixed + (1.0 - CARRY) * seed_rows).astype(jnp.bfloat16)
    return current


def solution(mesh):
    return jax.shard_map(
        on_device,
        mesh=mesh,
        in_specs=(
            P(("groups", "col"), None, "row"),
            P(("groups", "col"), None, "row"),
            P(("groups", "col", "row"), None),
            P(("groups", "col", "row")),
            P(("groups", "col", "row")),
        ),
        out_specs=P(("groups", "col", "row"), None),
        check_vma=False,
    )
```

time: 59.3 us -> 87.7 us (1.48)
  blocking collectives: 0 us -> 70.7 us
  starting transfers between devices: 35 us -> 7.66 us
  waiting for transfers between devices: 16.1 us -> 2.19 us
  Pallas kernels: 2.82 us -> 1.7 us
    all_gather x0 -> x2, blocking collectives: none -> 70.7 us  [gather_rows(): return lax.all_gather(own, 'row', axis=0, tiled=False)]
    ppermute x14 -> x0, starting transfers between devices: 27.3 us -> none  [gather_rows(): pieces.append(lax.ppermute(own, 'row', [(i, i ^ k) for i in range(count)]))]
    ppermute x14 -> x0, waiting for transfers between devices: 13.9 us -> none  [gather_rows(): pieces.append(lax.ppermute(own, 'row', [(i, i ^ k) for i in range(count)]))]
    pallas_call x2, Pallas kernels: 2.82 us -> 1.7 us  [spread_parts(): pl.pallas_call(lambda *refs: spread_kernel(with_degree, *refs), out_shape...]
  transfers between devices with their start and end apart: 17 -> 3, of which waited for: 8 -> 2; matrix products, arithmetic and copies ran while one was open for 0% -> 0% of each run, Pallas kernels for 0% -> 0%
where the time goes in v2:
time: 87.7 us; the launch traced here: 87.3 us
  blocking collectives  70.7 us (81%)
  starting transfers between devices  7.66 us (9%)
  other arithmetic  3.75 us (4%)
  waiting for transfers between devices  2.19 us (2%)
  Pallas kernels  1.7 us (2%)
  local copies, waits for them, and re-layouts  1.22 us (1%)
    all_gather x2, blocking collectives, gather_rows(): return lax.all_gather(own, 'row', axis=0, tiled=False)  70.7 us
    all_to_all x1, starting transfers between devices, on_device(): lax.all_to_all(stored.reshape(count * sides, width, width), ('row', 'col'...  7.52 us
    ppermute x2, waiting for transfers between devices, swap_cores(): return lax.ppermute(value, 'col', [(0, 1), (1, 0)])  2.19 us
    select_n x1, other arithmetic, on_device(): jnp.where(keep, shaped, jnp.zeros_like(shaped)).transpose(0, 2, 1, 3)  1.94 us
  transfers between devices with their start and end apart: 3, of which 2 were waited for; matrix products, arithmetic and copies ran while one was open for 0% of the time, Pallas kernels for 0%

profile of v2, /device:TPU:0, one launch (start us, length us, event | category | flops | bytes accessed | tf_op | source)
XLA Modules:
  0.0 87.3 jit_solution(10686389486893671700)
XLA Ops:
  0.0 0.7 broadcast_compare_fusion
  0.7 0.1 copy.10
  0.8 1.9 %copy_select_fusion = bf16[8,128,2,128]{3,1,2,0:T(8,128)(2,1)} fusion(bf16[8,128,2,128]{3,2,1,0:T(2,128)(2,1)} %bitcast.14, pred[8,2]{1,0:T(8,128)(4,1)S(1)} %bitcast.16), kind=kLoop, calls=%fused_computation | loop fusion | flops 262144 | bytes 1048592 | tf_op jit(solution)/shard_map/jit(_where)/select_n | solution.py:74
  2.7 0.0 copy-start.1
  2.7 7.5 %all-to-all-start = ((bf16[16,128,128]{2,1,0:T(8,128)(2,1)}), bf16[16,128,128]{2,1,0:T(8,128)(2,1)S(1)}, u32[]{:S(2)}, u32[]{:S(2)}) async-start(bf16[16,128,128]{2,1,0:T(8,128)(2,1)} %bitcast.4), calls=%async_computation | async-start | bytes 1048576 | tf_op jit(solution)/shard_map/all_to_all | solution.py:75
  10.2 0.0 copy-start
  10.3 0.0 copy-done.1
  10.3 39.4 %all-gather = bf16[1024,256]{1,0:T(8,128)(2,1)S(1)} all-gather(bf16[128,256]{1,0:T(8,128)(2,1)S(1)} %copy-done.1), channel_id=2, replica_groups=mesh['groups'=2,'row'=8,'col'=2] {'row'}, dimensions={0}, use_global_device_ids=true | all-gather | bytes 589824 | tf_op jit(solution)/shard_map/all_gather | solution.py:14
  49.7 0.0 copy-done
  49.7 0.1 fusion.8.refs_1_
  49.8 0.0 all-to-all-done
  49.8 1.0 %shard_map.55 = (f32[128,384]{1,0:T(8,128)S(1)}, f32[128,384]{1,0:T(8,128)S(1)}) custom-call(s32[1]{0:T(128)} %bitcast.refs_0_, bf16[8,2,128,128]{3,2,1,0:T(8,128)(2,1)S(1)} %fusion.8.refs_1_, bf16[8,2,128,128]{3,2,1,0:T(8,128)(2,1)S(1)} %bitcast.10, bf16[8,128,256]{2,1,0:T(8,128)(2,1)S(1)} %bitcast.12), custom_call_target="tpu_custom_call" | custom-call | flops 402653184 | bytes 1048576 | tf_op jit(solution)/shard_map/pallas_call | solution.py:56
  50.8 0.0 copy-start.3
  50.8 0.1 collective-permute-start
  50.9 0.6 copy-done.3
  51.4 0.9 collective-permute-done
  52.3 0.0 copy-start.2
  52.3 0.1 fusion.7
  52.5 0.5 copy-done.2
  53.0 0.1 fusion.4
  53.1 31.3 %all-gather.1 = bf16[1024,256]{1,0:T(8,128)(2,1)S(1)} all-gather(bf16[128,256]{1,0:T(8,128)(2,1)S(1)} %fusion.4), channel_id=3, replica_groups=mesh['groups'=2,'row'=8,'col'=2] {'row'}, dimensions={0}, use_global_device_ids=true | all-gather | bytes 589824 | tf_op jit(solution)/shard_map/all_gather | solution.py:14
  84.4 0.7 shard_map.56
  85.2 0.1 collective-permute-start.1
  85.2 1.3 %collective-permute-done.1 = f32[128,256]{1,0:T(8,128)S(1)} collective-permute-done((f32[128,256]{1,0:T(8,128)S(1)}, f32[128,256]{1,0:T(8,128)S(1)}, u32[]{:S(2)}, u32[]{:S(2)}) %collective-permute-start.1) | collective-permute-done | bytes 131104 | tf_op jit(solution)/shard_map/ppermute | solution.py:18
  86.6 0.8 add_convert_fusion
  (2 shorter events, 0.0 us)
Async XLA Ops:
  2.7 7.5 %copy-start.1 = (bf16[128,256]{1,0:T(8,128)(2,1)S(1)}, bf16[128,256]{1,0:T(8,128)(2,1)}, u32[]{:S(2)}) copy-start(bf16[128,256]{1,0:T(8,128)(2,1)} %param.7) | copy-start | bytes 196612
  2.7 47.1 %all-to-all-start = ((bf16[16,128,128]{2,1,0:T(8,128)(2,1)}), bf16[16,128,128]{2,1,0:T(8,128)(2,1)S(1)}, u32[]{:S(2)}, u32[]{:S(2)}) async-start(bf16[16,128,128]{2,1,0:T(8,128)(2,1)} %bitcast.4), calls=%async_computation | async-start | bytes 1048576 | tf_op jit(solution)/shard_map/all_to_all | solution.py:75
  10.2 39.4 %copy-start = (bf16[1024,2,128]{2,1,0:T(2,128)(2,1)S(1)}, bf16[1024,2,128]{2,1,0:T(2,128)(2,1)}, u32[]{:S(2)}) copy-start(bf16[1024,2,128]{2,1,0:T(2,128)(2,1)} %param.5) | copy-start | bytes 1572868
  50.8 0.7 copy-start.3
  50.8 1.5 %collective-permute-start = (f32[128,384]{1,0:T(8,128)S(1)}, f32[128,384]{1,0:T(8,128)S(1)}, u32[]{:S(2)}, u32[]{:S(2)}) collective-permute-start(f32[128,384]{1,0:T(8,128)S(1)} %get-tuple-element.10), channel_id=1, source_target_pairs={{0,1},{1,0},{2,3},{3,2},{4,5},{5,4},{6,7},{7,6},{8,9},{9,8},{10,11... | collective-permute-start | bytes 589832 | tf_op jit(solution)/shard_map/ppermute | solution.py:18
  52.3 0.7 copy-start.2
  85.2 1.4 %collective-permute-start.1 = (f32[128,256]{1,0:T(8,128)S(1)}, f32[128,256]{1,0:T(8,128)S(1)}, u32[]{:S(2)}, u32[]{:S(2)}) collective-permute-start(f32[128,256]{1,0:T(8,128)S(1)} %get-tuple-element.12), channel_id=1, source_target_pairs={{0,1},{1,0},{2,3},{3,2},{4,5},{5,4},{6,7},{7,6},{8,9},{9,8},{10,11... | collective-permute-start | bytes 393224 | tf_op jit(solution)/shard_map/ppermute | solution.py:18

commit v3 on v0

v3 whole, which is shorter than its diff:
```python
import jax
import jax.numpy as jnp
from jax import lax
from jax.experimental import pallas as pl
from jax.experimental.pallas import tpu as pltpu
from jax.sharding import PartitionSpec as P

ITERS = 2
CARRY = 0.8
SUBLANES = 8
VMEM_LIMIT = 48 * 1024 * 1024


def split_rows(count):
    inner = 1 << ((count.bit_length() - 1) // 2)
    return count // inner, inner


def swap_rows(value, shift):
    count = lax.axis_size("row")
    return lax.ppermute(value, "row", [(i, i ^ shift) for i in range(count)])


def swap_cores(value):
    return lax.ppermute(value, "col", [(0, 1), (1, 0)])


def call(kernel, out_shape, *operands, smem=0, flops=0):
    spaces = [pltpu.SMEM] * smem + [pltpu.VMEM] * (len(operands) - smem)
    size = sum(x.size * x.dtype.itemsize for x in operands)
    return pl.pallas_call(
        kernel,
        out_shape=out_shape,
        in_specs=[pl.BlockSpec(memory_space=space) for space in spaces],
        out_specs=jax.tree.map(lambda _: pl.BlockSpec(memory_space=pltpu.VMEM), out_shape),
        compiler_params=pltpu.CompilerParams(vmem_limit_bytes=VMEM_LIMIT),
        cost_estimate=pl.CostEstimate(flops=flops, bytes_accessed=size, transcendentals=0),
    )(*operands)


def prepare_kernel(z_count, y_count, place, live, tile, *outs):
    z, y, col = place[0], place[1], place[2]
    own_side, other_side, halves = outs[0], outs[1], outs[2:]
    width = tile.shape[1]
    out_row = lax.broadcasted_iota(jnp.int32, (2 * width, 2 * width), 0)
    in_row = lax.broadcasted_iota(jnp.int32, (2 * width, 2 * width), 1)
    side = lax.bitwise_xor((out_row >= width).astype(jnp.int32), col)
    spot = 2 * lax.rem(out_row, width) + side
    sort = jnp.where(in_row == spot, 1.0, 0.0).astype(jnp.bfloat16)
    for k in range(z_count):
        for j in range(y_count):
            block = lax.bitwise_xor(z, k) * y_count + lax.bitwise_xor(y, j)
            rows = tile[pl.ds(pl.multiple_of(block * 2 * width, 2 * width), 2 * width), :]
            sides = jnp.dot(sort, rows, preferred_element_type=jnp.float32)
            for i in range(2):
                keep = live[block, lax.bitwise_xor(col, i)] == 1
                piece = sides[i * width : (i + 1) * width]
                piece = jnp.where(keep, piece, jnp.zeros_like(piece)).astype(jnp.bfloat16)
                (own_side, other_side)[i][k, j] = piece
                halves[j][i, k] = piece


def merge_kernel(own_side, from_core, *outs):
    for k, out in enumerate(outs):
        out[0] = own_side[k + 1]
        out[1] = from_core[k + 1]


def spread_kernel(z_count, y_count, with_degree, *refs):
    halves, refs = refs[:y_count], refs[y_count:]
    own_side, from_core, refs = refs[0], refs[1], refs[2:]
    strips, refs = refs[: z_count - 1], refs[z_count - 1 :]
    pieces, refs = refs[:z_count], refs[z_count:]
    keeps, give = refs[:-1], refs[-1]
    values = jnp.concatenate([piece[...] for piece in pieces], axis=0)
    depth, classes = values.shape
    width = depth // z_count
    ones = jnp.ones((SUBLANES, depth), jnp.bfloat16)

    def strip(k, i, j):
        if k > 0:
            return strips[k - 1][i, j]
        return (own_side, from_core)[i][0, j]

    for i in range(2):
        for j in range(y_count):
            back = halves[j][i].reshape(depth, width)
            ahead = jnp.concatenate([strip(k, i, j) for k in range(z_count)], axis=1)
            total = lax.dot_general(back, values, (((0,), (0,)), ((), ())), preferred_element_type=jnp.float32)
            total += jnp.dot(ahead, values, preferred_element_type=jnp.float32)
            out = keeps[j] if i == 0 else give.at[j]
            out[:width, :] = total
            if with_degree:
                sums = jnp.dot(ones, back, preferred_element_type=jnp.float32)
                sums += lax.dot_general(ones, ahead, (((1,), (1,)), ((), ())), preferred_element_type=jnp.float32)
                out[width:, :] = jnp.concatenate([sums] * (classes // width), axis=1)


def on_device(affinity, block_live, labels, seed_class, seed_mask):
    stripe, sides, width = affinity.shape
    count = lax.axis_size("row")
    z_count, y_count = split_rows(count)
    classes = labels.shape[1]
    row = lax.axis_index("row").astype(jnp.int32)
    col = lax.axis_index("col").astype(jnp.int32)
    place = jnp.stack([row // y_count, row % y_count, col])

    blocks = jax.ShapeDtypeStruct((z_count, y_count, width, width), jnp.bfloat16)
    half = jax.ShapeDtypeStruct((2, z_count, width, width), jnp.bfloat16)
    own_side, other_side, *halves = call(
        lambda *refs: prepare_kernel(z_count, y_count, *refs),
        [blocks, blocks] + [half] * y_count,
        place,
        block_live.reshape(count, sides),
        affinity.reshape(stripe * sides, width),
        smem=2,
        flops=2 * 2 * stripe * width * 2 * width,
    )
    from_core = swap_cores(other_side)
    halves = [halves[0]] + [swap_rows(halves[j], j) for j in range(1, y_count)]
    strip = jax.ShapeDtypeStruct((2, y_count, width, width), jnp.bfloat16)
    strips = call(merge_kernel, [strip] * (z_count - 1), own_side, from_core)
    strips = [swap_rows(piece, (k + 1) * y_count) for k, piece in enumerate(strips)]

    slots = lax.broadcasted_iota(jnp.int32, (width, classes), 1)
    is_seed = (seed_class[:, None] == slots) & (seed_mask[:, None] == 1)
    seed_rows = jnp.where(is_seed, 1.0, 0.0).astype(jnp.float32)

    current = labels
    degree = None
    for step in range(ITERS):
        pieces = [current] + [swap_rows(current, k * y_count) for k in range(1, z_count)]
        height = width + (SUBLANES if step == 0 else 0)
        part = jax.ShapeDtypeStruct((height, classes), jnp.float32)
        parts = jax.ShapeDtypeStruct((y_count, height, classes), jnp.float32)
        *keeps, give = call(
            lambda *refs: spread_kernel(z_count, y_count, step == 0, *refs),
            [part] * y_count + [parts],
            *halves,
            own_side,
            from_core,
            *strips,
            *pieces,
            flops=2 * 2 * 2 * y_count * z_count * width * width * classes,
        )
        taken = swap_cores(give)
        spread = keeps[0] + taken[0]
        for j in range(1, y_count):
            spread = spread + swap_rows(keeps[j] + taken[j], j)
        if step == 0:
            degree = 1.0 + 0.5 * spread[width, :width][:, None]
        mixed = CARRY * (0.5 * spread[:width] + current.astype(jnp.float32)) / degree
        current = (mixed + (1.0 - CARRY) * seed_rows).astype(jnp.bfloat16)
    return current


def solution(mesh):
    return jax.shard_map(
        on_device,
        mesh=mesh,
        in_specs=(
            P(("groups", "col"), None, "row"),
            P(("groups", "col"), None, "row"),
            P(("groups", "col", "row"), None),
            P(("groups", "col", "row")),
            P(("groups", "col", "row")),
        ),
        out_specs=P(("groups", "col", "row"), None),
        check_vma=False,
    )
```

time: 177 us -> 53.7 us (0.30)
  waiting for transfers between devices: 100 us -> 25.9 us
  blocking collectives: 27.5 us -> 0 us
  other arithmetic: 18.8 us -> 1.03 us
  starting transfers between devices: 7.5 us -> 21.8 us
  between operations: 14.2 us -> 0.09 us
  matrix products: 3.39 us -> 0 us
  Pallas kernels: 0 us -> 2.13 us
  local copies, waits for them, and re-layouts: 4.63 us -> 2.51 us
    reduce_scatter x2 -> x0, waiting for transfers between devices: 89.3 us -> none  [narrow_spread(): return lax.psum_scatter(total, 'row', scatter_dimension=0, tiled=True)]
    ppermute x0 -> x15, waiting for transfers between devices: none -> 25.9 us  [the longest x12 22.9 us: swap_rows(): return lax.ppermute(value, 'row', [(i, i ^ shift) for i in range(count)])]
    ppermute x0 -> x15, starting transfers between devices: none -> 21.8 us  [the longest x12 21.1 us: swap_rows(): return lax.ppermute(value, 'row', [(i, i ^ shift) for i in range(count)])]
    unnamed x1 -> x0, blocking collectives: 19.6 us -> none
    reduce_sum x2 -> x0, other arithmetic: 15 us -> none  [row_degree(): totals = totals + jnp.sum(matrix, axis=1, dtype=jnp.float32)]
    all_to_all x1 -> x0, waiting for transfers between devices: 11.1 us -> none  [on_device(): lax.all_to_all(shaped, 'row', split_axis=0, concat_axis=0, tiled=True)]
    all_to_all x1 -> x0, starting transfers between devices: 7.41 us -> none  [on_device(): lax.all_to_all(shaped, 'row', split_axis=0, concat_axis=0, tiled=True)]
    all_to_all x1 -> x0, blocking collectives: 4.15 us -> none  [on_device(): lax.all_to_all(lax.all_to_all(shaped, 'row', split_axis=0, concat_axis=0,...]
  transfers between devices with their start and end apart: 3 -> 15, of which waited for: 3 -> 7; matrix products, arithmetic and copies ran while one was open for 10% -> 0% of each run, Pallas kernels for 0% -> 0%
where the time goes in v3:
time: 53.7 us; the launch traced here: 53.5 us
  waiting for transfers between devices  25.9 us (48%)
  starting transfers between devices  21.8 us (41%)
  local copies, waits for them, and re-layouts  2.51 us (5%)
  Pallas kernels  2.13 us (4%)
  other arithmetic  1.03 us (2%)
    ppermute x12, waiting for transfers between devices, swap_rows(): return lax.ppermute(value, 'row', [(i, i ^ shift) for i in range(count)])  22.9 us
    ppermute x12, starting transfers between devices, swap_rows(): return lax.ppermute(value, 'row', [(i, i ^ shift) for i in range(count)])  21.1 us
    ppermute x3, waiting for transfers between devices, swap_cores(): return lax.ppermute(value, 'col', [(0, 1), (1, 0)])  3.07 us
    unnamed x10, local copies, waits for them, and re-layouts  2.43 us
    pallas_call x4, Pallas kernels, call(): pl.pallas_call(kernel, out_shape=out_shape, in_specs=[pl.BlockSpec(memory...  2.13 us
  transfers between devices with their start and end apart: 15, of which 7 were waited for; matrix products, arithmetic and copies ran while one was open for 0% of the time, Pallas kernels for 0%

profile of v3, /device:TPU:0, one launch (start us, length us, event | category | flops | bytes accessed | tf_op | source)
XLA Modules:
  0.0 53.5 jit_solution(14989596789526332990)
XLA Ops:
  0.0 0.0 copy-start.3
  0.0 0.7 %copy-done.3 = s32[8,2,1]{0,2,1:T(1,128)S(1)} copy-done((s32[8,2,1]{0,2,1:T(1,128)S(1)}, s32[8,2,1]{0,2,1:T(1,128)}, u32[]{:S(2)}) %copy-start.3) | copy-done | bytes 88
  0.7 0.1 copy.6.refs_1_
  0.8 0.1 pad_add_fusion.refs_0_
  0.8 0.0 copy-start
  0.8 1.0 %copy-done = bf16[1024,2,128]{2,1,0:T(2,128)(2,1)S(1)} copy-done((bf16[1024,2,128]{2,1,0:T(2,128)(2,1)S(1)}, bf16[1024,2,128]{2,1,0:T(2,128)(2,1)}, u32[]{:S(2)}) %copy-start) | copy-done | bytes 524312
  1.9 0.0 copy-start.1
  1.9 1.0 %shard_map.55 = (bf16[4,2,128,128]{3,2,1,0:T(8,128)(2,1)S(1)}, bf16[4,2,128,128]{3,2,1,0:T(8,128)(2,1)S(1)}, bf16[2,4,128,128]{3,2,1,0:T(8,128)(2,1)S(1)}, bf16[2,4,128,128]{3,2,1,0:T(8,128)(2,1)S(1)}) custom-call(s32[3]{0:T(128)S(1)} %pad_add_fusion.refs_0_, s32[8,2]{1,0:T(8,128)S(1)} %copy.6.refs_1_, bf16[2048,128]{1,0:T(8,128)(2,1)S(1)} %bitcast.39), custom_call_target="tpu_custom_call" | custom-call | flops 134217728 | bytes 524364 | tf_op jit(solution)/shard_map/pallas_call | solution.py:31
  2.9 0.5 collective-permute-start.1
  3.4 2.6 %collective-permute-start = (bf16[2,4,128,128]{3,2,1,0:T(8,128)(2,1)S(1)}, bf16[2,4,128,128]{3,2,1,0:T(8,128)(2,1)S(1)}, u32[]{:S(2)}, u32[]{:S(2)}) collective-permute-start(bf16[2,4,128,128]{3,2,1,0:T(8,128)(2,1)S(1)} %get-tuple-element.19), channel_id=1, source_target_pairs={{0,2},{2,0},{4,6},{6,4},{8,10},{10,8},{12,14},{14,12},{1,3},{3,1},... | collective-permute-start | bytes 786440 | tf_op jit(solution)/shard_map/ppermute | solution.py:21
  6.0 0.0 copy-done.1
  6.0 1.6 %collective-permute-start.5 = (bf16[128,256]{1,0:T(8,128)(2,1)S(1)}, bf16[128,256]{1,0:T(8,128)(2,1)S(1)}, u32[]{:S(2)}, u32[]{:S(2)}) collective-permute-start(bf16[128,256]{1,0:T(8,128)(2,1)S(1)} %copy-done.1), channel_id=1, source_target_pairs={{0,4},{2,6},{4,0},{6,2},{8,12},{10,14},{12,8},{14,10},{1,5},{3,7},... | collective-permute-start | bytes 196616 | tf_op jit(solution)/shard_map/ppermute | solution.py:21
  7.6 2.6 %collective-permute-start.6 = (bf16[128,256]{1,0:T(8,128)(2,1)S(1)}, bf16[128,256]{1,0:T(8,128)(2,1)S(1)}, u32[]{:S(2)}, u32[]{:S(2)}) collective-permute-start(bf16[128,256]{1,0:T(8,128)(2,1)S(1)} %copy-done.1), channel_id=1, source_target_pairs={{0,8},{2,10},{4,12},{6,14},{8,0},{10,2},{12,4},{14,6},{1,9},{3,11}... | collective-permute-start | bytes 196616 | tf_op jit(solution)/shard_map/ppermute | solution.py:21
  10.2 0.0 collective-permute-done.1.from_core.refs_3_
  10.2 0.5 collective-permute-start.2
  10.7 0.3 collective-permute-start.3
  11.1 0.0 collective-permute-done.5.refs_8_
  11.1 4.7 %collective-permute-start.4 = (bf16[2,2,128,128]{3,2,1,0:T(8,128)(2,1)S(1)}, bf16[2,2,128,128]{3,2,1,0:T(8,128)(2,1)S(1)}, u32[]{:S(2)}, u32[]{:S(2)}) collective-permute-start(bf16[2,2,128,128]{3,2,1,0:T(8,128)(2,1)S(1)} %get-tuple-element.24), channel_id=1, source_target_pairs={{0,12},{2,14},{4,8},{6,10},{8,4},{10,6},{12,0},{14,2},{1,13},{3,15... | collective-permute-start | bytes 393224 | tf_op jit(solution)/shard_map/ppermute | solution.py:21
  15.8 0.0 collective-permute-done.6.refs_9_
  15.8 1.5 %collective-permute-start.7 = (bf16[128,256]{1,0:T(8,128)(2,1)S(1)}, bf16[128,256]{1,0:T(8,128)(2,1)S(1)}, u32[]{:S(2)}, u32[]{:S(2)}) collective-permute-start(bf16[128,256]{1,0:T(8,128)(2,1)S(1)} %copy-done.1), channel_id=1, source_target_pairs={{0,12},{2,14},{4,8},{6,10},{8,4},{10,6},{12,0},{14,2},{1,13},{3,15... | collective-permute-start | bytes 196616 | tf_op jit(solution)/shard_map/ppermute | solution.py:21
  17.3 6.3 %collective-permute-done.7.refs_10_ = bf16[128,256]{1,0:T(8,128)(2,1)S(1)} collective-permute-done((bf16[128,256]{1,0:T(8,128)(2,1)S(1)}, bf16[128,256]{1,0:T(8,128)(2,1)S(1)}, u32[]{:S(2)}, u32[]{:S(2)}) %collective-permute-start.7) | collective-permute-done | bytes 65568 | tf_op jit(solution)/shard_map/ppermute | solution.py:21
  23.6 0.0 collective-permute-done.refs_1_
  23.6 0.0 collective-permute-done.2.refs_4_
  23.6 1.5 %collective-permute-done.3.refs_5_ = bf16[2,2,128,128]{3,2,1,0:T(8,128)(2,1)S(1)} collective-permute-done((bf16[2,2,128,128]{3,2,1,0:T(8,128)(2,1)S(1)}, bf16[2,2,128,128]{3,2,1,0:T(8,128)(2,1)S(1)}, u32[]{:S(2)}, u32[]{:S(2)}) %collective-permute-start.3) | collective-permute-done | bytes 131104 | tf_op jit(solution)/shard_map/ppermute | solution.py:21
  25.1 0.0 collective-permute-done.4.refs_6_
  25.1 0.6 %shard_map.57 = (f32[136,256]{1,0:T(8,128)S(1)}, f32[136,256]{1,0:T(8,128)S(1)}, f32[2,136,256]{2,1,0:T(8,128)S(1)}) custom-call(bf16[2,4,128,128]{3,2,1,0:T(8,128)(2,1)S(1)} %get-tuple-element.18.refs_0_, bf16[2,4,128,128]{3,2,1,0:T(8,128)(2,1)S(1)} %collective-permute-done.refs_1_, bf16[4,2,128,128]{3,2,1,0:T(8,128)(2,1)S(1)} %get-tuple-element.20.own_side.refs_2_, ...), custom_call_target="tpu_custom_call" | custom-call | flops 268435456 | bytes 1703936 | tf_op jit(solution)/shard_map/pallas_call | solution.py:31
  25.7 0.1 collective-permute-start.8
  25.8 1.5 %collective-permute-done.8 = f32[2,136,256]{2,1,0:T(8,128)S(1)} collective-permute-done((f32[2,136,256]{2,1,0:T(8,128)S(1)}, f32[2,136,256]{2,1,0:T(8,128)S(1)}, u32[]{:S(2)}, u32[]{:S(2)}) %collective-permute-start.8) | collective-permute-done | bytes 278560 | tf_op jit(solution)/shard_map/ppermute | solution.py:25
  27.4 0.0 copy-start.4
  27.4 0.6 %collective-permute-start.9 = (f32[136,256]{1,0:T(8,128)S(1)}, f32[136,256]{1,0:T(8,128)S(1)}, u32[]{:S(2)}, u32[]{:S(2)}) collective-permute-start(f32[136,256]{1,0:T(8,128)S(1)} %fusion), channel_id=1, source_target_pairs={{0,2},{2,0},{4,6},{6,4},{8,10},{10,8},{12,14},{14,12},{1,3},{3,1},... | collective-permute-start | bytes 417800 | tf_op jit(solution)/shard_map/ppermute | solution.py:21
  28.0 0.1 copy-done.4
  28.0 5.1 %collective-permute-done.9 = f32[136,256]{1,0:T(8,128)S(1)} collective-permute-done((f32[136,256]{1,0:T(8,128)S(1)}, f32[136,256]{1,0:T(8,128)S(1)}, u32[]{:S(2)}, u32[]{:S(2)}) %collective-permute-start.9) | collective-permute-done | bytes 139296 | tf_op jit(solution)/shard_map/ppermute | solution.py:21
  33.2 0.0 copy-start.2
  33.2 0.6 %copy-done.2 = s32[128]{0:T(128)S(1)} copy-done((s32[128]{0:T(128)S(1)}, s32[128]{0:T(128)}, u32[]{:S(2)}) %copy-start.2) | copy-done | bytes 536
  33.9 0.1 fusion.15.refs_7_
  34.0 3.6 %collective-permute-start.10 = (bf16[128,256]{1,0:T(8,128)(2,1)S(1)}, bf16[128,256]{1,0:T(8,128)(2,1)S(1)}, u32[]{:S(2)}, u32[]{:S(2)}) collective-permute-start(bf16[128,256]{1,0:T(8,128)(2,1)S(1)} %fusion.15.refs_7_), channel_id=1, source_target_pairs={{0,4},{2,6},{4,0},{6,2},{8,12},{10,14},{12,8},{14,10},{1,5},{3,7},... | collective-permute-start | bytes 196616 | tf_op jit(solution)/shard_map/ppermute | solution.py:21
  37.6 1.2 %collective-permute-start.11 = (bf16[128,256]{1,0:T(8,128)(2,1)S(1)}, bf16[128,256]{1,0:T(8,128)(2,1)S(1)}, u32[]{:S(2)}, u32[]{:S(2)}) collective-permute-start(bf16[128,256]{1,0:T(8,128)(2,1)S(1)} %fusion.15.refs_7_), channel_id=1, source_target_pairs={{0,8},{2,10},{4,12},{6,14},{8,0},{10,2},{12,4},{14,6},{1,9},{3,11}... | collective-permute-start | bytes 196616 | tf_op jit(solution)/shard_map/ppermute | solution.py:21
  38.8 1.4 %collective-permute-start.12 = (bf16[128,256]{1,0:T(8,128)(2,1)S(1)}, bf16[128,256]{1,0:T(8,128)(2,1)S(1)}, u32[]{:S(2)}, u32[]{:S(2)}) collective-permute-start(bf16[128,256]{1,0:T(8,128)(2,1)S(1)} %fusion.15.refs_7_), channel_id=1, source_target_pairs={{0,12},{2,14},{4,8},{6,10},{8,4},{10,6},{12,0},{14,2},{1,13},{3,15... | collective-permute-start | bytes 196616 | tf_op jit(solution)/shard_map/ppermute | solution.py:21
  40.2 0.0 collective-permute-done.10.refs_8_
  40.2 4.8 %collective-permute-done.11.refs_9_ = bf16[128,256]{1,0:T(8,128)(2,1)S(1)} collective-permute-done((bf16[128,256]{1,0:T(8,128)(2,1)S(1)}, bf16[128,256]{1,0:T(8,128)(2,1)S(1)}, u32[]{:S(2)}, u32[]{:S(2)}) %collective-permute-start.11) | collective-permute-done | bytes 65568 | tf_op jit(solution)/shard_map/ppermute | solution.py:21
  45.0 0.0 collective-permute-done.12.refs_10_
  45.0 0.4 shard_map.58
  45.5 0.1 collective-permute-start.13
  45.6 1.5 %collective-permute-done.13 = f32[2,128,256]{2,1,0:T(8,128)S(1)} collective-permute-done((f32[2,128,256]{2,1,0:T(8,128)S(1)}, f32[2,128,256]{2,1,0:T(8,128)S(1)}, u32[]{:S(2)}, u32[]{:S(2)}) %collective-permute-start.13) | collective-permute-done | bytes 262176 | tf_op jit(solution)/shard_map/ppermute | solution.py:25
  47.1 0.6 %collective-permute-start.14 = (f32[128,256]{1,0:T(8,128)S(1)}, f32[128,256]{1,0:T(8,128)S(1)}, u32[]{:S(2)}, u32[]{:S(2)}) collective-permute-start(f32[128,256]{1,0:T(8,128)S(1)} %fusion.3), channel_id=1, source_target_pairs={{0,2},{2,0},{4,6},{6,4},{8,10},{10,8},{12,14},{14,12},{1,3},{3,1},... | collective-permute-start | bytes 393224 | tf_op jit(solution)/shard_map/ppermute | solution.py:21
  47.7 5.0 %collective-permute-done.14 = f32[128,256]{1,0:T(8,128)S(1)} collective-permute-done((f32[128,256]{1,0:T(8,128)S(1)}, f32[128,256]{1,0:T(8,128)S(1)}, u32[]{:S(2)}, u32[]{:S(2)}) %collective-permute-start.14) | collective-permute-done | bytes 131104 | tf_op jit(solution)/shard_map/ppermute | solution.py:21
  52.7 0.8 %fusion.16 = bf16[128,256]{1,0:T(8,128)(2,1)} fusion(bf16[128,256]{1,0:T(8,128)(2,1)S(1)} %fusion.15.refs_7_, f32[128,256]{1,0:T(8,128)S(1)} %collective-permute-done.14, f32[128,256]{1,0:T(8,128)S(1)} %get-tuple-element.28, f32[2,128,256]{2,1,0:T(8,128)S(1)} %collective-permute-done.13, s32[128]{0:T(128)S(1)} %copy-done.2, f32[128]{0:T(128)S(1)} %fusion.19, ...), kind=kLoop, calls=%fused_computation.23 | loop fusion | flops 425984 | bytes 525440 | tf_op jit(solution)/shard_map/convert_element_type | solution.py:153
  (6 shorter events, 0.1 us)
Async XLA Ops:
  0.0 0.7 %copy-start.3 = (s32[8,2,1]{0,2,1:T(1,128)S(1)}, s32[8,2,1]{0,2,1:T(1,128)}, u32[]{:S(2)}) copy-start(s32[8,2,1]{0,2,1:T(1,128)} %param.6) | copy-start | bytes 196
  0.8 1.0 %copy-start = (bf16[1024,2,128]{2,1,0:T(2,128)(2,1)S(1)}, bf16[1024,2,128]{2,1,0:T(2,128)(2,1)}, u32[]{:S(2)}) copy-start(bf16[1024,2,128]{2,1,0:T(2,128)(2,1)} %param.5) | copy-start | bytes 1572868
  1.9 4.1 %copy-start.1 = (bf16[128,256]{1,0:T(8,128)(2,1)S(1)}, bf16[128,256]{1,0:T(8,128)(2,1)}, u32[]{:S(2)}) copy-start(bf16[128,256]{1,0:T(8,128)(2,1)} %refs_7_.1) | copy-start | bytes 196612
  2.9 7.3 %collective-permute-start.1 = (bf16[4,2,128,128]{3,2,1,0:T(8,128)(2,1)S(1)}, bf16[4,2,128,128]{3,2,1,0:T(8,128)(2,1)S(1)}, u32[]{:S(2)}, u32[]{:S(2)}) collective-permute-start(bf16[4,2,128,128]{3,2,1,0:T(8,128)(2,1)S(1)} %get-tuple-element.21), channel_id=1, source_target_pairs={{0,1},{1,0},{2,3},{3,2},{4,5},{5,4},{6,7},{7,6},{8,9},{9,8},{10,11... | collective-permute-start | bytes 786440 | tf_op jit(solution)/shard_map/ppermute | solution.py:25
  3.4 20.1 %collective-permute-start = (bf16[2,4,128,128]{3,2,1,0:T(8,128)(2,1)S(1)}, bf16[2,4,128,128]{3,2,1,0:T(8,128)(2,1)S(1)}, u32[]{:S(2)}, u32[]{:S(2)}) collective-permute-start(bf16[2,4,128,128]{3,2,1,0:T(8,128)(2,1)S(1)} %get-tuple-element.19), channel_id=1, source_target_pairs={{0,2},{2,0},{4,6},{6,4},{8,10},{10,8},{12,14},{14,12},{1,3},{3,1},... | collective-permute-start | bytes 786440 | tf_op jit(solution)/shard_map/ppermute | solution.py:21
  6.0 5.1 %collective-permute-start.5 = (bf16[128,256]{1,0:T(8,128)(2,1)S(1)}, bf16[128,256]{1,0:T(8,128)(2,1)S(1)}, u32[]{:S(2)}, u32[]{:S(2)}) collective-permute-start(bf16[128,256]{1,0:T(8,128)(2,1)S(1)} %copy-done.1), channel_id=1, source_target_pairs={{0,4},{2,6},{4,0},{6,2},{8,12},{10,14},{12,8},{14,10},{1,5},{3,7},... | collective-permute-start | bytes 196616 | tf_op jit(solution)/shard_map/ppermute | solution.py:21
  7.6 8.2 %collective-permute-start.6 = (bf16[128,256]{1,0:T(8,128)(2,1)S(1)}, bf16[128,256]{1,0:T(8,128)(2,1)S(1)}, u32[]{:S(2)}, u32[]{:S(2)}) collective-permute-start(bf16[128,256]{1,0:T(8,128)(2,1)S(1)} %copy-done.1), channel_id=1, source_target_pairs={{0,8},{2,10},{4,12},{6,14},{8,0},{10,2},{12,4},{14,6},{1,9},{3,11}... | collective-permute-start | bytes 196616 | tf_op jit(solution)/shard_map/ppermute | solution.py:21
  10.2 13.3 %collective-permute-start.2 = (bf16[2,2,128,128]{3,2,1,0:T(8,128)(2,1)S(1)}, bf16[2,2,128,128]{3,2,1,0:T(8,128)(2,1)S(1)}, u32[]{:S(2)}, u32[]{:S(2)}) collective-permute-start(bf16[2,2,128,128]{3,2,1,0:T(8,128)(2,1)S(1)} %get-tuple-element.22), channel_id=1, source_target_pairs={{0,4},{2,6},{4,0},{6,2},{8,12},{10,14},{12,8},{14,10},{1,5},{3,7},... | collective-permute-start | bytes 393224 | tf_op jit(solution)/shard_map/ppermute | solution.py:21
  10.7 14.4 %collective-permute-start.3 = (bf16[2,2,128,128]{3,2,1,0:T(8,128)(2,1)S(1)}, bf16[2,2,128,128]{3,2,1,0:T(8,128)(2,1)S(1)}, u32[]{:S(2)}, u32[]{:S(2)}) collective-permute-start(bf16[2,2,128,128]{3,2,1,0:T(8,128)(2,1)S(1)} %get-tuple-element.23), channel_id=1, source_target_pairs={{0,8},{2,10},{4,12},{6,14},{8,0},{10,2},{12,4},{14,6},{1,9},{3,11}... | collective-permute-start | bytes 393224 | tf_op jit(solution)/shard_map/ppermute | solution.py:21
  11.1 14.0 %collective-permute-start.4 = (bf16[2,2,128,128]{3,2,1,0:T(8,128)(2,1)S(1)}, bf16[2,2,128,128]{3,2,1,0:T(8,128)(2,1)S(1)}, u32[]{:S(2)}, u32[]{:S(2)}) collective-permute-start(bf16[2,2,128,128]{3,2,1,0:T(8,128)(2,1)S(1)} %get-tuple-element.24), channel_id=1, source_target_pairs={{0,12},{2,14},{4,8},{6,10},{8,4},{10,6},{12,0},{14,2},{1,13},{3,15... | collective-permute-start | bytes 393224 | tf_op jit(solution)/shard_map/ppermute | solution.py:21
  15.8 7.8 %collective-permute-start.7 = (bf16[128,256]{1,0:T(8,128)(2,1)S(1)}, bf16[128,256]{1,0:T(8,128)(2,1)S(1)}, u32[]{:S(2)}, u32[]{:S(2)}) collective-permute-start(bf16[128,256]{1,0:T(8,128)(2,1)S(1)} %copy-done.1), channel_id=1, source_target_pairs={{0,12},{2,14},{4,8},{6,10},{8,4},{10,6},{12,0},{14,2},{1,13},{3,15... | collective-permute-start | bytes 196616 | tf_op jit(solution)/shard_map/ppermute | solution.py:21
  25.7 1.6 %collective-permute-start.8 = (f32[2,136,256]{2,1,0:T(8,128)S(1)}, f32[2,136,256]{2,1,0:T(8,128)S(1)}, u32[]{:S(2)}, u32[]{:S(2)}) collective-permute-start(f32[2,136,256]{2,1,0:T(8,128)S(1)} %get-tuple-element.26), channel_id=1, source_target_pairs={{0,1},{1,0},{2,3},{3,2},{4,5},{5,4},{6,7},{7,6},{8,9},{9,8},{10,11... | collective-permute-start | bytes 835592 | tf_op jit(solution)/shard_map/ppermute | solution.py:25
  27.4 0.7 %copy-start.4 = (s32[128]{0:T(128)S(1)}, s32[128]{0:T(128)}, u32[]{:S(2)}) copy-start(s32[128]{0:T(128)} %param.9) | copy-start | bytes 1540
  27.4 5.8 %collective-permute-start.9 = (f32[136,256]{1,0:T(8,128)S(1)}, f32[136,256]{1,0:T(8,128)S(1)}, u32[]{:S(2)}, u32[]{:S(2)}) collective-permute-start(f32[136,256]{1,0:T(8,128)S(1)} %fusion), channel_id=1, source_target_pairs={{0,2},{2,0},{4,6},{6,4},{8,10},{10,8},{12,14},{14,12},{1,3},{3,1},... | collective-permute-start | bytes 417800 | tf_op jit(solution)/shard_map/ppermute | solution.py:21
  33.2 0.7 %copy-start.2 = (s32[128]{0:T(128)S(1)}, s32[128]{0:T(128)}, u32[]{:S(2)}) copy-start(s32[128]{0:T(128)} %param.8) | copy-start | bytes 1540
  34.0 6.2 %collective-permute-start.10 = (bf16[128,256]{1,0:T(8,128)(2,1)S(1)}, bf16[128,256]{1,0:T(8,128)(2,1)S(1)}, u32[]{:S(2)}, u32[]{:S(2)}) collective-permute-start(bf16[128,256]{1,0:T(8,128)(2,1)S(1)} %fusion.15.refs_7_), channel_id=1, source_target_pairs={{0,4},{2,6},{4,0},{6,2},{8,12},{10,14},{12,8},{14,10},{1,5},{3,7},... | collective-permute-start | bytes 196616 | tf_op jit(solution)/shard_map/ppermute | solution.py:21
  37.6 7.5 %collective-permute-start.11 = (bf16[128,256]{1,0:T(8,128)(2,1)S(1)}, bf16[128,256]{1,0:T(8,128)(2,1)S(1)}, u32[]{:S(2)}, u32[]{:S(2)}) collective-permute-start(bf16[128,256]{1,0:T(8,128)(2,1)S(1)} %fusion.15.refs_7_), channel_id=1, source_target_pairs={{0,8},{2,10},{4,12},{6,14},{8,0},{10,2},{12,4},{14,6},{1,9},{3,11}... | collective-permute-start | bytes 196616 | tf_op jit(solution)/shard_map/ppermute | solution.py:21
  38.8 6.2 %collective-permute-start.12 = (bf16[128,256]{1,0:T(8,128)(2,1)S(1)}, bf16[128,256]{1,0:T(8,128)(2,1)S(1)}, u32[]{:S(2)}, u32[]{:S(2)}) collective-permute-start(bf16[128,256]{1,0:T(8,128)(2,1)S(1)} %fusion.15.refs_7_), channel_id=1, source_target_pairs={{0,12},{2,14},{4,8},{6,10},{8,4},{10,6},{12,0},{14,2},{1,13},{3,15... | collective-permute-start | bytes 196616 | tf_op jit(solution)/shard_map/ppermute | solution.py:21
  45.5 1.6 %collective-permute-start.13 = (f32[2,128,256]{2,1,0:T(8,128)S(1)}, f32[2,128,256]{2,1,0:T(8,128)S(1)}, u32[]{:S(2)}, u32[]{:S(2)}) collective-permute-start(f32[2,128,256]{2,1,0:T(8,128)S(1)} %get-tuple-element.29), channel_id=1, source_target_pairs={{0,1},{1,0},{2,3},{3,2},{4,5},{5,4},{6,7},{7,6},{8,9},{9,8},{10,11... | collective-permute-start | bytes 786440 | tf_op jit(solution)/shard_map/ppermute | solution.py:25
  47.1 5.6 %collective-permute-start.14 = (f32[128,256]{1,0:T(8,128)S(1)}, f32[128,256]{1,0:T(8,128)S(1)}, u32[]{:S(2)}, u32[]{:S(2)}) collective-permute-start(f32[128,256]{1,0:T(8,128)S(1)} %fusion.3), channel_id=1, source_target_pairs={{0,2},{2,0},{4,6},{6,4},{8,10},{10,8},{12,14},{14,12},{1,3},{3,1},... | collective-permute-start | bytes 393224 | tf_op jit(solution)/shard_map/ppermute | solution.py:21

commit v4 on v3

v4 whole, which is shorter than its diff:
```python
import jax
import jax.numpy as jnp
from jax import lax
from jax.experimental import pallas as pl
from jax.experimental.pallas import tpu as pltpu
from jax.sharding import PartitionSpec as P

ITERS = 2
CARRY = 0.8
SUBLANES = 8
VMEM_LIMIT = 48 * 1024 * 1024


def split_rows(count):
    inner = 1 << ((count.bit_length() - 1) // 2)
    return count // inner, inner


def swap_rows(value, shift):
    count = lax.axis_size("row")
    return lax.ppermute(value, "row", [(i, i ^ shift) for i in range(count)])


def swap_cores(value):
    return lax.ppermute(value, "col", [(0, 1), (1, 0)])


def call(kernel, out_shape, *operands, smem=0, flops=0):
    spaces = [pltpu.SMEM] * smem + [pltpu.VMEM] * (len(operands) - smem)
    size = sum(x.size * x.dtype.itemsize for x in operands)
    return pl.pallas_call(
        kernel,
        out_shape=out_shape,
        in_specs=[pl.BlockSpec(memory_space=space) for space in spaces],
        out_specs=jax.tree.map(lambda _: pl.BlockSpec(memory_space=pltpu.VMEM), out_shape),
        compiler_params=pltpu.CompilerParams(vmem_limit_bytes=VMEM_LIMIT),
        cost_estimate=pl.CostEstimate(flops=flops, bytes_accessed=size, transcendentals=0),
    )(*operands)


def far_first(count):
    half = count // 2
    return [k for k in range(half, count)] + [k for k in range(1, half)]


def prepare_kernel(z_count, y_count, live, tile_hbm, own_side, other_side, tile, arrived):
    row, col = lax.axis_index("row"), lax.axis_index("col")
    z, y = lax.div(row, y_count), lax.rem(row, y_count)
    width = tile_hbm.shape[1]
    span = 2 * y_count * width

    def fetch(k):
        start = pl.multiple_of(lax.bitwise_xor(z, k) * span, span)
        return pltpu.make_async_copy(tile_hbm.at[pl.ds(start, span)], tile.at[k], arrived.at[k])

    for k in range(z_count):
        fetch(k).start()
    out_row = lax.broadcasted_iota(jnp.int32, (2 * width, 2 * width), 0)
    in_row = lax.broadcasted_iota(jnp.int32, (2 * width, 2 * width), 1)
    side = lax.bitwise_xor((out_row >= width).astype(jnp.int32), col)
    spot = 2 * lax.rem(out_row, width) + side
    sort = jnp.where(in_row == spot, 1.0, 0.0).astype(jnp.bfloat16)
    for k in range(z_count):
        fetch(k).wait()
        for j in range(y_count):
            near = lax.bitwise_xor(y, j)
            block = lax.bitwise_xor(z, k) * y_count + near
            rows = tile[k, pl.ds(pl.multiple_of(near * 2 * width, 2 * width), 2 * width), :]
            sides = jnp.dot(sort, rows, preferred_element_type=jnp.float32)
            for i, out in enumerate((own_side, other_side)):
                keep = live[lax.bitwise_xor(col, i), 0, block] == 1
                piece = sides[i * width : (i + 1) * width]
                out[k, j] = jnp.where(keep, piece, jnp.zeros_like(piece)).astype(jnp.bfloat16)


def merge_kernel(z_count, y_count, own_side, other_side, from_core, own, far, seed_class, seed_mask, *outs):
    strips, halves, (pair, base) = outs[: z_count - 1], outs[z_count - 1 : -2], outs[-2:]
    for k, out in zip(far_first(z_count), strips):
        out[0] = own_side[k]
        out[1] = from_core[k]
    for j, out in enumerate(halves):
        out[0] = own_side[:, j + 1]
        out[1] = other_side[:, j + 1]
    width, classes = own.shape
    pair[:width] = own[...]
    pair[width:] = far[...]
    kind = jnp.where(seed_mask[...] == 1, seed_class[...], -1)
    kind = jnp.transpose(jnp.broadcast_to(kind, (width, width)))
    for start in range(0, classes, width):
        slots = lax.broadcasted_iota(jnp.int32, (width, width), 1) + start
        base[:, start : start + width] = jnp.where(kind == slots, 1.0 - CARRY, 0.0)


def spread_kernel(order, y_count, with_degree, *refs):
    z_count = len(order)
    own_side, other_side, from_core, refs = refs[0], refs[1], refs[2], refs[3:]
    strips, refs = dict(zip(far_first(z_count), refs)), refs[z_count - 1 :]
    halves, refs = refs[: y_count - 1], refs[y_count - 1 :]
    pieces, keeps, give = refs[: -y_count - 1], refs[-y_count - 1 : -1], refs[-1]
    values = jnp.concatenate([piece[...] for piece in pieces], axis=0)
    depth, classes = values.shape
    width = depth // z_count
    ones = jnp.ones((SUBLANES, depth), jnp.bfloat16)

    def back_block(k, i, j):
        if j > 0:
            return halves[j - 1][i, k]
        return (own_side, other_side)[i][k, 0]

    def ahead_block(k, i, j):
        if k > 0:
            return strips[k][i, j]
        return (own_side, from_core)[i][0, j]

    for i in (1, 0):
        for j in range(y_count):
            back = jnp.concatenate([back_block(k, i, j) for k in order], axis=0)
            ahead = jnp.concatenate([ahead_block(k, i, j) for k in order], axis=1)
            total = lax.dot_general(back, values, (((0,), (0,)), ((), ())), preferred_element_type=jnp.float32)
            total += jnp.dot(ahead, values, preferred_element_type=jnp.float32)
            out = keeps[j] if i == 0 else give.at[j]
            out[:width, :] = total
            if with_degree:
                sums = jnp.dot(ones, back, preferred_element_type=jnp.float32)
                sums += lax.dot_general(ones, ahead, (((1,), (1,)), ((), ())), preferred_element_type=jnp.float32)
                out[width:, :] = jnp.concatenate([sums] * (classes // width), axis=1)


def on_device(affinity, block_live, labels, seed_class, seed_mask):
    stripe, sides, width = affinity.shape
    count = lax.axis_size("row")
    z_count, y_count = split_rows(count)
    classes = labels.shape[1]

    blocks = jax.ShapeDtypeStruct((z_count, y_count, width, width), jnp.bfloat16)
    own_side, other_side = pl.pallas_call(
        lambda *refs: prepare_kernel(z_count, y_count, *refs),
        out_shape=[blocks, blocks],
        in_specs=[pl.BlockSpec(memory_space=pltpu.SMEM), pl.BlockSpec(memory_space=pltpu.HBM)],
        out_specs=[pl.BlockSpec(memory_space=pltpu.VMEM)] * 2,
        scratch_shapes=[
            pltpu.VMEM((z_count, 2 * y_count * width, width), jnp.bfloat16),
            pltpu.SemaphoreType.DMA((z_count,)),
        ],
        compiler_params=pltpu.CompilerParams(vmem_limit_bytes=VMEM_LIMIT),
    )(block_live.transpose(1, 2, 0), affinity.reshape(stripe * sides, width))
    from_core = swap_cores(other_side)
    far = swap_rows(labels, (z_count // 2) * y_count)

    strip = jax.ShapeDtypeStruct((2, y_count, width, width), jnp.bfloat16)
    half = jax.ShapeDtypeStruct((2, z_count, width, width), jnp.bfloat16)
    pair = jax.ShapeDtypeStruct((2 * width, classes), jnp.bfloat16)
    base = jax.ShapeDtypeStruct((width, classes), jnp.float32)
    merged = call(
        lambda *refs: merge_kernel(z_count, y_count, *refs),
        [strip] * (z_count - 1) + [half] * (y_count - 1) + [pair, base],
        own_side,
        other_side,
        from_core,
        labels,
        far,
        seed_class.reshape(1, width),
        seed_mask.reshape(1, width),
    )
    base = merged[-1]
    strips = [swap_rows(x, k * y_count) for k, x in zip(far_first(z_count), merged)]
    halves = [swap_rows(x, j + 1) for j, x in enumerate(merged[z_count - 1 : -2])]
    values, order, bit = merged[-2], [0, z_count // 2], z_count // 4
    pieces = [values]
    while bit:
        pieces.append(swap_rows(values, bit * y_count))
        order = order + [k ^ bit for k in order]
        bit //= 2
        if bit:
            values = jnp.concatenate(pieces, axis=0)
            pieces = [values]

    current = labels
    degree = None
    for step in range(ITERS):
        if step > 0:
            order = [0] + far_first(z_count)
            pieces = [current] + [swap_rows(current, k * y_count) for k in order[1:]]
        height = width + (SUBLANES if step == 0 else 0)
        part = jax.ShapeDtypeStruct((height, classes), jnp.float32)
        parts = jax.ShapeDtypeStruct((y_count, height, classes), jnp.float32)
        *keeps, give = call(
            lambda *refs: spread_kernel(order, y_count, step == 0, *refs),
            [part] * y_count + [parts],
            own_side,
            other_side,
            from_core,
            *strips,
            *halves,
            *pieces,
            flops=2 * 2 * 2 * y_count * z_count * width * width * classes,
        )
        taken = swap_cores(give)
        spread = keeps[0] + taken[0]
        for j in range(1, y_count):
            spread = spread + swap_rows(keeps[j] + taken[j], j)
        if step == 0:
            degree = 1.0 + 0.5 * spread[width, :width][:, None]
        mixed = CARRY * (0.5 * spread[:width] + current.astype(jnp.float32)) / degree
        current = (mixed + base).astype(jnp.bfloat16)
    return current


def solution(mesh):
    return jax.shard_map(
        on_device,
        mesh=mesh,
        in_specs=(
            P(("groups", "col"), None, "row"),
            P(("groups", "col"), None, "row"),
            P(("groups", "col", "row"), None),
            P(("groups", "col", "row")),
            P(("groups", "col", "row")),
        ),
        out_specs=P(("groups", "col", "row"), None),
        check_vma=False,
    )
```

time: 53.7 us -> 56.1 us (1.045)
  waiting for transfers between devices: 25.9 us -> 32.9 us
  starting transfers between devices: 21.8 us -> 16.2 us
  Pallas kernels: 2.13 us -> 3.4 us
    ppermute x12 -> x11, waiting for transfers between devices: 22.9 us -> 29.9 us  [swap_rows(): return lax.ppermute(value, 'row', [(i, i ^ shift) for i in range(count)])]
    ppermute x12 -> x11, starting transfers between devices: 21.1 us -> 15.5 us  [swap_rows(): return lax.ppermute(value, 'row', [(i, i ^ shift) for i in range(count)])]
    pallas_call x0 -> x1, Pallas kernels: none -> 2.17 us  [on_device(): pl.pallas_call(lambda *refs: prepare_kernel(z_count, y_count, *refs), out...]
    pallas_call x4 -> x3, Pallas kernels: 2.13 us -> 1.23 us  [call(): pl.pallas_call(kernel, out_shape=out_shape, in_specs=[pl.BlockSpec(memory...]
  transfers between devices with their start and end apart: 15 -> 14, of which waited for: 7 -> 11; matrix products, arithmetic and copies ran while one was open for 0% -> 0% of each run, Pallas kernels for 0% -> 0%
where the time goes in v4:
time: 56.1 us; the launch traced here: 55.9 us
  waiting for transfers between devices  32.9 us (59%)
  starting transfers between devices  16.2 us (29%)
  Pallas kernels  3.4 us (6%)
  local copies, waits for them, and re-layouts  2.39 us (4%)
  other arithmetic  0.89 us (2%)
    ppermute x11, waiting for transfers between devices, swap_rows(): return lax.ppermute(value, 'row', [(i, i ^ shift) for i in range(count)])  29.9 us
    ppermute x11, starting transfers between devices, swap_rows(): return lax.ppermute(value, 'row', [(i, i ^ shift) for i in range(count)])  15.5 us
    ppermute x3, waiting for transfers between devices, swap_cores(): return lax.ppermute(value, 'col', [(0, 1), (1, 0)])  3.07 us
    unnamed x10, local copies, waits for them, and re-layouts  2.39 us
    pallas_call x1, Pallas kernels, on_device(): pl.pallas_call(lambda *refs: prepare_kernel(z_count, y_count, *refs), out...  2.17 us
    pallas_call x3, Pallas kernels, call(): pl.pallas_call(kernel, out_shape=out_shape, in_specs=[pl.BlockSpec(memory...  1.23 us
  transfers between devices with their start and end apart: 14, of which 11 were waited for; matrix products, arithmetic and copies ran while one was open for 0% of the time, Pallas kernels for 0%

profile of v4, /device:TPU:0, one launch (start us, length us, event | category | flops | bytes accessed | tf_op | source)
XLA Modules:
  0.0 55.9 jit_solution(16596998649319141582)
XLA Ops:
  0.0 0.0 copy-start.2
  0.0 0.7 %copy-done.2 = s32[8,2,1]{0,2,1:T(1,128)S(1)} copy-done((s32[8,2,1]{0,2,1:T(1,128)S(1)}, s32[8,2,1]{0,2,1:T(1,128)}, u32[]{:S(2)}) %copy-start.2) | copy-done | bytes 88
  0.7 0.0 copy-start
  0.7 1.0 %copy-done = bf16[1024,2,128]{2,1,0:T(2,128)(2,1)S(1)} copy-done((bf16[1024,2,128]{2,1,0:T(2,128)(2,1)S(1)}, bf16[1024,2,128]{2,1,0:T(2,128)(2,1)}, u32[]{:S(2)}) %copy-start) | copy-done | bytes 524312
  1.7 0.0 copy-start.1
  1.7 2.2 %shard_map.55 = (bf16[4,2,128,128]{3,2,1,0:T(8,128)(2,1)S(1)}, bf16[4,2,128,128]{3,2,1,0:T(8,128)(2,1)S(1)}) custom-call(s32[2,1,8]{2,1,0:T(1,128)S(1)} %bitcast.39, bf16[2048,128]{1,0:T(8,128)(2,1)S(1)} %bitcast.38), custom_call_target="tpu_custom_call" | custom-call | tf_op jit(solution)/shard_map/pallas_call | solution.py:136
  3.9 0.5 collective-permute-start
  4.4 0.0 copy-done.1
  4.4 3.7 %collective-permute-start.1 = (bf16[128,256]{1,0:T(8,128)(2,1)S(1)}, bf16[128,256]{1,0:T(8,128)(2,1)S(1)}, u32[]{:S(2)}, u32[]{:S(2)}) collective-permute-start(bf16[128,256]{1,0:T(8,128)(2,1)S(1)} %copy-done.1), channel_id=1, source_target_pairs={{0,8},{2,10},{4,12},{6,14},{8,0},{10,2},{12,4},{14,6},{1,9},{3,11}... | collective-permute-start | bytes 196616 | tf_op jit(solution)/shard_map/ppermute | solution.py:21
  8.1 4.1 %collective-permute-done.1.refs_4_ = bf16[128,256]{1,0:T(8,128)(2,1)S(1)} collective-permute-done((bf16[128,256]{1,0:T(8,128)(2,1)S(1)}, bf16[128,256]{1,0:T(8,128)(2,1)S(1)}, u32[]{:S(2)}, u32[]{:S(2)}) %collective-permute-start.1) | collective-permute-done | bytes 65568 | tf_op jit(solution)/shard_map/ppermute | solution.py:21
  12.2 0.0 collective-permute-done.refs_2_
  12.2 0.0 copy-start.3
  12.2 0.0 copy-start.4
  12.2 0.7 %copy-done.3 = s32[128]{0:T(128)S(1)} copy-done((s32[128]{0:T(128)S(1)}, s32[128]{0:T(128)}, u32[]{:S(2)}) %copy-start.3) | copy-done | bytes 536
  12.8 0.0 copy-done.4
  12.9 0.2 shard_map.56
  13.0 1.6 %collective-permute-start.5 = (bf16[2,4,128,128]{3,2,1,0:T(8,128)(2,1)S(1)}, bf16[2,4,128,128]{3,2,1,0:T(8,128)(2,1)S(1)}, u32[]{:S(2)}, u32[]{:S(2)}) collective-permute-start(bf16[2,4,128,128]{3,2,1,0:T(8,128)(2,1)S(1)} %get-tuple-element.24), channel_id=1, source_target_pairs={{0,2},{2,0},{4,6},{6,4},{8,10},{10,8},{12,14},{14,12},{1,3},{3,1},... | collective-permute-start | bytes 786440 | tf_op jit(solution)/shard_map/ppermute | solution.py:21
  14.7 1.3 %collective-permute-start.2 = (bf16[2,2,128,128]{3,2,1,0:T(8,128)(2,1)S(1)}, bf16[2,2,128,128]{3,2,1,0:T(8,128)(2,1)S(1)}, u32[]{:S(2)}, u32[]{:S(2)}) collective-permute-start(bf16[2,2,128,128]{3,2,1,0:T(8,128)(2,1)S(1)} %get-tuple-element.21), channel_id=1, source_target_pairs={{0,8},{2,10},{4,12},{6,14},{8,0},{10,2},{12,4},{14,6},{1,9},{3,11}... | collective-permute-start | bytes 393224 | tf_op jit(solution)/shard_map/ppermute | solution.py:21
  16.0 2.2 %collective-permute-start.3 = (bf16[2,2,128,128]{3,2,1,0:T(8,128)(2,1)S(1)}, bf16[2,2,128,128]{3,2,1,0:T(8,128)(2,1)S(1)}, u32[]{:S(2)}, u32[]{:S(2)}) collective-permute-start(bf16[2,2,128,128]{3,2,1,0:T(8,128)(2,1)S(1)} %get-tuple-element.22), channel_id=1, source_target_pairs={{0,12},{2,14},{4,8},{6,10},{8,4},{10,6},{12,0},{14,2},{1,13},{3,15... | collective-permute-start | bytes 393224 | tf_op jit(solution)/shard_map/ppermute | solution.py:21
  18.2 0.6 %collective-permute-start.4 = (bf16[2,2,128,128]{3,2,1,0:T(8,128)(2,1)S(1)}, bf16[2,2,128,128]{3,2,1,0:T(8,128)(2,1)S(1)}, u32[]{:S(2)}, u32[]{:S(2)}) collective-permute-start(bf16[2,2,128,128]{3,2,1,0:T(8,128)(2,1)S(1)} %get-tuple-element.23), channel_id=1, source_target_pairs={{0,4},{2,6},{4,0},{6,2},{8,12},{10,14},{12,8},{14,10},{1,5},{3,7},... | collective-permute-start | bytes 393224 | tf_op jit(solution)/shard_map/ppermute | solution.py:21
  18.7 1.5 %collective-permute-start.6 = (bf16[256,256]{1,0:T(8,128)(2,1)S(1)}, bf16[256,256]{1,0:T(8,128)(2,1)S(1)}, u32[]{:S(2)}, u32[]{:S(2)}) collective-permute-start(bf16[256,256]{1,0:T(8,128)(2,1)S(1)} %get-tuple-element.25.refs_7_), channel_id=1, source_target_pairs={{0,4},{2,6},{4,0},{6,2},{8,12},{10,14},{12,8},{14,10},{1,5},{3,7},... | collective-permute-start | bytes 393224 | tf_op jit(solution)/shard_map/ppermute | solution.py:21
  20.2 7.0 %collective-permute-done.2.refs_3_ = bf16[2,2,128,128]{3,2,1,0:T(8,128)(2,1)S(1)} collective-permute-done((bf16[2,2,128,128]{3,2,1,0:T(8,128)(2,1)S(1)}, bf16[2,2,128,128]{3,2,1,0:T(8,128)(2,1)S(1)}, u32[]{:S(2)}, u32[]{:S(2)}) %collective-permute-start.2) | collective-permute-done | bytes 131104 | tf_op jit(solution)/shard_map/ppermute | solution.py:21
  27.2 0.0 collective-permute-done.3.refs_4_
  27.2 1.1 %collective-permute-done.4.refs_5_ = bf16[2,2,128,128]{3,2,1,0:T(8,128)(2,1)S(1)} collective-permute-done((bf16[2,2,128,128]{3,2,1,0:T(8,128)(2,1)S(1)}, bf16[2,2,128,128]{3,2,1,0:T(8,128)(2,1)S(1)}, u32[]{:S(2)}, u32[]{:S(2)}) %collective-permute-start.4) | collective-permute-done | bytes 131104 | tf_op jit(solution)/shard_map/ppermute | solution.py:21
  28.3 1.7 %collective-permute-done.6.refs_8_ = bf16[256,256]{1,0:T(8,128)(2,1)S(1)} collective-permute-done((bf16[256,256]{1,0:T(8,128)(2,1)S(1)}, bf16[256,256]{1,0:T(8,128)(2,1)S(1)}, u32[]{:S(2)}, u32[]{:S(2)}) %collective-permute-start.6) | collective-permute-done | bytes 131104 | tf_op jit(solution)/shard_map/ppermute | solution.py:21
  30.0 0.0 collective-permute-done.5.refs_6_
  30.0 0.6 %shard_map.57 = (f32[136,256]{1,0:T(8,128)S(1)}, f32[136,256]{1,0:T(8,128)S(1)}, f32[2,136,256]{2,1,0:T(8,128)S(1)}) custom-call(bf16[4,2,128,128]{3,2,1,0:T(8,128)(2,1)S(1)} %get-tuple-element.19.refs_0_, bf16[4,2,128,128]{3,2,1,0:T(8,128)(2,1)S(1)} %get-tuple-element.20.refs_1_, bf16[4,2,128,128]{3,2,1,0:T(8,128)(2,1)S(1)} %collective-permute-done.refs_2_, ...), custom_call_target="tpu_custom_call" | custom-call | flops 268435456 | bytes 1703936 | tf_op jit(solution)/shard_map/pallas_call | solution.py:31
  30.6 0.1 collective-permute-start.7
  30.7 1.5 %collective-permute-done.7 = f32[2,136,256]{2,1,0:T(8,128)S(1)} collective-permute-done((f32[2,136,256]{2,1,0:T(8,128)S(1)}, f32[2,136,256]{2,1,0:T(8,128)S(1)}, u32[]{:S(2)}, u32[]{:S(2)}) %collective-permute-start.7) | collective-permute-done | bytes 278560 | tf_op jit(solution)/shard_map/ppermute | solution.py:25
  32.3 0.6 %collective-permute-start.8 = (f32[136,256]{1,0:T(8,128)S(1)}, f32[136,256]{1,0:T(8,128)S(1)}, u32[]{:S(2)}, u32[]{:S(2)}) collective-permute-start(f32[136,256]{1,0:T(8,128)S(1)} %fusion), channel_id=1, source_target_pairs={{0,2},{2,0},{4,6},{6,4},{8,10},{10,8},{12,14},{14,12},{1,3},{3,1},... | collective-permute-start | bytes 417800 | tf_op jit(solution)/shard_map/ppermute | solution.py:21
  32.9 5.2 %collective-permute-done.8 = f32[136,256]{1,0:T(8,128)S(1)} collective-permute-done((f32[136,256]{1,0:T(8,128)S(1)}, f32[136,256]{1,0:T(8,128)S(1)}, u32[]{:S(2)}, u32[]{:S(2)}) %collective-permute-start.8) | collective-permute-done | bytes 139296 | tf_op jit(solution)/shard_map/ppermute | solution.py:21
  38.1 0.1 fusion.15.refs_7_
  38.2 0.1 collective-permute-start.11
  38.3 3.0 %collective-permute-start.10 = (bf16[128,256]{1,0:T(8,128)(2,1)S(1)}, bf16[128,256]{1,0:T(8,128)(2,1)S(1)}, u32[]{:S(2)}, u32[]{:S(2)}) collective-permute-start(bf16[128,256]{1,0:T(8,128)(2,1)S(1)} %fusion.15.refs_7_), channel_id=1, source_target_pairs={{0,12},{2,14},{4,8},{6,10},{8,4},{10,6},{12,0},{14,2},{1,13},{3,15... | collective-permute-start | bytes 196616 | tf_op jit(solution)/shard_map/ppermute | solution.py:21
  41.3 0.5 collective-permute-start.9
  41.8 1.5 %collective-permute-done.11.refs_10_ = bf16[128,256]{1,0:T(8,128)(2,1)S(1)} collective-permute-done((bf16[128,256]{1,0:T(8,128)(2,1)S(1)}, bf16[128,256]{1,0:T(8,128)(2,1)S(1)}, u32[]{:S(2)}, u32[]{:S(2)}) %collective-permute-start.11) | collective-permute-done | bytes 65568 | tf_op jit(solution)/shard_map/ppermute | solution.py:21
  43.2 1.7 %collective-permute-done.10.refs_9_ = bf16[128,256]{1,0:T(8,128)(2,1)S(1)} collective-permute-done((bf16[128,256]{1,0:T(8,128)(2,1)S(1)}, bf16[128,256]{1,0:T(8,128)(2,1)S(1)}, u32[]{:S(2)}, u32[]{:S(2)}) %collective-permute-start.10) | collective-permute-done | bytes 65568 | tf_op jit(solution)/shard_map/ppermute | solution.py:21
  44.9 2.6 %collective-permute-done.9.refs_8_ = bf16[128,256]{1,0:T(8,128)(2,1)S(1)} collective-permute-done((bf16[128,256]{1,0:T(8,128)(2,1)S(1)}, bf16[128,256]{1,0:T(8,128)(2,1)S(1)}, u32[]{:S(2)}, u32[]{:S(2)}) %collective-permute-start.9) | collective-permute-done | bytes 65568 | tf_op jit(solution)/shard_map/ppermute | solution.py:21
  47.5 0.4 shard_map.58
  48.0 0.1 collective-permute-start.12
  48.1 1.5 %collective-permute-done.12 = f32[2,128,256]{2,1,0:T(8,128)S(1)} collective-permute-done((f32[2,128,256]{2,1,0:T(8,128)S(1)}, f32[2,128,256]{2,1,0:T(8,128)S(1)}, u32[]{:S(2)}, u32[]{:S(2)}) %collective-permute-start.12) | collective-permute-done | bytes 262176 | tf_op jit(solution)/shard_map/ppermute | solution.py:25
  49.6 0.6 %collective-permute-start.13 = (f32[128,256]{1,0:T(8,128)S(1)}, f32[128,256]{1,0:T(8,128)S(1)}, u32[]{:S(2)}, u32[]{:S(2)}) collective-permute-start(f32[128,256]{1,0:T(8,128)S(1)} %fusion.3), channel_id=1, source_target_pairs={{0,2},{2,0},{4,6},{6,4},{8,10},{10,8},{12,14},{14,12},{1,3},{3,1},... | collective-permute-start | bytes 393224 | tf_op jit(solution)/shard_map/ppermute | solution.py:21
  50.2 5.0 %collective-permute-done.13 = f32[128,256]{1,0:T(8,128)S(1)} collective-permute-done((f32[128,256]{1,0:T(8,128)S(1)}, f32[128,256]{1,0:T(8,128)S(1)}, u32[]{:S(2)}, u32[]{:S(2)}) %collective-permute-start.13) | collective-permute-done | bytes 131104 | tf_op jit(solution)/shard_map/ppermute | solution.py:21
  55.2 0.7 %fusion.16 = bf16[128,256]{1,0:T(8,128)(2,1)} fusion(f32[128,256]{1,0:T(8,128)S(1)} %get-tuple-element.29, bf16[128,256]{1,0:T(8,128)(2,1)S(1)} %fusion.15.refs_7_, f32[128,256]{1,0:T(8,128)S(1)} %collective-permute-done.13, f32[128,256]{1,0:T(8,128)S(1)} %get-tuple-element.30, f32[2,128,256]{2,1,0:T(8,128)S(1)} %collective-permute-done.12, f32[128]{0:T(128)S(1)} %fusion.18), kind=kLoop, calls=%fused_computation.21 | loop fusion | flops 294912 | bytes 655872 | tf_op jit(solution)/shard_map/convert_element_type | solution.py:205
  (4 shorter events, 0.1 us)
Async XLA Ops:
  0.0 0.7 %copy-start.2 = (s32[8,2,1]{0,2,1:T(1,128)S(1)}, s32[8,2,1]{0,2,1:T(1,128)}, u32[]{:S(2)}) copy-start(s32[8,2,1]{0,2,1:T(1,128)} %param.6) | copy-start | bytes 196
  0.7 1.0 %copy-start = (bf16[1024,2,128]{2,1,0:T(2,128)(2,1)S(1)}, bf16[1024,2,128]{2,1,0:T(2,128)(2,1)}, u32[]{:S(2)}) copy-start(bf16[1024,2,128]{2,1,0:T(2,128)(2,1)} %param.5) | copy-start | bytes 1572868
  1.7 2.7 %copy-start.1 = (bf16[128,256]{1,0:T(8,128)(2,1)S(1)}, bf16[128,256]{1,0:T(8,128)(2,1)}, u32[]{:S(2)}) copy-start(bf16[128,256]{1,0:T(8,128)(2,1)} %refs_3_.1) | copy-start | bytes 196612
  3.9 8.3 %collective-permute-start = (bf16[4,2,128,128]{3,2,1,0:T(8,128)(2,1)S(1)}, bf16[4,2,128,128]{3,2,1,0:T(8,128)(2,1)S(1)}, u32[]{:S(2)}, u32[]{:S(2)}) collective-permute-start(bf16[4,2,128,128]{3,2,1,0:T(8,128)(2,1)S(1)} %get-tuple-element.20.refs_1_), channel_id=1, source_target_pairs={{0,1},{1,0},{2,3},{3,2},{4,5},{5,4},{6,7},{7,6},{8,9},{9,8},{10,11... | collective-permute-start | bytes 786440 | tf_op jit(solution)/shard_map/ppermute | solution.py:25
  4.4 7.7 %collective-permute-start.1 = (bf16[128,256]{1,0:T(8,128)(2,1)S(1)}, bf16[128,256]{1,0:T(8,128)(2,1)S(1)}, u32[]{:S(2)}, u32[]{:S(2)}) collective-permute-start(bf16[128,256]{1,0:T(8,128)(2,1)S(1)} %copy-done.1), channel_id=1, source_target_pairs={{0,8},{2,10},{4,12},{6,14},{8,0},{10,2},{12,4},{14,6},{1,9},{3,11}... | collective-permute-start | bytes 196616 | tf_op jit(solution)/shard_map/ppermute | solution.py:21
  12.2 0.7 %copy-start.3 = (s32[128]{0:T(128)S(1)}, s32[128]{0:T(128)}, u32[]{:S(2)}) copy-start(s32[128]{0:T(128)} %param.8) | copy-start | bytes 1540
  12.2 0.7 %copy-start.4 = (s32[128]{0:T(128)S(1)}, s32[128]{0:T(128)}, u32[]{:S(2)}) copy-start(s32[128]{0:T(128)} %param.9) | copy-start | bytes 1540
  13.0 17.0 %collective-permute-start.5 = (bf16[2,4,128,128]{3,2,1,0:T(8,128)(2,1)S(1)}, bf16[2,4,128,128]{3,2,1,0:T(8,128)(2,1)S(1)}, u32[]{:S(2)}, u32[]{:S(2)}) collective-permute-start(bf16[2,4,128,128]{3,2,1,0:T(8,128)(2,1)S(1)} %get-tuple-element.24), channel_id=1, source_target_pairs={{0,2},{2,0},{4,6},{6,4},{8,10},{10,8},{12,14},{14,12},{1,3},{3,1},... | collective-permute-start | bytes 786440 | tf_op jit(solution)/shard_map/ppermute | solution.py:21
  14.7 12.5 %collective-permute-start.2 = (bf16[2,2,128,128]{3,2,1,0:T(8,128)(2,1)S(1)}, bf16[2,2,128,128]{3,2,1,0:T(8,128)(2,1)S(1)}, u32[]{:S(2)}, u32[]{:S(2)}) collective-permute-start(bf16[2,2,128,128]{3,2,1,0:T(8,128)(2,1)S(1)} %get-tuple-element.21), channel_id=1, source_target_pairs={{0,8},{2,10},{4,12},{6,14},{8,0},{10,2},{12,4},{14,6},{1,9},{3,11}... | collective-permute-start | bytes 393224 | tf_op jit(solution)/shard_map/ppermute | solution.py:21
  16.0 11.2 %collective-permute-start.3 = (bf16[2,2,128,128]{3,2,1,0:T(8,128)(2,1)S(1)}, bf16[2,2,128,128]{3,2,1,0:T(8,128)(2,1)S(1)}, u32[]{:S(2)}, u32[]{:S(2)}) collective-permute-start(bf16[2,2,128,128]{3,2,1,0:T(8,128)(2,1)S(1)} %get-tuple-element.22), channel_id=1, source_target_pairs={{0,12},{2,14},{4,8},{6,10},{8,4},{10,6},{12,0},{14,2},{1,13},{3,15... | collective-permute-start | bytes 393224 | tf_op jit(solution)/shard_map/ppermute | solution.py:21
  18.2 10.1 %collective-permute-start.4 = (bf16[2,2,128,128]{3,2,1,0:T(8,128)(2,1)S(1)}, bf16[2,2,128,128]{3,2,1,0:T(8,128)(2,1)S(1)}, u32[]{:S(2)}, u32[]{:S(2)}) collective-permute-start(bf16[2,2,128,128]{3,2,1,0:T(8,128)(2,1)S(1)} %get-tuple-element.23), channel_id=1, source_target_pairs={{0,4},{2,6},{4,0},{6,2},{8,12},{10,14},{12,8},{14,10},{1,5},{3,7},... | collective-permute-start | bytes 393224 | tf_op jit(solution)/shard_map/ppermute | solution.py:21
  18.7 11.3 %collective-permute-start.6 = (bf16[256,256]{1,0:T(8,128)(2,1)S(1)}, bf16[256,256]{1,0:T(8,128)(2,1)S(1)}, u32[]{:S(2)}, u32[]{:S(2)}) collective-permute-start(bf16[256,256]{1,0:T(8,128)(2,1)S(1)} %get-tuple-element.25.refs_7_), channel_id=1, source_target_pairs={{0,4},{2,6},{4,0},{6,2},{8,12},{10,14},{12,8},{14,10},{1,5},{3,7},... | collective-permute-start | bytes 393224 | tf_op jit(solution)/shard_map/ppermute | solution.py:21
  30.6 1.6 %collective-permute-start.7 = (f32[2,136,256]{2,1,0:T(8,128)S(1)}, f32[2,136,256]{2,1,0:T(8,128)S(1)}, u32[]{:S(2)}, u32[]{:S(2)}) collective-permute-start(f32[2,136,256]{2,1,0:T(8,128)S(1)} %get-tuple-element.27), channel_id=1, source_target_pairs={{0,1},{1,0},{2,3},{3,2},{4,5},{5,4},{6,7},{7,6},{8,9},{9,8},{10,11... | collective-permute-start | bytes 835592 | tf_op jit(solution)/shard_map/ppermute | solution.py:25
  32.3 5.8 %collective-permute-start.8 = (f32[136,256]{1,0:T(8,128)S(1)}, f32[136,256]{1,0:T(8,128)S(1)}, u32[]{:S(2)}, u32[]{:S(2)}) collective-permute-start(f32[136,256]{1,0:T(8,128)S(1)} %fusion), channel_id=1, source_target_pairs={{0,2},{2,0},{4,6},{6,4},{8,10},{10,8},{12,14},{14,12},{1,3},{3,1},... | collective-permute-start | bytes 417800 | tf_op jit(solution)/shard_map/ppermute | solution.py:21
  38.2 5.0 %collective-permute-start.11 = (bf16[128,256]{1,0:T(8,128)(2,1)S(1)}, bf16[128,256]{1,0:T(8,128)(2,1)S(1)}, u32[]{:S(2)}, u32[]{:S(2)}) collective-permute-start(bf16[128,256]{1,0:T(8,128)(2,1)S(1)} %fusion.15.refs_7_), channel_id=1, source_target_pairs={{0,4},{2,6},{4,0},{6,2},{8,12},{10,14},{12,8},{14,10},{1,5},{3,7},... | collective-permute-start | bytes 196616 | tf_op jit(solution)/shard_map/ppermute | solution.py:21
  38.3 6.6 %collective-permute-start.10 = (bf16[128,256]{1,0:T(8,128)(2,1)S(1)}, bf16[128,256]{1,0:T(8,128)(2,1)S(1)}, u32[]{:S(2)}, u32[]{:S(2)}) collective-permute-start(bf16[128,256]{1,0:T(8,128)(2,1)S(1)} %fusion.15.refs_7_), channel_id=1, source_target_pairs={{0,12},{2,14},{4,8},{6,10},{8,4},{10,6},{12,0},{14,2},{1,13},{3,15... | collective-permute-start | bytes 196616 | tf_op jit(solution)/shard_map/ppermute | solution.py:21
  41.3 6.2 %collective-permute-start.9 = (bf16[128,256]{1,0:T(8,128)(2,1)S(1)}, bf16[128,256]{1,0:T(8,128)(2,1)S(1)}, u32[]{:S(2)}, u32[]{:S(2)}) collective-permute-start(bf16[128,256]{1,0:T(8,128)(2,1)S(1)} %fusion.15.refs_7_), channel_id=1, source_target_pairs={{0,8},{2,10},{4,12},{6,14},{8,0},{10,2},{12,4},{14,6},{1,9},{3,11}... | collective-permute-start | bytes 196616 | tf_op jit(solution)/shard_map/ppermute | solution.py:21
  48.0 1.6 %collective-permute-start.12 = (f32[2,128,256]{2,1,0:T(8,128)S(1)}, f32[2,128,256]{2,1,0:T(8,128)S(1)}, u32[]{:S(2)}, u32[]{:S(2)}) collective-permute-start(f32[2,128,256]{2,1,0:T(8,128)S(1)} %get-tuple-element.31), channel_id=1, source_target_pairs={{0,1},{1,0},{2,3},{3,2},{4,5},{5,4},{6,7},{7,6},{8,9},{9,8},{10,11... | collective-permute-start | bytes 786440 | tf_op jit(solution)/shard_map/ppermute | solution.py:25
  49.6 5.6 %collective-permute-start.13 = (f32[128,256]{1,0:T(8,128)S(1)}, f32[128,256]{1,0:T(8,128)S(1)}, u32[]{:S(2)}, u32[]{:S(2)}) collective-permute-start(f32[128,256]{1,0:T(8,128)S(1)} %fusion.3), channel_id=1, source_target_pairs={{0,2},{2,0},{4,6},{6,4},{8,10},{10,8},{12,14},{14,12},{1,3},{3,1},... | collective-permute-start | bytes 393224 | tf_op jit(solution)/shard_map/ppermute | solution.py:21

commit v5 on v3

v5 whole, which is shorter than its diff:
```python
import jax
import jax.numpy as jnp
from jax import lax
from jax.experimental import pallas as pl
from jax.experimental.pallas import tpu as pltpu
from jax.sharding import PartitionSpec as P

ITERS = 2
CARRY = 0.8
SUBLANES = 8
JOIN_FLOPS = 0
SIDES_FLOPS = 3_000_000_000
MIB = 1024 * 1024


def split_rows(count):
    inner = 1 << ((count.bit_length() - 1) // 2)
    return count // inner, inner


def swap_rows(value, shift):
    count = lax.axis_size("row")
    return lax.ppermute(value, "row", [(i, i ^ shift) for i in range(count)])


def swap_cores(value):
    return lax.ppermute(value, "col", [(0, 1), (1, 0)])


def call(kernel, out_shape, *operands, smem=0, flops=0):
    spaces = [pltpu.SMEM] * smem + [pltpu.VMEM] * (len(operands) - smem)
    size = sum(x.size * x.dtype.itemsize for x in (*operands, *jax.tree.leaves(out_shape)))
    return pl.pallas_call(
        kernel,
        out_shape=out_shape,
        in_specs=[pl.BlockSpec(memory_space=space) for space in spaces],
        out_specs=jax.tree.map(lambda _: pl.BlockSpec(memory_space=pltpu.VMEM), out_shape),
        compiler_params=pltpu.CompilerParams(vmem_limit_bytes=2 * size + 4 * MIB),
        cost_estimate=pl.CostEstimate(flops=flops, bytes_accessed=size, transcendentals=0),
    )(*operands)


def far_first(count):
    half = count // 2
    return [k for k in range(half, count)] + [k for k in range(1, half)]


def prepare_kernel(z_count, y_count, live, tile, *outs):
    strips, halves = outs[:z_count], outs[z_count:]
    row, col = lax.axis_index("row"), lax.axis_index("col")
    z, y = lax.div(row, y_count), lax.rem(row, y_count)
    width = tile.shape[1]
    out_row = lax.broadcasted_iota(jnp.int32, (2 * width, 2 * width), 0)
    in_row = lax.broadcasted_iota(jnp.int32, (2 * width, 2 * width), 1)
    side = lax.bitwise_xor((out_row >= width).astype(jnp.int32), col)
    spot = 2 * lax.rem(out_row, width) + side
    sort = jnp.where(in_row == spot, 1.0, 0.0).astype(jnp.bfloat16)
    for k in range(z_count):
        for j in range(y_count):
            block = lax.bitwise_xor(z, k) * y_count + lax.bitwise_xor(y, j)
            rows = tile[pl.ds(pl.multiple_of(block * 2 * width, 2 * width), 2 * width), :]
            sides = jnp.dot(sort, rows, preferred_element_type=jnp.float32)
            for i in range(2):
                keep = live[lax.bitwise_xor(col, i), 0, block] == 1
                piece = sides[i * width : (i + 1) * width]
                piece = jnp.where(keep, piece, jnp.zeros_like(piece)).astype(jnp.bfloat16)
                strips[k][i, j] = piece
                if j > 0:
                    halves[j - 1][i, k] = piece


def join_kernel(*refs):
    parts, out = refs[:-1], refs[-1]
    start = 0
    for part in parts:
        out[start : start + part.shape[0]] = part[...]
        start += part.shape[0]


def join(parts, flops=0):
    rows = sum(x.shape[0] for x in parts)
    return call(join_kernel, jax.ShapeDtypeStruct((rows,) + parts[0].shape[1:], parts[0].dtype), *parts, flops=flops)


def other_kernel(*refs):
    strips, out = refs[:-1], refs[-1]
    for k, strip in zip([0] + far_first(len(strips)), strips):
        out[k] = strip[1]


def seed_kernel(seed_class, seed_mask, base):
    width, classes = base.shape
    kind = jnp.where(seed_mask[...] == 1, seed_class[...], -1)
    kind = jnp.transpose(jnp.broadcast_to(kind, (width, width)))
    for start in range(0, classes, width):
        slots = lax.broadcasted_iota(jnp.int32, (width, width), 1) + start
        base[:, start : start + width] = jnp.where(kind == slots, 1.0 - CARRY, 0.0)


def spread_kernel(order, y_count, first, *refs):
    z_count = len(order)
    sent, refs = refs[:z_count], refs[z_count:]
    strips = dict(zip([0] + far_first(z_count), sent[:1] + refs))
    refs = refs[z_count - 1 :]
    halves, refs = refs[: y_count - 1], refs[y_count - 1 :]
    other, refs = refs[0], refs[1:]
    pieces, keeps, give = refs[: -y_count - 1], refs[-y_count - 1 : -1], refs[-1]
    if first:
        pieces, theirs = pieces[: len(pieces) // 2], pieces[len(pieces) // 2 :]
        theirs = jnp.concatenate([piece[...] for piece in theirs], axis=0)
    values = jnp.concatenate([piece[...] for piece in pieces], axis=0)
    depth, classes = values.shape
    width = depth // z_count
    ones = jnp.ones((SUBLANES, depth), jnp.bfloat16)

    def product(left, right, contract):
        return lax.dot_general(left, right, ((contract[:1], contract[1:]), ((), ())), preferred_element_type=jnp.float32)

    for i in (1, 0):
        for j in range(y_count):
            back = jnp.concatenate([sent[k][i, 0] if j == 0 else halves[j - 1][i, k] for k in order], axis=0)
            total = product(back, values, (0, 0))
            ahead = []
            if first and i == 0:
                ahead = [(0, values), (1, theirs)]
                ahead = [(jnp.concatenate([strips[k][s, j] for k in order], axis=1), v) for s, v in ahead]
            elif not first:
                ahead = [strips[k][0, j] if i == 0 else other[k, j] for k in order]
                ahead = [(jnp.concatenate(ahead, axis=1), values)]
            for blocks, right in ahead:
                total += product(blocks, right, (1, 0))
            out = keeps[j] if i == 0 else give.at[j]
            out[:width, :] = total
            if first:
                sums = product(ones, back, (1, 0))
                for blocks, _ in ahead:
                    sums += product(ones, blocks, (1, 1))
                out[width:, :] = jnp.concatenate([sums] * (classes // width), axis=1)


def on_device(affinity, block_live, labels, seed_class, seed_mask):
    stripe, sides, width = affinity.shape
    count = lax.axis_size("row")
    z_count, y_count = split_rows(count)
    classes = labels.shape[1]

    strip = jax.ShapeDtypeStruct((2, y_count, width, width), jnp.bfloat16)
    half = jax.ShapeDtypeStruct((2, z_count, width, width), jnp.bfloat16)
    sent = call(
        lambda *refs: prepare_kernel(z_count, y_count, *refs),
        [strip] * z_count + [half] * (y_count - 1),
        block_live.transpose(1, 2, 0),
        affinity.reshape(stripe * sides, width),
        smem=1,
    )
    sent, halves = sent[:z_count], sent[z_count:]
    arrived = {k: swap_rows(sent[k], k * y_count) for k in far_first(z_count)}
    strips = [arrived[k] for k in far_first(z_count)]
    halves = [swap_rows(x, j + 1) for j, x in enumerate(halves)]
    near = {k: swap_rows(labels, k * y_count) for k in far_first(z_count) if k & (k - 1) == 0}
    for k in far_first(z_count):
        if k not in near:
            low = k & -k
            near[k] = swap_rows(near[k ^ low], low * y_count)
    order = [0] + sorted(near, key=lambda k: (k & (k - 1) != 0, -k))
    values = join([labels] + [near[k] for k in order[1:]], flops=JOIN_FLOPS)
    swapped = swap_cores(values)
    other = jax.ShapeDtypeStruct((z_count, y_count, width, width), jnp.bfloat16)
    sides = call(other_kernel, other, sent[0], *strips, flops=SIDES_FLOPS)
    other = swap_cores(sides)
    pieces = [sides, values, swapped]
    base = call(
        seed_kernel,
        jax.ShapeDtypeStruct((width, classes), jnp.float32),
        seed_class.reshape(1, width),
        seed_mask.reshape(1, width),
    )

    current = labels
    degree = None
    for step in range(ITERS):
        if step > 0:
            order = [0] + far_first(z_count)
            pieces = [other, current] + [swap_rows(current, k * y_count) for k in order[1:]]
        height = width + (SUBLANES if step == 0 else 0)
        part = jax.ShapeDtypeStruct((height, classes), jnp.float32)
        parts = jax.ShapeDtypeStruct((y_count, height, classes), jnp.float32)
        *keeps, give = call(
            lambda *refs: spread_kernel(order, y_count, step == 0, *refs),
            [part] * y_count + [parts],
            *sent,
            *strips,
            *halves,
            *pieces,
            flops=2 * 2 * 2 * y_count * z_count * width * width * classes,
        )
        taken = swap_cores(give)
        spread = keeps[0] + taken[0]
        for j in range(1, y_count):
            spread = spread + swap_rows(keeps[j] + taken[j], j)
        if step == 0:
            degree = 1.0 + 0.5 * spread[width, :width][:, None]
        mixed = CARRY * (0.5 * spread[:width] + current.astype(jnp.float32)) / degree
        current = (mixed + base).astype(jnp.bfloat16)
    return current


def solution(mesh):
    return jax.shard_map(
        on_device,
        mesh=mesh,
        in_specs=(
            P(("groups", "col"), None, "row"),
            P(("groups", "col"), None, "row"),
            P(("groups", "col", "row"), None),
            P(("groups", "col", "row")),
            P(("groups", "col", "row")),
        ),
        out_specs=P(("groups", "col", "row"), None),
        check_vma=False,
    )
```

time: 53.7 us -> 52.5 us (0.978)
  starting transfers between devices: 21.8 us -> 18.6 us
  waiting for transfers between devices: 25.9 us -> 27.9 us
    ppermute x12, starting transfers between devices: 21.1 us -> 18.4 us  [swap_rows(): return lax.ppermute(value, 'row', [(i, i ^ shift) for i in range(count)])]
    ppermute x12, waiting for transfers between devices: 22.9 us -> 24.9 us  [swap_rows(): return lax.ppermute(value, 'row', [(i, i ^ shift) for i in range(count)])]
    pallas_call x4 -> x6, Pallas kernels: 2.13 us -> 2.26 us  [call(): pl.pallas_call(kernel, out_shape=out_shape, in_specs=[pl.BlockSpec(memory...]
    ppermute x3 -> x4, waiting for transfers between devices: 3.07 us -> 3.07 us  [swap_cores(): return lax.ppermute(value, 'col', [(0, 1), (1, 0)])]
  transfers between devices with their start and end apart: 15 -> 16, of which waited for: 7 -> 8; matrix products, arithmetic and copies ran while one was open for 0% -> 0% of each run, Pallas kernels for 0% -> 2%
where the time goes in v5:
time: 52.5 us; the launch traced here: 52.3 us
  waiting for transfers between devices  27.9 us (53%)
  starting transfers between devices  18.6 us (35%)
  local copies, waits for them, and re-layouts  2.39 us (5%)
  Pallas kernels  2.26 us (4%)
  other arithmetic  0.9 us (2%)
    ppermute x12, waiting for transfers between devices, swap_rows(): return lax.ppermute(value, 'row', [(i, i ^ shift) for i in range(count)])  24.9 us
    ppermute x12, starting transfers between devices, swap_rows(): return lax.ppermute(value, 'row', [(i, i ^ shift) for i in range(count)])  18.4 us
    ppermute x4, waiting for transfers between devices, swap_cores(): return lax.ppermute(value, 'col', [(0, 1), (1, 0)])  3.07 us
    unnamed x10, local copies, waits for them, and re-layouts  2.39 us
    pallas_call x6, Pallas kernels, call(): pl.pallas_call(kernel, out_shape=out_shape, in_specs=[pl.BlockSpec(memory...  2.26 us
  transfers between devices with their start and end apart: 16, of which 8 were waited for; matrix products, arithmetic and copies ran while one was open for 0% of the time, Pallas kernels for 2%

profile of v5, /device:TPU:0, one launch (start us, length us, event | category | flops | bytes accessed | tf_op | source)
XLA Modules:
  0.0 52.3 jit_solution(8953158676172221638)
XLA Ops:
  0.0 4.0 %collective-permute-start.5 = (bf16[128,256]{1,0:T(8,128)(2,1)}, bf16[128,256]{1,0:T(8,128)(2,1)S(1)}, u32[]{:S(2)}, u32[]{:S(2)}) collective-permute-start(bf16[128,256]{1,0:T(8,128)(2,1)} %refs_0_.1), channel_id=1, source_target_pairs={{0,8},{2,10},{4,12},{6,14},{8,0},{10,2},{12,4},{14,6},{1,9},{3,11}... | collective-permute-start | bytes 196616 | tf_op jit(solution)/shard_map/ppermute | solution.py:23
  4.0 0.0 copy-start.2
  4.0 0.7 %copy-done.2 = s32[8,2,1]{0,2,1:T(1,128)S(1)} copy-done((s32[8,2,1]{0,2,1:T(1,128)S(1)}, s32[8,2,1]{0,2,1:T(1,128)}, u32[]{:S(2)}) %copy-start.2) | copy-done | bytes 88
  4.7 0.0 copy-start
  4.7 1.0 %copy-done = bf16[1024,2,128]{2,1,0:T(2,128)(2,1)S(1)} copy-done((bf16[1024,2,128]{2,1,0:T(2,128)(2,1)S(1)}, bf16[1024,2,128]{2,1,0:T(2,128)(2,1)}, u32[]{:S(2)}) %copy-start) | copy-done | bytes 524312
  5.8 0.0 copy-start.1
  5.8 1.0 %shard_map.55 = (bf16[2,2,128,128]{3,2,1,0:T(8,128)(2,1)S(1)}, bf16[2,2,128,128]{3,2,1,0:T(8,128)(2,1)S(1)}, bf16[2,2,128,128]{3,2,1,0:T(8,128)(2,1)S(1)}, bf16[...) custom-call(s32[2,1,8]{2,1,0:T(1,128)S(1)} %bitcast.39, bf16[2048,128]{1,0:T(8,128)(2,1)S(1)} %bitcast.38), custom_call_target="tpu_custom_call" | custom-call | bytes 1310784 | tf_op jit(solution)/shard_map/pallas_call | solution.py:33
  6.8 0.1 collective-permute-start
  6.8 3.9 %collective-permute-start.1 = (bf16[2,2,128,128]{3,2,1,0:T(8,128)(2,1)S(1)}, bf16[2,2,128,128]{3,2,1,0:T(8,128)(2,1)S(1)}, u32[]{:S(2)}, u32[]{:S(2)}) collective-permute-start(bf16[2,2,128,128]{3,2,1,0:T(8,128)(2,1)S(1)} %get-tuple-element.19.refs_3_), channel_id=1, source_target_pairs={{0,12},{2,14},{4,8},{6,10},{8,4},{10,6},{12,0},{14,2},{1,13},{3,15... | collective-permute-start | bytes 393224 | tf_op jit(solution)/shard_map/ppermute | solution.py:23
  10.8 0.0 collective-permute-start.2
  10.8 0.0 copy-done.1
  10.8 2.0 %collective-permute-start.6 = (bf16[128,256]{1,0:T(8,128)(2,1)S(1)}, bf16[128,256]{1,0:T(8,128)(2,1)S(1)}, u32[]{:S(2)}, u32[]{:S(2)}) collective-permute-start(bf16[128,256]{1,0:T(8,128)(2,1)S(1)} %copy-done.1), channel_id=1, source_target_pairs={{0,4},{2,6},{4,0},{6,2},{8,12},{10,14},{12,8},{14,10},{1,5},{3,7},... | collective-permute-start | bytes 196616 | tf_op jit(solution)/shard_map/ppermute | solution.py:23
  12.8 0.0 collective-permute-done.5.refs_1_
  12.8 0.1 collective-permute-start.7
  12.9 8.9 %collective-permute-done.6.refs_2_ = bf16[128,256]{1,0:T(8,128)(2,1)S(1)} collective-permute-done((bf16[128,256]{1,0:T(8,128)(2,1)S(1)}, bf16[128,256]{1,0:T(8,128)(2,1)S(1)}, u32[]{:S(2)}, u32[]{:S(2)}) %collective-permute-start.6) | collective-permute-done | bytes 65568 | tf_op jit(solution)/shard_map/ppermute | solution.py:23
  21.8 1.5 %collective-permute-start.3 = (bf16[2,4,128,128]{3,2,1,0:T(8,128)(2,1)S(1)}, bf16[2,4,128,128]{3,2,1,0:T(8,128)(2,1)S(1)}, u32[]{:S(2)}, u32[]{:S(2)}) collective-permute-start(bf16[2,4,128,128]{3,2,1,0:T(8,128)(2,1)S(1)} %get-tuple-element.20), channel_id=1, source_target_pairs={{0,2},{2,0},{4,6},{6,4},{8,10},{10,8},{12,14},{14,12},{1,3},{3,1},... | collective-permute-start | bytes 786440 | tf_op jit(solution)/shard_map/ppermute | solution.py:23
  23.3 0.0 collective-permute-done.7.refs_3_
  23.3 0.1 collective-permute-start.8
  23.4 0.0 collective-permute-done.refs_1_.refs_4_
  23.4 0.0 collective-permute-done.1.refs_2_.refs_5_
  23.4 0.0 collective-permute-done.2.refs_3_.refs_6_
  23.4 4.9 %collective-permute-done.3.refs_7_ = bf16[2,4,128,128]{3,2,1,0:T(8,128)(2,1)S(1)} collective-permute-done((bf16[2,4,128,128]{3,2,1,0:T(8,128)(2,1)S(1)}, bf16[2,4,128,128]{3,2,1,0:T(8,128)(2,1)S(1)}, u32[]{:S(2)}, u32[]{:S(2)}) %collective-permute-start.3) | collective-permute-done | bytes 262176 | tf_op jit(solution)/shard_map/ppermute | solution.py:23
  28.3 0.0 collective-permute-done.8.refs_10_
  28.3 0.7 %shard_map.58 = (f32[136,256]{1,0:T(8,128)S(1)}, f32[136,256]{1,0:T(8,128)S(1)}, f32[2,136,256]{2,1,0:T(8,128)S(1)}) custom-call(bf16[2,2,128,128]{3,2,1,0:T(8,128)(2,1)S(1)} %get-tuple-element.16.refs_0_, bf16[2,2,128,128]{3,2,1,0:T(8,128)(2,1)S(1)} %get-tuple-element.17.refs_1_, bf16[2,2,128,128]{3,2,1,0:T(8,128)(2,1)S(1)} %get-tuple-element.18.refs_2_, ...), custom_call_target="tpu_custom_call" | custom-call | flops 268435456 | bytes 2523136 | tf_op jit(solution)/shard_map/pallas_call | solution.py:33
  29.0 0.1 collective-permute-start.9
  29.1 1.5 %collective-permute-done.9 = f32[2,136,256]{2,1,0:T(8,128)S(1)} collective-permute-done((f32[2,136,256]{2,1,0:T(8,128)S(1)}, f32[2,136,256]{2,1,0:T(8,128)S(1)}, u32[]{:S(2)}, u32[]{:S(2)}) %collective-permute-start.9) | collective-permute-done | bytes 278560 | tf_op jit(solution)/shard_map/ppermute | solution.py:27
  30.7 1.6 %collective-permute-start.10 = (f32[136,256]{1,0:T(8,128)S(1)}, f32[136,256]{1,0:T(8,128)S(1)}, u32[]{:S(2)}, u32[]{:S(2)}) collective-permute-start(f32[136,256]{1,0:T(8,128)S(1)} %fusion), channel_id=1, source_target_pairs={{0,2},{2,0},{4,6},{6,4},{8,10},{10,8},{12,14},{14,12},{1,3},{3,1},... | collective-permute-start | bytes 417800 | tf_op jit(solution)/shard_map/ppermute | solution.py:23
  32.2 0.0 copy-start.3
  32.2 0.0 copy-start.4
  32.2 0.7 %copy-done.3 = s32[128]{0:T(128)S(1)} copy-done((s32[128]{0:T(128)S(1)}, s32[128]{0:T(128)}, u32[]{:S(2)}) %copy-start.3) | copy-done | bytes 536
  32.9 0.0 copy-done.4
  32.9 0.1 shard_map.59
  33.0 0.1 collective-permute-start.4
  33.1 3.3 %collective-permute-done.10 = f32[136,256]{1,0:T(8,128)S(1)} collective-permute-done((f32[136,256]{1,0:T(8,128)S(1)}, f32[136,256]{1,0:T(8,128)S(1)}, u32[]{:S(2)}, u32[]{:S(2)}) %collective-permute-start.10) | collective-permute-done | bytes 139296 | tf_op jit(solution)/shard_map/ppermute | solution.py:23
  36.5 0.1 fusion.15.refs_9_
  36.6 0.1 collective-permute-start.11
  36.7 1.7 %collective-permute-start.12 = (bf16[128,256]{1,0:T(8,128)(2,1)S(1)}, bf16[128,256]{1,0:T(8,128)(2,1)S(1)}, u32[]{:S(2)}, u32[]{:S(2)}) collective-permute-start(bf16[128,256]{1,0:T(8,128)(2,1)S(1)} %fusion.15.refs_9_), channel_id=1, source_target_pairs={{0,12},{2,14},{4,8},{6,10},{8,4},{10,6},{12,0},{14,2},{1,13},{3,15... | collective-permute-start | bytes 196616 | tf_op jit(solution)/shard_map/ppermute | solution.py:23
  38.4 1.7 %collective-permute-start.13 = (bf16[128,256]{1,0:T(8,128)(2,1)S(1)}, bf16[128,256]{1,0:T(8,128)(2,1)S(1)}, u32[]{:S(2)}, u32[]{:S(2)}) collective-permute-start(bf16[128,256]{1,0:T(8,128)(2,1)S(1)} %fusion.15.refs_9_), channel_id=1, source_target_pairs={{0,4},{2,6},{4,0},{6,2},{8,12},{10,14},{12,8},{14,10},{1,5},{3,7},... | collective-permute-start | bytes 196616 | tf_op jit(solution)/shard_map/ppermute | solution.py:23
  40.1 0.0 collective-permute-done.4.refs_8_
  40.1 3.5 %collective-permute-done.11.refs_10_ = bf16[128,256]{1,0:T(8,128)(2,1)S(1)} collective-permute-done((bf16[128,256]{1,0:T(8,128)(2,1)S(1)}, bf16[128,256]{1,0:T(8,128)(2,1)S(1)}, u32[]{:S(2)}, u32[]{:S(2)}) %collective-permute-start.11) | collective-permute-done | bytes 65568 | tf_op jit(solution)/shard_map/ppermute | solution.py:23
  43.6 0.0 collective-permute-done.12.refs_11_
  43.6 0.2 collective-permute-done.13.refs_12_
  43.9 0.5 shard_map.60
  44.3 0.1 collective-permute-start.14
  44.4 1.5 %collective-permute-done.14 = f32[2,128,256]{2,1,0:T(8,128)S(1)} collective-permute-done((f32[2,128,256]{2,1,0:T(8,128)S(1)}, f32[2,128,256]{2,1,0:T(8,128)S(1)}, u32[]{:S(2)}, u32[]{:S(2)}) %collective-permute-start.14) | collective-permute-done | bytes 262176 | tf_op jit(solution)/shard_map/ppermute | solution.py:27
  45.9 1.6 %collective-permute-start.15 = (f32[128,256]{1,0:T(8,128)S(1)}, f32[128,256]{1,0:T(8,128)S(1)}, u32[]{:S(2)}, u32[]{:S(2)}) collective-permute-start(f32[128,256]{1,0:T(8,128)S(1)} %fusion.3), channel_id=1, source_target_pairs={{0,2},{2,0},{4,6},{6,4},{8,10},{10,8},{12,14},{14,12},{1,3},{3,1},... | collective-permute-start | bytes 393224 | tf_op jit(solution)/shard_map/ppermute | solution.py:23
  47.5 4.0 %collective-permute-done.15 = f32[128,256]{1,0:T(8,128)S(1)} collective-permute-done((f32[128,256]{1,0:T(8,128)S(1)}, f32[128,256]{1,0:T(8,128)S(1)}, u32[]{:S(2)}, u32[]{:S(2)}) %collective-permute-start.15) | collective-permute-done | bytes 131104 | tf_op jit(solution)/shard_map/ppermute | solution.py:23
  51.6 0.7 %fusion.16 = bf16[128,256]{1,0:T(8,128)(2,1)} fusion(f32[128,256]{1,0:T(8,128)S(1)} %shard_map.59, bf16[128,256]{1,0:T(8,128)(2,1)S(1)} %fusion.15.refs_9_, f32[128,256]{1,0:T(8,128)S(1)} %collective-permute-done.15, f32[128,256]{1,0:T(8,128)S(1)} %get-tuple-element.24, f32[2,128,256]{2,1,0:T(8,128)S(1)} %collective-permute-done.14, f32[128]{0:T(128)S(1)} %fusion.18), kind=kLoop, calls=%fused_computation.21 | loop fusion | flops 294912 | bytes 655872 | tf_op jit(solution)/shard_map/convert_element_type | solution.py:204
  (6 shorter events, 0.1 us)
Async XLA Ops:
  0.0 12.8 %collective-permute-start.5 = (bf16[128,256]{1,0:T(8,128)(2,1)}, bf16[128,256]{1,0:T(8,128)(2,1)S(1)}, u32[]{:S(2)}, u32[]{:S(2)}) collective-permute-start(bf16[128,256]{1,0:T(8,128)(2,1)} %refs_0_.1), channel_id=1, source_target_pairs={{0,8},{2,10},{4,12},{6,14},{8,0},{10,2},{12,4},{14,6},{1,9},{3,11}... | collective-permute-start | bytes 196616 | tf_op jit(solution)/shard_map/ppermute | solution.py:23
  4.0 0.7 %copy-start.2 = (s32[8,2,1]{0,2,1:T(1,128)S(1)}, s32[8,2,1]{0,2,1:T(1,128)}, u32[]{:S(2)}) copy-start(s32[8,2,1]{0,2,1:T(1,128)} %param.6) | copy-start | bytes 196
  4.7 1.0 %copy-start = (bf16[1024,2,128]{2,1,0:T(2,128)(2,1)S(1)}, bf16[1024,2,128]{2,1,0:T(2,128)(2,1)}, u32[]{:S(2)}) copy-start(bf16[1024,2,128]{2,1,0:T(2,128)(2,1)} %param.5) | copy-start | bytes 1572868
  5.8 5.0 %copy-start.1 = (bf16[128,256]{1,0:T(8,128)(2,1)S(1)}, bf16[128,256]{1,0:T(8,128)(2,1)}, u32[]{:S(2)}) copy-start(bf16[128,256]{1,0:T(8,128)(2,1)} %refs_0_.1) | copy-start | bytes 196612
  6.8 16.6 %collective-permute-start = (bf16[2,2,128,128]{3,2,1,0:T(8,128)(2,1)S(1)}, bf16[2,2,128,128]{3,2,1,0:T(8,128)(2,1)S(1)}, u32[]{:S(2)}, u32[]{:S(2)}) collective-permute-start(bf16[2,2,128,128]{3,2,1,0:T(8,128)(2,1)S(1)} %get-tuple-element.18.refs_2_), channel_id=1, source_target_pairs={{0,8},{2,10},{4,12},{6,14},{8,0},{10,2},{12,4},{14,6},{1,9},{3,11}... | collective-permute-start | bytes 393224 | tf_op jit(solution)/shard_map/ppermute | solution.py:23
  6.8 16.6 %collective-permute-start.1 = (bf16[2,2,128,128]{3,2,1,0:T(8,128)(2,1)S(1)}, bf16[2,2,128,128]{3,2,1,0:T(8,128)(2,1)S(1)}, u32[]{:S(2)}, u32[]{:S(2)}) collective-permute-start(bf16[2,2,128,128]{3,2,1,0:T(8,128)(2,1)S(1)} %get-tuple-element.19.refs_3_), channel_id=1, source_target_pairs={{0,12},{2,14},{4,8},{6,10},{8,4},{10,6},{12,0},{14,2},{1,13},{3,15... | collective-permute-start | bytes 393224 | tf_op jit(solution)/shard_map/ppermute | solution.py:23
  10.8 12.7 %collective-permute-start.2 = (bf16[2,2,128,128]{3,2,1,0:T(8,128)(2,1)S(1)}, bf16[2,2,128,128]{3,2,1,0:T(8,128)(2,1)S(1)}, u32[]{:S(2)}, u32[]{:S(2)}) collective-permute-start(bf16[2,2,128,128]{3,2,1,0:T(8,128)(2,1)S(1)} %get-tuple-element.17.refs_1_), channel_id=1, source_target_pairs={{0,4},{2,6},{4,0},{6,2},{8,12},{10,14},{12,8},{14,10},{1,5},{3,7},... | collective-permute-start | bytes 393224 | tf_op jit(solution)/shard_map/ppermute | solution.py:23
  10.8 11.0 %collective-permute-start.6 = (bf16[128,256]{1,0:T(8,128)(2,1)S(1)}, bf16[128,256]{1,0:T(8,128)(2,1)S(1)}, u32[]{:S(2)}, u32[]{:S(2)}) collective-permute-start(bf16[128,256]{1,0:T(8,128)(2,1)S(1)} %copy-done.1), channel_id=1, source_target_pairs={{0,4},{2,6},{4,0},{6,2},{8,12},{10,14},{12,8},{14,10},{1,5},{3,7},... | collective-permute-start | bytes 196616 | tf_op jit(solution)/shard_map/ppermute | solution.py:23
  12.8 10.5 %collective-permute-start.7 = (bf16[128,256]{1,0:T(8,128)(2,1)S(1)}, bf16[128,256]{1,0:T(8,128)(2,1)S(1)}, u32[]{:S(2)}, u32[]{:S(2)}) collective-permute-start(bf16[128,256]{1,0:T(8,128)(2,1)S(1)} %collective-permute-done.5.refs_1_), channel_id=1, source_target_pairs={{0,4},{2,6},{4,0},{6,2},{8,12},{10,14},{12,8},{14,10},{1,5},{3,7},... | collective-permute-start | bytes 196616 | tf_op jit(solution)/shard_map/ppermute | solution.py:23
  21.8 6.6 %collective-permute-start.3 = (bf16[2,4,128,128]{3,2,1,0:T(8,128)(2,1)S(1)}, bf16[2,4,128,128]{3,2,1,0:T(8,128)(2,1)S(1)}, u32[]{:S(2)}, u32[]{:S(2)}) collective-permute-start(bf16[2,4,128,128]{3,2,1,0:T(8,128)(2,1)S(1)} %get-tuple-element.20), channel_id=1, source_target_pairs={{0,2},{2,0},{4,6},{6,4},{8,10},{10,8},{12,14},{14,12},{1,3},{3,1},... | collective-permute-start | bytes 786440 | tf_op jit(solution)/shard_map/ppermute | solution.py:23
  23.3 5.0 %collective-permute-start.8 = (bf16[512,256]{1,0:T(8,128)(2,1)S(1)}, bf16[512,256]{1,0:T(8,128)(2,1)S(1)}, u32[]{:S(2)}, u32[]{:S(2)}) collective-permute-start(bf16[512,256]{1,0:T(8,128)(2,1)S(1)} %shard_map.57.refs_9_), channel_id=1, source_target_pairs={{0,1},{1,0},{2,3},{3,2},{4,5},{5,4},{6,7},{7,6},{8,9},{9,8},{10,11... | collective-permute-start | bytes 786440 | tf_op jit(solution)/shard_map/ppermute | solution.py:27
  29.0 1.6 %collective-permute-start.9 = (f32[2,136,256]{2,1,0:T(8,128)S(1)}, f32[2,136,256]{2,1,0:T(8,128)S(1)}, u32[]{:S(2)}, u32[]{:S(2)}) collective-permute-start(f32[2,136,256]{2,1,0:T(8,128)S(1)} %get-tuple-element.22), channel_id=1, source_target_pairs={{0,1},{1,0},{2,3},{3,2},{4,5},{5,4},{6,7},{7,6},{8,9},{9,8},{10,11... | collective-permute-start | bytes 835592 | tf_op jit(solution)/shard_map/ppermute | solution.py:27
  30.7 5.8 %collective-permute-start.10 = (f32[136,256]{1,0:T(8,128)S(1)}, f32[136,256]{1,0:T(8,128)S(1)}, u32[]{:S(2)}, u32[]{:S(2)}) collective-permute-start(f32[136,256]{1,0:T(8,128)S(1)} %fusion), channel_id=1, source_target_pairs={{0,2},{2,0},{4,6},{6,4},{8,10},{10,8},{12,14},{14,12},{1,3},{3,1},... | collective-permute-start | bytes 417800 | tf_op jit(solution)/shard_map/ppermute | solution.py:23
  32.2 0.7 %copy-start.3 = (s32[128]{0:T(128)S(1)}, s32[128]{0:T(128)}, u32[]{:S(2)}) copy-start(s32[128]{0:T(128)} %param.8) | copy-start | bytes 1540
  32.2 0.7 %copy-start.4 = (s32[128]{0:T(128)S(1)}, s32[128]{0:T(128)}, u32[]{:S(2)}) copy-start(s32[128]{0:T(128)} %param.9) | copy-start | bytes 1540
  33.0 7.1 %collective-permute-start.4 = (bf16[4,2,128,128]{3,2,1,0:T(8,128)(2,1)S(1)}, bf16[4,2,128,128]{3,2,1,0:T(8,128)(2,1)S(1)}, u32[]{:S(2)}, u32[]{:S(2)}) collective-permute-start(bf16[4,2,128,128]{3,2,1,0:T(8,128)(2,1)S(1)} %shard_map.56.refs_8_), channel_id=1, source_target_pairs={{0,1},{1,0},{2,3},{3,2},{4,5},{5,4},{6,7},{7,6},{8,9},{9,8},{10,11... | collective-permute-start | bytes 786440 | tf_op jit(solution)/shard_map/ppermute | solution.py:27
  36.6 7.0 %collective-permute-start.11 = (bf16[128,256]{1,0:T(8,128)(2,1)S(1)}, bf16[128,256]{1,0:T(8,128)(2,1)S(1)}, u32[]{:S(2)}, u32[]{:S(2)}) collective-permute-start(bf16[128,256]{1,0:T(8,128)(2,1)S(1)} %fusion.15.refs_9_), channel_id=1, source_target_pairs={{0,8},{2,10},{4,12},{6,14},{8,0},{10,2},{12,4},{14,6},{1,9},{3,11}... | collective-permute-start | bytes 196616 | tf_op jit(solution)/shard_map/ppermute | solution.py:23
  36.7 6.9 %collective-permute-start.12 = (bf16[128,256]{1,0:T(8,128)(2,1)S(1)}, bf16[128,256]{1,0:T(8,128)(2,1)S(1)}, u32[]{:S(2)}, u32[]{:S(2)}) collective-permute-start(bf16[128,256]{1,0:T(8,128)(2,1)S(1)} %fusion.15.refs_9_), channel_id=1, source_target_pairs={{0,12},{2,14},{4,8},{6,10},{8,4},{10,6},{12,0},{14,2},{1,13},{3,15... | collective-permute-start | bytes 196616 | tf_op jit(solution)/shard_map/ppermute | solution.py:23
  38.4 5.4 %collective-permute-start.13 = (bf16[128,256]{1,0:T(8,128)(2,1)S(1)}, bf16[128,256]{1,0:T(8,128)(2,1)S(1)}, u32[]{:S(2)}, u32[]{:S(2)}) collective-permute-start(bf16[128,256]{1,0:T(8,128)(2,1)S(1)} %fusion.15.refs_9_), channel_id=1, source_target_pairs={{0,4},{2,6},{4,0},{6,2},{8,12},{10,14},{12,8},{14,10},{1,5},{3,7},... | collective-permute-start | bytes 196616 | tf_op jit(solution)/shard_map/ppermute | solution.py:23
  44.3 1.6 %collective-permute-start.14 = (f32[2,128,256]{2,1,0:T(8,128)S(1)}, f32[2,128,256]{2,1,0:T(8,128)S(1)}, u32[]{:S(2)}, u32[]{:S(2)}) collective-permute-start(f32[2,128,256]{2,1,0:T(8,128)S(1)} %get-tuple-element.25), channel_id=1, source_target_pairs={{0,1},{1,0},{2,3},{3,2},{4,5},{5,4},{6,7},{7,6},{8,9},{9,8},{10,11... | collective-permute-start | bytes 786440 | tf_op jit(solution)/shard_map/ppermute | solution.py:27
  45.9 5.6 %collective-permute-start.15 = (f32[128,256]{1,0:T(8,128)S(1)}, f32[128,256]{1,0:T(8,128)S(1)}, u32[]{:S(2)}, u32[]{:S(2)}) collective-permute-start(f32[128,256]{1,0:T(8,128)S(1)} %fusion.3), channel_id=1, source_target_pairs={{0,2},{2,0},{4,6},{6,4},{8,10},{10,8},{12,14},{14,12},{1,3},{3,1},... | collective-permute-start | bytes 393224 | tf_op jit(solution)/shard_map/ppermute | solution.py:23

commit v6 on v5

--- a/solution.py
+++ b/solution.py
@@ -8,8 +8,8 @@
 ITERS = 2
 CARRY = 0.8
 SUBLANES = 8
-JOIN_FLOPS = 0
-SIDES_FLOPS = 3_000_000_000
+JOIN_FLOPS = 3_000_000_000
+SIDES_FLOPS = 2_000_000_000
 MIB = 1024 * 1024
 
 
@@ -69,6 +69,22 @@
                     halves[j - 1][i, k] = piece
 
 
+def fold_kernel(y_count, first, *refs):
+    keeps, taken, (total, *sends) = refs[:y_count], refs[y_count], refs[y_count + 1 :]
+    total[...] = keeps[0][...] + taken[0]
+    for j, send in enumerate(sends, 1):
+        both = keeps[j][...] + taken[j]
+        width = both.shape[0] - (SUBLANES if first else 0)
+        send[:width, :] = both[:width].astype(jnp.bfloat16)
+        if first:
+            sums = jnp.concatenate([both[width:]] * 2, axis=0)
+            high = sums.astype(jnp.bfloat16).astype(jnp.float32)
+            middle = (sums - high).astype(jnp.bfloat16).astype(jnp.float32)
+            row = lax.broadcasted_iota(jnp.int32, sums.shape, 0)
+            terms = jnp.where(row == 0, high, jnp.where(row == 1, middle, sums - high - middle))
+            send[width:, :] = terms.astype(jnp.bfloat16)
+
+
 def join_kernel(*refs):
     parts, out = refs[:-1], refs[-1]
     start = 0
@@ -153,17 +169,13 @@
         affinity.reshape(stripe * sides, width),
         smem=1,
     )
-    sent, halves = sent[:z_count], sent[z_count:]
+    sent, halves = list(sent[:z_count]), sent[z_count:]
+    current, sent[0] = lax.optimization_barrier((labels, sent[0]))
     arrived = {k: swap_rows(sent[k], k * y_count) for k in far_first(z_count)}
     strips = [arrived[k] for k in far_first(z_count)]
     halves = [swap_rows(x, j + 1) for j, x in enumerate(halves)]
-    near = {k: swap_rows(labels, k * y_count) for k in far_first(z_count) if k & (k - 1) == 0}
-    for k in far_first(z_count):
-        if k not in near:
-            low = k & -k
-            near[k] = swap_rows(near[k ^ low], low * y_count)
-    order = [0] + sorted(near, key=lambda k: (k & (k - 1) != 0, -k))
-    values = join([labels] + [near[k] for k in order[1:]], flops=JOIN_FLOPS)
+    order = [0] + far_first(z_count)
+    values = join([current] + [swap_rows(current, k * y_count) for k in order[1:]], flops=JOIN_FLOPS)
     swapped = swap_cores(values)
     other = jax.ShapeDtypeStruct((z_count, y_count, width, width), jnp.bfloat16)
     sides = call(other_kernel, other, sent[0], *strips, flops=SIDES_FLOPS)
@@ -176,11 +188,9 @@
         seed_mask.reshape(1, width),
     )
 
-    current = labels
     degree = None
     for step in range(ITERS):
         if step > 0:
-            order = [0] + far_first(z_count)
             pieces = [other, current] + [swap_rows(current, k * y_count) for k in order[1:]]
         height = width + (SUBLANES if step == 0 else 0)
         part = jax.ShapeDtypeStruct((height, classes), jnp.float32)
@@ -195,12 +205,16 @@
             flops=2 * 2 * 2 * y_count * z_count * width * width * classes,
         )
         taken = swap_cores(give)
-        spread = keeps[0] + taken[0]
-        for j in range(1, y_count):
-            spread = spread + swap_rows(keeps[j] + taken[j], j)
+        send = jax.ShapeDtypeStruct((width + (2 * SUBLANES if step == 0 else 0), classes), jnp.bfloat16)
+        total, *sends = call(
+            lambda *refs: fold_kernel(y_count, step == 0, *refs), [part] + [send] * (y_count - 1), *keeps, taken
+        )
+        sends = [swap_rows(x, j + 1).astype(jnp.float32) for j, x in enumerate(sends)]
+        spread = sum((x[:width] for x in sends), total[:width])
         if step == 0:
-            degree = 1.0 + 0.5 * spread[width, :width][:, None]
-        mixed = CARRY * (0.5 * spread[:width] + current.astype(jnp.float32)) / degree
+            sums = sum((x[width : width + 3, :width].sum(axis=0) for x in sends), total[width, :width])
+            degree = 1.0 + 0.5 * sums[:, None]
+        mixed = CARRY * (0.5 * spread + current.astype(jnp.float32)) / degree
         current = (mixed + base).astype(jnp.bfloat16)
     return current
 

time: 52.5 us -> 49.4 us (0.941)
  waiting for transfers between devices: 27.9 us -> 20.4 us
  starting transfers between devices: 18.6 us -> 23.1 us
    ppermute x12, waiting for transfers between devices: 24.9 us -> 17.3 us  [swap_rows(): return lax.ppermute(value, 'row', [(i, i ^ shift) for i in range(count)])]
    ppermute x12, starting transfers between devices: 18.4 us -> 22.8 us  [swap_rows(): return lax.ppermute(value, 'row', [(i, i ^ shift) for i in range(count)])]
    pallas_call x6 -> x8, Pallas kernels: 2.26 us -> 2.32 us  [call(): pl.pallas_call(kernel, out_shape=out_shape, in_specs=[pl.BlockSpec(memory...]
  transfers between devices with their start and end apart: 16 -> 16, of which waited for: 8 -> 9; matrix products, arithmetic and copies ran while one was open for 0% -> 0% of each run, Pallas kernels for 2% -> 0%
where the time goes in v6:
time: 49.4 us; the launch traced here: 49.2 us
  starting transfers between devices  23.1 us (47%)
  waiting for transfers between devices  20.4 us (41%)
  local copies, waits for them, and re-layouts  2.39 us (5%)
  Pallas kernels  2.32 us (5%)
  other arithmetic  0.86 us (2%)
    ppermute x12, starting transfers between devices, swap_rows(): return lax.ppermute(value, 'row', [(i, i ^ shift) for i in range(count)])  22.8 us
    ppermute x12, waiting for transfers between devices, swap_rows(): return lax.ppermute(value, 'row', [(i, i ^ shift) for i in range(count)])  17.3 us
    ppermute x4, waiting for transfers between devices, swap_cores(): return lax.ppermute(value, 'col', [(0, 1), (1, 0)])  3.07 us
    unnamed x10, local copies, waits for them, and re-layouts  2.39 us
    pallas_call x8, Pallas kernels, call(): pl.pallas_call(kernel, out_shape=out_shape, in_specs=[pl.BlockSpec(memory...  2.32 us
  transfers between devices with their start and end apart: 16, of which 9 were waited for; matrix products, arithmetic and copies ran while one was open for 0% of the time, Pallas kernels for 0%

profile of v6, /device:TPU:0, one launch (start us, length us, event | category | flops | bytes accessed | tf_op | source)
XLA Modules:
  0.0 49.2 jit_solution(10387430578278678093)
XLA Ops:
  0.0 0.0 copy-start.2
  0.0 0.7 %copy-done.2 = s32[8,2,1]{0,2,1:T(1,128)S(1)} copy-done((s32[8,2,1]{0,2,1:T(1,128)S(1)}, s32[8,2,1]{0,2,1:T(1,128)}, u32[]{:S(2)}) %copy-start.2) | copy-done | bytes 88
  0.7 0.0 copy-start
  0.7 1.0 %copy-done = bf16[1024,2,128]{2,1,0:T(2,128)(2,1)S(1)} copy-done((bf16[1024,2,128]{2,1,0:T(2,128)(2,1)S(1)}, bf16[1024,2,128]{2,1,0:T(2,128)(2,1)}, u32[]{:S(2)}) %copy-start) | copy-done | bytes 524312
  1.7 0.0 copy-start.1
  1.7 1.0 %shard_map.55 = (bf16[2,2,128,128]{3,2,1,0:T(8,128)(2,1)S(1)}, bf16[2,2,128,128]{3,2,1,0:T(8,128)(2,1)S(1)}, bf16[2,2,128,128]{3,2,1,0:T(8,128)(2,1)S(1)}, bf16[...) custom-call(s32[2,1,8]{2,1,0:T(1,128)S(1)} %bitcast.11, bf16[2048,128]{1,0:T(8,128)(2,1)S(1)} %bitcast.10), custom_call_target="tpu_custom_call" | custom-call | bytes 1310784 | tf_op jit(solution)/shard_map/pallas_call | solution.py:33
  2.7 0.0 copy-done.1
  2.7 4.1 %collective-permute-start.5 = (bf16[128,256]{1,0:T(8,128)(2,1)S(1)}, bf16[128,256]{1,0:T(8,128)(2,1)S(1)}, u32[]{:S(2)}, u32[]{:S(2)}) collective-permute-start(bf16[128,256]{1,0:T(8,128)(2,1)S(1)} %copy-done.1), channel_id=1, source_target_pairs={{0,8},{2,10},{4,12},{6,14},{8,0},{10,2},{12,4},{14,6},{1,9},{3,11}... | collective-permute-start | bytes 196616 | tf_op jit(solution)/shard_map/ppermute | solution.py:23
  6.8 1.3 %collective-permute-start.6 = (bf16[128,256]{1,0:T(8,128)(2,1)S(1)}, bf16[128,256]{1,0:T(8,128)(2,1)S(1)}, u32[]{:S(2)}, u32[]{:S(2)}) collective-permute-start(bf16[128,256]{1,0:T(8,128)(2,1)S(1)} %copy-done.1), channel_id=1, source_target_pairs={{0,12},{2,14},{4,8},{6,10},{8,4},{10,6},{12,0},{14,2},{1,13},{3,15... | collective-permute-start | bytes 196616 | tf_op jit(solution)/shard_map/ppermute | solution.py:23
  8.2 0.2 collective-permute-start.7
  8.4 2.8 %collective-permute-start = (bf16[2,2,128,128]{3,2,1,0:T(8,128)(2,1)S(1)}, bf16[2,2,128,128]{3,2,1,0:T(8,128)(2,1)S(1)}, u32[]{:S(2)}, u32[]{:S(2)}) collective-permute-start(bf16[2,2,128,128]{3,2,1,0:T(8,128)(2,1)S(1)} %get-tuple-element.25.refs_2_), channel_id=1, source_target_pairs={{0,8},{2,10},{4,12},{6,14},{8,0},{10,2},{12,4},{14,6},{1,9},{3,11}... | collective-permute-start | bytes 393224 | tf_op jit(solution)/shard_map/ppermute | solution.py:23
  11.2 1.3 %collective-permute-start.1 = (bf16[2,2,128,128]{3,2,1,0:T(8,128)(2,1)S(1)}, bf16[2,2,128,128]{3,2,1,0:T(8,128)(2,1)S(1)}, u32[]{:S(2)}, u32[]{:S(2)}) collective-permute-start(bf16[2,2,128,128]{3,2,1,0:T(8,128)(2,1)S(1)} %get-tuple-element.26.refs_3_), channel_id=1, source_target_pairs={{0,12},{2,14},{4,8},{6,10},{8,4},{10,6},{12,0},{14,2},{1,13},{3,15... | collective-permute-start | bytes 393224 | tf_op jit(solution)/shard_map/ppermute | solution.py:23
  12.6 0.0 collective-permute-done.5.refs_1_
  12.6 0.6 %collective-permute-start.2 = (bf16[2,2,128,128]{3,2,1,0:T(8,128)(2,1)S(1)}, bf16[2,2,128,128]{3,2,1,0:T(8,128)(2,1)S(1)}, u32[]{:S(2)}, u32[]{:S(2)}) collective-permute-start(bf16[2,2,128,128]{3,2,1,0:T(8,128)(2,1)S(1)} %get-tuple-element.24.refs_1_), channel_id=1, source_target_pairs={{0,4},{2,6},{4,0},{6,2},{8,12},{10,14},{12,8},{14,10},{1,5},{3,7},... | collective-permute-start | bytes 393224 | tf_op jit(solution)/shard_map/ppermute | solution.py:23
  13.2 0.5 %collective-permute-done.6.refs_2_ = bf16[128,256]{1,0:T(8,128)(2,1)S(1)} collective-permute-done((bf16[128,256]{1,0:T(8,128)(2,1)S(1)}, bf16[128,256]{1,0:T(8,128)(2,1)S(1)}, u32[]{:S(2)}, u32[]{:S(2)}) %collective-permute-start.6) | collective-permute-done | bytes 65568 | tf_op jit(solution)/shard_map/ppermute | solution.py:23
  13.7 1.5 %collective-permute-start.3 = (bf16[2,4,128,128]{3,2,1,0:T(8,128)(2,1)S(1)}, bf16[2,4,128,128]{3,2,1,0:T(8,128)(2,1)S(1)}, u32[]{:S(2)}, u32[]{:S(2)}) collective-permute-start(bf16[2,4,128,128]{3,2,1,0:T(8,128)(2,1)S(1)} %get-tuple-element.27), channel_id=1, source_target_pairs={{0,2},{2,0},{4,6},{6,4},{8,10},{10,8},{12,14},{14,12},{1,3},{3,1},... | collective-permute-start | bytes 786440 | tf_op jit(solution)/shard_map/ppermute | solution.py:23
  15.3 0.0 collective-permute-done.7.refs_3_
  15.3 0.1 collective-permute-start.8
  15.4 6.7 %collective-permute-done.refs_1_.refs_4_ = bf16[2,2,128,128]{3,2,1,0:T(8,128)(2,1)S(1)} collective-permute-done((bf16[2,2,128,128]{3,2,1,0:T(8,128)(2,1)S(1)}, bf16[2,2,128,128]{3,2,1,0:T(8,128)(2,1)S(1)}, u32[]{:S(2)}, u32[]{:S(2)}) %collective-permute-start) | collective-permute-done | bytes 131104 | tf_op jit(solution)/shard_map/ppermute | solution.py:23
  22.1 0.0 collective-permute-done.1.refs_2_.refs_5_
  22.1 0.1 collective-permute-done.2.refs_3_.refs_6_
  22.2 0.0 collective-permute-done.3.refs_7_
  22.2 0.0 collective-permute-done.8.refs_10_
  22.2 0.7 %shard_map.58 = (f32[136,256]{1,0:T(8,128)S(1)}, f32[136,256]{1,0:T(8,128)S(1)}, f32[2,136,256]{2,1,0:T(8,128)S(1)}) custom-call(bf16[2,2,128,128]{3,2,1,0:T(8,128)(2,1)S(1)} %get-tuple-element.23.refs_0_, bf16[2,2,128,128]{3,2,1,0:T(8,128)(2,1)S(1)} %get-tuple-element.24.refs_1_, bf16[2,2,128,128]{3,2,1,0:T(8,128)(2,1)S(1)} %get-tuple-element.25.refs_2_, ...), custom_call_target="tpu_custom_call" | custom-call | flops 268435456 | bytes 2523136 | tf_op jit(solution)/shard_map/pallas_call | solution.py:33
  22.9 0.1 collective-permute-start.9
  23.0 1.5 %collective-permute-done.9.refs_2_ = f32[2,136,256]{2,1,0:T(8,128)S(1)} collective-permute-done((f32[2,136,256]{2,1,0:T(8,128)S(1)}, f32[2,136,256]{2,1,0:T(8,128)S(1)}, u32[]{:S(2)}, u32[]{:S(2)}) %collective-permute-start.9) | collective-permute-done | bytes 278560 | tf_op jit(solution)/shard_map/ppermute | solution.py:27
  24.6 1.8 %collective-permute-start.10 = (bf16[144,256]{1,0:T(8,128)(2,1)S(1)}, bf16[144,256]{1,0:T(8,128)(2,1)S(1)}, u32[]{:S(2)}, u32[]{:S(2)}) collective-permute-start(bf16[144,256]{1,0:T(8,128)(2,1)S(1)} %get-tuple-element.33), channel_id=1, source_target_pairs={{0,2},{2,0},{4,6},{6,4},{8,10},{10,8},{12,14},{14,12},{1,3},{3,1},... | collective-permute-start | bytes 221192 | tf_op jit(solution)/shard_map/ppermute | solution.py:23
  26.4 0.0 copy-start.3
  26.4 0.0 copy-start.4
  26.4 0.7 %copy-done.3 = s32[128]{0:T(128)S(1)} copy-done((s32[128]{0:T(128)S(1)}, s32[128]{0:T(128)}, u32[]{:S(2)}) %copy-start.3) | copy-done | bytes 536
  27.0 0.0 copy-done.4
  27.0 0.1 shard_map.60
  27.1 0.1 collective-permute-start.4
  27.2 1.8 %collective-permute-done.10 = bf16[144,256]{1,0:T(8,128)(2,1)S(1)} collective-permute-done((bf16[144,256]{1,0:T(8,128)(2,1)S(1)}, bf16[144,256]{1,0:T(8,128)(2,1)S(1)}, u32[]{:S(2)}, u32[]{:S(2)}) %collective-permute-start.10) | collective-permute-done | bytes 73760 | tf_op jit(solution)/shard_map/ppermute | solution.py:23
  29.1 0.1 fusion.5.refs_9_
  29.2 6.8 %collective-permute-start.11 = (bf16[128,256]{1,0:T(8,128)(2,1)S(1)}, bf16[128,256]{1,0:T(8,128)(2,1)S(1)}, u32[]{:S(2)}, u32[]{:S(2)}) collective-permute-start(bf16[128,256]{1,0:T(8,128)(2,1)S(1)} %fusion.5.refs_9_), channel_id=1, source_target_pairs={{0,8},{2,10},{4,12},{6,14},{8,0},{10,2},{12,4},{14,6},{1,9},{3,11}... | collective-permute-start | bytes 196616 | tf_op jit(solution)/shard_map/ppermute | solution.py:23
  36.0 0.0 collective-permute-start.12
  36.0 0.6 %collective-permute-start.13 = (bf16[128,256]{1,0:T(8,128)(2,1)S(1)}, bf16[128,256]{1,0:T(8,128)(2,1)S(1)}, u32[]{:S(2)}, u32[]{:S(2)}) collective-permute-start(bf16[128,256]{1,0:T(8,128)(2,1)S(1)} %fusion.5.refs_9_), channel_id=1, source_target_pairs={{0,4},{2,6},{4,0},{6,2},{8,12},{10,14},{12,8},{14,10},{1,5},{3,7},... | collective-permute-start | bytes 196616 | tf_op jit(solution)/shard_map/ppermute | solution.py:23
  36.6 0.0 collective-permute-done.4.refs_8_
  36.6 2.4 %collective-permute-done.11.refs_10_ = bf16[128,256]{1,0:T(8,128)(2,1)S(1)} collective-permute-done((bf16[128,256]{1,0:T(8,128)(2,1)S(1)}, bf16[128,256]{1,0:T(8,128)(2,1)S(1)}, u32[]{:S(2)}, u32[]{:S(2)}) %collective-permute-start.11) | collective-permute-done | bytes 65568 | tf_op jit(solution)/shard_map/ppermute | solution.py:23
  39.0 3.0 %collective-permute-done.12.refs_11_ = bf16[128,256]{1,0:T(8,128)(2,1)S(1)} collective-permute-done((bf16[128,256]{1,0:T(8,128)(2,1)S(1)}, bf16[128,256]{1,0:T(8,128)(2,1)S(1)}, u32[]{:S(2)}, u32[]{:S(2)}) %collective-permute-start.12) | collective-permute-done | bytes 65568 | tf_op jit(solution)/shard_map/ppermute | solution.py:23
  42.0 0.0 collective-permute-done.13.refs_12_
  42.1 0.5 shard_map.61
  42.5 0.1 collective-permute-start.14
  42.6 1.5 %collective-permute-done.14.refs_2_ = f32[2,128,256]{2,1,0:T(8,128)S(1)} collective-permute-done((f32[2,128,256]{2,1,0:T(8,128)S(1)}, f32[2,128,256]{2,1,0:T(8,128)S(1)}, u32[]{:S(2)}, u32[]{:S(2)}) %collective-permute-start.14) | collective-permute-done | bytes 262176 | tf_op jit(solution)/shard_map/ppermute | solution.py:27
  44.1 1.6 %collective-permute-start.15 = (bf16[128,256]{1,0:T(8,128)(2,1)S(1)}, bf16[128,256]{1,0:T(8,128)(2,1)S(1)}, u32[]{:S(2)}, u32[]{:S(2)}) collective-permute-start(bf16[128,256]{1,0:T(8,128)(2,1)S(1)} %get-tuple-element.38), channel_id=1, source_target_pairs={{0,2},{2,0},{4,6},{6,4},{8,10},{10,8},{12,14},{14,12},{1,3},{3,1},... | collective-permute-start | bytes 196616 | tf_op jit(solution)/shard_map/ppermute | solution.py:23
  45.7 2.7 %collective-permute-done.15 = bf16[128,256]{1,0:T(8,128)(2,1)S(1)} collective-permute-done((bf16[128,256]{1,0:T(8,128)(2,1)S(1)}, bf16[128,256]{1,0:T(8,128)(2,1)S(1)}, u32[]{:S(2)}, u32[]{:S(2)}) %collective-permute-start.15) | collective-permute-done | bytes 65568 | tf_op jit(solution)/shard_map/ppermute | solution.py:23
  48.5 0.7 %add_convert_fusion = bf16[128,256]{1,0:T(8,128)(2,1)} fusion(f32[128,256]{1,0:T(8,128)S(1)} %shard_map.60, bf16[128,256]{1,0:T(8,128)(2,1)S(1)} %fusion.5.refs_9_, f32[128,256]{1,0:T(8,128)S(1)} %get-tuple-element.37, bf16[128,256]{1,0:T(8,128)(2,1)S(1)} %collective-permute-done.15, f32[128]{0:T(128)S(1)} %fusion.7), kind=kLoop, calls=%fused_computation.6 | loop fusion | flops 294912 | bytes 459264 | tf_op jit(solution)/shard_map/convert_element_type | solution.py:218
  (7 shorter events, 0.1 us)
Async XLA Ops:
  0.0 0.7 %copy-start.2 = (s32[8,2,1]{0,2,1:T(1,128)S(1)}, s32[8,2,1]{0,2,1:T(1,128)}, u32[]{:S(2)}) copy-start(s32[8,2,1]{0,2,1:T(1,128)} %param.6) | copy-start | bytes 196
  0.7 1.0 %copy-start = (bf16[1024,2,128]{2,1,0:T(2,128)(2,1)S(1)}, bf16[1024,2,128]{2,1,0:T(2,128)(2,1)}, u32[]{:S(2)}) copy-start(bf16[1024,2,128]{2,1,0:T(2,128)(2,1)} %param.5) | copy-start | bytes 1572868
  1.7 1.0 %copy-start.1 = (bf16[128,256]{1,0:T(8,128)(2,1)S(1)}, bf16[128,256]{1,0:T(8,128)(2,1)}, u32[]{:S(2)}) copy-start(bf16[128,256]{1,0:T(8,128)(2,1)} %refs_0_) | copy-start | bytes 196612
  2.7 9.8 %collective-permute-start.5 = (bf16[128,256]{1,0:T(8,128)(2,1)S(1)}, bf16[128,256]{1,0:T(8,128)(2,1)S(1)}, u32[]{:S(2)}, u32[]{:S(2)}) collective-permute-start(bf16[128,256]{1,0:T(8,128)(2,1)S(1)} %copy-done.1), channel_id=1, source_target_pairs={{0,8},{2,10},{4,12},{6,14},{8,0},{10,2},{12,4},{14,6},{1,9},{3,11}... | collective-permute-start | bytes 196616 | tf_op jit(solution)/shard_map/ppermute | solution.py:23
  6.8 6.9 %collective-permute-start.6 = (bf16[128,256]{1,0:T(8,128)(2,1)S(1)}, bf16[128,256]{1,0:T(8,128)(2,1)S(1)}, u32[]{:S(2)}, u32[]{:S(2)}) collective-permute-start(bf16[128,256]{1,0:T(8,128)(2,1)S(1)} %copy-done.1), channel_id=1, source_target_pairs={{0,12},{2,14},{4,8},{6,10},{8,4},{10,6},{12,0},{14,2},{1,13},{3,15... | collective-permute-start | bytes 196616 | tf_op jit(solution)/shard_map/ppermute | solution.py:23
  8.2 7.1 %collective-permute-start.7 = (bf16[128,256]{1,0:T(8,128)(2,1)S(1)}, bf16[128,256]{1,0:T(8,128)(2,1)S(1)}, u32[]{:S(2)}, u32[]{:S(2)}) collective-permute-start(bf16[128,256]{1,0:T(8,128)(2,1)S(1)} %copy-done.1), channel_id=1, source_target_pairs={{0,4},{2,6},{4,0},{6,2},{8,12},{10,14},{12,8},{14,10},{1,5},{3,7},... | collective-permute-start | bytes 196616 | tf_op jit(solution)/shard_map/ppermute | solution.py:23
  8.4 13.7 %collective-permute-start = (bf16[2,2,128,128]{3,2,1,0:T(8,128)(2,1)S(1)}, bf16[2,2,128,128]{3,2,1,0:T(8,128)(2,1)S(1)}, u32[]{:S(2)}, u32[]{:S(2)}) collective-permute-start(bf16[2,2,128,128]{3,2,1,0:T(8,128)(2,1)S(1)} %get-tuple-element.25.refs_2_), channel_id=1, source_target_pairs={{0,8},{2,10},{4,12},{6,14},{8,0},{10,2},{12,4},{14,6},{1,9},{3,11}... | collective-permute-start | bytes 393224 | tf_op jit(solution)/shard_map/ppermute | solution.py:23
  11.2 10.9 %collective-permute-start.1 = (bf16[2,2,128,128]{3,2,1,0:T(8,128)(2,1)S(1)}, bf16[2,2,128,128]{3,2,1,0:T(8,128)(2,1)S(1)}, u32[]{:S(2)}, u32[]{:S(2)}) collective-permute-start(bf16[2,2,128,128]{3,2,1,0:T(8,128)(2,1)S(1)} %get-tuple-element.26.refs_3_), channel_id=1, source_target_pairs={{0,12},{2,14},{4,8},{6,10},{8,4},{10,6},{12,0},{14,2},{1,13},{3,15... | collective-permute-start | bytes 393224 | tf_op jit(solution)/shard_map/ppermute | solution.py:23
  12.6 9.6 %collective-permute-start.2 = (bf16[2,2,128,128]{3,2,1,0:T(8,128)(2,1)S(1)}, bf16[2,2,128,128]{3,2,1,0:T(8,128)(2,1)S(1)}, u32[]{:S(2)}, u32[]{:S(2)}) collective-permute-start(bf16[2,2,128,128]{3,2,1,0:T(8,128)(2,1)S(1)} %get-tuple-element.24.refs_1_), channel_id=1, source_target_pairs={{0,4},{2,6},{4,0},{6,2},{8,12},{10,14},{12,8},{14,10},{1,5},{3,7},... | collective-permute-start | bytes 393224 | tf_op jit(solution)/shard_map/ppermute | solution.py:23
  13.7 8.5 %collective-permute-start.3 = (bf16[2,4,128,128]{3,2,1,0:T(8,128)(2,1)S(1)}, bf16[2,4,128,128]{3,2,1,0:T(8,128)(2,1)S(1)}, u32[]{:S(2)}, u32[]{:S(2)}) collective-permute-start(bf16[2,4,128,128]{3,2,1,0:T(8,128)(2,1)S(1)} %get-tuple-element.27), channel_id=1, source_target_pairs={{0,2},{2,0},{4,6},{6,4},{8,10},{10,8},{12,14},{14,12},{1,3},{3,1},... | collective-permute-start | bytes 786440 | tf_op jit(solution)/shard_map/ppermute | solution.py:23
  15.3 6.9 %collective-permute-start.8 = (bf16[512,256]{1,0:T(8,128)(2,1)S(1)}, bf16[512,256]{1,0:T(8,128)(2,1)S(1)}, u32[]{:S(2)}, u32[]{:S(2)}) collective-permute-start(bf16[512,256]{1,0:T(8,128)(2,1)S(1)} %shard_map.57.refs_9_), channel_id=1, source_target_pairs={{0,1},{1,0},{2,3},{3,2},{4,5},{5,4},{6,7},{7,6},{8,9},{9,8},{10,11... | collective-permute-start | bytes 786440 | tf_op jit(solution)/shard_map/ppermute | solution.py:27
  22.9 1.6 %collective-permute-start.9 = (f32[2,136,256]{2,1,0:T(8,128)S(1)}, f32[2,136,256]{2,1,0:T(8,128)S(1)}, u32[]{:S(2)}, u32[]{:S(2)}) collective-permute-start(f32[2,136,256]{2,1,0:T(8,128)S(1)} %get-tuple-element.31), channel_id=1, source_target_pairs={{0,1},{1,0},{2,3},{3,2},{4,5},{5,4},{6,7},{7,6},{8,9},{9,8},{10,11... | collective-permute-start | bytes 835592 | tf_op jit(solution)/shard_map/ppermute | solution.py:27
  24.6 4.4 %collective-permute-start.10 = (bf16[144,256]{1,0:T(8,128)(2,1)S(1)}, bf16[144,256]{1,0:T(8,128)(2,1)S(1)}, u32[]{:S(2)}, u32[]{:S(2)}) collective-permute-start(bf16[144,256]{1,0:T(8,128)(2,1)S(1)} %get-tuple-element.33), channel_id=1, source_target_pairs={{0,2},{2,0},{4,6},{6,4},{8,10},{10,8},{12,14},{14,12},{1,3},{3,1},... | collective-permute-start | bytes 221192 | tf_op jit(solution)/shard_map/ppermute | solution.py:23
  26.4 0.7 %copy-start.3 = (s32[128]{0:T(128)S(1)}, s32[128]{0:T(128)}, u32[]{:S(2)}) copy-start(s32[128]{0:T(128)} %param.8) | copy-start | bytes 1540
  26.4 0.7 %copy-start.4 = (s32[128]{0:T(128)S(1)}, s32[128]{0:T(128)}, u32[]{:S(2)}) copy-start(s32[128]{0:T(128)} %param.9) | copy-start | bytes 1540
  27.1 9.5 %collective-permute-start.4 = (bf16[4,2,128,128]{3,2,1,0:T(8,128)(2,1)S(1)}, bf16[4,2,128,128]{3,2,1,0:T(8,128)(2,1)S(1)}, u32[]{:S(2)}, u32[]{:S(2)}) collective-permute-start(bf16[4,2,128,128]{3,2,1,0:T(8,128)(2,1)S(1)} %shard_map.56.refs_8_), channel_id=1, source_target_pairs={{0,1},{1,0},{2,3},{3,2},{4,5},{5,4},{6,7},{7,6},{8,9},{9,8},{10,11... | collective-permute-start | bytes 786440 | tf_op jit(solution)/shard_map/ppermute | solution.py:27
  29.2 9.8 %collective-permute-start.11 = (bf16[128,256]{1,0:T(8,128)(2,1)S(1)}, bf16[128,256]{1,0:T(8,128)(2,1)S(1)}, u32[]{:S(2)}, u32[]{:S(2)}) collective-permute-start(bf16[128,256]{1,0:T(8,128)(2,1)S(1)} %fusion.5.refs_9_), channel_id=1, source_target_pairs={{0,8},{2,10},{4,12},{6,14},{8,0},{10,2},{12,4},{14,6},{1,9},{3,11}... | collective-permute-start | bytes 196616 | tf_op jit(solution)/shard_map/ppermute | solution.py:23
  36.0 6.1 %collective-permute-start.12 = (bf16[128,256]{1,0:T(8,128)(2,1)S(1)}, bf16[128,256]{1,0:T(8,128)(2,1)S(1)}, u32[]{:S(2)}, u32[]{:S(2)}) collective-permute-start(bf16[128,256]{1,0:T(8,128)(2,1)S(1)} %fusion.5.refs_9_), channel_id=1, source_target_pairs={{0,12},{2,14},{4,8},{6,10},{8,4},{10,6},{12,0},{14,2},{1,13},{3,15... | collective-permute-start | bytes 196616 | tf_op jit(solution)/shard_map/ppermute | solution.py:23
  36.0 6.1 %collective-permute-start.13 = (bf16[128,256]{1,0:T(8,128)(2,1)S(1)}, bf16[128,256]{1,0:T(8,128)(2,1)S(1)}, u32[]{:S(2)}, u32[]{:S(2)}) collective-permute-start(bf16[128,256]{1,0:T(8,128)(2,1)S(1)} %fusion.5.refs_9_), channel_id=1, source_target_pairs={{0,4},{2,6},{4,0},{6,2},{8,12},{10,14},{12,8},{14,10},{1,5},{3,7},... | collective-permute-start | bytes 196616 | tf_op jit(solution)/shard_map/ppermute | solution.py:23
  42.5 1.6 %collective-permute-start.14 = (f32[2,128,256]{2,1,0:T(8,128)S(1)}, f32[2,128,256]{2,1,0:T(8,128)S(1)}, u32[]{:S(2)}, u32[]{:S(2)}) collective-permute-start(f32[2,128,256]{2,1,0:T(8,128)S(1)} %get-tuple-element.36), channel_id=1, source_target_pairs={{0,1},{1,0},{2,3},{3,2},{4,5},{5,4},{6,7},{7,6},{8,9},{9,8},{10,11... | collective-permute-start | bytes 786440 | tf_op jit(solution)/shard_map/ppermute | solution.py:27
  44.1 4.3 %collective-permute-start.15 = (bf16[128,256]{1,0:T(8,128)(2,1)S(1)}, bf16[128,256]{1,0:T(8,128)(2,1)S(1)}, u32[]{:S(2)}, u32[]{:S(2)}) collective-permute-start(bf16[128,256]{1,0:T(8,128)(2,1)S(1)} %get-tuple-element.38), channel_id=1, source_target_pairs={{0,2},{2,0},{4,6},{6,4},{8,10},{10,8},{12,14},{14,12},{1,3},{3,1},... | collective-permute-start | bytes 196616 | tf_op jit(solution)/shard_map/ppermute | solution.py:23

commit v7 on v6

--- a/solution.py
+++ b/solution.py
@@ -8,8 +8,9 @@
 ITERS = 2
 CARRY = 0.8
 SUBLANES = 8
-JOIN_FLOPS = 3_000_000_000
-SIDES_FLOPS = 2_000_000_000
+LOAD_FLOPS = 2_000_000_000
+SIDES_FLOPS = 3_000_000_000
+FAR_FLOPS = 3_000_000_000
 MIB = 1024 * 1024
 
 
@@ -98,10 +99,50 @@
     return call(join_kernel, jax.ShapeDtypeStruct((rows,) + parts[0].shape[1:], parts[0].dtype), *parts, flops=flops)
 
 
-def other_kernel(*refs):
+def load_kernel(*refs):
+    strip, pieces, out = refs[0], refs[1:-1], refs[-1]
+    sides, blocks, width, _ = strip.shape
+    for i in range(sides):
+        for j in range(blocks):
+            out[i * blocks + j] = strip[i, j]
+    spot = sides * blocks
+    for piece in pieces:
+        for top in range(0, piece.shape[0], width):
+            for left in range(0, piece.shape[1], width):
+                out[spot] = piece[top : top + width, left : left + width]
+                spot += 1
+
+
+def unload_kernel(y_count, *refs):
+    pieces, loaded, out = refs[:-2], refs[-2], refs[-1]
+    width, classes = loaded.shape[1], out.shape[1]
+    start = 0
+    for piece in pieces:
+        out[start : start + piece.shape[0]] = piece[...]
+        start += piece.shape[0]
+    for spot in range(2 * y_count, loaded.shape[0], classes // width):
+        for part in range(classes // width):
+            out[start : start + width, part * width : (part + 1) * width] = loaded[spot + part]
+        start += width
+
+
+def block_of(strip, i, j, y_count):
+    return strip[i * y_count + j] if len(strip.shape) == 3 else strip[i, j]
+
+
+def far_kernel(*refs):
     strips, out = refs[:-1], refs[-1]
-    for k, strip in zip([0] + far_first(len(strips)), strips):
+    for k, strip in enumerate(strips):
         out[k] = strip[1]
+
+
+def other_kernel(far, own, loaded, out):
+    z_count, y_count = out.shape[:2]
+    for j in range(y_count):
+        out[0, j] = own[1, j]
+        out[1, j] = loaded[y_count + j]
+    for spot, k in enumerate(k for k in far_first(z_count) if k > 1):
+        out[k] = far[spot]
 
 
 def seed_kernel(seed_class, seed_mask, base):
@@ -139,9 +180,9 @@
             ahead = []
             if first and i == 0:
                 ahead = [(0, values), (1, theirs)]
-                ahead = [(jnp.concatenate([strips[k][s, j] for k in order], axis=1), v) for s, v in ahead]
+                ahead = [(jnp.concatenate([block_of(strips[k], s, j, y_count) for k in order], axis=1), v) for s, v in ahead]
             elif not first:
-                ahead = [strips[k][0, j] if i == 0 else other[k, j] for k in order]
+                ahead = [block_of(strips[k], 0, j, y_count) if i == 0 else other[k, j] for k in order]
                 ahead = [(jnp.concatenate(ahead, axis=1), values)]
             for blocks, right in ahead:
                 total += product(blocks, right, (1, 0))
@@ -169,18 +210,30 @@
         affinity.reshape(stripe * sides, width),
         smem=1,
     )
-    sent, halves = list(sent[:z_count]), sent[z_count:]
-    current, sent[0] = lax.optimization_barrier((labels, sent[0]))
-    arrived = {k: swap_rows(sent[k], k * y_count) for k in far_first(z_count)}
+    sent, halves = sent[:z_count], sent[z_count:]
+    halves = [swap_rows(x, j + 1) for j, x in enumerate(halves)]
+    have, order, bit = [labels], [0], z_count // 2
+    while bit > 1:
+        whole = have[0] if len(have) == 1 else join(have)
+        have = [whole, swap_rows(whole, bit * y_count)]
+        order = order + [k ^ bit for k in order]
+        bit //= 2
+    arrived = {k: swap_rows(sent[k], k * y_count) for k in far_first(z_count) if k > 1}
+    blocks = 2 * y_count + len(order) * classes // width
+    loaded = jax.ShapeDtypeStruct((blocks, width, width), jnp.bfloat16)
+    arrived[1] = swap_rows(call(load_kernel, loaded, sent[1], *have, flops=LOAD_FLOPS), y_count)
+    order = order + [k ^ 1 for k in order]
+    values = jax.ShapeDtypeStruct((z_count * width, classes), jnp.bfloat16)
+    values = call(lambda *refs: unload_kernel(y_count, *refs), values, *have, arrived[1])
     strips = [arrived[k] for k in far_first(z_count)]
-    halves = [swap_rows(x, j + 1) for j, x in enumerate(halves)]
-    order = [0] + far_first(z_count)
-    values = join([current] + [swap_rows(current, k * y_count) for k in order[1:]], flops=JOIN_FLOPS)
     swapped = swap_cores(values)
+    far_strips = [arrived[k] for k in far_first(z_count) if k > 1]
+    far = jax.ShapeDtypeStruct((len(far_strips), y_count, width, width), jnp.bfloat16)
+    far = call(far_kernel, far, *far_strips, flops=FAR_FLOPS)
+    far = join([far], flops=SIDES_FLOPS)
     other = jax.ShapeDtypeStruct((z_count, y_count, width, width), jnp.bfloat16)
-    sides = call(other_kernel, other, sent[0], *strips, flops=SIDES_FLOPS)
-    other = swap_cores(sides)
-    pieces = [sides, values, swapped]
+    other = swap_cores(call(other_kernel, other, far, sent[0], arrived[1]))
+    pieces = [far, values, swapped]
     base = call(
         seed_kernel,
         jax.ShapeDtypeStruct((width, classes), jnp.float32),
@@ -188,9 +241,10 @@
         seed_mask.reshape(1, width),
     )
 
-    degree = None
+    current, degree = labels, None
     for step in range(ITERS):
         if step > 0:
+            order = [0] + far_first(z_count)
             pieces = [other, current] + [swap_rows(current, k * y_count) for k in order[1:]]
         height = width + (SUBLANES if step == 0 else 0)
         part = jax.ShapeDtypeStruct((height, classes), jnp.float32)

time: 49.4 us -> 46.7 us (0.945)
  starting transfers between devices: 23.1 us -> 16.7 us
  waiting for transfers between devices: 20.4 us -> 24.1 us
    ppermute x12 -> x10, starting transfers between devices: 22.8 us -> 16.2 us  [swap_rows(): return lax.ppermute(value, 'row', [(i, i ^ shift) for i in range(count)])]
    ppermute x12 -> x10, waiting for transfers between devices: 17.3 us -> 19.6 us  [swap_rows(): return lax.ppermute(value, 'row', [(i, i ^ shift) for i in range(count)])]
    ppermute x4, waiting for transfers between devices: 3.07 us -> 4.44 us  [swap_cores(): return lax.ppermute(value, 'col', [(0, 1), (1, 0)])]
    pallas_call x8 -> x11, Pallas kernels: 2.32 us -> 2.36 us  [call(): pl.pallas_call(kernel, out_shape=out_shape, in_specs=[pl.BlockSpec(memory...]
  transfers between devices with their start and end apart: 16 -> 14, of which waited for: 9 -> 9; matrix products, arithmetic and copies ran while one was open for 0% -> 0% of each run, Pallas kernels for 0% -> 3%
where the time goes in v7:
time: 46.7 us; the launch traced here: 46.5 us
  waiting for transfers between devices  24.1 us (52%)
  starting transfers between devices  16.7 us (36%)
  local copies, waits for them, and re-layouts  2.39 us (5%)
  Pallas kernels  2.36 us (5%)
  other arithmetic  0.86 us (2%)
    ppermute x10, waiting for transfers between devices, swap_rows(): return lax.ppermute(value, 'row', [(i, i ^ shift) for i in range(count)])  19.6 us
    ppermute x10, starting transfers between devices, swap_rows(): return lax.ppermute(value, 'row', [(i, i ^ shift) for i in range(count)])  16.2 us
    ppermute x4, waiting for transfers between devices, swap_cores(): return lax.ppermute(value, 'col', [(0, 1), (1, 0)])  4.44 us
    unnamed x10, local copies, waits for them, and re-layouts  2.39 us
    pallas_call x11, Pallas kernels, call(): pl.pallas_call(kernel, out_shape=out_shape, in_specs=[pl.BlockSpec(memory...  2.36 us
  transfers between devices with their start and end apart: 14, of which 9 were waited for; matrix products, arithmetic and copies ran while one was open for 0% of the time, Pallas kernels for 3%

profile of v7, /device:TPU:0, one launch (start us, length us, event | category | flops | bytes accessed | tf_op | source)
XLA Modules:
  0.0 46.5 jit_solution(1017056446154877957)
XLA Ops:
  0.0 4.0 %collective-permute-start.2 = (bf16[128,256]{1,0:T(8,128)(2,1)}, bf16[128,256]{1,0:T(8,128)(2,1)S(1)}, u32[]{:S(2)}, u32[]{:S(2)}) collective-permute-start(bf16[128,256]{1,0:T(8,128)(2,1)} %refs_0_.1), channel_id=1, source_target_pairs={{0,8},{2,10},{4,12},{6,14},{8,0},{10,2},{12,4},{14,6},{1,9},{3,11}... | collective-permute-start | bytes 196616 | tf_op jit(solution)/shard_map/ppermute | solution.py:24
  4.0 0.0 copy-start.2
  4.0 0.7 %copy-done.2 = s32[8,2,1]{0,2,1:T(1,128)S(1)} copy-done((s32[8,2,1]{0,2,1:T(1,128)S(1)}, s32[8,2,1]{0,2,1:T(1,128)}, u32[]{:S(2)}) %copy-start.2) | copy-done | bytes 88
  4.7 0.0 copy-start
  4.7 1.0 %copy-done = bf16[1024,2,128]{2,1,0:T(2,128)(2,1)S(1)} copy-done((bf16[1024,2,128]{2,1,0:T(2,128)(2,1)S(1)}, bf16[1024,2,128]{2,1,0:T(2,128)(2,1)}, u32[]{:S(2)}) %copy-start) | copy-done | bytes 524312
  5.8 0.0 copy-start.1
  5.8 1.0 %shard_map.55 = (bf16[2,2,128,128]{3,2,1,0:T(8,128)(2,1)S(1)}, bf16[2,2,128,128]{3,2,1,0:T(8,128)(2,1)S(1)}, bf16[2,2,128,128]{3,2,1,0:T(8,128)(2,1)S(1)}, bf16[...) custom-call(s32[2,1,8]{2,1,0:T(1,128)S(1)} %bitcast.11, bf16[2048,128]{1,0:T(8,128)(2,1)S(1)} %bitcast.10), custom_call_target="tpu_custom_call" | custom-call | bytes 1310784 | tf_op jit(solution)/shard_map/pallas_call | solution.py:34
  6.8 0.1 collective-permute-start
  6.8 3.9 %collective-permute-start.1 = (bf16[2,2,128,128]{3,2,1,0:T(8,128)(2,1)S(1)}, bf16[2,2,128,128]{3,2,1,0:T(8,128)(2,1)S(1)}, u32[]{:S(2)}, u32[]{:S(2)}) collective-permute-start(bf16[2,2,128,128]{3,2,1,0:T(8,128)(2,1)S(1)} %get-tuple-element.23.refs_3_), channel_id=1, source_target_pairs={{0,12},{2,14},{4,8},{6,10},{8,4},{10,6},{12,0},{14,2},{1,13},{3,15... | collective-permute-start | bytes 393224 | tf_op jit(solution)/shard_map/ppermute | solution.py:24
  10.8 1.5 %collective-permute-start.4 = (bf16[2,4,128,128]{3,2,1,0:T(8,128)(2,1)S(1)}, bf16[2,4,128,128]{3,2,1,0:T(8,128)(2,1)S(1)}, u32[]{:S(2)}, u32[]{:S(2)}) collective-permute-start(bf16[2,4,128,128]{3,2,1,0:T(8,128)(2,1)S(1)} %get-tuple-element.24), channel_id=1, source_target_pairs={{0,2},{2,0},{4,6},{6,4},{8,10},{10,8},{12,14},{14,12},{1,3},{3,1},... | collective-permute-start | bytes 786440 | tf_op jit(solution)/shard_map/ppermute | solution.py:24
  12.3 0.0 collective-permute-done.2.refs_2_.refs_1_
  12.3 0.0 copy-done.1
  12.3 0.1 collective-permute-start.3
  12.4 7.1 %collective-permute-done.refs_0_.refs_4_ = bf16[2,2,128,128]{3,2,1,0:T(8,128)(2,1)S(1)} collective-permute-done((bf16[2,2,128,128]{3,2,1,0:T(8,128)(2,1)S(1)}, bf16[2,2,128,128]{3,2,1,0:T(8,128)(2,1)S(1)}, u32[]{:S(2)}, u32[]{:S(2)}) %collective-permute-start) | collective-permute-done | bytes 131104 | tf_op jit(solution)/shard_map/ppermute | solution.py:24
  19.5 0.0 collective-permute-done.1.refs_1_.refs_5_
  19.5 3.6 %collective-permute-done.3.loaded.refs_2_.refs_6_ = bf16[8,128,128]{2,1,0:T(8,128)(2,1)S(1)} collective-permute-done((bf16[8,128,128]{2,1,0:T(8,128)(2,1)S(1)}, bf16[8,128,128]{2,1,0:T(8,128)(2,1)S(1)}, u32[]{:S(2)}, u32[]{:S(2)}) %collective-permute-start.3) | collective-permute-done | bytes 262176 | tf_op jit(solution)/shard_map/ppermute | solution.py:24
  23.2 0.1 collective-permute-start.6
  23.3 0.0 collective-permute-done.4.refs_7_
  23.3 1.5 %collective-permute-done.6.refs_10_ = bf16[512,256]{1,0:T(8,128)(2,1)S(1)} collective-permute-done((bf16[512,256]{1,0:T(8,128)(2,1)S(1)}, bf16[512,256]{1,0:T(8,128)(2,1)S(1)}, u32[]{:S(2)}, u32[]{:S(2)}) %collective-permute-start.6) | collective-permute-done | bytes 262176 | tf_op jit(solution)/shard_map/ppermute | solution.py:28
  24.8 0.7 %shard_map.61 = (f32[136,256]{1,0:T(8,128)S(1)}, f32[136,256]{1,0:T(8,128)S(1)}, f32[2,136,256]{2,1,0:T(8,128)S(1)}) custom-call(bf16[2,2,128,128]{3,2,1,0:T(8,128)(2,1)S(1)} %get-tuple-element.20.own.refs_0_, bf16[2,2,128,128]{3,2,1,0:T(8,128)(2,1)S(1)} %get-tuple-element.21.refs_0_.refs_1_, bf16[2,2,128,128]{3,2,1,0:T(8,128)(2,1)S(1)} %get-tuple-element.22.refs_2_, ...), custom_call_target="tpu_custom_call" | custom-call | flops 268435456 | bytes 2523136 | tf_op jit(solution)/shard_map/pallas_call | solution.py:34
  25.5 0.2 collective-permute-start.7
  25.7 1.4 %collective-permute-done.7.refs_2_ = f32[2,136,256]{2,1,0:T(8,128)S(1)} collective-permute-done((f32[2,136,256]{2,1,0:T(8,128)S(1)}, f32[2,136,256]{2,1,0:T(8,128)S(1)}, u32[]{:S(2)}, u32[]{:S(2)}) %collective-permute-start.7) | collective-permute-done | bytes 278560 | tf_op jit(solution)/shard_map/ppermute | solution.py:28
  27.1 1.1 %collective-permute-start.8 = (bf16[144,256]{1,0:T(8,128)(2,1)S(1)}, bf16[144,256]{1,0:T(8,128)(2,1)S(1)}, u32[]{:S(2)}, u32[]{:S(2)}) collective-permute-start(bf16[144,256]{1,0:T(8,128)(2,1)S(1)} %get-tuple-element.29), channel_id=1, source_target_pairs={{0,2},{2,0},{4,6},{6,4},{8,10},{10,8},{12,14},{14,12},{1,3},{3,1},... | collective-permute-start | bytes 221192 | tf_op jit(solution)/shard_map/ppermute | solution.py:24
  28.2 0.0 copy-start.3
  28.2 0.0 copy-start.4
  28.2 0.7 %copy-done.3 = s32[128]{0:T(128)S(1)} copy-done((s32[128]{0:T(128)S(1)}, s32[128]{0:T(128)}, u32[]{:S(2)}) %copy-start.3) | copy-done | bytes 536
  28.9 0.0 copy-done.4
  28.9 0.1 shard_map.63
  29.0 0.1 collective-permute-start.5
  29.1 2.5 %collective-permute-done.8 = bf16[144,256]{1,0:T(8,128)(2,1)S(1)} collective-permute-done((bf16[144,256]{1,0:T(8,128)(2,1)S(1)}, bf16[144,256]{1,0:T(8,128)(2,1)S(1)}, u32[]{:S(2)}, u32[]{:S(2)}) %collective-permute-start.8) | collective-permute-done | bytes 73760 | tf_op jit(solution)/shard_map/ppermute | solution.py:24
  31.6 0.1 fusion.5.refs_9_
  31.7 2.2 %collective-permute-start.10 = (bf16[128,256]{1,0:T(8,128)(2,1)S(1)}, bf16[128,256]{1,0:T(8,128)(2,1)S(1)}, u32[]{:S(2)}, u32[]{:S(2)}) collective-permute-start(bf16[128,256]{1,0:T(8,128)(2,1)S(1)} %fusion.5.refs_9_), channel_id=1, source_target_pairs={{0,12},{2,14},{4,8},{6,10},{8,4},{10,6},{12,0},{14,2},{1,13},{3,15... | collective-permute-start | bytes 196616 | tf_op jit(solution)/shard_map/ppermute | solution.py:24
  33.9 0.0 collective-permute-start.11
  33.9 2.2 %collective-permute-start.9 = (bf16[128,256]{1,0:T(8,128)(2,1)S(1)}, bf16[128,256]{1,0:T(8,128)(2,1)S(1)}, u32[]{:S(2)}, u32[]{:S(2)}) collective-permute-start(bf16[128,256]{1,0:T(8,128)(2,1)S(1)} %fusion.5.refs_9_), channel_id=1, source_target_pairs={{0,8},{2,10},{4,12},{6,14},{8,0},{10,2},{12,4},{14,6},{1,9},{3,11}... | collective-permute-start | bytes 196616 | tf_op jit(solution)/shard_map/ppermute | solution.py:24
  36.1 0.0 collective-permute-done.5.refs_8_
  36.1 2.2 %collective-permute-done.10.refs_11_ = bf16[128,256]{1,0:T(8,128)(2,1)S(1)} collective-permute-done((bf16[128,256]{1,0:T(8,128)(2,1)S(1)}, bf16[128,256]{1,0:T(8,128)(2,1)S(1)}, u32[]{:S(2)}, u32[]{:S(2)}) %collective-permute-start.10) | collective-permute-done | bytes 65568 | tf_op jit(solution)/shard_map/ppermute | solution.py:24
  38.3 1.0 %collective-permute-done.11.refs_12_ = bf16[128,256]{1,0:T(8,128)(2,1)S(1)} collective-permute-done((bf16[128,256]{1,0:T(8,128)(2,1)S(1)}, bf16[128,256]{1,0:T(8,128)(2,1)S(1)}, u32[]{:S(2)}, u32[]{:S(2)}) %collective-permute-start.11) | collective-permute-done | bytes 65568 | tf_op jit(solution)/shard_map/ppermute | solution.py:24
  39.3 0.0 collective-permute-done.9.refs_10_
  39.3 0.4 shard_map.64
  39.8 0.1 collective-permute-start.12
  39.9 1.5 %collective-permute-done.12.refs_2_ = f32[2,128,256]{2,1,0:T(8,128)S(1)} collective-permute-done((f32[2,128,256]{2,1,0:T(8,128)S(1)}, f32[2,128,256]{2,1,0:T(8,128)S(1)}, u32[]{:S(2)}, u32[]{:S(2)}) %collective-permute-start.12) | collective-permute-done | bytes 262176 | tf_op jit(solution)/shard_map/ppermute | solution.py:28
  41.4 1.1 %collective-permute-start.13 = (bf16[128,256]{1,0:T(8,128)(2,1)S(1)}, bf16[128,256]{1,0:T(8,128)(2,1)S(1)}, u32[]{:S(2)}, u32[]{:S(2)}) collective-permute-start(bf16[128,256]{1,0:T(8,128)(2,1)S(1)} %get-tuple-element.34), channel_id=1, source_target_pairs={{0,2},{2,0},{4,6},{6,4},{8,10},{10,8},{12,14},{14,12},{1,3},{3,1},... | collective-permute-start | bytes 196616 | tf_op jit(solution)/shard_map/ppermute | solution.py:24
  42.5 3.2 %collective-permute-done.13 = bf16[128,256]{1,0:T(8,128)(2,1)S(1)} collective-permute-done((bf16[128,256]{1,0:T(8,128)(2,1)S(1)}, bf16[128,256]{1,0:T(8,128)(2,1)S(1)}, u32[]{:S(2)}, u32[]{:S(2)}) %collective-permute-start.13) | collective-permute-done | bytes 65568 | tf_op jit(solution)/shard_map/ppermute | solution.py:24
  45.8 0.7 %add_convert_fusion = bf16[128,256]{1,0:T(8,128)(2,1)} fusion(f32[128,256]{1,0:T(8,128)S(1)} %shard_map.63, bf16[128,256]{1,0:T(8,128)(2,1)S(1)} %fusion.5.refs_9_, f32[128,256]{1,0:T(8,128)S(1)} %get-tuple-element.33, bf16[128,256]{1,0:T(8,128)(2,1)S(1)} %collective-permute-done.13, f32[128]{0:T(128)S(1)} %fusion.7), kind=kLoop, calls=%fused_computation.6 | loop fusion | flops 294912 | bytes 459264 | tf_op jit(solution)/shard_map/convert_element_type | solution.py:272
  (10 shorter events, 0.2 us)
Async XLA Ops:
  0.0 12.3 %collective-permute-start.2 = (bf16[128,256]{1,0:T(8,128)(2,1)}, bf16[128,256]{1,0:T(8,128)(2,1)S(1)}, u32[]{:S(2)}, u32[]{:S(2)}) collective-permute-start(bf16[128,256]{1,0:T(8,128)(2,1)} %refs_0_.1), channel_id=1, source_target_pairs={{0,8},{2,10},{4,12},{6,14},{8,0},{10,2},{12,4},{14,6},{1,9},{3,11}... | collective-permute-start | bytes 196616 | tf_op jit(solution)/shard_map/ppermute | solution.py:24
  4.0 0.7 %copy-start.2 = (s32[8,2,1]{0,2,1:T(1,128)S(1)}, s32[8,2,1]{0,2,1:T(1,128)}, u32[]{:S(2)}) copy-start(s32[8,2,1]{0,2,1:T(1,128)} %param.6) | copy-start | bytes 196
  4.7 1.0 %copy-start = (bf16[1024,2,128]{2,1,0:T(2,128)(2,1)S(1)}, bf16[1024,2,128]{2,1,0:T(2,128)(2,1)}, u32[]{:S(2)}) copy-start(bf16[1024,2,128]{2,1,0:T(2,128)(2,1)} %param.5) | copy-start | bytes 1572868
  5.8 6.5 %copy-start.1 = (bf16[128,256]{1,0:T(8,128)(2,1)S(1)}, bf16[128,256]{1,0:T(8,128)(2,1)}, u32[]{:S(2)}) copy-start(bf16[128,256]{1,0:T(8,128)(2,1)} %refs_0_.1) | copy-start | bytes 196612
  6.8 12.7 %collective-permute-start = (bf16[2,2,128,128]{3,2,1,0:T(8,128)(2,1)S(1)}, bf16[2,2,128,128]{3,2,1,0:T(8,128)(2,1)S(1)}, u32[]{:S(2)}, u32[]{:S(2)}) collective-permute-start(bf16[2,2,128,128]{3,2,1,0:T(8,128)(2,1)S(1)} %get-tuple-element.22.refs_2_), channel_id=1, source_target_pairs={{0,8},{2,10},{4,12},{6,14},{8,0},{10,2},{12,4},{14,6},{1,9},{3,11}... | collective-permute-start | bytes 393224 | tf_op jit(solution)/shard_map/ppermute | solution.py:24
  6.8 12.7 %collective-permute-start.1 = (bf16[2,2,128,128]{3,2,1,0:T(8,128)(2,1)S(1)}, bf16[2,2,128,128]{3,2,1,0:T(8,128)(2,1)S(1)}, u32[]{:S(2)}, u32[]{:S(2)}) collective-permute-start(bf16[2,2,128,128]{3,2,1,0:T(8,128)(2,1)S(1)} %get-tuple-element.23.refs_3_), channel_id=1, source_target_pairs={{0,12},{2,14},{4,8},{6,10},{8,4},{10,6},{12,0},{14,2},{1,13},{3,15... | collective-permute-start | bytes 393224 | tf_op jit(solution)/shard_map/ppermute | solution.py:24
  10.8 12.5 %collective-permute-start.4 = (bf16[2,4,128,128]{3,2,1,0:T(8,128)(2,1)S(1)}, bf16[2,4,128,128]{3,2,1,0:T(8,128)(2,1)S(1)}, u32[]{:S(2)}, u32[]{:S(2)}) collective-permute-start(bf16[2,4,128,128]{3,2,1,0:T(8,128)(2,1)S(1)} %get-tuple-element.24), channel_id=1, source_target_pairs={{0,2},{2,0},{4,6},{6,4},{8,10},{10,8},{12,14},{14,12},{1,3},{3,1},... | collective-permute-start | bytes 786440 | tf_op jit(solution)/shard_map/ppermute | solution.py:24
  12.3 10.8 %collective-permute-start.3 = (bf16[8,128,128]{2,1,0:T(8,128)(2,1)S(1)}, bf16[8,128,128]{2,1,0:T(8,128)(2,1)S(1)}, u32[]{:S(2)}, u32[]{:S(2)}) collective-permute-start(bf16[8,128,128]{2,1,0:T(8,128)(2,1)S(1)} %shard_map.56), channel_id=1, source_target_pairs={{0,4},{2,6},{4,0},{6,2},{8,12},{10,14},{12,8},{14,10},{1,5},{3,7},... | collective-permute-start | bytes 786440 | tf_op jit(solution)/shard_map/ppermute | solution.py:24
  23.2 1.6 %collective-permute-start.6 = (bf16[512,256]{1,0:T(8,128)(2,1)S(1)}, bf16[512,256]{1,0:T(8,128)(2,1)S(1)}, u32[]{:S(2)}, u32[]{:S(2)}) collective-permute-start(bf16[512,256]{1,0:T(8,128)(2,1)S(1)} %shard_map.60.refs_9_), channel_id=1, source_target_pairs={{0,1},{1,0},{2,3},{3,2},{4,5},{5,4},{6,7},{7,6},{8,9},{9,8},{10,11... | collective-permute-start | bytes 786440 | tf_op jit(solution)/shard_map/ppermute | solution.py:28
  25.5 1.6 %collective-permute-start.7 = (f32[2,136,256]{2,1,0:T(8,128)S(1)}, f32[2,136,256]{2,1,0:T(8,128)S(1)}, u32[]{:S(2)}, u32[]{:S(2)}) collective-permute-start(f32[2,136,256]{2,1,0:T(8,128)S(1)} %get-tuple-element.27), channel_id=1, source_target_pairs={{0,1},{1,0},{2,3},{3,2},{4,5},{5,4},{6,7},{7,6},{8,9},{9,8},{10,11... | collective-permute-start | bytes 835592 | tf_op jit(solution)/shard_map/ppermute | solution.py:28
  27.1 4.4 %collective-permute-start.8 = (bf16[144,256]{1,0:T(8,128)(2,1)S(1)}, bf16[144,256]{1,0:T(8,128)(2,1)S(1)}, u32[]{:S(2)}, u32[]{:S(2)}) collective-permute-start(bf16[144,256]{1,0:T(8,128)(2,1)S(1)} %get-tuple-element.29), channel_id=1, source_target_pairs={{0,2},{2,0},{4,6},{6,4},{8,10},{10,8},{12,14},{14,12},{1,3},{3,1},... | collective-permute-start | bytes 221192 | tf_op jit(solution)/shard_map/ppermute | solution.py:24
  28.2 0.7 %copy-start.3 = (s32[128]{0:T(128)S(1)}, s32[128]{0:T(128)}, u32[]{:S(2)}) copy-start(s32[128]{0:T(128)} %param.8) | copy-start | bytes 1540
  28.2 0.7 %copy-start.4 = (s32[128]{0:T(128)S(1)}, s32[128]{0:T(128)}, u32[]{:S(2)}) copy-start(s32[128]{0:T(128)} %param.9) | copy-start | bytes 1540
  29.0 7.1 %collective-permute-start.5 = (bf16[4,2,128,128]{3,2,1,0:T(8,128)(2,1)S(1)}, bf16[4,2,128,128]{3,2,1,0:T(8,128)(2,1)S(1)}, u32[]{:S(2)}, u32[]{:S(2)}) collective-permute-start(bf16[4,2,128,128]{3,2,1,0:T(8,128)(2,1)S(1)} %shard_map.59), channel_id=1, source_target_pairs={{0,1},{1,0},{2,3},{3,2},{4,5},{5,4},{6,7},{7,6},{8,9},{9,8},{10,11... | collective-permute-start | bytes 786440 | tf_op jit(solution)/shard_map/ppermute | solution.py:28
  31.7 6.6 %collective-permute-start.10 = (bf16[128,256]{1,0:T(8,128)(2,1)S(1)}, bf16[128,256]{1,0:T(8,128)(2,1)S(1)}, u32[]{:S(2)}, u32[]{:S(2)}) collective-permute-start(bf16[128,256]{1,0:T(8,128)(2,1)S(1)} %fusion.5.refs_9_), channel_id=1, source_target_pairs={{0,12},{2,14},{4,8},{6,10},{8,4},{10,6},{12,0},{14,2},{1,13},{3,15... | collective-permute-start | bytes 196616 | tf_op jit(solution)/shard_map/ppermute | solution.py:24
  33.9 5.4 %collective-permute-start.11 = (bf16[128,256]{1,0:T(8,128)(2,1)S(1)}, bf16[128,256]{1,0:T(8,128)(2,1)S(1)}, u32[]{:S(2)}, u32[]{:S(2)}) collective-permute-start(bf16[128,256]{1,0:T(8,128)(2,1)S(1)} %fusion.5.refs_9_), channel_id=1, source_target_pairs={{0,4},{2,6},{4,0},{6,2},{8,12},{10,14},{12,8},{14,10},{1,5},{3,7},... | collective-permute-start | bytes 196616 | tf_op jit(solution)/shard_map/ppermute | solution.py:24
  33.9 5.4 %collective-permute-start.9 = (bf16[128,256]{1,0:T(8,128)(2,1)S(1)}, bf16[128,256]{1,0:T(8,128)(2,1)S(1)}, u32[]{:S(2)}, u32[]{:S(2)}) collective-permute-start(bf16[128,256]{1,0:T(8,128)(2,1)S(1)} %fusion.5.refs_9_), channel_id=1, source_target_pairs={{0,8},{2,10},{4,12},{6,14},{8,0},{10,2},{12,4},{14,6},{1,9},{3,11}... | collective-permute-start | bytes 196616 | tf_op jit(solution)/shard_map/ppermute | solution.py:24
  39.8 1.6 %collective-permute-start.12 = (f32[2,128,256]{2,1,0:T(8,128)S(1)}, f32[2,128,256]{2,1,0:T(8,128)S(1)}, u32[]{:S(2)}, u32[]{:S(2)}) collective-permute-start(f32[2,128,256]{2,1,0:T(8,128)S(1)} %get-tuple-element.32), channel_id=1, source_target_pairs={{0,1},{1,0},{2,3},{3,2},{4,5},{5,4},{6,7},{7,6},{8,9},{9,8},{10,11... | collective-permute-start | bytes 786440 | tf_op jit(solution)/shard_map/ppermute | solution.py:28
  41.4 4.3 %collective-permute-start.13 = (bf16[128,256]{1,0:T(8,128)(2,1)S(1)}, bf16[128,256]{1,0:T(8,128)(2,1)S(1)}, u32[]{:S(2)}, u32[]{:S(2)}) collective-permute-start(bf16[128,256]{1,0:T(8,128)(2,1)S(1)} %get-tuple-element.34), channel_id=1, source_target_pairs={{0,2},{2,0},{4,6},{6,4},{8,10},{10,8},{12,14},{14,12},{1,3},{3,1},... | collective-permute-start | bytes 196616 | tf_op jit(solution)/shard_map/ppermute | solution.py:24

commit v8 on v7

--- a/solution.py
+++ b/solution.py
@@ -8,6 +8,7 @@
 ITERS = 2
 CARRY = 0.8
 SUBLANES = 8
+LEAD_FLOPS = 2_000_000_000
 LOAD_FLOPS = 2_000_000_000
 SIDES_FLOPS = 3_000_000_000
 FAR_FLOPS = 3_000_000_000
@@ -46,8 +47,8 @@
     return [k for k in range(half, count)] + [k for k in range(1, half)]
 
 
-def prepare_kernel(z_count, y_count, live, tile, *outs):
-    strips, halves = outs[:z_count], outs[z_count:]
+def prepare_kernel(z_count, y_count, live, tile, lead, *outs):
+    strips = outs
     row, col = lax.axis_index("row"), lax.axis_index("col")
     z, y = lax.div(row, y_count), lax.rem(row, y_count)
     width = tile.shape[1]
@@ -66,8 +67,6 @@
                 piece = sides[i * width : (i + 1) * width]
                 piece = jnp.where(keep, piece, jnp.zeros_like(piece)).astype(jnp.bfloat16)
                 strips[k][i, j] = piece
-                if j > 0:
-                    halves[j - 1][i, k] = piece
 
 
 def fold_kernel(y_count, first, *refs):
@@ -99,9 +98,15 @@
     return call(join_kernel, jax.ShapeDtypeStruct((rows,) + parts[0].shape[1:], parts[0].dtype), *parts, flops=flops)
 
 
-def load_kernel(*refs):
-    strip, pieces, out = refs[0], refs[1:-1], refs[-1]
+def load_kernel(z_count, y_count, *refs):
+    strips, refs = refs[:z_count], refs[z_count:]
+    halves, refs = refs[1 - y_count :], refs[: 1 - y_count]
+    strip, pieces, out = strips[1], refs[:-1], refs[-1]
     sides, blocks, width, _ = strip.shape
+    for j, half in enumerate(halves, 1):
+        for k in range(z_count):
+            for i in range(sides):
+                half[i, k] = strips[k][i, j]
     for i in range(sides):
         for j in range(blocks):
             out[i * blocks + j] = strip[i, j]
@@ -143,6 +148,10 @@
         out[1, j] = loaded[y_count + j]
     for spot, k in enumerate(k for k in far_first(z_count) if k > 1):
         out[k] = far[spot]
+
+
+def lead_kernel(out):
+    out[...] = jnp.zeros_like(out)
 
 
 def seed_kernel(seed_class, seed_mask, base):
@@ -205,13 +214,12 @@
     half = jax.ShapeDtypeStruct((2, z_count, width, width), jnp.bfloat16)
     sent = call(
         lambda *refs: prepare_kernel(z_count, y_count, *refs),
-        [strip] * z_count + [half] * (y_count - 1),
+        [strip] * z_count,
         block_live.transpose(1, 2, 0),
         affinity.reshape(stripe * sides, width),
+        call(lead_kernel, jax.ShapeDtypeStruct((SUBLANES, width), jnp.float32), flops=LEAD_FLOPS),
         smem=1,
     )
-    sent, halves = sent[:z_count], sent[z_count:]
-    halves = [swap_rows(x, j + 1) for j, x in enumerate(halves)]
     have, order, bit = [labels], [0], z_count // 2
     while bit > 1:
         whole = have[0] if len(have) == 1 else join(have)
@@ -221,7 +229,15 @@
     arrived = {k: swap_rows(sent[k], k * y_count) for k in far_first(z_count) if k > 1}
     blocks = 2 * y_count + len(order) * classes // width
     loaded = jax.ShapeDtypeStruct((blocks, width, width), jnp.bfloat16)
-    arrived[1] = swap_rows(call(load_kernel, loaded, sent[1], *have, flops=LOAD_FLOPS), y_count)
+    loaded, *halves = call(
+        lambda *refs: load_kernel(z_count, y_count, *refs),
+        [loaded] + [half] * (y_count - 1),
+        *sent,
+        *have,
+        flops=LOAD_FLOPS,
+    )
+    arrived[1] = swap_rows(loaded, y_count)
+    halves = [swap_rows(x, j + 1) for j, x in enumerate(halves)]
     order = order + [k ^ 1 for k in order]
     values = jax.ShapeDtypeStruct((z_count * width, classes), jnp.bfloat16)
     values = call(lambda *refs: unload_kernel(y_count, *refs), values, *have, arrived[1])

time: 46.7 us -> 46.4 us (level)
  starting transfers between devices: 16.7 us -> 21.8 us
  waiting for transfers between devices: 24.1 us -> 19.7 us
  local copies, waits for them, and re-layouts: 2.39 us -> 1.35 us
    ppermute x10, starting transfers between devices: 16.2 us -> 21.4 us  [swap_rows(): return lax.ppermute(value, 'row', [(i, i ^ shift) for i in range(count)])]
    ppermute x10, waiting for transfers between devices: 19.6 us -> 15.3 us  [swap_rows(): return lax.ppermute(value, 'row', [(i, i ^ shift) for i in range(count)])]
    unnamed x10, local copies, waits for them, and re-layouts: 2.39 us -> 1.35 us
    pallas_call x11 -> x12, Pallas kernels: 2.36 us -> 2.39 us  [call(): pl.pallas_call(kernel, out_shape=out_shape, in_specs=[pl.BlockSpec(memory...]
  transfers between devices with their start and end apart: 14 -> 14, of which waited for: 9 -> 10; matrix products, arithmetic and copies ran while one was open for 0% -> 0% of each run, Pallas kernels for 3% -> 3%
where the time goes in v8:
time: 46.4 us; the launch traced here: 46.3 us
  starting transfers between devices  21.8 us (47%)
  waiting for transfers between devices  19.7 us (42%)
  Pallas kernels  2.39 us (5%)
  local copies, waits for them, and re-layouts  1.35 us (3%)
  other arithmetic  0.86 us (2%)
    ppermute x10, starting transfers between devices, swap_rows(): return lax.ppermute(value, 'row', [(i, i ^ shift) for i in range(count)])  21.4 us
    ppermute x10, waiting for transfers between devices, swap_rows(): return lax.ppermute(value, 'row', [(i, i ^ shift) for i in range(count)])  15.3 us
    ppermute x4, waiting for transfers between devices, swap_cores(): return lax.ppermute(value, 'col', [(0, 1), (1, 0)])  4.44 us
    pallas_call x12, Pallas kernels, call(): pl.pallas_call(kernel, out_shape=out_shape, in_specs=[pl.BlockSpec(memory...  2.39 us
    unnamed x10, local copies, waits for them, and re-layouts  1.35 us
  transfers between devices with their start and end apart: 14, of which 10 were waited for; matrix products, arithmetic and copies ran while one was open for 0% of the time, Pallas kernels for 3%

profile of v8, /device:TPU:0, one launch (start us, length us, event | category | flops | bytes accessed | tf_op | source)
XLA Modules:
  0.0 46.3 jit_solution(16163463947460234600)
XLA Ops:
  0.0 0.0 copy-start
  0.0 4.0 %collective-permute-start.2 = (bf16[128,256]{1,0:T(8,128)(2,1)}, bf16[128,256]{1,0:T(8,128)(2,1)S(1)}, u32[]{:S(2)}, u32[]{:S(2)}) collective-permute-start(bf16[128,256]{1,0:T(8,128)(2,1)} %refs_0_.1), channel_id=1, source_target_pairs={{0,8},{2,10},{4,12},{6,14},{8,0},{10,2},{12,4},{14,6},{1,9},{3,11}... | collective-permute-start | bytes 196616 | tf_op jit(solution)/shard_map/ppermute | solution.py:25
  4.0 0.0 copy-start.2
  4.0 0.0 copy-done
  4.0 0.7 %copy-done.2 = s32[8,2,1]{0,2,1:T(1,128)S(1)} copy-done((s32[8,2,1]{0,2,1:T(1,128)S(1)}, s32[8,2,1]{0,2,1:T(1,128)}, u32[]{:S(2)}) %copy-start.2) | copy-done | bytes 88
  4.7 0.0 copy-start.1
  4.7 1.0 %shard_map.56 = (bf16[2,2,128,128]{3,2,1,0:T(8,128)(2,1)S(1)}, bf16[2,2,128,128]{3,2,1,0:T(8,128)(2,1)S(1)}, bf16[2,2,128,128]{3,2,1,0:T(8,128)(2,1)S(1)}, bf16[2,2,128,128]{3,2,1,0:T(8,128)(2,1)S(1)}) custom-call(s32[2,1,8]{2,1,0:T(1,128)S(1)} %bitcast.11, bf16[2048,128]{1,0:T(8,128)(2,1)S(1)} %bitcast.10, f32[8,128]{1,0:T(8,128)S(1)} %shard_map.55.refs_2_), custom_call_target="tpu_custom_call" | custom-call | bytes 1052736 | tf_op jit(solution)/shard_map/pallas_call | solution.py:35
  5.7 0.4 collective-permute-start
  6.1 3.6 %collective-permute-start.1 = (bf16[2,2,128,128]{3,2,1,0:T(8,128)(2,1)S(1)}, bf16[2,2,128,128]{3,2,1,0:T(8,128)(2,1)S(1)}, u32[]{:S(2)}, u32[]{:S(2)}) collective-permute-start(bf16[2,2,128,128]{3,2,1,0:T(8,128)(2,1)S(1)} %get-tuple-element.24.refs_3_), channel_id=1, source_target_pairs={{0,12},{2,14},{4,8},{6,10},{8,4},{10,6},{12,0},{14,2},{1,13},{3,15... | collective-permute-start | bytes 393224 | tf_op jit(solution)/shard_map/ppermute | solution.py:25
  9.7 0.0 collective-permute-done.2.refs_5_.refs_1_
  9.7 0.0 copy-done.1
  9.7 0.1 shard_map.57
  9.8 4.2 %collective-permute-start.3 = (bf16[8,128,128]{2,1,0:T(8,128)(2,1)S(1)}, bf16[8,128,128]{2,1,0:T(8,128)(2,1)S(1)}, u32[]{:S(2)}, u32[]{:S(2)}) collective-permute-start(bf16[8,128,128]{2,1,0:T(8,128)(2,1)S(1)} %get-tuple-element.25), channel_id=1, source_target_pairs={{0,4},{2,6},{4,0},{6,2},{8,12},{10,14},{12,8},{14,10},{1,5},{3,7},... | collective-permute-start | bytes 786440 | tf_op jit(solution)/shard_map/ppermute | solution.py:25
  14.0 1.5 %collective-permute-start.4 = (bf16[2,4,128,128]{3,2,1,0:T(8,128)(2,1)S(1)}, bf16[2,4,128,128]{3,2,1,0:T(8,128)(2,1)S(1)}, u32[]{:S(2)}, u32[]{:S(2)}) collective-permute-start(bf16[2,4,128,128]{3,2,1,0:T(8,128)(2,1)S(1)} %get-tuple-element.26), channel_id=1, source_target_pairs={{0,2},{2,0},{4,6},{6,4},{8,10},{10,8},{12,14},{14,12},{1,3},{3,1},... | collective-permute-start | bytes 786440 | tf_op jit(solution)/shard_map/ppermute | solution.py:25
  15.5 3.0 %collective-permute-done.refs_0_.refs_4_ = bf16[2,2,128,128]{3,2,1,0:T(8,128)(2,1)S(1)} collective-permute-done((bf16[2,2,128,128]{3,2,1,0:T(8,128)(2,1)S(1)}, bf16[2,2,128,128]{3,2,1,0:T(8,128)(2,1)S(1)}, u32[]{:S(2)}, u32[]{:S(2)}) %collective-permute-start) | collective-permute-done | bytes 131104 | tf_op jit(solution)/shard_map/ppermute | solution.py:25
  18.5 0.0 collective-permute-done.1.refs_1_.refs_5_
  18.5 3.3 %collective-permute-done.3.loaded.refs_2_.refs_6_ = bf16[8,128,128]{2,1,0:T(8,128)(2,1)S(1)} collective-permute-done((bf16[8,128,128]{2,1,0:T(8,128)(2,1)S(1)}, bf16[8,128,128]{2,1,0:T(8,128)(2,1)S(1)}, u32[]{:S(2)}, u32[]{:S(2)}) %collective-permute-start.3) | collective-permute-done | bytes 262176 | tf_op jit(solution)/shard_map/ppermute | solution.py:25
  21.8 0.1 collective-permute-start.6
  21.9 0.0 collective-permute-done.4.refs_7_
  21.9 1.5 %collective-permute-done.6.refs_10_ = bf16[512,256]{1,0:T(8,128)(2,1)S(1)} collective-permute-done((bf16[512,256]{1,0:T(8,128)(2,1)S(1)}, bf16[512,256]{1,0:T(8,128)(2,1)S(1)}, u32[]{:S(2)}, u32[]{:S(2)}) %collective-permute-start.6) | collective-permute-done | bytes 262176 | tf_op jit(solution)/shard_map/ppermute | solution.py:29
  23.4 0.7 %shard_map.62 = (f32[136,256]{1,0:T(8,128)S(1)}, f32[136,256]{1,0:T(8,128)S(1)}, f32[2,136,256]{2,1,0:T(8,128)S(1)}) custom-call(bf16[2,2,128,128]{3,2,1,0:T(8,128)(2,1)S(1)} %get-tuple-element.21.refs_0_.own, bf16[2,2,128,128]{3,2,1,0:T(8,128)(2,1)S(1)} %get-tuple-element.22.refs_1_, bf16[2,2,128,128]{3,2,1,0:T(8,128)(2,1)S(1)} %get-tuple-element.23.refs_2_, ...), custom_call_target="tpu_custom_call" | custom-call | flops 268435456 | bytes 2523136 | tf_op jit(solution)/shard_map/pallas_call | solution.py:35
  24.0 0.2 collective-permute-start.7
  24.2 1.4 %collective-permute-done.7.refs_2_ = f32[2,136,256]{2,1,0:T(8,128)S(1)} collective-permute-done((f32[2,136,256]{2,1,0:T(8,128)S(1)}, f32[2,136,256]{2,1,0:T(8,128)S(1)}, u32[]{:S(2)}, u32[]{:S(2)}) %collective-permute-start.7) | collective-permute-done | bytes 278560 | tf_op jit(solution)/shard_map/ppermute | solution.py:29
  25.7 1.6 %collective-permute-start.8 = (bf16[144,256]{1,0:T(8,128)(2,1)S(1)}, bf16[144,256]{1,0:T(8,128)(2,1)S(1)}, u32[]{:S(2)}, u32[]{:S(2)}) collective-permute-start(bf16[144,256]{1,0:T(8,128)(2,1)S(1)} %get-tuple-element.31), channel_id=1, source_target_pairs={{0,2},{2,0},{4,6},{6,4},{8,10},{10,8},{12,14},{14,12},{1,3},{3,1},... | collective-permute-start | bytes 221192 | tf_op jit(solution)/shard_map/ppermute | solution.py:25
  27.3 0.0 copy-start.3
  27.3 0.0 copy-start.4
  27.3 0.7 %copy-done.3 = s32[128]{0:T(128)S(1)} copy-done((s32[128]{0:T(128)S(1)}, s32[128]{0:T(128)}, u32[]{:S(2)}) %copy-start.3) | copy-done | bytes 536
  27.9 0.0 copy-done.4
  28.0 0.1 shard_map.64
  28.1 0.1 collective-permute-start.5
  28.2 1.9 %collective-permute-done.8 = bf16[144,256]{1,0:T(8,128)(2,1)S(1)} collective-permute-done((bf16[144,256]{1,0:T(8,128)(2,1)S(1)}, bf16[144,256]{1,0:T(8,128)(2,1)S(1)}, u32[]{:S(2)}, u32[]{:S(2)}) %collective-permute-start.8) | collective-permute-done | bytes 73760 | tf_op jit(solution)/shard_map/ppermute | solution.py:25
  30.2 0.1 fusion.5.refs_9_
  30.3 3.7 %collective-permute-start.10 = (bf16[128,256]{1,0:T(8,128)(2,1)S(1)}, bf16[128,256]{1,0:T(8,128)(2,1)S(1)}, u32[]{:S(2)}, u32[]{:S(2)}) collective-permute-start(bf16[128,256]{1,0:T(8,128)(2,1)S(1)} %fusion.5.refs_9_), channel_id=1, source_target_pairs={{0,12},{2,14},{4,8},{6,10},{8,4},{10,6},{12,0},{14,2},{1,13},{3,15... | collective-permute-start | bytes 196616 | tf_op jit(solution)/shard_map/ppermute | solution.py:25
  33.9 0.0 collective-permute-start.11
  33.9 0.8 %collective-permute-start.9 = (bf16[128,256]{1,0:T(8,128)(2,1)S(1)}, bf16[128,256]{1,0:T(8,128)(2,1)S(1)}, u32[]{:S(2)}, u32[]{:S(2)}) collective-permute-start(bf16[128,256]{1,0:T(8,128)(2,1)S(1)} %fusion.5.refs_9_), channel_id=1, source_target_pairs={{0,8},{2,10},{4,12},{6,14},{8,0},{10,2},{12,4},{14,6},{1,9},{3,11}... | collective-permute-start | bytes 196616 | tf_op jit(solution)/shard_map/ppermute | solution.py:25
  34.7 0.0 collective-permute-done.5.refs_8_
  34.7 1.8 %collective-permute-done.10.refs_11_ = bf16[128,256]{1,0:T(8,128)(2,1)S(1)} collective-permute-done((bf16[128,256]{1,0:T(8,128)(2,1)S(1)}, bf16[128,256]{1,0:T(8,128)(2,1)S(1)}, u32[]{:S(2)}, u32[]{:S(2)}) %collective-permute-start.10) | collective-permute-done | bytes 65568 | tf_op jit(solution)/shard_map/ppermute | solution.py:25
  36.5 1.7 %collective-permute-done.11.refs_12_ = bf16[128,256]{1,0:T(8,128)(2,1)S(1)} collective-permute-done((bf16[128,256]{1,0:T(8,128)(2,1)S(1)}, bf16[128,256]{1,0:T(8,128)(2,1)S(1)}, u32[]{:S(2)}, u32[]{:S(2)}) %collective-permute-start.11) | collective-permute-done | bytes 65568 | tf_op jit(solution)/shard_map/ppermute | solution.py:25
  38.2 0.9 %collective-permute-done.9.refs_10_ = bf16[128,256]{1,0:T(8,128)(2,1)S(1)} collective-permute-done((bf16[128,256]{1,0:T(8,128)(2,1)S(1)}, bf16[128,256]{1,0:T(8,128)(2,1)S(1)}, u32[]{:S(2)}, u32[]{:S(2)}) %collective-permute-start.9) | collective-permute-done | bytes 65568 | tf_op jit(solution)/shard_map/ppermute | solution.py:25
  39.1 0.4 shard_map.65
  39.6 0.1 collective-permute-start.12
  39.6 1.5 %collective-permute-done.12.refs_2_ = f32[2,128,256]{2,1,0:T(8,128)S(1)} collective-permute-done((f32[2,128,256]{2,1,0:T(8,128)S(1)}, f32[2,128,256]{2,1,0:T(8,128)S(1)}, u32[]{:S(2)}, u32[]{:S(2)}) %collective-permute-start.12) | collective-permute-done | bytes 262176 | tf_op jit(solution)/shard_map/ppermute | solution.py:29
  41.2 1.6 %collective-permute-start.13 = (bf16[128,256]{1,0:T(8,128)(2,1)S(1)}, bf16[128,256]{1,0:T(8,128)(2,1)S(1)}, u32[]{:S(2)}, u32[]{:S(2)}) collective-permute-start(bf16[128,256]{1,0:T(8,128)(2,1)S(1)} %get-tuple-element.36), channel_id=1, source_target_pairs={{0,2},{2,0},{4,6},{6,4},{8,10},{10,8},{12,14},{14,12},{1,3},{3,1},... | collective-permute-start | bytes 196616 | tf_op jit(solution)/shard_map/ppermute | solution.py:25
  42.8 2.7 %collective-permute-done.13 = bf16[128,256]{1,0:T(8,128)(2,1)S(1)} collective-permute-done((bf16[128,256]{1,0:T(8,128)(2,1)S(1)}, bf16[128,256]{1,0:T(8,128)(2,1)S(1)}, u32[]{:S(2)}, u32[]{:S(2)}) %collective-permute-start.13) | collective-permute-done | bytes 65568 | tf_op jit(solution)/shard_map/ppermute | solution.py:25
  45.5 0.7 %add_convert_fusion = bf16[128,256]{1,0:T(8,128)(2,1)} fusion(f32[128,256]{1,0:T(8,128)S(1)} %shard_map.64, bf16[128,256]{1,0:T(8,128)(2,1)S(1)} %fusion.5.refs_9_, f32[128,256]{1,0:T(8,128)S(1)} %get-tuple-element.35, bf16[128,256]{1,0:T(8,128)(2,1)S(1)} %collective-permute-done.13, f32[128]{0:T(128)S(1)} %fusion.7), kind=kLoop, calls=%fused_computation.6 | loop fusion | flops 294912 | bytes 459264 | tf_op jit(solution)/shard_map/convert_element_type | solution.py:288
  (10 shorter events, 0.2 us)
Async XLA Ops:
  0.0 4.0 %copy-start = (bf16[1024,2,128]{2,1,0:T(2,128)(2,1)S(1)}, bf16[1024,2,128]{2,1,0:T(2,128)(2,1)}, u32[]{:S(2)}) copy-start(bf16[1024,2,128]{2,1,0:T(2,128)(2,1)} %param.5) | copy-start | bytes 1572868
  0.0 9.7 %collective-permute-start.2 = (bf16[128,256]{1,0:T(8,128)(2,1)}, bf16[128,256]{1,0:T(8,128)(2,1)S(1)}, u32[]{:S(2)}, u32[]{:S(2)}) collective-permute-start(bf16[128,256]{1,0:T(8,128)(2,1)} %refs_0_.1), channel_id=1, source_target_pairs={{0,8},{2,10},{4,12},{6,14},{8,0},{10,2},{12,4},{14,6},{1,9},{3,11}... | collective-permute-start | bytes 196616 | tf_op jit(solution)/shard_map/ppermute | solution.py:25
  4.0 0.7 %copy-start.2 = (s32[8,2,1]{0,2,1:T(1,128)S(1)}, s32[8,2,1]{0,2,1:T(1,128)}, u32[]{:S(2)}) copy-start(s32[8,2,1]{0,2,1:T(1,128)} %param.6) | copy-start | bytes 196
  4.7 5.0 %copy-start.1 = (bf16[128,256]{1,0:T(8,128)(2,1)S(1)}, bf16[128,256]{1,0:T(8,128)(2,1)}, u32[]{:S(2)}) copy-start(bf16[128,256]{1,0:T(8,128)(2,1)} %refs_0_.1) | copy-start | bytes 196612
  5.7 12.7 %collective-permute-start = (bf16[2,2,128,128]{3,2,1,0:T(8,128)(2,1)S(1)}, bf16[2,2,128,128]{3,2,1,0:T(8,128)(2,1)S(1)}, u32[]{:S(2)}, u32[]{:S(2)}) collective-permute-start(bf16[2,2,128,128]{3,2,1,0:T(8,128)(2,1)S(1)} %get-tuple-element.23.refs_2_), channel_id=1, source_target_pairs={{0,8},{2,10},{4,12},{6,14},{8,0},{10,2},{12,4},{14,6},{1,9},{3,11}... | collective-permute-start | bytes 393224 | tf_op jit(solution)/shard_map/ppermute | solution.py:25
  6.1 12.3 %collective-permute-start.1 = (bf16[2,2,128,128]{3,2,1,0:T(8,128)(2,1)S(1)}, bf16[2,2,128,128]{3,2,1,0:T(8,128)(2,1)S(1)}, u32[]{:S(2)}, u32[]{:S(2)}) collective-permute-start(bf16[2,2,128,128]{3,2,1,0:T(8,128)(2,1)S(1)} %get-tuple-element.24.refs_3_), channel_id=1, source_target_pairs={{0,12},{2,14},{4,8},{6,10},{8,4},{10,6},{12,0},{14,2},{1,13},{3,15... | collective-permute-start | bytes 393224 | tf_op jit(solution)/shard_map/ppermute | solution.py:25
  9.8 11.9 %collective-permute-start.3 = (bf16[8,128,128]{2,1,0:T(8,128)(2,1)S(1)}, bf16[8,128,128]{2,1,0:T(8,128)(2,1)S(1)}, u32[]{:S(2)}, u32[]{:S(2)}) collective-permute-start(bf16[8,128,128]{2,1,0:T(8,128)(2,1)S(1)} %get-tuple-element.25), channel_id=1, source_target_pairs={{0,4},{2,6},{4,0},{6,2},{8,12},{10,14},{12,8},{14,10},{1,5},{3,7},... | collective-permute-start | bytes 786440 | tf_op jit(solution)/shard_map/ppermute | solution.py:25
  14.0 7.9 %collective-permute-start.4 = (bf16[2,4,128,128]{3,2,1,0:T(8,128)(2,1)S(1)}, bf16[2,4,128,128]{3,2,1,0:T(8,128)(2,1)S(1)}, u32[]{:S(2)}, u32[]{:S(2)}) collective-permute-start(bf16[2,4,128,128]{3,2,1,0:T(8,128)(2,1)S(1)} %get-tuple-element.26), channel_id=1, source_target_pairs={{0,2},{2,0},{4,6},{6,4},{8,10},{10,8},{12,14},{14,12},{1,3},{3,1},... | collective-permute-start | bytes 786440 | tf_op jit(solution)/shard_map/ppermute | solution.py:25
  21.8 1.6 %collective-permute-start.6 = (bf16[512,256]{1,0:T(8,128)(2,1)S(1)}, bf16[512,256]{1,0:T(8,128)(2,1)S(1)}, u32[]{:S(2)}, u32[]{:S(2)}) collective-permute-start(bf16[512,256]{1,0:T(8,128)(2,1)S(1)} %shard_map.61.refs_9_), channel_id=1, source_target_pairs={{0,1},{1,0},{2,3},{3,2},{4,5},{5,4},{6,7},{7,6},{8,9},{9,8},{10,11... | collective-permute-start | bytes 786440 | tf_op jit(solution)/shard_map/ppermute | solution.py:29
  24.0 1.6 %collective-permute-start.7 = (f32[2,136,256]{2,1,0:T(8,128)S(1)}, f32[2,136,256]{2,1,0:T(8,128)S(1)}, u32[]{:S(2)}, u32[]{:S(2)}) collective-permute-start(f32[2,136,256]{2,1,0:T(8,128)S(1)} %get-tuple-element.29), channel_id=1, source_target_pairs={{0,1},{1,0},{2,3},{3,2},{4,5},{5,4},{6,7},{7,6},{8,9},{9,8},{10,11... | collective-permute-start | bytes 835592 | tf_op jit(solution)/shard_map/ppermute | solution.py:29
  25.7 4.4 %collective-permute-start.8 = (bf16[144,256]{1,0:T(8,128)(2,1)S(1)}, bf16[144,256]{1,0:T(8,128)(2,1)S(1)}, u32[]{:S(2)}, u32[]{:S(2)}) collective-permute-start(bf16[144,256]{1,0:T(8,128)(2,1)S(1)} %get-tuple-element.31), channel_id=1, source_target_pairs={{0,2},{2,0},{4,6},{6,4},{8,10},{10,8},{12,14},{14,12},{1,3},{3,1},... | collective-permute-start | bytes 221192 | tf_op jit(solution)/shard_map/ppermute | solution.py:25
  27.3 0.7 %copy-start.3 = (s32[128]{0:T(128)S(1)}, s32[128]{0:T(128)}, u32[]{:S(2)}) copy-start(s32[128]{0:T(128)} %param.8) | copy-start | bytes 1540
  27.3 0.7 %copy-start.4 = (s32[128]{0:T(128)S(1)}, s32[128]{0:T(128)}, u32[]{:S(2)}) copy-start(s32[128]{0:T(128)} %param.9) | copy-start | bytes 1540
  28.1 6.6 %collective-permute-start.5 = (bf16[4,2,128,128]{3,2,1,0:T(8,128)(2,1)S(1)}, bf16[4,2,128,128]{3,2,1,0:T(8,128)(2,1)S(1)}, u32[]{:S(2)}, u32[]{:S(2)}) collective-permute-start(bf16[4,2,128,128]{3,2,1,0:T(8,128)(2,1)S(1)} %shard_map.60), channel_id=1, source_target_pairs={{0,1},{1,0},{2,3},{3,2},{4,5},{5,4},{6,7},{7,6},{8,9},{9,8},{10,11... | collective-permute-start | bytes 786440 | tf_op jit(solution)/shard_map/ppermute | solution.py:29
  30.3 6.3 %collective-permute-start.10 = (bf16[128,256]{1,0:T(8,128)(2,1)S(1)}, bf16[128,256]{1,0:T(8,128)(2,1)S(1)}, u32[]{:S(2)}, u32[]{:S(2)}) collective-permute-start(bf16[128,256]{1,0:T(8,128)(2,1)S(1)} %fusion.5.refs_9_), channel_id=1, source_target_pairs={{0,12},{2,14},{4,8},{6,10},{8,4},{10,6},{12,0},{14,2},{1,13},{3,15... | collective-permute-start | bytes 196616 | tf_op jit(solution)/shard_map/ppermute | solution.py:25
  33.9 4.3 %collective-permute-start.11 = (bf16[128,256]{1,0:T(8,128)(2,1)S(1)}, bf16[128,256]{1,0:T(8,128)(2,1)S(1)}, u32[]{:S(2)}, u32[]{:S(2)}) collective-permute-start(bf16[128,256]{1,0:T(8,128)(2,1)S(1)} %fusion.5.refs_9_), channel_id=1, source_target_pairs={{0,4},{2,6},{4,0},{6,2},{8,12},{10,14},{12,8},{14,10},{1,5},{3,7},... | collective-permute-start | bytes 196616 | tf_op jit(solution)/shard_map/ppermute | solution.py:25
  33.9 5.2 %collective-permute-start.9 = (bf16[128,256]{1,0:T(8,128)(2,1)S(1)}, bf16[128,256]{1,0:T(8,128)(2,1)S(1)}, u32[]{:S(2)}, u32[]{:S(2)}) collective-permute-start(bf16[128,256]{1,0:T(8,128)(2,1)S(1)} %fusion.5.refs_9_), channel_id=1, source_target_pairs={{0,8},{2,10},{4,12},{6,14},{8,0},{10,2},{12,4},{14,6},{1,9},{3,11}... | collective-permute-start | bytes 196616 | tf_op jit(solution)/shard_map/ppermute | solution.py:25
  39.6 1.6 %collective-permute-start.12 = (f32[2,128,256]{2,1,0:T(8,128)S(1)}, f32[2,128,256]{2,1,0:T(8,128)S(1)}, u32[]{:S(2)}, u32[]{:S(2)}) collective-permute-start(f32[2,128,256]{2,1,0:T(8,128)S(1)} %get-tuple-element.34), channel_id=1, source_target_pairs={{0,1},{1,0},{2,3},{3,2},{4,5},{5,4},{6,7},{7,6},{8,9},{9,8},{10,11... | collective-permute-start | bytes 786440 | tf_op jit(solution)/shard_map/ppermute | solution.py:29
  41.2 4.3 %collective-permute-start.13 = (bf16[128,256]{1,0:T(8,128)(2,1)S(1)}, bf16[128,256]{1,0:T(8,128)(2,1)S(1)}, u32[]{:S(2)}, u32[]{:S(2)}) collective-permute-start(bf16[128,256]{1,0:T(8,128)(2,1)S(1)} %get-tuple-element.36), channel_id=1, source_target_pairs={{0,2},{2,0},{4,6},{6,4},{8,10},{10,8},{12,14},{14,12},{1,3},{3,1},... | collective-permute-start | bytes 196616 | tf_op jit(solution)/shard_map/ppermute | solution.py:25

commit v9 on v6

v9 whole, which is shorter than its diff:
```python
import jax
import jax.numpy as jnp
from jax import lax
from jax.experimental import pallas as pl
from jax.experimental.pallas import tpu as pltpu
from jax.sharding import PartitionSpec as P

ITERS = 2
CARRY = 0.8
SUBLANES = 8
LEAD_FLOPS = 2_000_000_000
HALVES_FLOPS = 4_000_000_000
MIB = 1024 * 1024


def split_rows(count):
    high = 1 << ((count.bit_length() - 1) // 2)
    return count // high, high


def swap_rows(value, shift):
    count = lax.axis_size("row")
    return lax.ppermute(value, "row", [(i, i ^ shift) for i in range(count)])


def swap_cores(value):
    return lax.ppermute(value, "col", [(0, 1), (1, 0)])


def call(kernel, out_shape, *operands, smem=0, flops=0):
    spaces = [pltpu.SMEM] * smem + [pltpu.VMEM] * (len(operands) - smem)
    size = sum(x.size * x.dtype.itemsize for x in (*operands, *jax.tree.leaves(out_shape)))
    return pl.pallas_call(
        kernel,
        out_shape=out_shape,
        in_specs=[pl.BlockSpec(memory_space=space) for space in spaces],
        out_specs=jax.tree.map(lambda _: pl.BlockSpec(memory_space=pltpu.VMEM), out_shape),
        compiler_params=pltpu.CompilerParams(vmem_limit_bytes=2 * size + 4 * MIB),
        cost_estimate=pl.CostEstimate(flops=flops, bytes_accessed=size, transcendentals=0),
    )(*operands)


def far_first(count):
    half = count // 2
    return [k for k in range(half, count)] + [k for k in range(1, half)]


def prepare_kernel(low_count, high_count, live, tile, labels, lead, own, *outs):
    strips, halves = outs[: low_count - 1], outs[low_count - 1 :]
    row, col = lax.axis_index("row"), lax.axis_index("col")
    high, low = lax.div(row, low_count), lax.rem(row, low_count)
    width = tile.shape[1]
    out_row = lax.broadcasted_iota(jnp.int32, (2 * width, 2 * width), 0)
    in_row = lax.broadcasted_iota(jnp.int32, (2 * width, 2 * width), 1)
    side = lax.bitwise_xor((out_row >= width).astype(jnp.int32), col)
    spot = 2 * lax.rem(out_row, width) + side
    sort = jnp.where(in_row == spot, 1.0, 0.0).astype(jnp.bfloat16)
    for j in reversed(range(high_count)):
        for k in range(low_count):
            block = lax.bitwise_xor(high, j) * low_count + lax.bitwise_xor(low, k)
            rows = tile[pl.ds(pl.multiple_of(block * 2 * width, 2 * width), 2 * width), :]
            sides = jnp.dot(sort, rows, preferred_element_type=jnp.float32)
            for i in range(2):
                keep = live[lax.bitwise_xor(col, i), 0, block] == 1
                piece = sides[i * width : (i + 1) * width]
                piece = jnp.where(keep, piece, jnp.zeros_like(piece)).astype(jnp.bfloat16)
                out = own if k == 0 else strips[k - 1]
                out[i * high_count + j] = piece
                if j > 0:
                    halves[j - 1][i, k] = piece
    for strip in strips:
        for part in range(labels.shape[1] // width):
            strip[2 * high_count + part] = labels[:, part * width : (part + 1) * width]


def fold_kernel(high_count, first, *refs):
    keeps, taken, (total, *sends) = refs[:high_count], refs[high_count], refs[high_count + 1 :]
    total[...] = keeps[0][...] + taken[0]
    for j, send in enumerate(sends, 1):
        both = keeps[j][...] + taken[j]
        width = both.shape[0] - (SUBLANES if first else 0)
        send[:width, :] = both[:width].astype(jnp.bfloat16)
        if first:
            sums = jnp.concatenate([both[width:]] * 2, axis=0)
            high = sums.astype(jnp.bfloat16).astype(jnp.float32)
            middle = (sums - high).astype(jnp.bfloat16).astype(jnp.float32)
            row = lax.broadcasted_iota(jnp.int32, sums.shape, 0)
            terms = jnp.where(row == 0, high, jnp.where(row == 1, middle, sums - high - middle))
            send[width:, :] = terms.astype(jnp.bfloat16)


def unload_kernel(spot, own, *refs):
    strips, out = refs[:-1], refs[-1]
    width, classes = own.shape
    out[:width] = own[...]
    for k, strip in enumerate(strips, 1):
        for part in range(classes // width):
            out[k * width : (k + 1) * width, part * width : (part + 1) * width] = strip[spot + part]


def guard_kernel(*refs):
    refs[-1][...] = jnp.zeros_like(refs[-1])


def other_kernel(*refs):
    strips, out = refs[:-1], refs[-1]
    high_count = out.shape[1]
    for k, strip in enumerate(strips):
        for j in range(high_count):
            out[k, j] = strip[high_count + j]


def lead_kernel(out):
    out[...] = jnp.zeros_like(out)


def seed_kernel(seed_class, seed_mask, base):
    width, classes = base.shape
    kind = jnp.where(seed_mask[...] == 1, seed_class[...], -1)
    kind = jnp.transpose(jnp.broadcast_to(kind, (width, width)))
    for start in range(0, classes, width):
        slots = lax.broadcasted_iota(jnp.int32, (width, width), 1) + start
        base[:, start : start + width] = jnp.where(kind == slots, 1.0 - CARRY, 0.0)


def spread_kernel(low_count, high_count, first, *refs):
    sent, refs = refs[:low_count], refs[low_count:]
    strips, refs = sent[:1] + refs[: low_count - 1], refs[low_count - 1 :]
    halves, refs = refs[: high_count - 1], refs[high_count - 1 :]
    other, refs = refs[0], refs[1:]
    pieces, keeps, give = refs[: -high_count - 1], refs[-high_count - 1 : -1], refs[-1]
    if first:
        pieces, theirs = pieces[:1], pieces[1][...]
    values = jnp.concatenate([piece[...] for piece in pieces], axis=0)
    depth, classes = values.shape
    width = depth // low_count
    ones = jnp.ones((SUBLANES, depth), jnp.bfloat16)

    def product(left, right, contract):
        return lax.dot_general(left, right, ((contract[:1], contract[1:]), ((), ())), preferred_element_type=jnp.float32)

    def strip_blocks(i, j):
        return jnp.concatenate([strip[i * high_count + j] for strip in strips], axis=1)

    for i in (1, 0):
        for j in range(high_count):
            back = [sent[k][i * high_count] if j == 0 else halves[j - 1][i, k] for k in range(low_count)]
            back = jnp.concatenate(back, axis=0)
            total = product(back, values, (0, 0))
            ahead = []
            if first and i == 0:
                ahead = [(strip_blocks(0, j), values), (strip_blocks(1, j), theirs)]
            elif not first and i == 0:
                ahead = [(strip_blocks(0, j), values)]
            elif not first:
                ahead = [(jnp.concatenate([other[k, j] for k in range(low_count)], axis=1), values)]
            for blocks, right in ahead:
                total += product(blocks, right, (1, 0))
            out = keeps[j] if i == 0 else give.at[j]
            out[:width, :] = total
            if first:
                sums = product(ones, back, (1, 0))
                for blocks, _ in ahead:
                    sums += product(ones, blocks, (1, 1))
                out[width:, :] = jnp.concatenate([sums] * (classes // width), axis=1)


def on_device(affinity, block_live, labels, seed_class, seed_mask):
    stripe, sides, width = affinity.shape
    count = lax.axis_size("row")
    low_count, high_count = split_rows(count)
    classes = labels.shape[1]

    blocks = 2 * high_count
    own = jax.ShapeDtypeStruct((blocks, width, width), jnp.bfloat16)
    strip = jax.ShapeDtypeStruct((blocks + classes // width, width, width), jnp.bfloat16)
    half = jax.ShapeDtypeStruct((2, low_count, width, width), jnp.bfloat16)
    sent = call(
        lambda *refs: prepare_kernel(low_count, high_count, *refs),
        [own] + [strip] * (low_count - 1) + [half] * (high_count - 1),
        block_live.transpose(1, 2, 0),
        affinity.reshape(stripe * sides, width),
        labels,
        call(lead_kernel, jax.ShapeDtypeStruct((SUBLANES, width), jnp.float32), flops=LEAD_FLOPS),
        smem=1,
    )
    sent, halves = sent[:low_count], sent[low_count:]
    halves = [swap_rows(x, (j + 1) * low_count) for j, x in enumerate(halves)]
    arrived = {k: swap_rows(sent[k], k) for k in far_first(low_count)}
    strips = [arrived[k] for k in range(1, low_count)]
    values = jax.ShapeDtypeStruct((low_count * width, classes), jnp.bfloat16)
    values = call(lambda *refs: unload_kernel(blocks, *refs), values, labels, *strips)
    swapped = swap_cores(values)
    mark = jax.ShapeDtypeStruct((SUBLANES, width), jnp.float32)
    mark = call(guard_kernel, mark, *halves, flops=HALVES_FLOPS)
    other = jax.ShapeDtypeStruct((low_count, high_count, width, width), jnp.bfloat16)
    other = swap_cores(call(other_kernel, other, sent[0], *strips))
    pieces = [mark, values, swapped]
    base = call(
        seed_kernel,
        jax.ShapeDtypeStruct((width, classes), jnp.float32),
        seed_class.reshape(1, width),
        seed_mask.reshape(1, width),
    )

    current, degree = labels, None
    for step in range(ITERS):
        if step > 0:
            taken = {k: swap_rows(current, k) for k in far_first(low_count)}
            pieces = [other, current] + [taken[k] for k in range(1, low_count)]
        height = width + (SUBLANES if step == 0 else 0)
        part = jax.ShapeDtypeStruct((height, classes), jnp.float32)
        parts = jax.ShapeDtypeStruct((high_count, height, classes), jnp.float32)
        *keeps, give = call(
            lambda *refs: spread_kernel(low_count, high_count, step == 0, *refs),
            [part] * high_count + [parts],
            *sent,
            *strips,
            *halves,
            *pieces,
            flops=2 * 2 * 2 * high_count * low_count * width * width * classes,
        )
        taken = swap_cores(give)
        send = jax.ShapeDtypeStruct((width + (2 * SUBLANES if step == 0 else 0), classes), jnp.bfloat16)
        total, *sends = call(
            lambda *refs: fold_kernel(high_count, step == 0, *refs), [part] + [send] * (high_count - 1), *keeps, taken
        )
        sends = [swap_rows(x, (j + 1) * low_count).astype(jnp.float32) for j, x in enumerate(sends)]
        spread = sum((x[:width] for x in sends), total[:width])
        if step == 0:
            sums = sum((x[width : width + 3, :width].sum(axis=0) for x in sends), total[width, :width])
            degree = 1.0 + 0.5 * sums[:, None]
        mixed = CARRY * (0.5 * spread + current.astype(jnp.float32)) / degree
        current = (mixed + base).astype(jnp.bfloat16)
    return current


def solution(mesh):
    return jax.shard_map(
        on_device,
        mesh=mesh,
        in_specs=(
            P(("groups", "col"), None, "row"),
            P(("groups", "col"), None, "row"),
            P(("groups", "col", "row"), None),
            P(("groups", "col", "row")),
            P(("groups", "col", "row")),
        ),
        out_specs=P(("groups", "col", "row"), None),
        check_vma=False,
    )
```

time: 49.4 us -> 49.3 us (level)
  waiting for transfers between devices: 20.4 us -> 29.2 us
  starting transfers between devices: 23.1 us -> 14.9 us
  local copies, waits for them, and re-layouts: 2.39 us -> 1.71 us
    ppermute x12 -> x9, starting transfers between devices: 22.8 us -> 14.4 us  [swap_rows(): return lax.ppermute(value, 'row', [(i, i ^ shift) for i in range(count)])]
    ppermute x12 -> x9, waiting for transfers between devices: 17.3 us -> 24.8 us  [swap_rows(): return lax.ppermute(value, 'row', [(i, i ^ shift) for i in range(count)])]
    ppermute x4, waiting for transfers between devices: 3.07 us -> 4.45 us  [swap_cores(): return lax.ppermute(value, 'col', [(0, 1), (1, 0)])]
    unnamed x10, local copies, waits for them, and re-layouts: 2.39 us -> 1.71 us
    pallas_call x8 -> x10, Pallas kernels: 2.32 us -> 2.35 us  [call(): pl.pallas_call(kernel, out_shape=out_shape, in_specs=[pl.BlockSpec(memory...]
  transfers between devices with their start and end apart: 16 -> 13, of which waited for: 9 -> 10; matrix products, arithmetic and copies ran while one was open for 0% -> 0% of each run, Pallas kernels for 0% -> 0%
where the time goes in v9:
time: 49.3 us; the launch traced here: 49.1 us
  waiting for transfers between devices  29.2 us (59%)
  starting transfers between devices  14.9 us (30%)
  Pallas kernels  2.35 us (5%)
  local copies, waits for them, and re-layouts  1.71 us (3%)
  other arithmetic  0.86 us (2%)
    ppermute x9, waiting for transfers between devices, swap_rows(): return lax.ppermute(value, 'row', [(i, i ^ shift) for i in range(count)])  24.8 us
    ppermute x9, starting transfers between devices, swap_rows(): return lax.ppermute(value, 'row', [(i, i ^ shift) for i in range(count)])  14.4 us
    ppermute x4, waiting for transfers between devices, swap_cores(): return lax.ppermute(value, 'col', [(0, 1), (1, 0)])  4.45 us
    pallas_call x10, Pallas kernels, call(): pl.pallas_call(kernel, out_shape=out_shape, in_specs=[pl.BlockSpec(memory...  2.35 us
    unnamed x10, local copies, waits for them, and re-layouts  1.71 us
  transfers between devices with their start and end apart: 13, of which 10 were waited for; matrix products, arithmetic and copies ran while one was open for 0% of the time, Pallas kernels for 0%

profile of v9, /device:TPU:0, one launch (start us, length us, event | category | flops | bytes accessed | tf_op | source)
XLA Modules:
  0.0 49.1 jit_solution(6662235756218797695)
XLA Ops:
  0.0 0.0 copy-start.1
  0.0 0.0 copy-start
  0.0 0.0 copy-start.2
  0.0 1.0 %copy-done.1 = bf16[1024,2,128]{2,1,0:T(2,128)(2,1)S(1)} copy-done((bf16[1024,2,128]{2,1,0:T(2,128)(2,1)S(1)}, bf16[1024,2,128]{2,1,0:T(2,128)(2,1)}, u32[]{:S(2)}) %copy-start.1) | copy-done | bytes 524312
  1.0 0.0 copy-done
  1.0 0.0 copy-done.2
  1.0 1.0 %shard_map.56 = (bf16[4,128,128]{2,1,0:T(8,128)(2,1)S(1)}, bf16[6,128,128]{2,1,0:T(8,128)(2,1)S(1)}, bf16[6,128,128]{2,1,0:T(8,128)(2,1)S(1)}, bf16[6,128,128]{2...) custom-call(s32[2,1,8]{2,1,0:T(1,128)S(1)} %bitcast.11, bf16[2048,128]{1,0:T(8,128)(2,1)S(1)} %bitcast.10, ...), custom_call_target="tpu_custom_call" | custom-call | bytes 1577024 | tf_op jit(solution)/shard_map/pallas_call | solution.py:33
  2.0 4.1 %collective-permute-start.3 = (bf16[2,4,128,128]{3,2,1,0:T(8,128)(2,1)S(1)}, bf16[2,4,128,128]{3,2,1,0:T(8,128)(2,1)S(1)}, u32[]{:S(2)}, u32[]{:S(2)}) collective-permute-start(bf16[2,4,128,128]{3,2,1,0:T(8,128)(2,1)S(1)} %get-tuple-element.24), channel_id=1, source_target_pairs={{0,8},{2,10},{4,12},{6,14},{8,0},{10,2},{12,4},{14,6},{1,9},{3,11}... | collective-permute-start | bytes 786440 | tf_op jit(solution)/shard_map/ppermute | solution.py:23
  6.1 1.5 %collective-permute-start = (bf16[6,128,128]{2,1,0:T(8,128)(2,1)S(1)}, bf16[6,128,128]{2,1,0:T(8,128)(2,1)S(1)}, u32[]{:S(2)}, u32[]{:S(2)}) collective-permute-start(bf16[6,128,128]{2,1,0:T(8,128)(2,1)S(1)} %get-tuple-element.21.refs_1_), channel_id=1, source_target_pairs={{0,2},{2,0},{4,6},{6,4},{8,10},{10,8},{12,14},{14,12},{1,3},{3,1},... | collective-permute-start | bytes 589832 | tf_op jit(solution)/shard_map/ppermute | solution.py:23
  7.7 1.6 %collective-permute-start.1 = (bf16[6,128,128]{2,1,0:T(8,128)(2,1)S(1)}, bf16[6,128,128]{2,1,0:T(8,128)(2,1)S(1)}, u32[]{:S(2)}, u32[]{:S(2)}) collective-permute-start(bf16[6,128,128]{2,1,0:T(8,128)(2,1)S(1)} %get-tuple-element.22.refs_2_), channel_id=1, source_target_pairs={{0,4},{2,6},{4,0},{6,2},{8,12},{10,14},{12,8},{14,10},{1,5},{3,7},... | collective-permute-start | bytes 589832 | tf_op jit(solution)/shard_map/ppermute | solution.py:23
  9.2 0.4 collective-permute-start.2
  9.6 3.4 %collective-permute-done.refs_1_.refs_4_ = bf16[6,128,128]{2,1,0:T(8,128)(2,1)S(1)} collective-permute-done((bf16[6,128,128]{2,1,0:T(8,128)(2,1)S(1)}, bf16[6,128,128]{2,1,0:T(8,128)(2,1)S(1)}, u32[]{:S(2)}, u32[]{:S(2)}) %collective-permute-start) | collective-permute-done | bytes 196640 | tf_op jit(solution)/shard_map/ppermute | solution.py:23
  13.1 6.9 %collective-permute-done.1.refs_2_.refs_5_ = bf16[6,128,128]{2,1,0:T(8,128)(2,1)S(1)} collective-permute-done((bf16[6,128,128]{2,1,0:T(8,128)(2,1)S(1)}, bf16[6,128,128]{2,1,0:T(8,128)(2,1)S(1)}, u32[]{:S(2)}, u32[]{:S(2)}) %collective-permute-start.1) | collective-permute-done | bytes 196640 | tf_op jit(solution)/shard_map/ppermute | solution.py:23
  20.0 2.5 %collective-permute-done.2.refs_3_.refs_6_ = bf16[6,128,128]{2,1,0:T(8,128)(2,1)S(1)} collective-permute-done((bf16[6,128,128]{2,1,0:T(8,128)(2,1)S(1)}, bf16[6,128,128]{2,1,0:T(8,128)(2,1)S(1)}, u32[]{:S(2)}, u32[]{:S(2)}) %collective-permute-start.2) | collective-permute-done | bytes 196640 | tf_op jit(solution)/shard_map/ppermute | solution.py:23
  22.4 0.1 collective-permute-start.5
  22.5 0.0 collective-permute-done.3.refs_0_.refs_7_
  22.5 1.5 %collective-permute-done.5.refs_10_ = bf16[512,256]{1,0:T(8,128)(2,1)S(1)} collective-permute-done((bf16[512,256]{1,0:T(8,128)(2,1)S(1)}, bf16[512,256]{1,0:T(8,128)(2,1)S(1)}, u32[]{:S(2)}, u32[]{:S(2)}) %collective-permute-start.5) | collective-permute-done | bytes 262176 | tf_op jit(solution)/shard_map/ppermute | solution.py:27
  24.0 0.7 %shard_map.60 = (f32[136,256]{1,0:T(8,128)S(1)}, f32[136,256]{1,0:T(8,128)S(1)}, f32[2,136,256]{2,1,0:T(8,128)S(1)}) custom-call(bf16[4,128,128]{2,1,0:T(8,128)(2,1)S(1)} %get-tuple-element.20.refs_0_, bf16[6,128,128]{2,1,0:T(8,128)(2,1)S(1)} %get-tuple-element.21.refs_1_, bf16[6,128,128]{2,1,0:T(8,128)(2,1)S(1)} %get-tuple-element.22.refs_2_, ...), custom_call_target="tpu_custom_call" | custom-call | flops 268435456 | bytes 2658304 | tf_op jit(solution)/shard_map/pallas_call | solution.py:33
  24.7 0.2 collective-permute-start.6
  24.9 1.4 %collective-permute-done.6.refs_2_ = f32[2,136,256]{2,1,0:T(8,128)S(1)} collective-permute-done((f32[2,136,256]{2,1,0:T(8,128)S(1)}, f32[2,136,256]{2,1,0:T(8,128)S(1)}, u32[]{:S(2)}, u32[]{:S(2)}) %collective-permute-start.6) | collective-permute-done | bytes 278560 | tf_op jit(solution)/shard_map/ppermute | solution.py:27
  26.4 1.2 %collective-permute-start.7 = (bf16[144,256]{1,0:T(8,128)(2,1)S(1)}, bf16[144,256]{1,0:T(8,128)(2,1)S(1)}, u32[]{:S(2)}, u32[]{:S(2)}) collective-permute-start(bf16[144,256]{1,0:T(8,128)(2,1)S(1)} %get-tuple-element.29), channel_id=1, source_target_pairs={{0,8},{2,10},{4,12},{6,14},{8,0},{10,2},{12,4},{14,6},{1,9},{3,11}... | collective-permute-start | bytes 221192 | tf_op jit(solution)/shard_map/ppermute | solution.py:23
  27.6 0.0 copy-start.3
  27.6 0.0 copy-start.4
  27.6 0.7 %copy-done.3 = s32[128]{0:T(128)S(1)} copy-done((s32[128]{0:T(128)S(1)}, s32[128]{0:T(128)}, u32[]{:S(2)}) %copy-start.3) | copy-done | bytes 536
  28.2 0.0 copy-done.4
  28.2 0.1 shard_map.62
  28.4 0.1 collective-permute-start.4
  28.4 4.8 %collective-permute-done.7 = bf16[144,256]{1,0:T(8,128)(2,1)S(1)} collective-permute-done((bf16[144,256]{1,0:T(8,128)(2,1)S(1)}, bf16[144,256]{1,0:T(8,128)(2,1)S(1)}, u32[]{:S(2)}, u32[]{:S(2)}) %collective-permute-start.7) | collective-permute-done | bytes 73760 | tf_op jit(solution)/shard_map/ppermute | solution.py:23
  33.3 0.1 fusion.5.refs_9_
  33.4 0.1 collective-permute-start.10
  33.5 1.4 %collective-permute-start.8 = (bf16[128,256]{1,0:T(8,128)(2,1)S(1)}, bf16[128,256]{1,0:T(8,128)(2,1)S(1)}, u32[]{:S(2)}, u32[]{:S(2)}) collective-permute-start(bf16[128,256]{1,0:T(8,128)(2,1)S(1)} %fusion.5.refs_9_), channel_id=1, source_target_pairs={{0,2},{2,0},{4,6},{6,4},{8,10},{10,8},{12,14},{14,12},{1,3},{3,1},... | collective-permute-start | bytes 196616 | tf_op jit(solution)/shard_map/ppermute | solution.py:23
  34.9 2.1 %collective-permute-start.9 = (bf16[128,256]{1,0:T(8,128)(2,1)S(1)}, bf16[128,256]{1,0:T(8,128)(2,1)S(1)}, u32[]{:S(2)}, u32[]{:S(2)}) collective-permute-start(bf16[128,256]{1,0:T(8,128)(2,1)S(1)} %fusion.5.refs_9_), channel_id=1, source_target_pairs={{0,4},{2,6},{4,0},{6,2},{8,12},{10,14},{12,8},{14,10},{1,5},{3,7},... | collective-permute-start | bytes 196616 | tf_op jit(solution)/shard_map/ppermute | solution.py:23
  37.0 0.0 collective-permute-done.4.refs_8_
  37.0 2.3 %collective-permute-done.10.refs_12_ = bf16[128,256]{1,0:T(8,128)(2,1)S(1)} collective-permute-done((bf16[128,256]{1,0:T(8,128)(2,1)S(1)}, bf16[128,256]{1,0:T(8,128)(2,1)S(1)}, u32[]{:S(2)}, u32[]{:S(2)}) %collective-permute-start.10) | collective-permute-done | bytes 65568 | tf_op jit(solution)/shard_map/ppermute | solution.py:23
  39.2 0.0 collective-permute-done.8.refs_10_
  39.2 0.4 collective-permute-done.9.refs_11_
  39.7 0.5 shard_map.63
  40.1 0.1 collective-permute-start.11
  40.2 1.5 %collective-permute-done.11.refs_2_ = f32[2,128,256]{2,1,0:T(8,128)S(1)} collective-permute-done((f32[2,128,256]{2,1,0:T(8,128)S(1)}, f32[2,128,256]{2,1,0:T(8,128)S(1)}, u32[]{:S(2)}, u32[]{:S(2)}) %collective-permute-start.11) | collective-permute-done | bytes 262176 | tf_op jit(solution)/shard_map/ppermute | solution.py:27
  41.8 2.1 %collective-permute-start.12 = (bf16[128,256]{1,0:T(8,128)(2,1)S(1)}, bf16[128,256]{1,0:T(8,128)(2,1)S(1)}, u32[]{:S(2)}, u32[]{:S(2)}) collective-permute-start(bf16[128,256]{1,0:T(8,128)(2,1)S(1)} %get-tuple-element.34), channel_id=1, source_target_pairs={{0,8},{2,10},{4,12},{6,14},{8,0},{10,2},{12,4},{14,6},{1,9},{3,11}... | collective-permute-start | bytes 196616 | tf_op jit(solution)/shard_map/ppermute | solution.py:23
  43.9 4.5 %collective-permute-done.12 = bf16[128,256]{1,0:T(8,128)(2,1)S(1)} collective-permute-done((bf16[128,256]{1,0:T(8,128)(2,1)S(1)}, bf16[128,256]{1,0:T(8,128)(2,1)S(1)}, u32[]{:S(2)}, u32[]{:S(2)}) %collective-permute-start.12) | collective-permute-done | bytes 65568 | tf_op jit(solution)/shard_map/ppermute | solution.py:23
  48.4 0.7 %add_convert_fusion = bf16[128,256]{1,0:T(8,128)(2,1)} fusion(f32[128,256]{1,0:T(8,128)S(1)} %shard_map.62, bf16[128,256]{1,0:T(8,128)(2,1)S(1)} %fusion.5.refs_9_, f32[128,256]{1,0:T(8,128)S(1)} %get-tuple-element.33, bf16[128,256]{1,0:T(8,128)(2,1)S(1)} %collective-permute-done.12, f32[128]{0:T(128)S(1)} %fusion.7), kind=kLoop, calls=%fused_computation.6 | loop fusion | flops 294912 | bytes 459264 | tf_op jit(solution)/shard_map/convert_element_type | solution.py:234
  (9 shorter events, 0.2 us)
Async XLA Ops:
  0.0 1.0 %copy-start.1 = (bf16[1024,2,128]{2,1,0:T(2,128)(2,1)S(1)}, bf16[1024,2,128]{2,1,0:T(2,128)(2,1)}, u32[]{:S(2)}) copy-start(bf16[1024,2,128]{2,1,0:T(2,128)(2,1)} %param.5) | copy-start | bytes 1572868
  0.0 1.0 %copy-start = (bf16[128,256]{1,0:T(8,128)(2,1)S(1)}, bf16[128,256]{1,0:T(8,128)(2,1)}, u32[]{:S(2)}) copy-start(bf16[128,256]{1,0:T(8,128)(2,1)} %refs_0_.1) | copy-start | bytes 196612
  0.0 1.0 %copy-start.2 = (s32[8,2,1]{0,2,1:T(1,128)S(1)}, s32[8,2,1]{0,2,1:T(1,128)}, u32[]{:S(2)}) copy-start(s32[8,2,1]{0,2,1:T(1,128)} %param.6) | copy-start | bytes 196
  2.0 20.5 %collective-permute-start.3 = (bf16[2,4,128,128]{3,2,1,0:T(8,128)(2,1)S(1)}, bf16[2,4,128,128]{3,2,1,0:T(8,128)(2,1)S(1)}, u32[]{:S(2)}, u32[]{:S(2)}) collective-permute-start(bf16[2,4,128,128]{3,2,1,0:T(8,128)(2,1)S(1)} %get-tuple-element.24), channel_id=1, source_target_pairs={{0,8},{2,10},{4,12},{6,14},{8,0},{10,2},{12,4},{14,6},{1,9},{3,11}... | collective-permute-start | bytes 786440 | tf_op jit(solution)/shard_map/ppermute | solution.py:23
  6.1 6.9 %collective-permute-start = (bf16[6,128,128]{2,1,0:T(8,128)(2,1)S(1)}, bf16[6,128,128]{2,1,0:T(8,128)(2,1)S(1)}, u32[]{:S(2)}, u32[]{:S(2)}) collective-permute-start(bf16[6,128,128]{2,1,0:T(8,128)(2,1)S(1)} %get-tuple-element.21.refs_1_), channel_id=1, source_target_pairs={{0,2},{2,0},{4,6},{6,4},{8,10},{10,8},{12,14},{14,12},{1,3},{3,1},... | collective-permute-start | bytes 589832 | tf_op jit(solution)/shard_map/ppermute | solution.py:23
  7.7 12.3 %collective-permute-start.1 = (bf16[6,128,128]{2,1,0:T(8,128)(2,1)S(1)}, bf16[6,128,128]{2,1,0:T(8,128)(2,1)S(1)}, u32[]{:S(2)}, u32[]{:S(2)}) collective-permute-start(bf16[6,128,128]{2,1,0:T(8,128)(2,1)S(1)} %get-tuple-element.22.refs_2_), channel_id=1, source_target_pairs={{0,4},{2,6},{4,0},{6,2},{8,12},{10,14},{12,8},{14,10},{1,5},{3,7},... | collective-permute-start | bytes 589832 | tf_op jit(solution)/shard_map/ppermute | solution.py:23
  9.2 13.2 %collective-permute-start.2 = (bf16[6,128,128]{2,1,0:T(8,128)(2,1)S(1)}, bf16[6,128,128]{2,1,0:T(8,128)(2,1)S(1)}, u32[]{:S(2)}, u32[]{:S(2)}) collective-permute-start(bf16[6,128,128]{2,1,0:T(8,128)(2,1)S(1)} %get-tuple-element.23.refs_3_), channel_id=1, source_target_pairs={{0,6},{2,4},{4,2},{6,0},{8,14},{10,12},{12,10},{14,8},{1,7},{3,5},... | collective-permute-start | bytes 589832 | tf_op jit(solution)/shard_map/ppermute | solution.py:23
  22.4 1.6 %collective-permute-start.5 = (bf16[512,256]{1,0:T(8,128)(2,1)S(1)}, bf16[512,256]{1,0:T(8,128)(2,1)S(1)}, u32[]{:S(2)}, u32[]{:S(2)}) collective-permute-start(bf16[512,256]{1,0:T(8,128)(2,1)S(1)} %shard_map.59.refs_9_), channel_id=1, source_target_pairs={{0,1},{1,0},{2,3},{3,2},{4,5},{5,4},{6,7},{7,6},{8,9},{9,8},{10,11... | collective-permute-start | bytes 786440 | tf_op jit(solution)/shard_map/ppermute | solution.py:27
  24.7 1.6 %collective-permute-start.6 = (f32[2,136,256]{2,1,0:T(8,128)S(1)}, f32[2,136,256]{2,1,0:T(8,128)S(1)}, u32[]{:S(2)}, u32[]{:S(2)}) collective-permute-start(f32[2,136,256]{2,1,0:T(8,128)S(1)} %get-tuple-element.27), channel_id=1, source_target_pairs={{0,1},{1,0},{2,3},{3,2},{4,5},{5,4},{6,7},{7,6},{8,9},{9,8},{10,11... | collective-permute-start | bytes 835592 | tf_op jit(solution)/shard_map/ppermute | solution.py:27
  26.4 6.9 %collective-permute-start.7 = (bf16[144,256]{1,0:T(8,128)(2,1)S(1)}, bf16[144,256]{1,0:T(8,128)(2,1)S(1)}, u32[]{:S(2)}, u32[]{:S(2)}) collective-permute-start(bf16[144,256]{1,0:T(8,128)(2,1)S(1)} %get-tuple-element.29), channel_id=1, source_target_pairs={{0,8},{2,10},{4,12},{6,14},{8,0},{10,2},{12,4},{14,6},{1,9},{3,11}... | collective-permute-start | bytes 221192 | tf_op jit(solution)/shard_map/ppermute | solution.py:23
  27.6 0.7 %copy-start.3 = (s32[128]{0:T(128)S(1)}, s32[128]{0:T(128)}, u32[]{:S(2)}) copy-start(s32[128]{0:T(128)} %param.8) | copy-start | bytes 1540
  27.6 0.7 %copy-start.4 = (s32[128]{0:T(128)S(1)}, s32[128]{0:T(128)}, u32[]{:S(2)}) copy-start(s32[128]{0:T(128)} %param.9) | copy-start | bytes 1540
  28.4 8.6 %collective-permute-start.4 = (bf16[4,2,128,128]{3,2,1,0:T(8,128)(2,1)S(1)}, bf16[4,2,128,128]{3,2,1,0:T(8,128)(2,1)S(1)}, u32[]{:S(2)}, u32[]{:S(2)}) collective-permute-start(bf16[4,2,128,128]{3,2,1,0:T(8,128)(2,1)S(1)} %shard_map.57), channel_id=1, source_target_pairs={{0,1},{1,0},{2,3},{3,2},{4,5},{5,4},{6,7},{7,6},{8,9},{9,8},{10,11... | collective-permute-start | bytes 786440 | tf_op jit(solution)/shard_map/ppermute | solution.py:27
  33.4 5.8 %collective-permute-start.10 = (bf16[128,256]{1,0:T(8,128)(2,1)S(1)}, bf16[128,256]{1,0:T(8,128)(2,1)S(1)}, u32[]{:S(2)}, u32[]{:S(2)}) collective-permute-start(bf16[128,256]{1,0:T(8,128)(2,1)S(1)} %fusion.5.refs_9_), channel_id=1, source_target_pairs={{0,6},{2,4},{4,2},{6,0},{8,14},{10,12},{12,10},{14,8},{1,7},{3,5},... | collective-permute-start | bytes 196616 | tf_op jit(solution)/shard_map/ppermute | solution.py:23
  33.5 5.7 %collective-permute-start.8 = (bf16[128,256]{1,0:T(8,128)(2,1)S(1)}, bf16[128,256]{1,0:T(8,128)(2,1)S(1)}, u32[]{:S(2)}, u32[]{:S(2)}) collective-permute-start(bf16[128,256]{1,0:T(8,128)(2,1)S(1)} %fusion.5.refs_9_), channel_id=1, source_target_pairs={{0,2},{2,0},{4,6},{6,4},{8,10},{10,8},{12,14},{14,12},{1,3},{3,1},... | collective-permute-start | bytes 196616 | tf_op jit(solution)/shard_map/ppermute | solution.py:23
  34.9 4.8 %collective-permute-start.9 = (bf16[128,256]{1,0:T(8,128)(2,1)S(1)}, bf16[128,256]{1,0:T(8,128)(2,1)S(1)}, u32[]{:S(2)}, u32[]{:S(2)}) collective-permute-start(bf16[128,256]{1,0:T(8,128)(2,1)S(1)} %fusion.5.refs_9_), channel_id=1, source_target_pairs={{0,4},{2,6},{4,0},{6,2},{8,12},{10,14},{12,8},{14,10},{1,5},{3,7},... | collective-permute-start | bytes 196616 | tf_op jit(solution)/shard_map/ppermute | solution.py:23
  40.1 1.6 %collective-permute-start.11 = (f32[2,128,256]{2,1,0:T(8,128)S(1)}, f32[2,128,256]{2,1,0:T(8,128)S(1)}, u32[]{:S(2)}, u32[]{:S(2)}) collective-permute-start(f32[2,128,256]{2,1,0:T(8,128)S(1)} %get-tuple-element.32), channel_id=1, source_target_pairs={{0,1},{1,0},{2,3},{3,2},{4,5},{5,4},{6,7},{7,6},{8,9},{9,8},{10,11... | collective-permute-start | bytes 786440 | tf_op jit(solution)/shard_map/ppermute | solution.py:27
  41.8 6.6 %collective-permute-start.12 = (bf16[128,256]{1,0:T(8,128)(2,1)S(1)}, bf16[128,256]{1,0:T(8,128)(2,1)S(1)}, u32[]{:S(2)}, u32[]{:S(2)}) collective-permute-start(bf16[128,256]{1,0:T(8,128)(2,1)S(1)} %get-tuple-element.34), channel_id=1, source_target_pairs={{0,8},{2,10},{4,12},{6,14},{8,0},{10,2},{12,4},{14,6},{1,9},{3,11}... | collective-permute-start | bytes 196616 | tf_op jit(solution)/shard_map/ppermute | solution.py:23

commit v10 on v5

v10 whole, which is shorter than its diff:
```python
import jax
import jax.numpy as jnp
from jax import lax
from jax.experimental import pallas as pl
from jax.experimental.pallas import tpu as pltpu
from jax.sharding import PartitionSpec as P

ITERS = 2
CARRY = 0.8
SUBLANES = 8
LANES = 128
LEAD_FLOPS = 2_000_000_000
PAIR_FLOPS = 4_000_000_000
STRIPS_FLOPS = 3_000_000_000
MARK_FLOPS = 3_000_000_000
MIB = 1024 * 1024


def split_rows(count):
    inner = 1 << ((count.bit_length() - 1) // 2)
    return count // inner, inner


def swap_rows(value, shift):
    count = lax.axis_size("row")
    return lax.ppermute(value, "row", [(i, i ^ shift) for i in range(count)])


def swap_cores(value):
    return lax.ppermute(value, "col", [(0, 1), (1, 0)])


def call(kernel, out_shape, *operands, smem=0, flops=0):
    spaces = [pltpu.SMEM] * smem + [pltpu.VMEM] * (len(operands) - smem)
    size = sum(x.size * x.dtype.itemsize for x in (*operands, *jax.tree.leaves(out_shape)))
    return pl.pallas_call(
        kernel,
        out_shape=out_shape,
        in_specs=[pl.BlockSpec(memory_space=space) for space in spaces],
        out_specs=jax.tree.map(lambda _: pl.BlockSpec(memory_space=pltpu.VMEM), out_shape),
        compiler_params=pltpu.CompilerParams(vmem_limit_bytes=2 * size + 4 * MIB),
        cost_estimate=pl.CostEstimate(flops=flops, bytes_accessed=size, transcendentals=0),
    )(*operands)


def far_first(count):
    half = count // 2
    return [k for k in range(half, count)] + [k for k in range(1, half)]


def prepare_kernel(z_count, y_count, live, tile, lead, *outs):
    strips, other = outs[:z_count], outs[z_count]
    row, col = lax.axis_index("row"), lax.axis_index("col")
    z, y = lax.div(row, y_count), lax.rem(row, y_count)
    width = tile.shape[1]
    out_row = lax.broadcasted_iota(jnp.int32, (2 * width, 2 * width), 0)
    in_row = lax.broadcasted_iota(jnp.int32, (2 * width, 2 * width), 1)
    side = lax.bitwise_xor((out_row >= width).astype(jnp.int32), col)
    spot = 2 * lax.rem(out_row, width) + side
    sort = jnp.where(in_row == spot, 1.0, 0.0).astype(jnp.bfloat16)
    for k in range(z_count):
        for j in range(y_count):
            block = lax.bitwise_xor(z, k) * y_count + lax.bitwise_xor(y, j)
            rows = tile[pl.ds(pl.multiple_of(block * 2 * width, 2 * width), 2 * width), :]
            sides = jnp.dot(sort, rows, preferred_element_type=jnp.float32)
            for i in range(2):
                keep = live[lax.bitwise_xor(col, i), 0, block] == 1
                piece = sides[i * width : (i + 1) * width]
                piece = jnp.where(keep, piece, jnp.zeros_like(piece)).astype(jnp.bfloat16)
                strips[k][i, j] = piece
                if i == 1:
                    other[k, j] = piece


def halves_kernel(z_count, *refs):
    strips, from_core, halves = refs[:z_count], refs[z_count], refs[z_count + 1 :]
    for j, half in enumerate(halves, 1):
        for k in range(z_count):
            half[0, k] = strips[k][0, j]
            half[1, k] = from_core[k, j]


def join_kernel(*refs):
    parts, out = refs[:-1], refs[-1]
    start = 0
    for part in parts:
        out[start : start + part.shape[0]] = part[...]
        start += part.shape[0]


def join(parts, flops=0):
    rows = sum(x.shape[0] for x in parts)
    return call(join_kernel, jax.ShapeDtypeStruct((rows,) + parts[0].shape[1:], parts[0].dtype), *parts, flops=flops)


def guard_kernel(*refs):
    refs[-1][...] = jnp.zeros_like(refs[-1])


def guard(parts, flops):
    return call(guard_kernel, jax.ShapeDtypeStruct((SUBLANES, LANES), jnp.float32), *parts, flops=flops)


def lead_kernel(out):
    out[...] = jnp.zeros_like(out)


def seed_kernel(seed_class, seed_mask, base):
    width, classes = base.shape
    kind = jnp.where(seed_mask[...] == 1, seed_class[...], -1)
    kind = jnp.transpose(jnp.broadcast_to(kind, (width, width)))
    for start in range(0, classes, width):
        slots = lax.broadcasted_iota(jnp.int32, (width, width), 1) + start
        base[:, start : start + width] = jnp.where(kind == slots, 1.0 - CARRY, 0.0)


def spread_kernel(order, y_count, first, *refs):
    z_count = len(order)
    sent, refs = refs[:z_count], refs[z_count:]
    strips = dict(zip([0] + far_first(z_count), sent[:1] + refs))
    refs = refs[z_count - 1 :]
    from_core, halves, refs = refs[0], refs[1:y_count], refs[y_count:]
    (ours, theirs), outs = refs[:2], refs[-y_count:]
    values = jnp.concatenate([ours[...], theirs[...]], axis=0)
    depth, classes = values.shape
    width = depth // (2 * z_count)
    ones = jnp.ones((SUBLANES, depth), jnp.bfloat16)

    def product(left, right, contract):
        return lax.dot_general(left, right, ((contract[:1], contract[1:]), ((), ())), preferred_element_type=jnp.float32)

    def back_block(i, j, k):
        if j > 0:
            return halves[j - 1][i, k]
        return sent[k][0, 0] if i == 0 else from_core[k, 0]

    for j, out in reversed(list(enumerate(outs))):
        back = jnp.concatenate([back_block(i, j, k) for i in range(2) for k in order], axis=0)
        ahead = jnp.concatenate([strips[k][i, j] for i in range(2) for k in order], axis=1)
        total = product(back, values, (0, 0)) + product(ahead, values, (1, 0))
        out[:width, :] = total.astype(out.dtype)
        if first:
            sums = product(ones, back, (1, 0)) + product(ones, ahead, (1, 1))
            sums = jnp.concatenate([sums] * (classes // width), axis=1)
            if j > 0:
                sums = jnp.concatenate([sums] * 2, axis=0)
                high = sums.astype(jnp.bfloat16).astype(jnp.float32)
                middle = (sums - high).astype(jnp.bfloat16).astype(jnp.float32)
                row = lax.broadcasted_iota(jnp.int32, sums.shape, 0)
                sums = jnp.where(row == 0, high, jnp.where(row == 1, middle, sums - high - middle))
            out[width:, :] = sums.astype(out.dtype)


def on_device(affinity, block_live, labels, seed_class, seed_mask):
    stripe, sides, width = affinity.shape
    count = lax.axis_size("row")
    z_count, y_count = split_rows(count)
    classes = labels.shape[1]

    strip = jax.ShapeDtypeStruct((2, y_count, width, width), jnp.bfloat16)
    half = jax.ShapeDtypeStruct((2, z_count, width, width), jnp.bfloat16)
    *sent, other = call(
        lambda *refs: prepare_kernel(z_count, y_count, *refs),
        [strip] * z_count + [jax.ShapeDtypeStruct((z_count, y_count, width, width), jnp.bfloat16)],
        block_live.transpose(1, 2, 0),
        affinity.reshape(stripe * sides, width),
        call(lead_kernel, jax.ShapeDtypeStruct((SUBLANES, width), jnp.float32), flops=LEAD_FLOPS),
        smem=1,
    )
    from_core = swap_cores(other)
    halves = call(lambda *refs: halves_kernel(z_count, *refs), [half] * (y_count - 1), *sent, from_core)
    halves = [swap_rows(x, j + 1) for j, x in enumerate(halves)]
    arrived = {k: swap_rows(sent[k], k * y_count) for k in far_first(z_count)}
    strips = [arrived[k] for k in far_first(z_count)]
    mark = guard([guard(strips, STRIPS_FLOPS)] + halves, MARK_FLOPS)
    have, order, bit = [labels], [0], z_count // 2
    while bit:
        whole = have[0] if len(have) == 1 else join(have, PAIR_FLOPS)
        have = [whole, swap_rows(whole, bit * y_count)]
        order = order + [k ^ bit for k in order]
        bit //= 2
    base = call(
        seed_kernel,
        jax.ShapeDtypeStruct((width, classes), jnp.float32),
        seed_class.reshape(1, width),
        seed_mask.reshape(1, width),
    )

    current, degree = labels, None
    for step in range(ITERS):
        if step > 0:
            order = [0] + far_first(z_count)
            have = [current] + [swap_rows(current, k * y_count) for k in order[1:]]
        values = join(have)
        pieces = [values, swap_cores(values)] + ([mark] if step == 0 else [])
        extra = SUBLANES if step == 0 else 0
        total, *sends = call(
            lambda *refs: spread_kernel(order, y_count, step == 0, *refs),
            [jax.ShapeDtypeStruct((width + extra, classes), jnp.float32)]
            + [jax.ShapeDtypeStruct((width + 2 * extra, classes), jnp.bfloat16)] * (y_count - 1),
            *sent,
            *strips,
            from_core,
            *halves,
            *pieces,
            flops=2 * 2 * 2 * y_count * z_count * width * width * classes,
        )
        sends = [swap_rows(x, j + 1).astype(jnp.float32) for j, x in enumerate(sends)]
        spread = sum((x[:width] for x in sends), total[:width])
        if step == 0:
            sums = sum((x[width : width + 3, :width].sum(axis=0) for x in sends), total[width, :width])
            degree = 1.0 + 0.5 * sums[:, None]
        mixed = CARRY * (0.5 * spread + current.astype(jnp.float32)) / degree
        current = (mixed + base).astype(jnp.bfloat16)
    return current


def solution(mesh):
    return jax.shard_map(
        on_device,
        mesh=mesh,
        in_specs=(
            P(("groups", "col"), None, "row"),
            P(("groups", "col"), None, "row"),
            P(("groups", "col", "row"), None),
            P(("groups", "col", "row")),
            P(("groups", "col", "row")),
        ),
        out_specs=P(("groups", "col", "row"), None),
        check_vma=False,
    )
```

time: 52.5 us -> 43.8 us (0.83)
  waiting for transfers between devices: 27.9 us -> 19.5 us
  local copies, waits for them, and re-layouts: 2.39 us -> 1.35 us
  starting transfers between devices: 18.6 us -> 19.5 us
    ppermute x12 -> x11, waiting for transfers between devices: 24.9 us -> 16.5 us  [swap_rows(): return lax.ppermute(value, 'row', [(i, i ^ shift) for i in range(count)])]
    unnamed x10, local copies, waits for them, and re-layouts: 2.39 us -> 1.35 us
    ppermute x12 -> x11, starting transfers between devices: 18.4 us -> 19.3 us  [swap_rows(): return lax.ppermute(value, 'row', [(i, i ^ shift) for i in range(count)])]
    ppermute x4 -> x3, waiting for transfers between devices: 3.07 us -> 3.03 us  [swap_cores(): return lax.ppermute(value, 'col', [(0, 1), (1, 0)])]
    pallas_call x6 -> x11, Pallas kernels: 2.26 us -> 2.26 us  [call(): pl.pallas_call(kernel, out_shape=out_shape, in_specs=[pl.BlockSpec(memory...]
  transfers between devices with their start and end apart: 16 -> 14, of which waited for: 8 -> 9; matrix products, arithmetic and copies ran while one was open for 0% -> 0% of each run, Pallas kernels for 2% -> 3%
where the time goes in v10:
time: 43.8 us; the launch traced here: 43.6 us
  starting transfers between devices  19.5 us (45%)
  waiting for transfers between devices  19.5 us (45%)
  Pallas kernels  2.26 us (5%)
  local copies, waits for them, and re-layouts  1.35 us (3%)
  other arithmetic  0.86 us (2%)
    ppermute x11, starting transfers between devices, swap_rows(): return lax.ppermute(value, 'row', [(i, i ^ shift) for i in range(count)])  19.3 us
    ppermute x11, waiting for transfers between devices, swap_rows(): return lax.ppermute(value, 'row', [(i, i ^ shift) for i in range(count)])  16.5 us
    ppermute x3, waiting for transfers between devices, swap_cores(): return lax.ppermute(value, 'col', [(0, 1), (1, 0)])  3.03 us
    pallas_call x11, Pallas kernels, call(): pl.pallas_call(kernel, out_shape=out_shape, in_specs=[pl.BlockSpec(memory...  2.26 us
    unnamed x10, local copies, waits for them, and re-layouts  1.35 us
  transfers between devices with their start and end apart: 14, of which 9 were waited for; matrix products, arithmetic and copies ran while one was open for 0% of the time, Pallas kernels for 3%

profile of v10, /device:TPU:0, one launch (start us, length us, event | category | flops | bytes accessed | tf_op | source)
XLA Modules:
  0.0 43.6 jit_solution(4665893577975411035)
XLA Ops:
  0.0 0.0 copy-start
  0.0 4.0 %collective-permute-start.5 = (bf16[128,256]{1,0:T(8,128)(2,1)}, bf16[128,256]{1,0:T(8,128)(2,1)S(1)}, u32[]{:S(2)}, u32[]{:S(2)}) collective-permute-start(bf16[128,256]{1,0:T(8,128)(2,1)} %refs_0_.1), channel_id=1, source_target_pairs={{0,8},{2,10},{4,12},{6,14},{8,0},{10,2},{12,4},{14,6},{1,9},{3,11}... | collective-permute-start | bytes 196616 | tf_op jit(solution)/shard_map/ppermute | solution.py:26
  4.0 0.0 copy-start.2
  4.0 0.0 copy-done
  4.0 0.7 %copy-done.2 = s32[8,2,1]{0,2,1:T(1,128)S(1)} copy-done((s32[8,2,1]{0,2,1:T(1,128)S(1)}, s32[8,2,1]{0,2,1:T(1,128)}, u32[]{:S(2)}) %copy-start.2) | copy-done | bytes 88
  4.7 0.0 copy-start.1
  4.7 1.0 %shard_map.56 = (bf16[2,2,128,128]{3,2,1,0:T(8,128)(2,1)S(1)}, bf16[2,2,128,128]{3,2,1,0:T(8,128)(2,1)S(1)}, bf16[2,2,128,128]{3,2,1,0:T(8,128)(2,1)S(1)}, bf16[...) custom-call(s32[2,1,8]{2,1,0:T(1,128)S(1)} %bitcast.11, bf16[2048,128]{1,0:T(8,128)(2,1)S(1)} %bitcast.10, ...), custom_call_target="tpu_custom_call" | custom-call | bytes 1314880 | tf_op jit(solution)/shard_map/pallas_call | solution.py:36
  5.7 0.1 collective-permute-start.3
  5.8 0.4 collective-permute-start
  6.2 3.6 %collective-permute-start.1 = (bf16[2,2,128,128]{3,2,1,0:T(8,128)(2,1)S(1)}, bf16[2,2,128,128]{3,2,1,0:T(8,128)(2,1)S(1)}, u32[]{:S(2)}, u32[]{:S(2)}) collective-permute-start(bf16[2,2,128,128]{3,2,1,0:T(8,128)(2,1)S(1)} %get-tuple-element.17.refs_3_), channel_id=1, source_target_pairs={{0,12},{2,14},{4,8},{6,10},{8,4},{10,6},{12,0},{14,2},{1,13},{3,15... | collective-permute-start | bytes 393224 | tf_op jit(solution)/shard_map/ppermute | solution.py:26
  9.8 0.0 collective-permute-start.2
  9.8 0.0 collective-permute-done.5.refs_1_
  9.8 0.0 copy-done.1
  9.8 2.1 %collective-permute-start.6 = (bf16[256,256]{1,0:T(8,128)(2,1)S(1)}, bf16[256,256]{1,0:T(8,128)(2,1)S(1)}, u32[]{:S(2)}, u32[]{:S(2)}) collective-permute-start(bf16[256,256]{1,0:T(8,128)(2,1)S(1)} %shard_map.58.refs_0_), channel_id=1, source_target_pairs={{0,4},{2,6},{4,0},{6,2},{8,12},{10,14},{12,8},{14,10},{1,5},{3,7},... | collective-permute-start | bytes 393224 | tf_op jit(solution)/shard_map/ppermute | solution.py:26
  11.9 0.0 collective-permute-done.3.refs_4_.refs_7_
  11.9 1.6 %collective-permute-start.4 = (bf16[2,4,128,128]{3,2,1,0:T(8,128)(2,1)S(1)}, bf16[2,4,128,128]{3,2,1,0:T(8,128)(2,1)S(1)}, u32[]{:S(2)}, u32[]{:S(2)}) collective-permute-start(bf16[2,4,128,128]{3,2,1,0:T(8,128)(2,1)S(1)} %shard_map.57), channel_id=1, source_target_pairs={{0,2},{2,0},{4,6},{6,4},{8,10},{10,8},{12,14},{14,12},{1,3},{3,1},... | collective-permute-start | bytes 786440 | tf_op jit(solution)/shard_map/ppermute | solution.py:26
  13.5 5.2 %collective-permute-done.refs_0_.refs_4_ = bf16[2,2,128,128]{3,2,1,0:T(8,128)(2,1)S(1)} collective-permute-done((bf16[2,2,128,128]{3,2,1,0:T(8,128)(2,1)S(1)}, bf16[2,2,128,128]{3,2,1,0:T(8,128)(2,1)S(1)}, u32[]{:S(2)}, u32[]{:S(2)}) %collective-permute-start) | collective-permute-done | bytes 131104 | tf_op jit(solution)/shard_map/ppermute | solution.py:26
  18.7 0.0 collective-permute-done.1.refs_1_.refs_5_
  18.7 1.9 %collective-permute-done.2.refs_2_.refs_6_ = bf16[2,2,128,128]{3,2,1,0:T(8,128)(2,1)S(1)} collective-permute-done((bf16[2,2,128,128]{3,2,1,0:T(8,128)(2,1)S(1)}, bf16[2,2,128,128]{3,2,1,0:T(8,128)(2,1)S(1)}, u32[]{:S(2)}, u32[]{:S(2)}) %collective-permute-start.2) | collective-permute-done | bytes 131104 | tf_op jit(solution)/shard_map/ppermute | solution.py:26
  20.6 1.8 %collective-permute-done.6.refs_1_ = bf16[256,256]{1,0:T(8,128)(2,1)S(1)} collective-permute-done((bf16[256,256]{1,0:T(8,128)(2,1)S(1)}, bf16[256,256]{1,0:T(8,128)(2,1)S(1)}, u32[]{:S(2)}, u32[]{:S(2)}) %collective-permute-start.6) | collective-permute-done | bytes 131104 | tf_op jit(solution)/shard_map/ppermute | solution.py:26
  22.4 0.1 collective-permute-start.7
  22.5 0.0 collective-permute-done.4.refs_1_.refs_8_
  22.5 1.5 %collective-permute-done.7.refs_10_ = bf16[512,256]{1,0:T(8,128)(2,1)S(1)} collective-permute-done((bf16[512,256]{1,0:T(8,128)(2,1)S(1)}, bf16[512,256]{1,0:T(8,128)(2,1)S(1)}, u32[]{:S(2)}, u32[]{:S(2)}) %collective-permute-start.7) | collective-permute-done | bytes 262176 | tf_op jit(solution)/shard_map/ppermute | solution.py:30
  24.0 0.6 %shard_map.62 = (f32[136,256]{1,0:T(8,128)S(1)}, bf16[144,256]{1,0:T(8,128)(2,1)S(1)}) custom-call(bf16[2,2,128,128]{3,2,1,0:T(8,128)(2,1)S(1)} %get-tuple-element.14.refs_0_, bf16[2,2,128,128]{3,2,1,0:T(8,128)(2,1)S(1)} %get-tuple-element.15.refs_1_, bf16[2,2,128,128]{3,2,1,0:T(8,128)(2,1)S(1)} %get-tuple-element.16.refs_2_, ...), custom_call_target="tpu_custom_call" | custom-call | flops 268435456 | bytes 2183168 | tf_op jit(solution)/shard_map/pallas_call | solution.py:36
  24.7 1.6 %collective-permute-start.8 = (bf16[144,256]{1,0:T(8,128)(2,1)S(1)}, bf16[144,256]{1,0:T(8,128)(2,1)S(1)}, u32[]{:S(2)}, u32[]{:S(2)}) collective-permute-start(bf16[144,256]{1,0:T(8,128)(2,1)S(1)} %get-tuple-element.20), channel_id=1, source_target_pairs={{0,2},{2,0},{4,6},{6,4},{8,10},{10,8},{12,14},{14,12},{1,3},{3,1},... | collective-permute-start | bytes 221192 | tf_op jit(solution)/shard_map/ppermute | solution.py:26
  26.3 0.0 copy-start.3
  26.3 0.0 copy-start.4
  26.3 0.7 %copy-done.3 = s32[128]{0:T(128)S(1)} copy-done((s32[128]{0:T(128)S(1)}, s32[128]{0:T(128)}, u32[]{:S(2)}) %copy-start.3) | copy-done | bytes 536
  26.9 0.0 copy-done.4
  26.9 0.1 shard_map.63
  27.0 2.1 %collective-permute-done.8 = bf16[144,256]{1,0:T(8,128)(2,1)S(1)} collective-permute-done((bf16[144,256]{1,0:T(8,128)(2,1)S(1)}, bf16[144,256]{1,0:T(8,128)(2,1)S(1)}, u32[]{:S(2)}, u32[]{:S(2)}) %collective-permute-start.8) | collective-permute-done | bytes 73760 | tf_op jit(solution)/shard_map/ppermute | solution.py:26
  29.1 0.1 fusion.5.refs_0_
  29.2 1.6 %collective-permute-start.10 = (bf16[128,256]{1,0:T(8,128)(2,1)S(1)}, bf16[128,256]{1,0:T(8,128)(2,1)S(1)}, u32[]{:S(2)}, u32[]{:S(2)}) collective-permute-start(bf16[128,256]{1,0:T(8,128)(2,1)S(1)} %fusion.5.refs_0_), channel_id=1, source_target_pairs={{0,12},{2,14},{4,8},{6,10},{8,4},{10,6},{12,0},{14,2},{1,13},{3,15... | collective-permute-start | bytes 196616 | tf_op jit(solution)/shard_map/ppermute | solution.py:26
  30.8 0.0 collective-permute-start.11
  30.8 2.9 %collective-permute-start.9 = (bf16[128,256]{1,0:T(8,128)(2,1)S(1)}, bf16[128,256]{1,0:T(8,128)(2,1)S(1)}, u32[]{:S(2)}, u32[]{:S(2)}) collective-permute-start(bf16[128,256]{1,0:T(8,128)(2,1)S(1)} %fusion.5.refs_0_), channel_id=1, source_target_pairs={{0,8},{2,10},{4,12},{6,14},{8,0},{10,2},{12,4},{14,6},{1,9},{3,11}... | collective-permute-start | bytes 196616 | tf_op jit(solution)/shard_map/ppermute | solution.py:26
  33.7 2.0 %collective-permute-done.10.refs_2_ = bf16[128,256]{1,0:T(8,128)(2,1)S(1)} collective-permute-done((bf16[128,256]{1,0:T(8,128)(2,1)S(1)}, bf16[128,256]{1,0:T(8,128)(2,1)S(1)}, u32[]{:S(2)}, u32[]{:S(2)}) %collective-permute-start.10) | collective-permute-done | bytes 65568 | tf_op jit(solution)/shard_map/ppermute | solution.py:26
  35.7 0.8 %collective-permute-done.11.refs_3_ = bf16[128,256]{1,0:T(8,128)(2,1)S(1)} collective-permute-done((bf16[128,256]{1,0:T(8,128)(2,1)S(1)}, bf16[128,256]{1,0:T(8,128)(2,1)S(1)}, u32[]{:S(2)}, u32[]{:S(2)}) %collective-permute-start.11) | collective-permute-done | bytes 65568 | tf_op jit(solution)/shard_map/ppermute | solution.py:26
  36.5 0.0 collective-permute-done.9.refs_1_
  36.5 0.1 collective-permute-start.12
  36.6 1.5 %collective-permute-done.12.refs_10_ = bf16[512,256]{1,0:T(8,128)(2,1)S(1)} collective-permute-done((bf16[512,256]{1,0:T(8,128)(2,1)S(1)}, bf16[512,256]{1,0:T(8,128)(2,1)S(1)}, u32[]{:S(2)}, u32[]{:S(2)}) %collective-permute-start.12) | collective-permute-done | bytes 262176 | tf_op jit(solution)/shard_map/ppermute | solution.py:30
  38.1 0.5 %shard_map.65 = (f32[128,256]{1,0:T(8,128)S(1)}, bf16[128,256]{1,0:T(8,128)(2,1)S(1)}) custom-call(bf16[2,2,128,128]{3,2,1,0:T(8,128)(2,1)S(1)} %get-tuple-element.14.refs_0_, bf16[2,2,128,128]{3,2,1,0:T(8,128)(2,1)S(1)} %get-tuple-element.15.refs_1_, bf16[2,2,128,128]{3,2,1,0:T(8,128)(2,1)S(1)} %get-tuple-element.16.refs_2_, ...), custom_call_target="tpu_custom_call" | custom-call | flops 268435456 | bytes 2162688 | tf_op jit(solution)/shard_map/pallas_call | solution.py:36
  38.6 1.6 %collective-permute-start.13 = (bf16[128,256]{1,0:T(8,128)(2,1)S(1)}, bf16[128,256]{1,0:T(8,128)(2,1)S(1)}, u32[]{:S(2)}, u32[]{:S(2)}) collective-permute-start(bf16[128,256]{1,0:T(8,128)(2,1)S(1)} %get-tuple-element.22), channel_id=1, source_target_pairs={{0,2},{2,0},{4,6},{6,4},{8,10},{10,8},{12,14},{14,12},{1,3},{3,1},... | collective-permute-start | bytes 196616 | tf_op jit(solution)/shard_map/ppermute | solution.py:26
  40.2 2.7 %collective-permute-done.13 = bf16[128,256]{1,0:T(8,128)(2,1)S(1)} collective-permute-done((bf16[128,256]{1,0:T(8,128)(2,1)S(1)}, bf16[128,256]{1,0:T(8,128)(2,1)S(1)}, u32[]{:S(2)}, u32[]{:S(2)}) %collective-permute-start.13) | collective-permute-done | bytes 65568 | tf_op jit(solution)/shard_map/ppermute | solution.py:26
  42.9 0.7 %add_convert_fusion = bf16[128,256]{1,0:T(8,128)(2,1)} fusion(f32[128,256]{1,0:T(8,128)S(1)} %shard_map.63, bf16[128,256]{1,0:T(8,128)(2,1)S(1)} %fusion.5.refs_0_, f32[128,256]{1,0:T(8,128)S(1)} %get-tuple-element.21, bf16[128,256]{1,0:T(8,128)(2,1)S(1)} %collective-permute-done.13, f32[128]{0:T(128)S(1)} %fusion.7), kind=kLoop, calls=%fused_computation.6 | loop fusion | flops 294912 | bytes 459264 | tf_op jit(solution)/shard_map/convert_element_type | solution.py:214
  (10 shorter events, 0.1 us)
Async XLA Ops:
  0.0 4.0 %copy-start = (bf16[1024,2,128]{2,1,0:T(2,128)(2,1)S(1)}, bf16[1024,2,128]{2,1,0:T(2,128)(2,1)}, u32[]{:S(2)}) copy-start(bf16[1024,2,128]{2,1,0:T(2,128)(2,1)} %param.5) | copy-start | bytes 1572868
  0.0 9.8 %collective-permute-start.5 = (bf16[128,256]{1,0:T(8,128)(2,1)}, bf16[128,256]{1,0:T(8,128)(2,1)S(1)}, u32[]{:S(2)}, u32[]{:S(2)}) collective-permute-start(bf16[128,256]{1,0:T(8,128)(2,1)} %refs_0_.1), channel_id=1, source_target_pairs={{0,8},{2,10},{4,12},{6,14},{8,0},{10,2},{12,4},{14,6},{1,9},{3,11}... | collective-permute-start | bytes 196616 | tf_op jit(solution)/shard_map/ppermute | solution.py:26
  4.0 0.7 %copy-start.2 = (s32[8,2,1]{0,2,1:T(1,128)S(1)}, s32[8,2,1]{0,2,1:T(1,128)}, u32[]{:S(2)}) copy-start(s32[8,2,1]{0,2,1:T(1,128)} %param.6) | copy-start | bytes 196
  4.7 5.1 %copy-start.1 = (bf16[128,256]{1,0:T(8,128)(2,1)S(1)}, bf16[128,256]{1,0:T(8,128)(2,1)}, u32[]{:S(2)}) copy-start(bf16[128,256]{1,0:T(8,128)(2,1)} %refs_0_.1) | copy-start | bytes 196612
  5.7 6.2 %collective-permute-start.3 = (bf16[4,2,128,128]{3,2,1,0:T(8,128)(2,1)S(1)}, bf16[4,2,128,128]{3,2,1,0:T(8,128)(2,1)S(1)}, u32[]{:S(2)}, u32[]{:S(2)}) collective-permute-start(bf16[4,2,128,128]{3,2,1,0:T(8,128)(2,1)S(1)} %get-tuple-element.18), channel_id=1, source_target_pairs={{0,1},{1,0},{2,3},{3,2},{4,5},{5,4},{6,7},{7,6},{8,9},{9,8},{10,11... | collective-permute-start | bytes 786440 | tf_op jit(solution)/shard_map/ppermute | solution.py:30
  5.8 12.9 %collective-permute-start = (bf16[2,2,128,128]{3,2,1,0:T(8,128)(2,1)S(1)}, bf16[2,2,128,128]{3,2,1,0:T(8,128)(2,1)S(1)}, u32[]{:S(2)}, u32[]{:S(2)}) collective-permute-start(bf16[2,2,128,128]{3,2,1,0:T(8,128)(2,1)S(1)} %get-tuple-element.16.refs_2_), channel_id=1, source_target_pairs={{0,8},{2,10},{4,12},{6,14},{8,0},{10,2},{12,4},{14,6},{1,9},{3,11}... | collective-permute-start | bytes 393224 | tf_op jit(solution)/shard_map/ppermute | solution.py:26
  6.2 12.5 %collective-permute-start.1 = (bf16[2,2,128,128]{3,2,1,0:T(8,128)(2,1)S(1)}, bf16[2,2,128,128]{3,2,1,0:T(8,128)(2,1)S(1)}, u32[]{:S(2)}, u32[]{:S(2)}) collective-permute-start(bf16[2,2,128,128]{3,2,1,0:T(8,128)(2,1)S(1)} %get-tuple-element.17.refs_3_), channel_id=1, source_target_pairs={{0,12},{2,14},{4,8},{6,10},{8,4},{10,6},{12,0},{14,2},{1,13},{3,15... | collective-permute-start | bytes 393224 | tf_op jit(solution)/shard_map/ppermute | solution.py:26
  9.8 10.8 %collective-permute-start.2 = (bf16[2,2,128,128]{3,2,1,0:T(8,128)(2,1)S(1)}, bf16[2,2,128,128]{3,2,1,0:T(8,128)(2,1)S(1)}, u32[]{:S(2)}, u32[]{:S(2)}) collective-permute-start(bf16[2,2,128,128]{3,2,1,0:T(8,128)(2,1)S(1)} %get-tuple-element.15.refs_1_), channel_id=1, source_target_pairs={{0,4},{2,6},{4,0},{6,2},{8,12},{10,14},{12,8},{14,10},{1,5},{3,7},... | collective-permute-start | bytes 393224 | tf_op jit(solution)/shard_map/ppermute | solution.py:26
  9.8 12.6 %collective-permute-start.6 = (bf16[256,256]{1,0:T(8,128)(2,1)S(1)}, bf16[256,256]{1,0:T(8,128)(2,1)S(1)}, u32[]{:S(2)}, u32[]{:S(2)}) collective-permute-start(bf16[256,256]{1,0:T(8,128)(2,1)S(1)} %shard_map.58.refs_0_), channel_id=1, source_target_pairs={{0,4},{2,6},{4,0},{6,2},{8,12},{10,14},{12,8},{14,10},{1,5},{3,7},... | collective-permute-start | bytes 393224 | tf_op jit(solution)/shard_map/ppermute | solution.py:26
  11.9 10.6 %collective-permute-start.4 = (bf16[2,4,128,128]{3,2,1,0:T(8,128)(2,1)S(1)}, bf16[2,4,128,128]{3,2,1,0:T(8,128)(2,1)S(1)}, u32[]{:S(2)}, u32[]{:S(2)}) collective-permute-start(bf16[2,4,128,128]{3,2,1,0:T(8,128)(2,1)S(1)} %shard_map.57), channel_id=1, source_target_pairs={{0,2},{2,0},{4,6},{6,4},{8,10},{10,8},{12,14},{14,12},{1,3},{3,1},... | collective-permute-start | bytes 786440 | tf_op jit(solution)/shard_map/ppermute | solution.py:26
  22.4 1.6 %collective-permute-start.7 = (bf16[512,256]{1,0:T(8,128)(2,1)S(1)}, bf16[512,256]{1,0:T(8,128)(2,1)S(1)}, u32[]{:S(2)}, u32[]{:S(2)}) collective-permute-start(bf16[512,256]{1,0:T(8,128)(2,1)S(1)} %shard_map.59.refs_9_), channel_id=1, source_target_pairs={{0,1},{1,0},{2,3},{3,2},{4,5},{5,4},{6,7},{7,6},{8,9},{9,8},{10,11... | collective-permute-start | bytes 786440 | tf_op jit(solution)/shard_map/ppermute | solution.py:30
  24.7 4.4 %collective-permute-start.8 = (bf16[144,256]{1,0:T(8,128)(2,1)S(1)}, bf16[144,256]{1,0:T(8,128)(2,1)S(1)}, u32[]{:S(2)}, u32[]{:S(2)}) collective-permute-start(bf16[144,256]{1,0:T(8,128)(2,1)S(1)} %get-tuple-element.20), channel_id=1, source_target_pairs={{0,2},{2,0},{4,6},{6,4},{8,10},{10,8},{12,14},{14,12},{1,3},{3,1},... | collective-permute-start | bytes 221192 | tf_op jit(solution)/shard_map/ppermute | solution.py:26
  26.3 0.7 %copy-start.3 = (s32[128]{0:T(128)S(1)}, s32[128]{0:T(128)}, u32[]{:S(2)}) copy-start(s32[128]{0:T(128)} %param.8) | copy-start | bytes 1540
  26.3 0.7 %copy-start.4 = (s32[128]{0:T(128)S(1)}, s32[128]{0:T(128)}, u32[]{:S(2)}) copy-start(s32[128]{0:T(128)} %param.9) | copy-start | bytes 1540
  29.2 6.5 %collective-permute-start.10 = (bf16[128,256]{1,0:T(8,128)(2,1)S(1)}, bf16[128,256]{1,0:T(8,128)(2,1)S(1)}, u32[]{:S(2)}, u32[]{:S(2)}) collective-permute-start(bf16[128,256]{1,0:T(8,128)(2,1)S(1)} %fusion.5.refs_0_), channel_id=1, source_target_pairs={{0,12},{2,14},{4,8},{6,10},{8,4},{10,6},{12,0},{14,2},{1,13},{3,15... | collective-permute-start | bytes 196616 | tf_op jit(solution)/shard_map/ppermute | solution.py:26
  30.8 5.7 %collective-permute-start.11 = (bf16[128,256]{1,0:T(8,128)(2,1)S(1)}, bf16[128,256]{1,0:T(8,128)(2,1)S(1)}, u32[]{:S(2)}, u32[]{:S(2)}) collective-permute-start(bf16[128,256]{1,0:T(8,128)(2,1)S(1)} %fusion.5.refs_0_), channel_id=1, source_target_pairs={{0,4},{2,6},{4,0},{6,2},{8,12},{10,14},{12,8},{14,10},{1,5},{3,7},... | collective-permute-start | bytes 196616 | tf_op jit(solution)/shard_map/ppermute | solution.py:26
  30.8 5.7 %collective-permute-start.9 = (bf16[128,256]{1,0:T(8,128)(2,1)S(1)}, bf16[128,256]{1,0:T(8,128)(2,1)S(1)}, u32[]{:S(2)}, u32[]{:S(2)}) collective-permute-start(bf16[128,256]{1,0:T(8,128)(2,1)S(1)} %fusion.5.refs_0_), channel_id=1, source_target_pairs={{0,8},{2,10},{4,12},{6,14},{8,0},{10,2},{12,4},{14,6},{1,9},{3,11}... | collective-permute-start | bytes 196616 | tf_op jit(solution)/shard_map/ppermute | solution.py:26
  36.5 1.6 %collective-permute-start.12 = (bf16[512,256]{1,0:T(8,128)(2,1)S(1)}, bf16[512,256]{1,0:T(8,128)(2,1)S(1)}, u32[]{:S(2)}, u32[]{:S(2)}) collective-permute-start(bf16[512,256]{1,0:T(8,128)(2,1)S(1)} %shard_map.64.refs_9_), channel_id=1, source_target_pairs={{0,1},{1,0},{2,3},{3,2},{4,5},{5,4},{6,7},{7,6},{8,9},{9,8},{10,11... | collective-permute-start | bytes 786440 | tf_op jit(solution)/shard_map/ppermute | solution.py:30
  38.6 4.3 %collective-permute-start.13 = (bf16[128,256]{1,0:T(8,128)(2,1)S(1)}, bf16[128,256]{1,0:T(8,128)(2,1)S(1)}, u32[]{:S(2)}, u32[]{:S(2)}) collective-permute-start(bf16[128,256]{1,0:T(8,128)(2,1)S(1)} %get-tuple-element.22), channel_id=1, source_target_pairs={{0,2},{2,0},{4,6},{6,4},{8,10},{10,8},{12,14},{14,12},{1,3},{3,1},... | collective-permute-start | bytes 196616 | tf_op jit(solution)/shard_map/ppermute | solution.py:26

commit v11 on v10

--- a/solution.py
+++ b/solution.py
@@ -12,7 +12,7 @@
 LEAD_FLOPS = 2_000_000_000
 PAIR_FLOPS = 4_000_000_000
 STRIPS_FLOPS = 3_000_000_000
-MARK_FLOPS = 3_000_000_000
+OURS_FLOPS = 3_000_000_000
 MIB = 1024 * 1024
 
 
@@ -45,7 +45,7 @@
 
 def far_first(count):
     half = count // 2
-    return [k for k in range(half, count)] + [k for k in range(1, half)]
+    return [half] + [k for k in range(1, count) if k != half]
 
 
 def prepare_kernel(z_count, y_count, live, tile, lead, *outs):
@@ -114,34 +114,52 @@
         base[:, start : start + width] = jnp.where(kind == slots, 1.0 - CARRY, 0.0)
 
 
-def spread_kernel(order, y_count, first, *refs):
+def product(left, right, contract):
+    return lax.dot_general(left, right, ((contract[:1], contract[1:]), ((), ())), preferred_element_type=jnp.float32)
+
+
+def blocks_of(order, y_count, refs, i, j):
     z_count = len(order)
     sent, refs = refs[:z_count], refs[z_count:]
     strips = dict(zip([0] + far_first(z_count), sent[:1] + refs))
-    refs = refs[z_count - 1 :]
-    from_core, halves, refs = refs[0], refs[1:y_count], refs[y_count:]
-    (ours, theirs), outs = refs[:2], refs[-y_count:]
-    values = jnp.concatenate([ours[...], theirs[...]], axis=0)
-    depth, classes = values.shape
-    width = depth // (2 * z_count)
-    ones = jnp.ones((SUBLANES, depth), jnp.bfloat16)
-
-    def product(left, right, contract):
-        return lax.dot_general(left, right, ((contract[:1], contract[1:]), ((), ())), preferred_element_type=jnp.float32)
-
-    def back_block(i, j, k):
+    from_core, halves = refs[z_count - 1], refs[z_count:]
+
+    def back_block(k):
         if j > 0:
             return halves[j - 1][i, k]
         return sent[k][0, 0] if i == 0 else from_core[k, 0]
 
-    for j, out in reversed(list(enumerate(outs))):
-        back = jnp.concatenate([back_block(i, j, k) for i in range(2) for k in order], axis=0)
-        ahead = jnp.concatenate([strips[k][i, j] for i in range(2) for k in order], axis=1)
-        total = product(back, values, (0, 0)) + product(ahead, values, (1, 0))
+    back = jnp.concatenate([back_block(k) for k in order], axis=0)
+    return back, jnp.concatenate([strips[k][i, j] for k in order], axis=1)
+
+
+def ours_kernel(order, y_count, first, *refs):
+    blocks, values, outs = refs[: 2 * len(order) + y_count - 1], refs[2 * len(order) + y_count - 1], refs[-y_count:]
+    values = values[...]
+    depth, classes = values.shape
+    width = depth // len(order)
+    ones = jnp.ones((SUBLANES, depth), jnp.bfloat16)
+    for j, out in enumerate(outs):
+        back, ahead = blocks_of(order, y_count, blocks, 0, j)
+        out[:width, :] = product(back, values, (0, 0)) + product(ahead, values, (1, 0))
+        if first:
+            sums = product(ones, back, (1, 0)) + product(ones, ahead, (1, 1))
+            back, ahead = blocks_of(order, y_count, blocks, 1, j)
+            sums += product(ones, back, (1, 0)) + product(ones, ahead, (1, 1))
+            out[width:, :] = jnp.concatenate([sums] * (classes // width), axis=1)
+
+
+def theirs_kernel(order, y_count, first, *refs):
+    blocks, values, refs = refs[: 2 * len(order) + y_count - 1], refs[2 * len(order) + y_count - 1], refs[-2 * y_count :]
+    values = values[...]
+    width = values.shape[0] // len(order)
+    for j in reversed(range(y_count)):
+        part, out = refs[j], refs[y_count + j]
+        back, ahead = blocks_of(order, y_count, blocks, 1, j)
+        total = part[:width, :] + product(back, values, (0, 0)) + product(ahead, values, (1, 0))
         out[:width, :] = total.astype(out.dtype)
         if first:
-            sums = product(ones, back, (1, 0)) + product(ones, ahead, (1, 1))
-            sums = jnp.concatenate([sums] * (classes // width), axis=1)
+            sums = part[width:, :]
             if j > 0:
                 sums = jnp.concatenate([sums] * 2, axis=0)
                 high = sums.astype(jnp.bfloat16).astype(jnp.float32)
@@ -172,7 +190,9 @@
     halves = [swap_rows(x, j + 1) for j, x in enumerate(halves)]
     arrived = {k: swap_rows(sent[k], k * y_count) for k in far_first(z_count)}
     strips = [arrived[k] for k in far_first(z_count)]
-    mark = guard([guard(strips, STRIPS_FLOPS)] + halves, MARK_FLOPS)
+    strips = [arrived[k] for k in far_first(z_count)]
+    mark = guard(strips, STRIPS_FLOPS)
+    blocks = [*sent, *strips, from_core, *halves]
     have, order, bit = [labels], [0], z_count // 2
     while bit:
         whole = have[0] if len(have) == 1 else join(have, PAIR_FLOPS)
@@ -192,22 +212,28 @@
             order = [0] + far_first(z_count)
             have = [current] + [swap_rows(current, k * y_count) for k in order[1:]]
         values = join(have)
-        pieces = [values, swap_cores(values)] + ([mark] if step == 0 else [])
-        extra = SUBLANES if step == 0 else 0
+        first = step == 0
+        extra = SUBLANES if first else 0
+        part = jax.ShapeDtypeStruct((width + extra, classes), jnp.float32)
+        send = jax.ShapeDtypeStruct((width + 2 * extra, classes), jnp.bfloat16)
+        parts = call(
+            lambda *refs: ours_kernel(order, y_count, first, *refs),
+            [part] * y_count,
+            *blocks,
+            values,
+            *([mark] if first else []),
+            flops=OURS_FLOPS if first else 0,
+        )
         total, *sends = call(
-            lambda *refs: spread_kernel(order, y_count, step == 0, *refs),
-            [jax.ShapeDtypeStruct((width + extra, classes), jnp.float32)]
-            + [jax.ShapeDtypeStruct((width + 2 * extra, classes), jnp.bfloat16)] * (y_count - 1),
-            *sent,
-            *strips,
-            from_core,
-            *halves,
-            *pieces,
-            flops=2 * 2 * 2 * y_count * z_count * width * width * classes,
+            lambda *refs: theirs_kernel(order, y_count, first, *refs),
+            [part] + [send] * (y_count - 1),
+            *blocks,
+            swap_cores(values),
+            *parts,
         )
         sends = [swap_rows(x, j + 1).astype(jnp.float32) for j, x in enumerate(sends)]
         spread = sum((x[:width] for x in sends), total[:width])
-        if step == 0:
+        if first:
             sums = sum((x[width : width + 3, :width].sum(axis=0) for x in sends), total[width, :width])
             degree = 1.0 + 0.5 * sums[:, None]
         mixed = CARRY * (0.5 * spread + current.astype(jnp.float32)) / degree

time: 43.8 us -> 44.2 us (level)
    ppermute x11, waiting for transfers between devices: 16.5 us -> 17.6 us  [swap_rows(): return lax.ppermute(value, 'row', [(i, i ^ shift) for i in range(count)])]
    ppermute x3, waiting for transfers between devices: 3.03 us -> 2.18 us  [swap_cores(): return lax.ppermute(value, 'col', [(0, 1), (1, 0)])]
    pallas_call x11 -> x12, Pallas kernels: 2.26 us -> 2.66 us  [call(): pl.pallas_call(kernel, out_shape=out_shape, in_specs=[pl.BlockSpec(memory...]
  transfers between devices with their start and end apart: 14 -> 14, of which waited for: 9 -> 12; matrix products, arithmetic and copies ran while one was open for 0% -> 0% of each run, Pallas kernels for 3% -> 4%
where the time goes in v11:
time: 44.2 us; the launch traced here: 44 us
  waiting for transfers between devices  19.8 us (45%)
  starting transfers between devices  19.3 us (44%)
  Pallas kernels  2.66 us (6%)
  local copies, waits for them, and re-layouts  1.35 us (3%)
  other arithmetic  0.86 us (2%)
    ppermute x11, starting transfers between devices, swap_rows(): return lax.ppermute(value, 'row', [(i, i ^ shift) for i in range(count)])  19.1 us
    ppermute x11, waiting for transfers between devices, swap_rows(): return lax.ppermute(value, 'row', [(i, i ^ shift) for i in range(count)])  17.6 us
    pallas_call x12, Pallas kernels, call(): pl.pallas_call(kernel, out_shape=out_shape, in_specs=[pl.BlockSpec(memory...  2.66 us
    ppermute x3, waiting for transfers between devices, swap_cores(): return lax.ppermute(value, 'col', [(0, 1), (1, 0)])  2.18 us
    unnamed x10, local copies, waits for them, and re-layouts  1.35 us
  transfers between devices with their start and end apart: 14, of which 12 were waited for; matrix products, arithmetic and copies ran while one was open for 0% of the time, Pallas kernels for 4%

profile of v11, /device:TPU:0, one launch (start us, length us, event | category | flops | bytes accessed | tf_op | source)
XLA Modules:
  0.0 44.0 jit_solution(15786818183738640304)
XLA Ops:
  0.0 0.0 copy-start
  0.0 4.0 %collective-permute-start.5 = (bf16[128,256]{1,0:T(8,128)(2,1)}, bf16[128,256]{1,0:T(8,128)(2,1)S(1)}, u32[]{:S(2)}, u32[]{:S(2)}) collective-permute-start(bf16[128,256]{1,0:T(8,128)(2,1)} %refs_0_.1), channel_id=1, source_target_pairs={{0,8},{2,10},{4,12},{6,14},{8,0},{10,2},{12,4},{14,6},{1,9},{3,11}... | collective-permute-start | bytes 196616 | tf_op jit(solution)/shard_map/ppermute | solution.py:26
  4.0 0.0 copy-start.2
  4.0 0.0 copy-done
  4.0 0.7 %copy-done.2 = s32[8,2,1]{0,2,1:T(1,128)S(1)} copy-done((s32[8,2,1]{0,2,1:T(1,128)S(1)}, s32[8,2,1]{0,2,1:T(1,128)}, u32[]{:S(2)}) %copy-start.2) | copy-done | bytes 88
  4.7 0.0 copy-start.1
  4.7 1.0 %shard_map.56 = (bf16[2,2,128,128]{3,2,1,0:T(8,128)(2,1)S(1)}, bf16[2,2,128,128]{3,2,1,0:T(8,128)(2,1)S(1)}, bf16[2,2,128,128]{3,2,1,0:T(8,128)(2,1)S(1)}, bf16[...) custom-call(s32[2,1,8]{2,1,0:T(1,128)S(1)} %bitcast.11, bf16[2048,128]{1,0:T(8,128)(2,1)S(1)} %bitcast.10, ...), custom_call_target="tpu_custom_call" | custom-call | bytes 1314880 | tf_op jit(solution)/shard_map/pallas_call | solution.py:36
  5.7 0.4 collective-permute-start
  6.1 1.6 %collective-permute-start.1 = (bf16[2,2,128,128]{3,2,1,0:T(8,128)(2,1)S(1)}, bf16[2,2,128,128]{3,2,1,0:T(8,128)(2,1)S(1)}, u32[]{:S(2)}, u32[]{:S(2)}) collective-permute-start(bf16[2,2,128,128]{3,2,1,0:T(8,128)(2,1)S(1)} %get-tuple-element.19.refs_1_), channel_id=1, source_target_pairs={{0,4},{2,6},{4,0},{6,2},{8,12},{10,14},{12,8},{14,10},{1,5},{3,7},... | collective-permute-start | bytes 393224 | tf_op jit(solution)/shard_map/ppermute | solution.py:26
  7.7 2.4 %collective-permute-start.2 = (bf16[2,2,128,128]{3,2,1,0:T(8,128)(2,1)S(1)}, bf16[2,2,128,128]{3,2,1,0:T(8,128)(2,1)S(1)}, u32[]{:S(2)}, u32[]{:S(2)}) collective-permute-start(bf16[2,2,128,128]{3,2,1,0:T(8,128)(2,1)S(1)} %get-tuple-element.21.refs_3_), channel_id=1, source_target_pairs={{0,12},{2,14},{4,8},{6,10},{8,4},{10,6},{12,0},{14,2},{1,13},{3,15... | collective-permute-start | bytes 393224 | tf_op jit(solution)/shard_map/ppermute | solution.py:26
  10.2 0.0 collective-permute-start.3
  10.2 0.0 collective-permute-done.5.refs_1_
  10.2 0.0 copy-done.1
  10.2 1.4 %collective-permute-start.6 = (bf16[256,256]{1,0:T(8,128)(2,1)S(1)}, bf16[256,256]{1,0:T(8,128)(2,1)S(1)}, u32[]{:S(2)}, u32[]{:S(2)}) collective-permute-start(bf16[256,256]{1,0:T(8,128)(2,1)S(1)} %shard_map.58.refs_0_), channel_id=1, source_target_pairs={{0,4},{2,6},{4,0},{6,2},{8,12},{10,14},{12,8},{14,10},{1,5},{3,7},... | collective-permute-start | bytes 393224 | tf_op jit(solution)/shard_map/ppermute | solution.py:26
  11.6 0.1 collective-permute-done.3.refs_4_.refs_7_
  11.7 1.6 %collective-permute-start.4 = (bf16[2,4,128,128]{3,2,1,0:T(8,128)(2,1)S(1)}, bf16[2,4,128,128]{3,2,1,0:T(8,128)(2,1)S(1)}, u32[]{:S(2)}, u32[]{:S(2)}) collective-permute-start(bf16[2,4,128,128]{3,2,1,0:T(8,128)(2,1)S(1)} %shard_map.57), channel_id=1, source_target_pairs={{0,2},{2,0},{4,6},{6,4},{8,10},{10,8},{12,14},{14,12},{1,3},{3,1},... | collective-permute-start | bytes 786440 | tf_op jit(solution)/shard_map/ppermute | solution.py:26
  13.3 3.8 %collective-permute-done.refs_0_.refs_4_ = bf16[2,2,128,128]{3,2,1,0:T(8,128)(2,1)S(1)} collective-permute-done((bf16[2,2,128,128]{3,2,1,0:T(8,128)(2,1)S(1)}, bf16[2,2,128,128]{3,2,1,0:T(8,128)(2,1)S(1)}, u32[]{:S(2)}, u32[]{:S(2)}) %collective-permute-start) | collective-permute-done | bytes 131104 | tf_op jit(solution)/shard_map/ppermute | solution.py:26
  17.1 0.0 collective-permute-done.1.refs_1_.refs_5_
  17.1 2.6 %collective-permute-done.2.refs_2_.refs_6_ = bf16[2,2,128,128]{3,2,1,0:T(8,128)(2,1)S(1)} collective-permute-done((bf16[2,2,128,128]{3,2,1,0:T(8,128)(2,1)S(1)}, bf16[2,2,128,128]{3,2,1,0:T(8,128)(2,1)S(1)}, u32[]{:S(2)}, u32[]{:S(2)}) %collective-permute-start.2) | collective-permute-done | bytes 131104 | tf_op jit(solution)/shard_map/ppermute | solution.py:26
  19.7 0.2 collective-permute-done.6.refs_1_
  19.9 0.1 collective-permute-start.7
  20.0 0.1 collective-permute-done.4.refs_8_
  20.1 0.5 %shard_map.61 = (f32[136,256]{1,0:T(8,128)S(1)}, f32[136,256]{1,0:T(8,128)S(1)}) custom-call(bf16[2,2,128,128]{3,2,1,0:T(8,128)(2,1)S(1)} %get-tuple-element.18.refs_0_, bf16[2,2,128,128]{3,2,1,0:T(8,128)(2,1)S(1)} %get-tuple-element.19.refs_1_, bf16[2,2,128,128]{3,2,1,0:T(8,128)(2,1)S(1)} %get-tuple-element.20.refs_2_, ...), custom_call_target="tpu_custom_call" | custom-call | flops 3000000000 | bytes 1986560 | tf_op jit(solution)/shard_map/pallas_call | solution.py:36
  20.6 0.9 %collective-permute-done.7.refs_9_ = bf16[512,256]{1,0:T(8,128)(2,1)S(1)} collective-permute-done((bf16[512,256]{1,0:T(8,128)(2,1)S(1)}, bf16[512,256]{1,0:T(8,128)(2,1)S(1)}, u32[]{:S(2)}, u32[]{:S(2)}) %collective-permute-start.7) | collective-permute-done | bytes 262176 | tf_op jit(solution)/shard_map/ppermute | solution.py:30
  21.5 0.4 shard_map.62
  21.9 1.6 %collective-permute-start.8 = (bf16[144,256]{1,0:T(8,128)(2,1)S(1)}, bf16[144,256]{1,0:T(8,128)(2,1)S(1)}, u32[]{:S(2)}, u32[]{:S(2)}) collective-permute-start(bf16[144,256]{1,0:T(8,128)(2,1)S(1)} %get-tuple-element.26), channel_id=1, source_target_pairs={{0,2},{2,0},{4,6},{6,4},{8,10},{10,8},{12,14},{14,12},{1,3},{3,1},... | collective-permute-start | bytes 221192 | tf_op jit(solution)/shard_map/ppermute | solution.py:26
  23.5 0.0 copy-start.3
  23.5 0.0 copy-start.4
  23.5 0.7 %copy-done.3 = s32[128]{0:T(128)S(1)} copy-done((s32[128]{0:T(128)S(1)}, s32[128]{0:T(128)}, u32[]{:S(2)}) %copy-start.3) | copy-done | bytes 536
  24.1 0.0 copy-done.4
  24.1 0.1 shard_map.63
  24.3 2.0 %collective-permute-done.8 = bf16[144,256]{1,0:T(8,128)(2,1)S(1)} collective-permute-done((bf16[144,256]{1,0:T(8,128)(2,1)S(1)}, bf16[144,256]{1,0:T(8,128)(2,1)S(1)}, u32[]{:S(2)}, u32[]{:S(2)}) %collective-permute-start.8) | collective-permute-done | bytes 73760 | tf_op jit(solution)/shard_map/ppermute | solution.py:26
  26.3 0.1 fusion.5.refs_0_
  26.5 2.0 %collective-permute-start.9 = (bf16[128,256]{1,0:T(8,128)(2,1)S(1)}, bf16[128,256]{1,0:T(8,128)(2,1)S(1)}, u32[]{:S(2)}, u32[]{:S(2)}) collective-permute-start(bf16[128,256]{1,0:T(8,128)(2,1)S(1)} %fusion.5.refs_0_), channel_id=1, source_target_pairs={{0,8},{2,10},{4,12},{6,14},{8,0},{10,2},{12,4},{14,6},{1,9},{3,11}... | collective-permute-start | bytes 196616 | tf_op jit(solution)/shard_map/ppermute | solution.py:26
  28.4 2.5 %collective-permute-start.10 = (bf16[128,256]{1,0:T(8,128)(2,1)S(1)}, bf16[128,256]{1,0:T(8,128)(2,1)S(1)}, u32[]{:S(2)}, u32[]{:S(2)}) collective-permute-start(bf16[128,256]{1,0:T(8,128)(2,1)S(1)} %fusion.5.refs_0_), channel_id=1, source_target_pairs={{0,4},{2,6},{4,0},{6,2},{8,12},{10,14},{12,8},{14,10},{1,5},{3,7},... | collective-permute-start | bytes 196616 | tf_op jit(solution)/shard_map/ppermute | solution.py:26
  30.9 0.0 collective-permute-start.11
  30.9 0.9 %collective-permute-done.9.refs_1_ = bf16[128,256]{1,0:T(8,128)(2,1)S(1)} collective-permute-done((bf16[128,256]{1,0:T(8,128)(2,1)S(1)}, bf16[128,256]{1,0:T(8,128)(2,1)S(1)}, u32[]{:S(2)}, u32[]{:S(2)}) %collective-permute-start.9) | collective-permute-done | bytes 65568 | tf_op jit(solution)/shard_map/ppermute | solution.py:26
  31.8 1.4 %collective-permute-done.10.refs_2_ = bf16[128,256]{1,0:T(8,128)(2,1)S(1)} collective-permute-done((bf16[128,256]{1,0:T(8,128)(2,1)S(1)}, bf16[128,256]{1,0:T(8,128)(2,1)S(1)}, u32[]{:S(2)}, u32[]{:S(2)}) %collective-permute-start.10) | collective-permute-done | bytes 65568 | tf_op jit(solution)/shard_map/ppermute | solution.py:26
  33.1 3.8 %collective-permute-done.11.refs_3_ = bf16[128,256]{1,0:T(8,128)(2,1)S(1)} collective-permute-done((bf16[128,256]{1,0:T(8,128)(2,1)S(1)}, bf16[128,256]{1,0:T(8,128)(2,1)S(1)}, u32[]{:S(2)}, u32[]{:S(2)}) %collective-permute-start.11) | collective-permute-done | bytes 65568 | tf_op jit(solution)/shard_map/ppermute | solution.py:26
  37.0 0.1 collective-permute-start.12
  37.1 0.3 shard_map.65
  37.4 1.2 %collective-permute-done.12.refs_9_ = bf16[512,256]{1,0:T(8,128)(2,1)S(1)} collective-permute-done((bf16[512,256]{1,0:T(8,128)(2,1)S(1)}, bf16[512,256]{1,0:T(8,128)(2,1)S(1)}, u32[]{:S(2)}, u32[]{:S(2)}) %collective-permute-start.12) | collective-permute-done | bytes 262176 | tf_op jit(solution)/shard_map/ppermute | solution.py:30
  38.6 0.3 shard_map.66
  39.0 1.6 %collective-permute-start.13 = (bf16[128,256]{1,0:T(8,128)(2,1)S(1)}, bf16[128,256]{1,0:T(8,128)(2,1)S(1)}, u32[]{:S(2)}, u32[]{:S(2)}) collective-permute-start(bf16[128,256]{1,0:T(8,128)(2,1)S(1)} %get-tuple-element.30), channel_id=1, source_target_pairs={{0,2},{2,0},{4,6},{6,4},{8,10},{10,8},{12,14},{14,12},{1,3},{3,1},... | collective-permute-start | bytes 196616 | tf_op jit(solution)/shard_map/ppermute | solution.py:26
  40.5 2.7 %collective-permute-done.13 = bf16[128,256]{1,0:T(8,128)(2,1)S(1)} collective-permute-done((bf16[128,256]{1,0:T(8,128)(2,1)S(1)}, bf16[128,256]{1,0:T(8,128)(2,1)S(1)}, u32[]{:S(2)}, u32[]{:S(2)}) %collective-permute-start.13) | collective-permute-done | bytes 65568 | tf_op jit(solution)/shard_map/ppermute | solution.py:26
  43.3 0.7 %add_convert_fusion = bf16[128,256]{1,0:T(8,128)(2,1)} fusion(f32[128,256]{1,0:T(8,128)S(1)} %shard_map.63, bf16[128,256]{1,0:T(8,128)(2,1)S(1)} %fusion.5.refs_0_, f32[128,256]{1,0:T(8,128)S(1)} %get-tuple-element.29, bf16[128,256]{1,0:T(8,128)(2,1)S(1)} %collective-permute-done.13, f32[128]{0:T(128)S(1)} %fusion.7), kind=kLoop, calls=%fused_computation.6 | loop fusion | flops 294912 | bytes 459264 | tf_op jit(solution)/shard_map/convert_element_type | solution.py:240
  (9 shorter events, 0.1 us)
Async XLA Ops:
  0.0 4.0 %copy-start = (bf16[1024,2,128]{2,1,0:T(2,128)(2,1)S(1)}, bf16[1024,2,128]{2,1,0:T(2,128)(2,1)}, u32[]{:S(2)}) copy-start(bf16[1024,2,128]{2,1,0:T(2,128)(2,1)} %param.5) | copy-start | bytes 1572868
  0.0 10.2 %collective-permute-start.5 = (bf16[128,256]{1,0:T(8,128)(2,1)}, bf16[128,256]{1,0:T(8,128)(2,1)S(1)}, u32[]{:S(2)}, u32[]{:S(2)}) collective-permute-start(bf16[128,256]{1,0:T(8,128)(2,1)} %refs_0_.1), channel_id=1, source_target_pairs={{0,8},{2,10},{4,12},{6,14},{8,0},{10,2},{12,4},{14,6},{1,9},{3,11}... | collective-permute-start | bytes 196616 | tf_op jit(solution)/shard_map/ppermute | solution.py:26
  4.0 0.7 %copy-start.2 = (s32[8,2,1]{0,2,1:T(1,128)S(1)}, s32[8,2,1]{0,2,1:T(1,128)}, u32[]{:S(2)}) copy-start(s32[8,2,1]{0,2,1:T(1,128)} %param.6) | copy-start | bytes 196
  4.7 5.5 %copy-start.1 = (bf16[128,256]{1,0:T(8,128)(2,1)S(1)}, bf16[128,256]{1,0:T(8,128)(2,1)}, u32[]{:S(2)}) copy-start(bf16[128,256]{1,0:T(8,128)(2,1)} %refs_0_.1) | copy-start | bytes 196612
  5.7 11.4 %collective-permute-start = (bf16[2,2,128,128]{3,2,1,0:T(8,128)(2,1)S(1)}, bf16[2,2,128,128]{3,2,1,0:T(8,128)(2,1)S(1)}, u32[]{:S(2)}, u32[]{:S(2)}) collective-permute-start(bf16[2,2,128,128]{3,2,1,0:T(8,128)(2,1)S(1)} %get-tuple-element.20.refs_2_), channel_id=1, source_target_pairs={{0,8},{2,10},{4,12},{6,14},{8,0},{10,2},{12,4},{14,6},{1,9},{3,11}... | collective-permute-start | bytes 393224 | tf_op jit(solution)/shard_map/ppermute | solution.py:26
  6.1 10.9 %collective-permute-start.1 = (bf16[2,2,128,128]{3,2,1,0:T(8,128)(2,1)S(1)}, bf16[2,2,128,128]{3,2,1,0:T(8,128)(2,1)S(1)}, u32[]{:S(2)}, u32[]{:S(2)}) collective-permute-start(bf16[2,2,128,128]{3,2,1,0:T(8,128)(2,1)S(1)} %get-tuple-element.19.refs_1_), channel_id=1, source_target_pairs={{0,4},{2,6},{4,0},{6,2},{8,12},{10,14},{12,8},{14,10},{1,5},{3,7},... | collective-permute-start | bytes 393224 | tf_op jit(solution)/shard_map/ppermute | solution.py:26
  7.7 12.0 %collective-permute-start.2 = (bf16[2,2,128,128]{3,2,1,0:T(8,128)(2,1)S(1)}, bf16[2,2,128,128]{3,2,1,0:T(8,128)(2,1)S(1)}, u32[]{:S(2)}, u32[]{:S(2)}) collective-permute-start(bf16[2,2,128,128]{3,2,1,0:T(8,128)(2,1)S(1)} %get-tuple-element.21.refs_3_), channel_id=1, source_target_pairs={{0,12},{2,14},{4,8},{6,10},{8,4},{10,6},{12,0},{14,2},{1,13},{3,15... | collective-permute-start | bytes 393224 | tf_op jit(solution)/shard_map/ppermute | solution.py:26
  10.2 1.5 %collective-permute-start.3 = (bf16[4,2,128,128]{3,2,1,0:T(8,128)(2,1)S(1)}, bf16[4,2,128,128]{3,2,1,0:T(8,128)(2,1)S(1)}, u32[]{:S(2)}, u32[]{:S(2)}) collective-permute-start(bf16[4,2,128,128]{3,2,1,0:T(8,128)(2,1)S(1)} %get-tuple-element.22), channel_id=1, source_target_pairs={{0,1},{1,0},{2,3},{3,2},{4,5},{5,4},{6,7},{7,6},{8,9},{9,8},{10,11... | collective-permute-start | bytes 786440 | tf_op jit(solution)/shard_map/ppermute | solution.py:30
  10.2 9.7 %collective-permute-start.6 = (bf16[256,256]{1,0:T(8,128)(2,1)S(1)}, bf16[256,256]{1,0:T(8,128)(2,1)S(1)}, u32[]{:S(2)}, u32[]{:S(2)}) collective-permute-start(bf16[256,256]{1,0:T(8,128)(2,1)S(1)} %shard_map.58.refs_0_), channel_id=1, source_target_pairs={{0,4},{2,6},{4,0},{6,2},{8,12},{10,14},{12,8},{14,10},{1,5},{3,7},... | collective-permute-start | bytes 393224 | tf_op jit(solution)/shard_map/ppermute | solution.py:26
  11.7 8.4 %collective-permute-start.4 = (bf16[2,4,128,128]{3,2,1,0:T(8,128)(2,1)S(1)}, bf16[2,4,128,128]{3,2,1,0:T(8,128)(2,1)S(1)}, u32[]{:S(2)}, u32[]{:S(2)}) collective-permute-start(bf16[2,4,128,128]{3,2,1,0:T(8,128)(2,1)S(1)} %shard_map.57), channel_id=1, source_target_pairs={{0,2},{2,0},{4,6},{6,4},{8,10},{10,8},{12,14},{14,12},{1,3},{3,1},... | collective-permute-start | bytes 786440 | tf_op jit(solution)/shard_map/ppermute | solution.py:26
  19.9 1.6 %collective-permute-start.7 = (bf16[512,256]{1,0:T(8,128)(2,1)S(1)}, bf16[512,256]{1,0:T(8,128)(2,1)S(1)}, u32[]{:S(2)}, u32[]{:S(2)}) collective-permute-start(bf16[512,256]{1,0:T(8,128)(2,1)S(1)} %shard_map.59.refs_9_), channel_id=1, source_target_pairs={{0,1},{1,0},{2,3},{3,2},{4,5},{5,4},{6,7},{7,6},{8,9},{9,8},{10,11... | collective-permute-start | bytes 786440 | tf_op jit(solution)/shard_map/ppermute | solution.py:30
  21.9 4.4 %collective-permute-start.8 = (bf16[144,256]{1,0:T(8,128)(2,1)S(1)}, bf16[144,256]{1,0:T(8,128)(2,1)S(1)}, u32[]{:S(2)}, u32[]{:S(2)}) collective-permute-start(bf16[144,256]{1,0:T(8,128)(2,1)S(1)} %get-tuple-element.26), channel_id=1, source_target_pairs={{0,2},{2,0},{4,6},{6,4},{8,10},{10,8},{12,14},{14,12},{1,3},{3,1},... | collective-permute-start | bytes 221192 | tf_op jit(solution)/shard_map/ppermute | solution.py:26
  23.5 0.7 %copy-start.3 = (s32[128]{0:T(128)S(1)}, s32[128]{0:T(128)}, u32[]{:S(2)}) copy-start(s32[128]{0:T(128)} %param.8) | copy-start | bytes 1540
  23.5 0.7 %copy-start.4 = (s32[128]{0:T(128)S(1)}, s32[128]{0:T(128)}, u32[]{:S(2)}) copy-start(s32[128]{0:T(128)} %param.9) | copy-start | bytes 1540
  26.5 5.3 %collective-permute-start.9 = (bf16[128,256]{1,0:T(8,128)(2,1)S(1)}, bf16[128,256]{1,0:T(8,128)(2,1)S(1)}, u32[]{:S(2)}, u32[]{:S(2)}) collective-permute-start(bf16[128,256]{1,0:T(8,128)(2,1)S(1)} %fusion.5.refs_0_), channel_id=1, source_target_pairs={{0,8},{2,10},{4,12},{6,14},{8,0},{10,2},{12,4},{14,6},{1,9},{3,11}... | collective-permute-start | bytes 196616 | tf_op jit(solution)/shard_map/ppermute | solution.py:26
  28.4 4.7 %collective-permute-start.10 = (bf16[128,256]{1,0:T(8,128)(2,1)S(1)}, bf16[128,256]{1,0:T(8,128)(2,1)S(1)}, u32[]{:S(2)}, u32[]{:S(2)}) collective-permute-start(bf16[128,256]{1,0:T(8,128)(2,1)S(1)} %fusion.5.refs_0_), channel_id=1, source_target_pairs={{0,4},{2,6},{4,0},{6,2},{8,12},{10,14},{12,8},{14,10},{1,5},{3,7},... | collective-permute-start | bytes 196616 | tf_op jit(solution)/shard_map/ppermute | solution.py:26
  30.9 6.1 %collective-permute-start.11 = (bf16[128,256]{1,0:T(8,128)(2,1)S(1)}, bf16[128,256]{1,0:T(8,128)(2,1)S(1)}, u32[]{:S(2)}, u32[]{:S(2)}) collective-permute-start(bf16[128,256]{1,0:T(8,128)(2,1)S(1)} %fusion.5.refs_0_), channel_id=1, source_target_pairs={{0,12},{2,14},{4,8},{6,10},{8,4},{10,6},{12,0},{14,2},{1,13},{3,15... | collective-permute-start | bytes 196616 | tf_op jit(solution)/shard_map/ppermute | solution.py:26
  37.0 1.6 %collective-permute-start.12 = (bf16[512,256]{1,0:T(8,128)(2,1)S(1)}, bf16[512,256]{1,0:T(8,128)(2,1)S(1)}, u32[]{:S(2)}, u32[]{:S(2)}) collective-permute-start(bf16[512,256]{1,0:T(8,128)(2,1)S(1)} %shard_map.64.refs_9_), channel_id=1, source_target_pairs={{0,1},{1,0},{2,3},{3,2},{4,5},{5,4},{6,7},{7,6},{8,9},{9,8},{10,11... | collective-permute-start | bytes 786440 | tf_op jit(solution)/shard_map/ppermute | solution.py:30
  39.0 4.3 %collective-permute-start.13 = (bf16[128,256]{1,0:T(8,128)(2,1)S(1)}, bf16[128,256]{1,0:T(8,128)(2,1)S(1)}, u32[]{:S(2)}, u32[]{:S(2)}) collective-permute-start(bf16[128,256]{1,0:T(8,128)(2,1)S(1)} %get-tuple-element.30), channel_id=1, source_target_pairs={{0,2},{2,0},{4,6},{6,4},{8,10},{10,8},{12,14},{14,12},{1,3},{3,1},... | collective-permute-start | bytes 196616 | tf_op jit(solution)/shard_map/ppermute | solution.py:26

commit v12 on v11

--- a/solution.py
+++ b/solution.py
@@ -209,7 +209,7 @@
     current, degree = labels, None
     for step in range(ITERS):
         if step > 0:
-            order = [0] + far_first(z_count)
+            order = [0] + far_first(z_count)[::-1]
             have = [current] + [swap_rows(current, k * y_count) for k in order[1:]]
         values = join(have)
         first = step == 0

time: 44.2 us -> 42.7 us (0.966)
  waiting for transfers between devices: 19.8 us -> 18.2 us
    ppermute x11, waiting for transfers between devices: 17.6 us -> 16 us  [swap_rows(): return lax.ppermute(value, 'row', [(i, i ^ shift) for i in range(count)])]
  transfers between devices with their start and end apart: 14 -> 14, of which waited for: 12 -> 12; matrix products, arithmetic and copies ran while one was open for 0% -> 0% of each run, Pallas kernels for 4% -> 5%
where the time goes in v12:
time: 42.7 us; the launch traced here: 42.5 us
  starting transfers between devices  19.4 us (45%)
  waiting for transfers between devices  18.2 us (43%)
  Pallas kernels  2.66 us (6%)
  local copies, waits for them, and re-layouts  1.35 us (3%)
  other arithmetic  0.86 us (2%)
    ppermute x11, starting transfers between devices, swap_rows(): return lax.ppermute(value, 'row', [(i, i ^ shift) for i in range(count)])  19.2 us
    ppermute x11, waiting for transfers between devices, swap_rows(): return lax.ppermute(value, 'row', [(i, i ^ shift) for i in range(count)])  16 us
    pallas_call x12, Pallas kernels, call(): pl.pallas_call(kernel, out_shape=out_shape, in_specs=[pl.BlockSpec(memory...  2.66 us
    ppermute x3, waiting for transfers between devices, swap_cores(): return lax.ppermute(value, 'col', [(0, 1), (1, 0)])  2.18 us
    unnamed x10, local copies, waits for them, and re-layouts  1.35 us
  transfers between devices with their start and end apart: 14, of which 12 were waited for; matrix products, arithmetic and copies ran while one was open for 0% of the time, Pallas kernels for 5%

profile of v12, /device:TPU:0, one launch (start us, length us, event | category | flops | bytes accessed | tf_op | source)
XLA Modules:
  0.0 42.5 jit_solution(12331686305814820751)
XLA Ops:
  0.0 0.0 copy-start
  0.0 4.0 %collective-permute-start.5 = (bf16[128,256]{1,0:T(8,128)(2,1)}, bf16[128,256]{1,0:T(8,128)(2,1)S(1)}, u32[]{:S(2)}, u32[]{:S(2)}) collective-permute-start(bf16[128,256]{1,0:T(8,128)(2,1)} %refs_0_.1), channel_id=1, source_target_pairs={{0,8},{2,10},{4,12},{6,14},{8,0},{10,2},{12,4},{14,6},{1,9},{3,11}... | collective-permute-start | bytes 196616 | tf_op jit(solution)/shard_map/ppermute | solution.py:26
  4.0 0.0 copy-start.2
  4.0 0.0 copy-done
  4.0 0.7 %copy-done.2 = s32[8,2,1]{0,2,1:T(1,128)S(1)} copy-done((s32[8,2,1]{0,2,1:T(1,128)S(1)}, s32[8,2,1]{0,2,1:T(1,128)}, u32[]{:S(2)}) %copy-start.2) | copy-done | bytes 88
  4.7 0.0 copy-start.1
  4.7 1.0 %shard_map.56 = (bf16[2,2,128,128]{3,2,1,0:T(8,128)(2,1)S(1)}, bf16[2,2,128,128]{3,2,1,0:T(8,128)(2,1)S(1)}, bf16[2,2,128,128]{3,2,1,0:T(8,128)(2,1)S(1)}, bf16[...) custom-call(s32[2,1,8]{2,1,0:T(1,128)S(1)} %bitcast.11, bf16[2048,128]{1,0:T(8,128)(2,1)S(1)} %bitcast.10, ...), custom_call_target="tpu_custom_call" | custom-call | bytes 1314880 | tf_op jit(solution)/shard_map/pallas_call | solution.py:36
  5.7 0.4 %collective-permute-start = (bf16[2,2,128,128]{3,2,1,0:T(8,128)(2,1)S(1)}, bf16[2,2,128,128]{3,2,1,0:T(8,128)(2,1)S(1)}, u32[]{:S(2)}, u32[]{:S(2)}) collective-permute-start(bf16[2,2,128,128]{3,2,1,0:T(8,128)(2,1)S(1)} %get-tuple-element.20.refs_2_), channel_id=1, source_target_pairs={{0,8},{2,10},{4,12},{6,14},{8,0},{10,2},{12,4},{14,6},{1,9},{3,11}... | collective-permute-start | bytes 393224 | tf_op jit(solution)/shard_map/ppermute | solution.py:26
  6.1 1.6 %collective-permute-start.1 = (bf16[2,2,128,128]{3,2,1,0:T(8,128)(2,1)S(1)}, bf16[2,2,128,128]{3,2,1,0:T(8,128)(2,1)S(1)}, u32[]{:S(2)}, u32[]{:S(2)}) collective-permute-start(bf16[2,2,128,128]{3,2,1,0:T(8,128)(2,1)S(1)} %get-tuple-element.19.refs_1_), channel_id=1, source_target_pairs={{0,4},{2,6},{4,0},{6,2},{8,12},{10,14},{12,8},{14,10},{1,5},{3,7},... | collective-permute-start | bytes 393224 | tf_op jit(solution)/shard_map/ppermute | solution.py:26
  7.7 2.4 %collective-permute-start.2 = (bf16[2,2,128,128]{3,2,1,0:T(8,128)(2,1)S(1)}, bf16[2,2,128,128]{3,2,1,0:T(8,128)(2,1)S(1)}, u32[]{:S(2)}, u32[]{:S(2)}) collective-permute-start(bf16[2,2,128,128]{3,2,1,0:T(8,128)(2,1)S(1)} %get-tuple-element.21.refs_3_), channel_id=1, source_target_pairs={{0,12},{2,14},{4,8},{6,10},{8,4},{10,6},{12,0},{14,2},{1,13},{3,15... | collective-permute-start | bytes 393224 | tf_op jit(solution)/shard_map/ppermute | solution.py:26
  10.2 0.0 collective-permute-start.3
  10.2 0.0 collective-permute-done.5.refs_1_
  10.2 0.0 copy-done.1
  10.2 1.4 %collective-permute-start.6 = (bf16[256,256]{1,0:T(8,128)(2,1)S(1)}, bf16[256,256]{1,0:T(8,128)(2,1)S(1)}, u32[]{:S(2)}, u32[]{:S(2)}) collective-permute-start(bf16[256,256]{1,0:T(8,128)(2,1)S(1)} %shard_map.58.refs_0_), channel_id=1, source_target_pairs={{0,4},{2,6},{4,0},{6,2},{8,12},{10,14},{12,8},{14,10},{1,5},{3,7},... | collective-permute-start | bytes 393224 | tf_op jit(solution)/shard_map/ppermute | solution.py:26
  11.6 0.1 collective-permute-done.3.refs_4_.refs_7_
  11.7 1.6 %collective-permute-start.4 = (bf16[2,4,128,128]{3,2,1,0:T(8,128)(2,1)S(1)}, bf16[2,4,128,128]{3,2,1,0:T(8,128)(2,1)S(1)}, u32[]{:S(2)}, u32[]{:S(2)}) collective-permute-start(bf16[2,4,128,128]{3,2,1,0:T(8,128)(2,1)S(1)} %shard_map.57), channel_id=1, source_target_pairs={{0,2},{2,0},{4,6},{6,4},{8,10},{10,8},{12,14},{14,12},{1,3},{3,1},... | collective-permute-start | bytes 786440 | tf_op jit(solution)/shard_map/ppermute | solution.py:26
  13.3 3.8 %collective-permute-done.refs_0_.refs_4_ = bf16[2,2,128,128]{3,2,1,0:T(8,128)(2,1)S(1)} collective-permute-done((bf16[2,2,128,128]{3,2,1,0:T(8,128)(2,1)S(1)}, bf16[2,2,128,128]{3,2,1,0:T(8,128)(2,1)S(1)}, u32[]{:S(2)}, u32[]{:S(2)}) %collective-permute-start) | collective-permute-done | bytes 131104 | tf_op jit(solution)/shard_map/ppermute | solution.py:26
  17.1 0.0 collective-permute-done.1.refs_1_.refs_5_
  17.1 2.6 %collective-permute-done.2.refs_2_.refs_6_ = bf16[2,2,128,128]{3,2,1,0:T(8,128)(2,1)S(1)} collective-permute-done((bf16[2,2,128,128]{3,2,1,0:T(8,128)(2,1)S(1)}, bf16[2,2,128,128]{3,2,1,0:T(8,128)(2,1)S(1)}, u32[]{:S(2)}, u32[]{:S(2)}) %collective-permute-start.2) | collective-permute-done | bytes 131104 | tf_op jit(solution)/shard_map/ppermute | solution.py:26
  19.7 0.2 collective-permute-done.6.refs_1_
  19.9 0.1 collective-permute-start.7
  20.0 0.1 collective-permute-done.4.refs_8_
  20.1 0.5 %shard_map.61 = (f32[136,256]{1,0:T(8,128)S(1)}, f32[136,256]{1,0:T(8,128)S(1)}) custom-call(bf16[2,2,128,128]{3,2,1,0:T(8,128)(2,1)S(1)} %get-tuple-element.18.refs_0_, bf16[2,2,128,128]{3,2,1,0:T(8,128)(2,1)S(1)} %get-tuple-element.19.refs_1_, bf16[2,2,128,128]{3,2,1,0:T(8,128)(2,1)S(1)} %get-tuple-element.20.refs_2_, ...), custom_call_target="tpu_custom_call" | custom-call | flops 3000000000 | bytes 1986560 | tf_op jit(solution)/shard_map/pallas_call | solution.py:36
  20.6 0.9 %collective-permute-done.7.refs_9_ = bf16[512,256]{1,0:T(8,128)(2,1)S(1)} collective-permute-done((bf16[512,256]{1,0:T(8,128)(2,1)S(1)}, bf16[512,256]{1,0:T(8,128)(2,1)S(1)}, u32[]{:S(2)}, u32[]{:S(2)}) %collective-permute-start.7) | collective-permute-done | bytes 262176 | tf_op jit(solution)/shard_map/ppermute | solution.py:30
  21.5 0.4 shard_map.62
  21.9 1.6 %collective-permute-start.8 = (bf16[144,256]{1,0:T(8,128)(2,1)S(1)}, bf16[144,256]{1,0:T(8,128)(2,1)S(1)}, u32[]{:S(2)}, u32[]{:S(2)}) collective-permute-start(bf16[144,256]{1,0:T(8,128)(2,1)S(1)} %get-tuple-element.26), channel_id=1, source_target_pairs={{0,2},{2,0},{4,6},{6,4},{8,10},{10,8},{12,14},{14,12},{1,3},{3,1},... | collective-permute-start | bytes 221192 | tf_op jit(solution)/shard_map/ppermute | solution.py:26
  23.5 0.0 copy-start.3
  23.5 0.0 copy-start.4
  23.5 0.7 %copy-done.3 = s32[128]{0:T(128)S(1)} copy-done((s32[128]{0:T(128)S(1)}, s32[128]{0:T(128)}, u32[]{:S(2)}) %copy-start.3) | copy-done | bytes 536
  24.1 0.0 copy-done.4
  24.1 0.1 shard_map.63
  24.3 2.0 %collective-permute-done.8 = bf16[144,256]{1,0:T(8,128)(2,1)S(1)} collective-permute-done((bf16[144,256]{1,0:T(8,128)(2,1)S(1)}, bf16[144,256]{1,0:T(8,128)(2,1)S(1)}, u32[]{:S(2)}, u32[]{:S(2)}) %collective-permute-start.8) | collective-permute-done | bytes 73760 | tf_op jit(solution)/shard_map/ppermute | solution.py:26
  26.3 0.1 fusion.5.refs_0_
  26.5 3.9 %collective-permute-start.9 = (bf16[128,256]{1,0:T(8,128)(2,1)S(1)}, bf16[128,256]{1,0:T(8,128)(2,1)S(1)}, u32[]{:S(2)}, u32[]{:S(2)}) collective-permute-start(bf16[128,256]{1,0:T(8,128)(2,1)S(1)} %fusion.5.refs_0_), channel_id=1, source_target_pairs={{0,12},{2,14},{4,8},{6,10},{8,4},{10,6},{12,0},{14,2},{1,13},{3,15... | collective-permute-start | bytes 196616 | tf_op jit(solution)/shard_map/ppermute | solution.py:26
  30.3 0.0 collective-permute-start.10
  30.3 0.6 %collective-permute-start.11 = (bf16[128,256]{1,0:T(8,128)(2,1)S(1)}, bf16[128,256]{1,0:T(8,128)(2,1)S(1)}, u32[]{:S(2)}, u32[]{:S(2)}) collective-permute-start(bf16[128,256]{1,0:T(8,128)(2,1)S(1)} %fusion.5.refs_0_), channel_id=1, source_target_pairs={{0,8},{2,10},{4,12},{6,14},{8,0},{10,2},{12,4},{14,6},{1,9},{3,11}... | collective-permute-start | bytes 196616 | tf_op jit(solution)/shard_map/ppermute | solution.py:26
  31.0 1.7 %collective-permute-done.9.refs_1_ = bf16[128,256]{1,0:T(8,128)(2,1)S(1)} collective-permute-done((bf16[128,256]{1,0:T(8,128)(2,1)S(1)}, bf16[128,256]{1,0:T(8,128)(2,1)S(1)}, u32[]{:S(2)}, u32[]{:S(2)}) %collective-permute-start.9) | collective-permute-done | bytes 65568 | tf_op jit(solution)/shard_map/ppermute | solution.py:26
  32.7 1.9 %collective-permute-done.10.refs_2_ = bf16[128,256]{1,0:T(8,128)(2,1)S(1)} collective-permute-done((bf16[128,256]{1,0:T(8,128)(2,1)S(1)}, bf16[128,256]{1,0:T(8,128)(2,1)S(1)}, u32[]{:S(2)}, u32[]{:S(2)}) %collective-permute-start.10) | collective-permute-done | bytes 65568 | tf_op jit(solution)/shard_map/ppermute | solution.py:26
  34.6 0.9 %collective-permute-done.11.refs_3_ = bf16[128,256]{1,0:T(8,128)(2,1)S(1)} collective-permute-done((bf16[128,256]{1,0:T(8,128)(2,1)S(1)}, bf16[128,256]{1,0:T(8,128)(2,1)S(1)}, u32[]{:S(2)}, u32[]{:S(2)}) %collective-permute-start.11) | collective-permute-done | bytes 65568 | tf_op jit(solution)/shard_map/ppermute | solution.py:26
  35.5 0.1 collective-permute-start.12
  35.6 0.3 shard_map.65
  35.9 1.2 %collective-permute-done.12.refs_9_ = bf16[512,256]{1,0:T(8,128)(2,1)S(1)} collective-permute-done((bf16[512,256]{1,0:T(8,128)(2,1)S(1)}, bf16[512,256]{1,0:T(8,128)(2,1)S(1)}, u32[]{:S(2)}, u32[]{:S(2)}) %collective-permute-start.12) | collective-permute-done | bytes 262176 | tf_op jit(solution)/shard_map/ppermute | solution.py:30
  37.1 0.3 shard_map.66
  37.5 1.6 %collective-permute-start.13 = (bf16[128,256]{1,0:T(8,128)(2,1)S(1)}, bf16[128,256]{1,0:T(8,128)(2,1)S(1)}, u32[]{:S(2)}, u32[]{:S(2)}) collective-permute-start(bf16[128,256]{1,0:T(8,128)(2,1)S(1)} %get-tuple-element.30), channel_id=1, source_target_pairs={{0,2},{2,0},{4,6},{6,4},{8,10},{10,8},{12,14},{14,12},{1,3},{3,1},... | collective-permute-start | bytes 196616 | tf_op jit(solution)/shard_map/ppermute | solution.py:26
  39.1 2.7 %collective-permute-done.13 = bf16[128,256]{1,0:T(8,128)(2,1)S(1)} collective-permute-done((bf16[128,256]{1,0:T(8,128)(2,1)S(1)}, bf16[128,256]{1,0:T(8,128)(2,1)S(1)}, u32[]{:S(2)}, u32[]{:S(2)}) %collective-permute-start.13) | collective-permute-done | bytes 65568 | tf_op jit(solution)/shard_map/ppermute | solution.py:26
  41.8 0.7 %add_convert_fusion = bf16[128,256]{1,0:T(8,128)(2,1)} fusion(f32[128,256]{1,0:T(8,128)S(1)} %shard_map.63, bf16[128,256]{1,0:T(8,128)(2,1)S(1)} %fusion.5.refs_0_, f32[128,256]{1,0:T(8,128)S(1)} %get-tuple-element.29, bf16[128,256]{1,0:T(8,128)(2,1)S(1)} %collective-permute-done.13, f32[128]{0:T(128)S(1)} %fusion.7), kind=kLoop, calls=%fused_computation.6 | loop fusion | flops 294912 | bytes 459264 | tf_op jit(solution)/shard_map/convert_element_type | solution.py:240
  (9 shorter events, 0.1 us)
Async XLA Ops:
  0.0 4.0 %copy-start = (bf16[1024,2,128]{2,1,0:T(2,128)(2,1)S(1)}, bf16[1024,2,128]{2,1,0:T(2,128)(2,1)}, u32[]{:S(2)}) copy-start(bf16[1024,2,128]{2,1,0:T(2,128)(2,1)} %param.5) | copy-start | bytes 1572868
  0.0 10.2 %collective-permute-start.5 = (bf16[128,256]{1,0:T(8,128)(2,1)}, bf16[128,256]{1,0:T(8,128)(2,1)S(1)}, u32[]{:S(2)}, u32[]{:S(2)}) collective-permute-start(bf16[128,256]{1,0:T(8,128)(2,1)} %refs_0_.1), channel_id=1, source_target_pairs={{0,8},{2,10},{4,12},{6,14},{8,0},{10,2},{12,4},{14,6},{1,9},{3,11}... | collective-permute-start | bytes 196616 | tf_op jit(solution)/shard_map/ppermute | solution.py:26
  4.0 0.7 %copy-start.2 = (s32[8,2,1]{0,2,1:T(1,128)S(1)}, s32[8,2,1]{0,2,1:T(1,128)}, u32[]{:S(2)}) copy-start(s32[8,2,1]{0,2,1:T(1,128)} %param.6) | copy-start | bytes 196
  4.7 5.5 %copy-start.1 = (bf16[128,256]{1,0:T(8,128)(2,1)S(1)}, bf16[128,256]{1,0:T(8,128)(2,1)}, u32[]{:S(2)}) copy-start(bf16[128,256]{1,0:T(8,128)(2,1)} %refs_0_.1) | copy-start | bytes 196612
  5.7 11.4 %collective-permute-start = (bf16[2,2,128,128]{3,2,1,0:T(8,128)(2,1)S(1)}, bf16[2,2,128,128]{3,2,1,0:T(8,128)(2,1)S(1)}, u32[]{:S(2)}, u32[]{:S(2)}) collective-permute-start(bf16[2,2,128,128]{3,2,1,0:T(8,128)(2,1)S(1)} %get-tuple-element.20.refs_2_), channel_id=1, source_target_pairs={{0,8},{2,10},{4,12},{6,14},{8,0},{10,2},{12,4},{14,6},{1,9},{3,11}... | collective-permute-start | bytes 393224 | tf_op jit(solution)/shard_map/ppermute | solution.py:26
  6.1 10.9 %collective-permute-start.1 = (bf16[2,2,128,128]{3,2,1,0:T(8,128)(2,1)S(1)}, bf16[2,2,128,128]{3,2,1,0:T(8,128)(2,1)S(1)}, u32[]{:S(2)}, u32[]{:S(2)}) collective-permute-start(bf16[2,2,128,128]{3,2,1,0:T(8,128)(2,1)S(1)} %get-tuple-element.19.refs_1_), channel_id=1, source_target_pairs={{0,4},{2,6},{4,0},{6,2},{8,12},{10,14},{12,8},{14,10},{1,5},{3,7},... | collective-permute-start | bytes 393224 | tf_op jit(solution)/shard_map/ppermute | solution.py:26
  7.7 12.0 %collective-permute-start.2 = (bf16[2,2,128,128]{3,2,1,0:T(8,128)(2,1)S(1)}, bf16[2,2,128,128]{3,2,1,0:T(8,128)(2,1)S(1)}, u32[]{:S(2)}, u32[]{:S(2)}) collective-permute-start(bf16[2,2,128,128]{3,2,1,0:T(8,128)(2,1)S(1)} %get-tuple-element.21.refs_3_), channel_id=1, source_target_pairs={{0,12},{2,14},{4,8},{6,10},{8,4},{10,6},{12,0},{14,2},{1,13},{3,15... | collective-permute-start | bytes 393224 | tf_op jit(solution)/shard_map/ppermute | solution.py:26
  10.2 1.5 %collective-permute-start.3 = (bf16[4,2,128,128]{3,2,1,0:T(8,128)(2,1)S(1)}, bf16[4,2,128,128]{3,2,1,0:T(8,128)(2,1)S(1)}, u32[]{:S(2)}, u32[]{:S(2)}) collective-permute-start(bf16[4,2,128,128]{3,2,1,0:T(8,128)(2,1)S(1)} %get-tuple-element.22), channel_id=1, source_target_pairs={{0,1},{1,0},{2,3},{3,2},{4,5},{5,4},{6,7},{7,6},{8,9},{9,8},{10,11... | collective-permute-start | bytes 786440 | tf_op jit(solution)/shard_map/ppermute | solution.py:30
  10.2 9.7 %collective-permute-start.6 = (bf16[256,256]{1,0:T(8,128)(2,1)S(1)}, bf16[256,256]{1,0:T(8,128)(2,1)S(1)}, u32[]{:S(2)}, u32[]{:S(2)}) collective-permute-start(bf16[256,256]{1,0:T(8,128)(2,1)S(1)} %shard_map.58.refs_0_), channel_id=1, source_target_pairs={{0,4},{2,6},{4,0},{6,2},{8,12},{10,14},{12,8},{14,10},{1,5},{3,7},... | collective-permute-start | bytes 393224 | tf_op jit(solution)/shard_map/ppermute | solution.py:26
  11.7 8.4 %collective-permute-start.4 = (bf16[2,4,128,128]{3,2,1,0:T(8,128)(2,1)S(1)}, bf16[2,4,128,128]{3,2,1,0:T(8,128)(2,1)S(1)}, u32[]{:S(2)}, u32[]{:S(2)}) collective-permute-start(bf16[2,4,128,128]{3,2,1,0:T(8,128)(2,1)S(1)} %shard_map.57), channel_id=1, source_target_pairs={{0,2},{2,0},{4,6},{6,4},{8,10},{10,8},{12,14},{14,12},{1,3},{3,1},... | collective-permute-start | bytes 786440 | tf_op jit(solution)/shard_map/ppermute | solution.py:26
  19.9 1.6 %collective-permute-start.7 = (bf16[512,256]{1,0:T(8,128)(2,1)S(1)}, bf16[512,256]{1,0:T(8,128)(2,1)S(1)}, u32[]{:S(2)}, u32[]{:S(2)}) collective-permute-start(bf16[512,256]{1,0:T(8,128)(2,1)S(1)} %shard_map.59.refs_9_), channel_id=1, source_target_pairs={{0,1},{1,0},{2,3},{3,2},{4,5},{5,4},{6,7},{7,6},{8,9},{9,8},{10,11... | collective-permute-start | bytes 786440 | tf_op jit(solution)/shard_map/ppermute | solution.py:30
  21.9 4.4 %collective-permute-start.8 = (bf16[144,256]{1,0:T(8,128)(2,1)S(1)}, bf16[144,256]{1,0:T(8,128)(2,1)S(1)}, u32[]{:S(2)}, u32[]{:S(2)}) collective-permute-start(bf16[144,256]{1,0:T(8,128)(2,1)S(1)} %get-tuple-element.26), channel_id=1, source_target_pairs={{0,2},{2,0},{4,6},{6,4},{8,10},{10,8},{12,14},{14,12},{1,3},{3,1},... | collective-permute-start | bytes 221192 | tf_op jit(solution)/shard_map/ppermute | solution.py:26
  23.5 0.7 %copy-start.3 = (s32[128]{0:T(128)S(1)}, s32[128]{0:T(128)}, u32[]{:S(2)}) copy-start(s32[128]{0:T(128)} %param.8) | copy-start | bytes 1540
  23.5 0.7 %copy-start.4 = (s32[128]{0:T(128)S(1)}, s32[128]{0:T(128)}, u32[]{:S(2)}) copy-start(s32[128]{0:T(128)} %param.9) | copy-start | bytes 1540
  26.5 6.2 %collective-permute-start.9 = (bf16[128,256]{1,0:T(8,128)(2,1)S(1)}, bf16[128,256]{1,0:T(8,128)(2,1)S(1)}, u32[]{:S(2)}, u32[]{:S(2)}) collective-permute-start(bf16[128,256]{1,0:T(8,128)(2,1)S(1)} %fusion.5.refs_0_), channel_id=1, source_target_pairs={{0,12},{2,14},{4,8},{6,10},{8,4},{10,6},{12,0},{14,2},{1,13},{3,15... | collective-permute-start | bytes 196616 | tf_op jit(solution)/shard_map/ppermute | solution.py:26
  30.3 4.3 %collective-permute-start.10 = (bf16[128,256]{1,0:T(8,128)(2,1)S(1)}, bf16[128,256]{1,0:T(8,128)(2,1)S(1)}, u32[]{:S(2)}, u32[]{:S(2)}) collective-permute-start(bf16[128,256]{1,0:T(8,128)(2,1)S(1)} %fusion.5.refs_0_), channel_id=1, source_target_pairs={{0,4},{2,6},{4,0},{6,2},{8,12},{10,14},{12,8},{14,10},{1,5},{3,7},... | collective-permute-start | bytes 196616 | tf_op jit(solution)/shard_map/ppermute | solution.py:26
  30.3 5.2 %collective-permute-start.11 = (bf16[128,256]{1,0:T(8,128)(2,1)S(1)}, bf16[128,256]{1,0:T(8,128)(2,1)S(1)}, u32[]{:S(2)}, u32[]{:S(2)}) collective-permute-start(bf16[128,256]{1,0:T(8,128)(2,1)S(1)} %fusion.5.refs_0_), channel_id=1, source_target_pairs={{0,8},{2,10},{4,12},{6,14},{8,0},{10,2},{12,4},{14,6},{1,9},{3,11}... | collective-permute-start | bytes 196616 | tf_op jit(solution)/shard_map/ppermute | solution.py:26
  35.5 1.6 %collective-permute-start.12 = (bf16[512,256]{1,0:T(8,128)(2,1)S(1)}, bf16[512,256]{1,0:T(8,128)(2,1)S(1)}, u32[]{:S(2)}, u32[]{:S(2)}) collective-permute-start(bf16[512,256]{1,0:T(8,128)(2,1)S(1)} %shard_map.64.refs_9_), channel_id=1, source_target_pairs={{0,1},{1,0},{2,3},{3,2},{4,5},{5,4},{6,7},{7,6},{8,9},{9,8},{10,11... | collective-permute-start | bytes 786440 | tf_op jit(solution)/shard_map/ppermute | solution.py:30
  37.5 4.3 %collective-permute-start.13 = (bf16[128,256]{1,0:T(8,128)(2,1)S(1)}, bf16[128,256]{1,0:T(8,128)(2,1)S(1)}, u32[]{:S(2)}, u32[]{:S(2)}) collective-permute-start(bf16[128,256]{1,0:T(8,128)(2,1)S(1)} %get-tuple-element.30), channel_id=1, source_target_pairs={{0,2},{2,0},{4,6},{6,4},{8,10},{10,8},{12,14},{14,12},{1,3},{3,1},... | collective-permute-start | bytes 196616 | tf_op jit(solution)/shard_map/ppermute | solution.py:26

commit v13 on v12

--- a/solution.py
+++ b/solution.py
@@ -43,9 +43,13 @@
     )(*operands)
 
 
-def far_first(count):
+def others(count):
+    return list(range(1, count))
+
+
+def others_late(count):
     half = count // 2
-    return [half] + [k for k in range(1, count) if k != half]
+    return list(range(half + 1, count)) + list(range(1, half)) + [half]
 
 
 def prepare_kernel(z_count, y_count, live, tile, lead, *outs):
@@ -121,7 +125,7 @@
 def blocks_of(order, y_count, refs, i, j):
     z_count = len(order)
     sent, refs = refs[:z_count], refs[z_count:]
-    strips = dict(zip([0] + far_first(z_count), sent[:1] + refs))
+    strips = dict(zip([0] + others(z_count), sent[:1] + refs))
     from_core, halves = refs[z_count - 1], refs[z_count:]
 
     def back_block(k):
@@ -188,9 +192,9 @@
     from_core = swap_cores(other)
     halves = call(lambda *refs: halves_kernel(z_count, *refs), [half] * (y_count - 1), *sent, from_core)
     halves = [swap_rows(x, j + 1) for j, x in enumerate(halves)]
-    arrived = {k: swap_rows(sent[k], k * y_count) for k in far_first(z_count)}
-    strips = [arrived[k] for k in far_first(z_count)]
-    strips = [arrived[k] for k in far_first(z_count)]
+    arrived = {k: swap_rows(sent[k], k * y_count) for k in others(z_count)}
+    strips = [arrived[k] for k in others(z_count)]
+    strips = [arrived[k] for k in others(z_count)]
     mark = guard(strips, STRIPS_FLOPS)
     blocks = [*sent, *strips, from_core, *halves]
     have, order, bit = [labels], [0], z_count // 2
@@ -209,7 +213,7 @@
     current, degree = labels, None
     for step in range(ITERS):
         if step > 0:
-            order = [0] + far_first(z_count)[::-1]
+            order = [0] + others_late(z_count)
             have = [current] + [swap_rows(current, k * y_count) for k in order[1:]]
         values = join(have)
         first = step == 0

time: 42.7 us -> 42.7 us (level)
  waiting for transfers between devices: 18.2 us -> 19 us
  starting transfers between devices: 19.4 us -> 18.6 us
    ppermute x3, waiting for transfers between devices: 2.18 us -> 2.97 us  [swap_cores(): return lax.ppermute(value, 'col', [(0, 1), (1, 0)])]
    ppermute x11, starting transfers between devices: 19.2 us -> 18.4 us  [swap_rows(): return lax.ppermute(value, 'row', [(i, i ^ shift) for i in range(count)])]
  transfers between devices with their start and end apart: 14 -> 14, of which waited for: 12 -> 9; matrix products, arithmetic and copies ran while one was open for 0% -> 0% of each run, Pallas kernels for 5% -> 5%
where the time goes in v13:
time: 42.7 us; the launch traced here: 42.6 us
  waiting for transfers between devices  19 us (44%)
  starting transfers between devices  18.6 us (44%)
  Pallas kernels  2.66 us (6%)
  local copies, waits for them, and re-layouts  1.35 us (3%)
  other arithmetic  0.86 us (2%)
    ppermute x11, starting transfers between devices, swap_rows(): return lax.ppermute(value, 'row', [(i, i ^ shift) for i in range(count)])  18.4 us
    ppermute x11, waiting for transfers between devices, swap_rows(): return lax.ppermute(value, 'row', [(i, i ^ shift) for i in range(count)])  16 us
    ppermute x3, waiting for transfers between devices, swap_cores(): return lax.ppermute(value, 'col', [(0, 1), (1, 0)])  2.97 us
    pallas_call x12, Pallas kernels, call(): pl.pallas_call(kernel, out_shape=out_shape, in_specs=[pl.BlockSpec(memory...  2.66 us
    unnamed x10, local copies, waits for them, and re-layouts  1.35 us
  transfers between devices with their start and end apart: 14, of which 9 were waited for; matrix products, arithmetic and copies ran while one was open for 0% of the time, Pallas kernels for 5%

profile of v13, /device:TPU:0, one launch (start us, length us, event | category | flops | bytes accessed | tf_op | source)
XLA Modules:
  0.0 42.6 jit_solution(4820818391771730584)
XLA Ops:
  0.0 0.0 copy-start
  0.0 4.0 %collective-permute-start.5 = (bf16[128,256]{1,0:T(8,128)(2,1)}, bf16[128,256]{1,0:T(8,128)(2,1)S(1)}, u32[]{:S(2)}, u32[]{:S(2)}) collective-permute-start(bf16[128,256]{1,0:T(8,128)(2,1)} %refs_0_.1), channel_id=1, source_target_pairs={{0,8},{2,10},{4,12},{6,14},{8,0},{10,2},{12,4},{14,6},{1,9},{3,11}... | collective-permute-start | bytes 196616 | tf_op jit(solution)/shard_map/ppermute | solution.py:26
  4.0 0.0 copy-start.2
  4.0 0.0 copy-done
  4.0 0.7 %copy-done.2 = s32[8,2,1]{0,2,1:T(1,128)S(1)} copy-done((s32[8,2,1]{0,2,1:T(1,128)S(1)}, s32[8,2,1]{0,2,1:T(1,128)}, u32[]{:S(2)}) %copy-start.2) | copy-done | bytes 88
  4.7 0.0 copy-start.1
  4.7 1.0 %shard_map.56 = (bf16[2,2,128,128]{3,2,1,0:T(8,128)(2,1)S(1)}, bf16[2,2,128,128]{3,2,1,0:T(8,128)(2,1)S(1)}, bf16[2,2,128,128]{3,2,1,0:T(8,128)(2,1)S(1)}, bf16[...) custom-call(s32[2,1,8]{2,1,0:T(1,128)S(1)} %bitcast.11, bf16[2048,128]{1,0:T(8,128)(2,1)S(1)} %bitcast.10, ...), custom_call_target="tpu_custom_call" | custom-call | bytes 1314880 | tf_op jit(solution)/shard_map/pallas_call | solution.py:36
  5.7 1.6 %collective-permute-start = (bf16[2,2,128,128]{3,2,1,0:T(8,128)(2,1)S(1)}, bf16[2,2,128,128]{3,2,1,0:T(8,128)(2,1)S(1)}, u32[]{:S(2)}, u32[]{:S(2)}) collective-permute-start(bf16[2,2,128,128]{3,2,1,0:T(8,128)(2,1)S(1)} %get-tuple-element.19.refs_1_), channel_id=1, source_target_pairs={{0,4},{2,6},{4,0},{6,2},{8,12},{10,14},{12,8},{14,10},{1,5},{3,7},... | collective-permute-start | bytes 393224 | tf_op jit(solution)/shard_map/ppermute | solution.py:26
  7.4 0.4 collective-permute-start.1
  7.7 2.4 %collective-permute-start.2 = (bf16[2,2,128,128]{3,2,1,0:T(8,128)(2,1)S(1)}, bf16[2,2,128,128]{3,2,1,0:T(8,128)(2,1)S(1)}, u32[]{:S(2)}, u32[]{:S(2)}) collective-permute-start(bf16[2,2,128,128]{3,2,1,0:T(8,128)(2,1)S(1)} %get-tuple-element.21.refs_3_), channel_id=1, source_target_pairs={{0,12},{2,14},{4,8},{6,10},{8,4},{10,6},{12,0},{14,2},{1,13},{3,15... | collective-permute-start | bytes 393224 | tf_op jit(solution)/shard_map/ppermute | solution.py:26
  10.2 0.0 collective-permute-start.3
  10.2 0.0 collective-permute-done.5.refs_1_
  10.2 0.0 copy-done.1
  10.2 0.7 %collective-permute-start.6 = (bf16[256,256]{1,0:T(8,128)(2,1)S(1)}, bf16[256,256]{1,0:T(8,128)(2,1)S(1)}, u32[]{:S(2)}, u32[]{:S(2)}) collective-permute-start(bf16[256,256]{1,0:T(8,128)(2,1)S(1)} %shard_map.58.refs_0_), channel_id=1, source_target_pairs={{0,4},{2,6},{4,0},{6,2},{8,12},{10,14},{12,8},{14,10},{1,5},{3,7},... | collective-permute-start | bytes 393224 | tf_op jit(solution)/shard_map/ppermute | solution.py:26
  10.9 0.8 %collective-permute-done.3.refs_4_.refs_7_ = bf16[4,2,128,128]{3,2,1,0:T(8,128)(2,1)S(1)} collective-permute-done((bf16[4,2,128,128]{3,2,1,0:T(8,128)(2,1)S(1)}, bf16[4,2,128,128]{3,2,1,0:T(8,128)(2,1)S(1)}, u32[]{:S(2)}, u32[]{:S(2)}) %collective-permute-start.3) | collective-permute-done | bytes 262176 | tf_op jit(solution)/shard_map/ppermute | solution.py:30
  11.7 1.6 %collective-permute-start.4 = (bf16[2,4,128,128]{3,2,1,0:T(8,128)(2,1)S(1)}, bf16[2,4,128,128]{3,2,1,0:T(8,128)(2,1)S(1)}, u32[]{:S(2)}, u32[]{:S(2)}) collective-permute-start(bf16[2,4,128,128]{3,2,1,0:T(8,128)(2,1)S(1)} %shard_map.57), channel_id=1, source_target_pairs={{0,2},{2,0},{4,6},{6,4},{8,10},{10,8},{12,14},{14,12},{1,3},{3,1},... | collective-permute-start | bytes 786440 | tf_op jit(solution)/shard_map/ppermute | solution.py:26
  13.3 0.0 collective-permute-done.refs_0_.refs_4_
  13.3 6.1 %collective-permute-done.1.refs_1_.refs_5_ = bf16[2,2,128,128]{3,2,1,0:T(8,128)(2,1)S(1)} collective-permute-done((bf16[2,2,128,128]{3,2,1,0:T(8,128)(2,1)S(1)}, bf16[2,2,128,128]{3,2,1,0:T(8,128)(2,1)S(1)}, u32[]{:S(2)}, u32[]{:S(2)}) %collective-permute-start.1) | collective-permute-done | bytes 131104 | tf_op jit(solution)/shard_map/ppermute | solution.py:26
  19.4 0.0 collective-permute-done.2.refs_2_.refs_6_
  19.4 1.2 %collective-permute-done.6.refs_1_ = bf16[256,256]{1,0:T(8,128)(2,1)S(1)} collective-permute-done((bf16[256,256]{1,0:T(8,128)(2,1)S(1)}, bf16[256,256]{1,0:T(8,128)(2,1)S(1)}, u32[]{:S(2)}, u32[]{:S(2)}) %collective-permute-start.6) | collective-permute-done | bytes 131104 | tf_op jit(solution)/shard_map/ppermute | solution.py:26
  20.7 0.1 collective-permute-start.7
  20.7 0.0 collective-permute-done.4.refs_8_
  20.7 0.5 %shard_map.61 = (f32[136,256]{1,0:T(8,128)S(1)}, f32[136,256]{1,0:T(8,128)S(1)}) custom-call(bf16[2,2,128,128]{3,2,1,0:T(8,128)(2,1)S(1)} %get-tuple-element.18.refs_0_, bf16[2,2,128,128]{3,2,1,0:T(8,128)(2,1)S(1)} %get-tuple-element.19.refs_1_, bf16[2,2,128,128]{3,2,1,0:T(8,128)(2,1)S(1)} %get-tuple-element.20.refs_2_, ...), custom_call_target="tpu_custom_call" | custom-call | flops 3000000000 | bytes 1986560 | tf_op jit(solution)/shard_map/pallas_call | solution.py:36
  21.2 1.0 %collective-permute-done.7.refs_9_ = bf16[512,256]{1,0:T(8,128)(2,1)S(1)} collective-permute-done((bf16[512,256]{1,0:T(8,128)(2,1)S(1)}, bf16[512,256]{1,0:T(8,128)(2,1)S(1)}, u32[]{:S(2)}, u32[]{:S(2)}) %collective-permute-start.7) | collective-permute-done | bytes 262176 | tf_op jit(solution)/shard_map/ppermute | solution.py:30
  22.3 0.4 shard_map.62
  22.6 1.6 %collective-permute-start.8 = (bf16[144,256]{1,0:T(8,128)(2,1)S(1)}, bf16[144,256]{1,0:T(8,128)(2,1)S(1)}, u32[]{:S(2)}, u32[]{:S(2)}) collective-permute-start(bf16[144,256]{1,0:T(8,128)(2,1)S(1)} %get-tuple-element.26), channel_id=1, source_target_pairs={{0,2},{2,0},{4,6},{6,4},{8,10},{10,8},{12,14},{14,12},{1,3},{3,1},... | collective-permute-start | bytes 221192 | tf_op jit(solution)/shard_map/ppermute | solution.py:26
  24.2 0.0 copy-start.3
  24.2 0.0 copy-start.4
  24.2 0.7 %copy-done.3 = s32[128]{0:T(128)S(1)} copy-done((s32[128]{0:T(128)S(1)}, s32[128]{0:T(128)}, u32[]{:S(2)}) %copy-start.3) | copy-done | bytes 536
  24.8 0.0 copy-done.4
  24.9 0.1 shard_map.63
  25.0 2.1 %collective-permute-done.8 = bf16[144,256]{1,0:T(8,128)(2,1)S(1)} collective-permute-done((bf16[144,256]{1,0:T(8,128)(2,1)S(1)}, bf16[144,256]{1,0:T(8,128)(2,1)S(1)}, u32[]{:S(2)}, u32[]{:S(2)}) %collective-permute-start.8) | collective-permute-done | bytes 73760 | tf_op jit(solution)/shard_map/ppermute | solution.py:26
  27.1 0.1 fusion.5.refs_0_
  27.2 1.3 %collective-permute-start.9 = (bf16[128,256]{1,0:T(8,128)(2,1)S(1)}, bf16[128,256]{1,0:T(8,128)(2,1)S(1)}, u32[]{:S(2)}, u32[]{:S(2)}) collective-permute-start(bf16[128,256]{1,0:T(8,128)(2,1)S(1)} %fusion.5.refs_0_), channel_id=1, source_target_pairs={{0,12},{2,14},{4,8},{6,10},{8,4},{10,6},{12,0},{14,2},{1,13},{3,15... | collective-permute-start | bytes 196616 | tf_op jit(solution)/shard_map/ppermute | solution.py:26
  28.4 0.4 collective-permute-start.10
  28.8 2.8 %collective-permute-start.11 = (bf16[128,256]{1,0:T(8,128)(2,1)S(1)}, bf16[128,256]{1,0:T(8,128)(2,1)S(1)}, u32[]{:S(2)}, u32[]{:S(2)}) collective-permute-start(bf16[128,256]{1,0:T(8,128)(2,1)S(1)} %fusion.5.refs_0_), channel_id=1, source_target_pairs={{0,8},{2,10},{4,12},{6,14},{8,0},{10,2},{12,4},{14,6},{1,9},{3,11}... | collective-permute-start | bytes 196616 | tf_op jit(solution)/shard_map/ppermute | solution.py:26
  31.6 1.9 %collective-permute-done.9.refs_1_ = bf16[128,256]{1,0:T(8,128)(2,1)S(1)} collective-permute-done((bf16[128,256]{1,0:T(8,128)(2,1)S(1)}, bf16[128,256]{1,0:T(8,128)(2,1)S(1)}, u32[]{:S(2)}, u32[]{:S(2)}) %collective-permute-start.9) | collective-permute-done | bytes 65568 | tf_op jit(solution)/shard_map/ppermute | solution.py:26
  33.5 0.0 collective-permute-done.10.refs_2_
  33.5 2.0 %collective-permute-done.11.refs_3_ = bf16[128,256]{1,0:T(8,128)(2,1)S(1)} collective-permute-done((bf16[128,256]{1,0:T(8,128)(2,1)S(1)}, bf16[128,256]{1,0:T(8,128)(2,1)S(1)}, u32[]{:S(2)}, u32[]{:S(2)}) %collective-permute-start.11) | collective-permute-done | bytes 65568 | tf_op jit(solution)/shard_map/ppermute | solution.py:26
  35.6 0.1 collective-permute-start.12
  35.6 0.3 shard_map.65
  36.0 1.2 %collective-permute-done.12.refs_9_ = bf16[512,256]{1,0:T(8,128)(2,1)S(1)} collective-permute-done((bf16[512,256]{1,0:T(8,128)(2,1)S(1)}, bf16[512,256]{1,0:T(8,128)(2,1)S(1)}, u32[]{:S(2)}, u32[]{:S(2)}) %collective-permute-start.12) | collective-permute-done | bytes 262176 | tf_op jit(solution)/shard_map/ppermute | solution.py:30
  37.2 0.3 shard_map.66
  37.5 1.6 %collective-permute-start.13 = (bf16[128,256]{1,0:T(8,128)(2,1)S(1)}, bf16[128,256]{1,0:T(8,128)(2,1)S(1)}, u32[]{:S(2)}, u32[]{:S(2)}) collective-permute-start(bf16[128,256]{1,0:T(8,128)(2,1)S(1)} %get-tuple-element.30), channel_id=1, source_target_pairs={{0,2},{2,0},{4,6},{6,4},{8,10},{10,8},{12,14},{14,12},{1,3},{3,1},... | collective-permute-start | bytes 196616 | tf_op jit(solution)/shard_map/ppermute | solution.py:26
  39.1 2.7 %collective-permute-done.13 = bf16[128,256]{1,0:T(8,128)(2,1)S(1)} collective-permute-done((bf16[128,256]{1,0:T(8,128)(2,1)S(1)}, bf16[128,256]{1,0:T(8,128)(2,1)S(1)}, u32[]{:S(2)}, u32[]{:S(2)}) %collective-permute-start.13) | collective-permute-done | bytes 65568 | tf_op jit(solution)/shard_map/ppermute | solution.py:26
  41.8 0.7 %add_convert_fusion = bf16[128,256]{1,0:T(8,128)(2,1)} fusion(f32[128,256]{1,0:T(8,128)S(1)} %shard_map.63, bf16[128,256]{1,0:T(8,128)(2,1)S(1)} %fusion.5.refs_0_, f32[128,256]{1,0:T(8,128)S(1)} %get-tuple-element.29, bf16[128,256]{1,0:T(8,128)(2,1)S(1)} %collective-permute-done.13, f32[128]{0:T(128)S(1)} %fusion.7), kind=kLoop, calls=%fused_computation.6 | loop fusion | flops 294912 | bytes 459264 | tf_op jit(solution)/shard_map/convert_element_type | solution.py:244
  (9 shorter events, 0.1 us)
Async XLA Ops:
  0.0 4.0 %copy-start = (bf16[1024,2,128]{2,1,0:T(2,128)(2,1)S(1)}, bf16[1024,2,128]{2,1,0:T(2,128)(2,1)}, u32[]{:S(2)}) copy-start(bf16[1024,2,128]{2,1,0:T(2,128)(2,1)} %param.5) | copy-start | bytes 1572868
  0.0 10.2 %collective-permute-start.5 = (bf16[128,256]{1,0:T(8,128)(2,1)}, bf16[128,256]{1,0:T(8,128)(2,1)S(1)}, u32[]{:S(2)}, u32[]{:S(2)}) collective-permute-start(bf16[128,256]{1,0:T(8,128)(2,1)} %refs_0_.1), channel_id=1, source_target_pairs={{0,8},{2,10},{4,12},{6,14},{8,0},{10,2},{12,4},{14,6},{1,9},{3,11}... | collective-permute-start | bytes 196616 | tf_op jit(solution)/shard_map/ppermute | solution.py:26
  4.0 0.7 %copy-start.2 = (s32[8,2,1]{0,2,1:T(1,128)S(1)}, s32[8,2,1]{0,2,1:T(1,128)}, u32[]{:S(2)}) copy-start(s32[8,2,1]{0,2,1:T(1,128)} %param.6) | copy-start | bytes 196
  4.7 5.5 %copy-start.1 = (bf16[128,256]{1,0:T(8,128)(2,1)S(1)}, bf16[128,256]{1,0:T(8,128)(2,1)}, u32[]{:S(2)}) copy-start(bf16[128,256]{1,0:T(8,128)(2,1)} %refs_0_.1) | copy-start | bytes 196612
  5.7 7.6 %collective-permute-start = (bf16[2,2,128,128]{3,2,1,0:T(8,128)(2,1)S(1)}, bf16[2,2,128,128]{3,2,1,0:T(8,128)(2,1)S(1)}, u32[]{:S(2)}, u32[]{:S(2)}) collective-permute-start(bf16[2,2,128,128]{3,2,1,0:T(8,128)(2,1)S(1)} %get-tuple-element.19.refs_1_), channel_id=1, source_target_pairs={{0,4},{2,6},{4,0},{6,2},{8,12},{10,14},{12,8},{14,10},{1,5},{3,7},... | collective-permute-start | bytes 393224 | tf_op jit(solution)/shard_map/ppermute | solution.py:26
  7.4 12.1 %collective-permute-start.1 = (bf16[2,2,128,128]{3,2,1,0:T(8,128)(2,1)S(1)}, bf16[2,2,128,128]{3,2,1,0:T(8,128)(2,1)S(1)}, u32[]{:S(2)}, u32[]{:S(2)}) collective-permute-start(bf16[2,2,128,128]{3,2,1,0:T(8,128)(2,1)S(1)} %get-tuple-element.20.refs_2_), channel_id=1, source_target_pairs={{0,8},{2,10},{4,12},{6,14},{8,0},{10,2},{12,4},{14,6},{1,9},{3,11}... | collective-permute-start | bytes 393224 | tf_op jit(solution)/shard_map/ppermute | solution.py:26
  7.7 11.7 %collective-permute-start.2 = (bf16[2,2,128,128]{3,2,1,0:T(8,128)(2,1)S(1)}, bf16[2,2,128,128]{3,2,1,0:T(8,128)(2,1)S(1)}, u32[]{:S(2)}, u32[]{:S(2)}) collective-permute-start(bf16[2,2,128,128]{3,2,1,0:T(8,128)(2,1)S(1)} %get-tuple-element.21.refs_3_), channel_id=1, source_target_pairs={{0,12},{2,14},{4,8},{6,10},{8,4},{10,6},{12,0},{14,2},{1,13},{3,15... | collective-permute-start | bytes 393224 | tf_op jit(solution)/shard_map/ppermute | solution.py:26
  10.2 1.5 %collective-permute-start.3 = (bf16[4,2,128,128]{3,2,1,0:T(8,128)(2,1)S(1)}, bf16[4,2,128,128]{3,2,1,0:T(8,128)(2,1)S(1)}, u32[]{:S(2)}, u32[]{:S(2)}) collective-permute-start(bf16[4,2,128,128]{3,2,1,0:T(8,128)(2,1)S(1)} %get-tuple-element.22), channel_id=1, source_target_pairs={{0,1},{1,0},{2,3},{3,2},{4,5},{5,4},{6,7},{7,6},{8,9},{9,8},{10,11... | collective-permute-start | bytes 786440 | tf_op jit(solution)/shard_map/ppermute | solution.py:30
  10.2 10.4 %collective-permute-start.6 = (bf16[256,256]{1,0:T(8,128)(2,1)S(1)}, bf16[256,256]{1,0:T(8,128)(2,1)S(1)}, u32[]{:S(2)}, u32[]{:S(2)}) collective-permute-start(bf16[256,256]{1,0:T(8,128)(2,1)S(1)} %shard_map.58.refs_0_), channel_id=1, source_target_pairs={{0,4},{2,6},{4,0},{6,2},{8,12},{10,14},{12,8},{14,10},{1,5},{3,7},... | collective-permute-start | bytes 393224 | tf_op jit(solution)/shard_map/ppermute | solution.py:26
  11.7 9.0 %collective-permute-start.4 = (bf16[2,4,128,128]{3,2,1,0:T(8,128)(2,1)S(1)}, bf16[2,4,128,128]{3,2,1,0:T(8,128)(2,1)S(1)}, u32[]{:S(2)}, u32[]{:S(2)}) collective-permute-start(bf16[2,4,128,128]{3,2,1,0:T(8,128)(2,1)S(1)} %shard_map.57), channel_id=1, source_target_pairs={{0,2},{2,0},{4,6},{6,4},{8,10},{10,8},{12,14},{14,12},{1,3},{3,1},... | collective-permute-start | bytes 786440 | tf_op jit(solution)/shard_map/ppermute | solution.py:26
  20.7 1.6 %collective-permute-start.7 = (bf16[512,256]{1,0:T(8,128)(2,1)S(1)}, bf16[512,256]{1,0:T(8,128)(2,1)S(1)}, u32[]{:S(2)}, u32[]{:S(2)}) collective-permute-start(bf16[512,256]{1,0:T(8,128)(2,1)S(1)} %shard_map.59.refs_9_), channel_id=1, source_target_pairs={{0,1},{1,0},{2,3},{3,2},{4,5},{5,4},{6,7},{7,6},{8,9},{9,8},{10,11... | collective-permute-start | bytes 786440 | tf_op jit(solution)/shard_map/ppermute | solution.py:30
  22.6 4.4 %collective-permute-start.8 = (bf16[144,256]{1,0:T(8,128)(2,1)S(1)}, bf16[144,256]{1,0:T(8,128)(2,1)S(1)}, u32[]{:S(2)}, u32[]{:S(2)}) collective-permute-start(bf16[144,256]{1,0:T(8,128)(2,1)S(1)} %get-tuple-element.26), channel_id=1, source_target_pairs={{0,2},{2,0},{4,6},{6,4},{8,10},{10,8},{12,14},{14,12},{1,3},{3,1},... | collective-permute-start | bytes 221192 | tf_op jit(solution)/shard_map/ppermute | solution.py:26
  24.2 0.7 %copy-start.3 = (s32[128]{0:T(128)S(1)}, s32[128]{0:T(128)}, u32[]{:S(2)}) copy-start(s32[128]{0:T(128)} %param.8) | copy-start | bytes 1540
  24.2 0.7 %copy-start.4 = (s32[128]{0:T(128)S(1)}, s32[128]{0:T(128)}, u32[]{:S(2)}) copy-start(s32[128]{0:T(128)} %param.9) | copy-start | bytes 1540
  27.2 6.3 %collective-permute-start.9 = (bf16[128,256]{1,0:T(8,128)(2,1)S(1)}, bf16[128,256]{1,0:T(8,128)(2,1)S(1)}, u32[]{:S(2)}, u32[]{:S(2)}) collective-permute-start(bf16[128,256]{1,0:T(8,128)(2,1)S(1)} %fusion.5.refs_0_), channel_id=1, source_target_pairs={{0,12},{2,14},{4,8},{6,10},{8,4},{10,6},{12,0},{14,2},{1,13},{3,15... | collective-permute-start | bytes 196616 | tf_op jit(solution)/shard_map/ppermute | solution.py:26
  28.4 5.1 %collective-permute-start.10 = (bf16[128,256]{1,0:T(8,128)(2,1)S(1)}, bf16[128,256]{1,0:T(8,128)(2,1)S(1)}, u32[]{:S(2)}, u32[]{:S(2)}) collective-permute-start(bf16[128,256]{1,0:T(8,128)(2,1)S(1)} %fusion.5.refs_0_), channel_id=1, source_target_pairs={{0,4},{2,6},{4,0},{6,2},{8,12},{10,14},{12,8},{14,10},{1,5},{3,7},... | collective-permute-start | bytes 196616 | tf_op jit(solution)/shard_map/ppermute | solution.py:26
  28.8 6.7 %collective-permute-start.11 = (bf16[128,256]{1,0:T(8,128)(2,1)S(1)}, bf16[128,256]{1,0:T(8,128)(2,1)S(1)}, u32[]{:S(2)}, u32[]{:S(2)}) collective-permute-start(bf16[128,256]{1,0:T(8,128)(2,1)S(1)} %fusion.5.refs_0_), channel_id=1, source_target_pairs={{0,8},{2,10},{4,12},{6,14},{8,0},{10,2},{12,4},{14,6},{1,9},{3,11}... | collective-permute-start | bytes 196616 | tf_op jit(solution)/shard_map/ppermute | solution.py:26
  35.6 1.6 %collective-permute-start.12 = (bf16[512,256]{1,0:T(8,128)(2,1)S(1)}, bf16[512,256]{1,0:T(8,128)(2,1)S(1)}, u32[]{:S(2)}, u32[]{:S(2)}) collective-permute-start(bf16[512,256]{1,0:T(8,128)(2,1)S(1)} %shard_map.64.refs_9_), channel_id=1, source_target_pairs={{0,1},{1,0},{2,3},{3,2},{4,5},{5,4},{6,7},{7,6},{8,9},{9,8},{10,11... | collective-permute-start | bytes 786440 | tf_op jit(solution)/shard_map/ppermute | solution.py:30
  37.5 4.3 %collective-permute-start.13 = (bf16[128,256]{1,0:T(8,128)(2,1)S(1)}, bf16[128,256]{1,0:T(8,128)(2,1)S(1)}, u32[]{:S(2)}, u32[]{:S(2)}) collective-permute-start(bf16[128,256]{1,0:T(8,128)(2,1)S(1)} %get-tuple-element.30), channel_id=1, source_target_pairs={{0,2},{2,0},{4,6},{6,4},{8,10},{10,8},{12,14},{14,12},{1,3},{3,1},... | collective-permute-start | bytes 196616 | tf_op jit(solution)/shard_map/ppermute | solution.py:26

commit v14 on v13

--- a/solution.py
+++ b/solution.py
@@ -57,23 +57,16 @@
     row, col = lax.axis_index("row"), lax.axis_index("col")
     z, y = lax.div(row, y_count), lax.rem(row, y_count)
     width = tile.shape[1]
-    out_row = lax.broadcasted_iota(jnp.int32, (2 * width, 2 * width), 0)
-    in_row = lax.broadcasted_iota(jnp.int32, (2 * width, 2 * width), 1)
-    side = lax.bitwise_xor((out_row >= width).astype(jnp.int32), col)
-    spot = 2 * lax.rem(out_row, width) + side
-    sort = jnp.where(in_row == spot, 1.0, 0.0).astype(jnp.bfloat16)
     for k in range(z_count):
         for j in range(y_count):
             block = lax.bitwise_xor(z, k) * y_count + lax.bitwise_xor(y, j)
-            rows = tile[pl.ds(pl.multiple_of(block * 2 * width, 2 * width), 2 * width), :]
-            sides = jnp.dot(sort, rows, preferred_element_type=jnp.float32)
-            for i in range(2):
-                keep = live[lax.bitwise_xor(col, i), 0, block] == 1
-                piece = sides[i * width : (i + 1) * width]
-                piece = jnp.where(keep, piece, jnp.zeros_like(piece)).astype(jnp.bfloat16)
-                strips[k][i, j] = piece
-                if i == 1:
-                    other[k, j] = piece
+            rows = tile.at[pl.ds(pl.multiple_of(block * 2 * width, 2 * width), 2 * width)]
+            pair = []
+            for side in range(2):
+                piece = rows[pl.ds(side, width, stride=2), :]
+                pair.append(jnp.where(live[side, 0, block] == 1, piece, jnp.zeros_like(piece)))
+                strips[k][lax.bitwise_xor(col, side), j] = pair[-1]
+            other[k, j] = jnp.where(col == 0, pair[1], pair[0])
 
 
 def halves_kernel(z_count, *refs):
@@ -138,8 +131,10 @@
 
 
 def ours_kernel(order, y_count, first, *refs):
-    blocks, values, outs = refs[: 2 * len(order) + y_count - 1], refs[2 * len(order) + y_count - 1], refs[-y_count:]
-    values = values[...]
+    count = 2 * len(order) + y_count - 1
+    blocks, pieces, outs = refs[:count], refs[count:-y_count], refs[-y_count:]
+    pieces = pieces[:-1] if first else pieces
+    values = jnp.concatenate([piece[...] for piece in pieces], axis=0)
     depth, classes = values.shape
     width = depth // len(order)
     ones = jnp.ones((SUBLANES, depth), jnp.bfloat16)
@@ -153,12 +148,12 @@
             out[width:, :] = jnp.concatenate([sums] * (classes // width), axis=1)
 
 
-def theirs_kernel(order, y_count, first, *refs):
-    blocks, values, refs = refs[: 2 * len(order) + y_count - 1], refs[2 * len(order) + y_count - 1], refs[-2 * y_count :]
-    values = values[...]
+def theirs_kernel(order, y_count, wanted, first, *refs):
+    count = 2 * len(order) + y_count - 1
+    blocks, pieces, refs = refs[:count], refs[count : -2 * len(wanted)], refs[-2 * len(wanted) :]
+    values = jnp.concatenate([piece[...] for piece in pieces], axis=0)
     width = values.shape[0] // len(order)
-    for j in reversed(range(y_count)):
-        part, out = refs[j], refs[y_count + j]
+    for j, part, out in zip(wanted, refs[: len(wanted)], refs[len(wanted) :]):
         back, ahead = blocks_of(order, y_count, blocks, 1, j)
         total = part[:width, :] + product(back, values, (0, 0)) + product(ahead, values, (1, 0))
         out[:width, :] = total.astype(out.dtype)
@@ -215,8 +210,8 @@
         if step > 0:
             order = [0] + others_late(z_count)
             have = [current] + [swap_rows(current, k * y_count) for k in order[1:]]
-        values = join(have)
         first = step == 0
+        have = [join(have)]
         extra = SUBLANES if first else 0
         part = jax.ShapeDtypeStruct((width + extra, classes), jnp.float32)
         send = jax.ShapeDtypeStruct((width + 2 * extra, classes), jnp.bfloat16)
@@ -224,17 +219,16 @@
             lambda *refs: ours_kernel(order, y_count, first, *refs),
             [part] * y_count,
             *blocks,
-            values,
+            *have,
             *([mark] if first else []),
             flops=OURS_FLOPS if first else 0,
         )
-        total, *sends = call(
-            lambda *refs: theirs_kernel(order, y_count, first, *refs),
-            [part] + [send] * (y_count - 1),
-            *blocks,
-            swap_cores(values),
-            *parts,
+        have = [swap_cores(x) for x in have]
+        wanted = range(1, y_count)
+        sends = call(
+            lambda *refs: theirs_kernel(order, y_count, wanted, first, *refs), [send] * (y_count - 1), *blocks, *have, *parts[1:]
         )
+        (total,) = call(lambda *refs: theirs_kernel(order, y_count, [0], first, *refs), [part], *blocks, *have, parts[0])
         sends = [swap_rows(x, j + 1).astype(jnp.float32) for j, x in enumerate(sends)]
         spread = sum((x[:width] for x in sends), total[:width])
         if first:

time: 42.7 us -> 42.2 us (0.988)
  waiting for transfers between devices: 19 us -> 18.5 us
    ppermute x11, waiting for transfers between devices: 16 us -> 15.5 us  [swap_rows(): return lax.ppermute(value, 'row', [(i, i ^ shift) for i in range(count)])]
    pallas_call x12 -> x14, Pallas kernels: 2.66 us -> 2.71 us  [call(): pl.pallas_call(kernel, out_shape=out_shape, in_specs=[pl.BlockSpec(memory...]
  transfers between devices with their start and end apart: 14 -> 14, of which waited for: 9 -> 10; matrix products, arithmetic and copies ran while one was open for 0% -> 0% of each run, Pallas kernels for 5% -> 5%
where the time goes in v14:
time: 42.2 us; the launch traced here: 42.1 us
  starting transfers between devices  18.6 us (44%)
  waiting for transfers between devices  18.5 us (44%)
  Pallas kernels  2.71 us (6%)
  local copies, waits for them, and re-layouts  1.35 us (3%)
  other arithmetic  0.86 us (2%)
    ppermute x11, starting transfers between devices, swap_rows(): return lax.ppermute(value, 'row', [(i, i ^ shift) for i in range(count)])  18.4 us
    ppermute x11, waiting for transfers between devices, swap_rows(): return lax.ppermute(value, 'row', [(i, i ^ shift) for i in range(count)])  15.5 us
    ppermute x3, waiting for transfers between devices, swap_cores(): return lax.ppermute(value, 'col', [(0, 1), (1, 0)])  2.97 us
    pallas_call x14, Pallas kernels, call(): pl.pallas_call(kernel, out_shape=out_shape, in_specs=[pl.BlockSpec(memory...  2.71 us
    unnamed x10, local copies, waits for them, and re-layouts  1.35 us
  transfers between devices with their start and end apart: 14, of which 10 were waited for; matrix products, arithmetic and copies ran while one was open for 0% of the time, Pallas kernels for 5%

profile of v14, /device:TPU:0, one launch (start us, length us, event | category | flops | bytes accessed | tf_op | source)
XLA Modules:
  0.0 42.1 jit_solution(9668148551979159706)
XLA Ops:
  0.0 0.0 copy-start
  0.0 4.0 %collective-permute-start.5 = (bf16[128,256]{1,0:T(8,128)(2,1)}, bf16[128,256]{1,0:T(8,128)(2,1)S(1)}, u32[]{:S(2)}, u32[]{:S(2)}) collective-permute-start(bf16[128,256]{1,0:T(8,128)(2,1)} %refs_0_.1), channel_id=1, source_target_pairs={{0,8},{2,10},{4,12},{6,14},{8,0},{10,2},{12,4},{14,6},{1,9},{3,11}... | collective-permute-start | bytes 196616 | tf_op jit(solution)/shard_map/ppermute | solution.py:26
  4.0 0.0 copy-start.2
  4.0 0.0 copy-done
  4.0 0.7 %copy-done.2 = s32[8,2,1]{0,2,1:T(1,128)S(1)} copy-done((s32[8,2,1]{0,2,1:T(1,128)S(1)}, s32[8,2,1]{0,2,1:T(1,128)}, u32[]{:S(2)}) %copy-start.2) | copy-done | bytes 88
  4.7 0.0 copy-start.1
  4.7 0.7 %shard_map.56 = (bf16[2,2,128,128]{3,2,1,0:T(8,128)(2,1)S(1)}, bf16[2,2,128,128]{3,2,1,0:T(8,128)(2,1)S(1)}, bf16[2,2,128,128]{3,2,1,0:T(8,128)(2,1)S(1)}, bf16[...) custom-call(s32[2,1,8]{2,1,0:T(1,128)S(1)} %bitcast.13, bf16[2048,128]{1,0:T(8,128)(2,1)S(1)} %bitcast.12, ...), custom_call_target="tpu_custom_call" | custom-call | bytes 1314880 | tf_op jit(solution)/shard_map/pallas_call | solution.py:36
  5.4 1.6 %collective-permute-start = (bf16[2,2,128,128]{3,2,1,0:T(8,128)(2,1)S(1)}, bf16[2,2,128,128]{3,2,1,0:T(8,128)(2,1)S(1)}, u32[]{:S(2)}, u32[]{:S(2)}) collective-permute-start(bf16[2,2,128,128]{3,2,1,0:T(8,128)(2,1)S(1)} %get-tuple-element.15.refs_1_), channel_id=1, source_target_pairs={{0,4},{2,6},{4,0},{6,2},{8,12},{10,14},{12,8},{14,10},{1,5},{3,7},... | collective-permute-start | bytes 393224 | tf_op jit(solution)/shard_map/ppermute | solution.py:26
  7.1 0.4 collective-permute-start.1
  7.5 2.4 %collective-permute-start.2 = (bf16[2,2,128,128]{3,2,1,0:T(8,128)(2,1)S(1)}, bf16[2,2,128,128]{3,2,1,0:T(8,128)(2,1)S(1)}, u32[]{:S(2)}, u32[]{:S(2)}) collective-permute-start(bf16[2,2,128,128]{3,2,1,0:T(8,128)(2,1)S(1)} %get-tuple-element.17.refs_3_), channel_id=1, source_target_pairs={{0,12},{2,14},{4,8},{6,10},{8,4},{10,6},{12,0},{14,2},{1,13},{3,15... | collective-permute-start | bytes 393224 | tf_op jit(solution)/shard_map/ppermute | solution.py:26
  9.9 0.0 collective-permute-start.3
  9.9 0.0 collective-permute-done.5.refs_1_
  9.9 0.0 copy-done.1
  9.9 0.7 %collective-permute-start.6 = (bf16[256,256]{1,0:T(8,128)(2,1)S(1)}, bf16[256,256]{1,0:T(8,128)(2,1)S(1)}, u32[]{:S(2)}, u32[]{:S(2)}) collective-permute-start(bf16[256,256]{1,0:T(8,128)(2,1)S(1)} %shard_map.58.refs_0_), channel_id=1, source_target_pairs={{0,4},{2,6},{4,0},{6,2},{8,12},{10,14},{12,8},{14,10},{1,5},{3,7},... | collective-permute-start | bytes 393224 | tf_op jit(solution)/shard_map/ppermute | solution.py:26
  10.7 0.8 %collective-permute-done.3.refs_4_.refs_7_ = bf16[4,2,128,128]{3,2,1,0:T(8,128)(2,1)S(1)} collective-permute-done((bf16[4,2,128,128]{3,2,1,0:T(8,128)(2,1)S(1)}, bf16[4,2,128,128]{3,2,1,0:T(8,128)(2,1)S(1)}, u32[]{:S(2)}, u32[]{:S(2)}) %collective-permute-start.3) | collective-permute-done | bytes 262176 | tf_op jit(solution)/shard_map/ppermute | solution.py:30
  11.5 1.6 %collective-permute-start.4 = (bf16[2,4,128,128]{3,2,1,0:T(8,128)(2,1)S(1)}, bf16[2,4,128,128]{3,2,1,0:T(8,128)(2,1)S(1)}, u32[]{:S(2)}, u32[]{:S(2)}) collective-permute-start(bf16[2,4,128,128]{3,2,1,0:T(8,128)(2,1)S(1)} %shard_map.57), channel_id=1, source_target_pairs={{0,2},{2,0},{4,6},{6,4},{8,10},{10,8},{12,14},{14,12},{1,3},{3,1},... | collective-permute-start | bytes 786440 | tf_op jit(solution)/shard_map/ppermute | solution.py:26
  13.0 0.0 collective-permute-done.refs_0_.refs_4_
  13.0 6.1 %collective-permute-done.1.refs_1_.refs_5_ = bf16[2,2,128,128]{3,2,1,0:T(8,128)(2,1)S(1)} collective-permute-done((bf16[2,2,128,128]{3,2,1,0:T(8,128)(2,1)S(1)}, bf16[2,2,128,128]{3,2,1,0:T(8,128)(2,1)S(1)}, u32[]{:S(2)}, u32[]{:S(2)}) %collective-permute-start.1) | collective-permute-done | bytes 131104 | tf_op jit(solution)/shard_map/ppermute | solution.py:26
  19.2 0.0 collective-permute-done.2.refs_2_.refs_6_
  19.2 1.2 %collective-permute-done.6.refs_1_ = bf16[256,256]{1,0:T(8,128)(2,1)S(1)} collective-permute-done((bf16[256,256]{1,0:T(8,128)(2,1)S(1)}, bf16[256,256]{1,0:T(8,128)(2,1)S(1)}, u32[]{:S(2)}, u32[]{:S(2)}) %collective-permute-start.6) | collective-permute-done | bytes 131104 | tf_op jit(solution)/shard_map/ppermute | solution.py:26
  20.3 0.1 collective-permute-start.7
  20.4 0.0 collective-permute-done.4.refs_8_
  20.4 0.5 %shard_map.61 = (f32[136,256]{1,0:T(8,128)S(1)}, f32[136,256]{1,0:T(8,128)S(1)}) custom-call(bf16[2,2,128,128]{3,2,1,0:T(8,128)(2,1)S(1)} %get-tuple-element.14.refs_0_, bf16[2,2,128,128]{3,2,1,0:T(8,128)(2,1)S(1)} %get-tuple-element.15.refs_1_, bf16[2,2,128,128]{3,2,1,0:T(8,128)(2,1)S(1)} %get-tuple-element.16.refs_2_, ...), custom_call_target="tpu_custom_call" | custom-call | flops 3000000000 | bytes 1986560 | tf_op jit(solution)/shard_map/pallas_call | solution.py:36
  20.9 1.0 %collective-permute-done.7.refs_9_ = bf16[512,256]{1,0:T(8,128)(2,1)S(1)} collective-permute-done((bf16[512,256]{1,0:T(8,128)(2,1)S(1)}, bf16[512,256]{1,0:T(8,128)(2,1)S(1)}, u32[]{:S(2)}, u32[]{:S(2)}) %collective-permute-start.7) | collective-permute-done | bytes 262176 | tf_op jit(solution)/shard_map/ppermute | solution.py:30
  21.9 0.3 shard_map.63
  22.2 1.6 %collective-permute-start.8 = (bf16[144,256]{1,0:T(8,128)(2,1)S(1)}, bf16[144,256]{1,0:T(8,128)(2,1)S(1)}, u32[]{:S(2)}, u32[]{:S(2)}) collective-permute-start(bf16[144,256]{1,0:T(8,128)(2,1)S(1)} %shard_map.63), channel_id=1, source_target_pairs={{0,2},{2,0},{4,6},{6,4},{8,10},{10,8},{12,14},{14,12},{1,3},{3,1},... | collective-permute-start | bytes 221192 | tf_op jit(solution)/shard_map/ppermute | solution.py:26
  23.8 0.0 copy-start.3
  23.8 0.0 copy-start.4
  23.8 0.7 %copy-done.3 = s32[128]{0:T(128)S(1)} copy-done((s32[128]{0:T(128)S(1)}, s32[128]{0:T(128)}, u32[]{:S(2)}) %copy-start.3) | copy-done | bytes 536
  24.4 0.0 copy-done.4
  24.5 0.1 shard_map.64
  24.6 0.3 shard_map.62
  24.8 1.8 %collective-permute-done.8 = bf16[144,256]{1,0:T(8,128)(2,1)S(1)} collective-permute-done((bf16[144,256]{1,0:T(8,128)(2,1)S(1)}, bf16[144,256]{1,0:T(8,128)(2,1)S(1)}, u32[]{:S(2)}, u32[]{:S(2)}) %collective-permute-start.8) | collective-permute-done | bytes 73760 | tf_op jit(solution)/shard_map/ppermute | solution.py:26
  26.7 0.1 fusion.5.refs_0_
  26.8 1.6 %collective-permute-start.9 = (bf16[128,256]{1,0:T(8,128)(2,1)S(1)}, bf16[128,256]{1,0:T(8,128)(2,1)S(1)}, u32[]{:S(2)}, u32[]{:S(2)}) collective-permute-start(bf16[128,256]{1,0:T(8,128)(2,1)S(1)} %fusion.5.refs_0_), channel_id=1, source_target_pairs={{0,12},{2,14},{4,8},{6,10},{8,4},{10,6},{12,0},{14,2},{1,13},{3,15... | collective-permute-start | bytes 196616 | tf_op jit(solution)/shard_map/ppermute | solution.py:26
  28.3 0.4 collective-permute-start.10
  28.7 2.5 %collective-permute-start.11 = (bf16[128,256]{1,0:T(8,128)(2,1)S(1)}, bf16[128,256]{1,0:T(8,128)(2,1)S(1)}, u32[]{:S(2)}, u32[]{:S(2)}) collective-permute-start(bf16[128,256]{1,0:T(8,128)(2,1)S(1)} %fusion.5.refs_0_), channel_id=1, source_target_pairs={{0,8},{2,10},{4,12},{6,14},{8,0},{10,2},{12,4},{14,6},{1,9},{3,11}... | collective-permute-start | bytes 196616 | tf_op jit(solution)/shard_map/ppermute | solution.py:26
  31.2 2.0 %collective-permute-done.9.refs_1_ = bf16[128,256]{1,0:T(8,128)(2,1)S(1)} collective-permute-done((bf16[128,256]{1,0:T(8,128)(2,1)S(1)}, bf16[128,256]{1,0:T(8,128)(2,1)S(1)}, u32[]{:S(2)}, u32[]{:S(2)}) %collective-permute-start.9) | collective-permute-done | bytes 65568 | tf_op jit(solution)/shard_map/ppermute | solution.py:26
  33.3 0.1 collective-permute-done.10.refs_2_
  33.4 1.8 %collective-permute-done.11.refs_3_ = bf16[128,256]{1,0:T(8,128)(2,1)S(1)} collective-permute-done((bf16[128,256]{1,0:T(8,128)(2,1)S(1)}, bf16[128,256]{1,0:T(8,128)(2,1)S(1)}, u32[]{:S(2)}, u32[]{:S(2)}) %collective-permute-start.11) | collective-permute-done | bytes 65568 | tf_op jit(solution)/shard_map/ppermute | solution.py:26
  35.2 0.1 collective-permute-start.12
  35.2 0.3 shard_map.66
  35.6 1.2 %collective-permute-done.12.refs_9_ = bf16[512,256]{1,0:T(8,128)(2,1)S(1)} collective-permute-done((bf16[512,256]{1,0:T(8,128)(2,1)S(1)}, bf16[512,256]{1,0:T(8,128)(2,1)S(1)}, u32[]{:S(2)}, u32[]{:S(2)}) %collective-permute-start.12) | collective-permute-done | bytes 262176 | tf_op jit(solution)/shard_map/ppermute | solution.py:30
  36.8 0.3 shard_map.68
  37.0 1.6 %collective-permute-start.13 = (bf16[128,256]{1,0:T(8,128)(2,1)S(1)}, bf16[128,256]{1,0:T(8,128)(2,1)S(1)}, u32[]{:S(2)}, u32[]{:S(2)}) collective-permute-start(bf16[128,256]{1,0:T(8,128)(2,1)S(1)} %shard_map.68), channel_id=1, source_target_pairs={{0,2},{2,0},{4,6},{6,4},{8,10},{10,8},{12,14},{14,12},{1,3},{3,1},... | collective-permute-start | bytes 196616 | tf_op jit(solution)/shard_map/ppermute | solution.py:26
  38.6 0.3 shard_map.67
  38.9 2.5 %collective-permute-done.13 = bf16[128,256]{1,0:T(8,128)(2,1)S(1)} collective-permute-done((bf16[128,256]{1,0:T(8,128)(2,1)S(1)}, bf16[128,256]{1,0:T(8,128)(2,1)S(1)}, u32[]{:S(2)}, u32[]{:S(2)}) %collective-permute-start.13) | collective-permute-done | bytes 65568 | tf_op jit(solution)/shard_map/ppermute | solution.py:26
  41.4 0.7 %add_convert_fusion = bf16[128,256]{1,0:T(8,128)(2,1)} fusion(f32[128,256]{1,0:T(8,128)S(1)} %shard_map.64, bf16[128,256]{1,0:T(8,128)(2,1)S(1)} %fusion.5.refs_0_, f32[128,256]{1,0:T(8,128)S(1)} %shard_map.67, bf16[128,256]{1,0:T(8,128)(2,1)S(1)} %collective-permute-done.13, f32[128]{0:T(128)S(1)} %fusion.8), kind=kLoop, calls=%fused_computation.6 | loop fusion | flops 294912 | bytes 459264 | tf_op jit(solution)/shard_map/convert_element_type | solution.py:238
  (9 shorter events, 0.1 us)
Async XLA Ops:
  0.0 4.0 %copy-start = (bf16[1024,2,128]{2,1,0:T(2,128)(2,1)S(1)}, bf16[1024,2,128]{2,1,0:T(2,128)(2,1)}, u32[]{:S(2)}) copy-start(bf16[1024,2,128]{2,1,0:T(2,128)(2,1)} %param.5) | copy-start | bytes 1572868
  0.0 9.9 %collective-permute-start.5 = (bf16[128,256]{1,0:T(8,128)(2,1)}, bf16[128,256]{1,0:T(8,128)(2,1)S(1)}, u32[]{:S(2)}, u32[]{:S(2)}) collective-permute-start(bf16[128,256]{1,0:T(8,128)(2,1)} %refs_0_.1), channel_id=1, source_target_pairs={{0,8},{2,10},{4,12},{6,14},{8,0},{10,2},{12,4},{14,6},{1,9},{3,11}... | collective-permute-start | bytes 196616 | tf_op jit(solution)/shard_map/ppermute | solution.py:26
  4.0 0.7 %copy-start.2 = (s32[8,2,1]{0,2,1:T(1,128)S(1)}, s32[8,2,1]{0,2,1:T(1,128)}, u32[]{:S(2)}) copy-start(s32[8,2,1]{0,2,1:T(1,128)} %param.6) | copy-start | bytes 196
  4.7 5.2 %copy-start.1 = (bf16[128,256]{1,0:T(8,128)(2,1)S(1)}, bf16[128,256]{1,0:T(8,128)(2,1)}, u32[]{:S(2)}) copy-start(bf16[128,256]{1,0:T(8,128)(2,1)} %refs_0_.1) | copy-start | bytes 196612
  5.4 7.6 %collective-permute-start = (bf16[2,2,128,128]{3,2,1,0:T(8,128)(2,1)S(1)}, bf16[2,2,128,128]{3,2,1,0:T(8,128)(2,1)S(1)}, u32[]{:S(2)}, u32[]{:S(2)}) collective-permute-start(bf16[2,2,128,128]{3,2,1,0:T(8,128)(2,1)S(1)} %get-tuple-element.15.refs_1_), channel_id=1, source_target_pairs={{0,4},{2,6},{4,0},{6,2},{8,12},{10,14},{12,8},{14,10},{1,5},{3,7},... | collective-permute-start | bytes 393224 | tf_op jit(solution)/shard_map/ppermute | solution.py:26
  7.1 12.1 %collective-permute-start.1 = (bf16[2,2,128,128]{3,2,1,0:T(8,128)(2,1)S(1)}, bf16[2,2,128,128]{3,2,1,0:T(8,128)(2,1)S(1)}, u32[]{:S(2)}, u32[]{:S(2)}) collective-permute-start(bf16[2,2,128,128]{3,2,1,0:T(8,128)(2,1)S(1)} %get-tuple-element.16.refs_2_), channel_id=1, source_target_pairs={{0,8},{2,10},{4,12},{6,14},{8,0},{10,2},{12,4},{14,6},{1,9},{3,11}... | collective-permute-start | bytes 393224 | tf_op jit(solution)/shard_map/ppermute | solution.py:26
  7.5 11.7 %collective-permute-start.2 = (bf16[2,2,128,128]{3,2,1,0:T(8,128)(2,1)S(1)}, bf16[2,2,128,128]{3,2,1,0:T(8,128)(2,1)S(1)}, u32[]{:S(2)}, u32[]{:S(2)}) collective-permute-start(bf16[2,2,128,128]{3,2,1,0:T(8,128)(2,1)S(1)} %get-tuple-element.17.refs_3_), channel_id=1, source_target_pairs={{0,12},{2,14},{4,8},{6,10},{8,4},{10,6},{12,0},{14,2},{1,13},{3,15... | collective-permute-start | bytes 393224 | tf_op jit(solution)/shard_map/ppermute | solution.py:26
  9.9 1.5 %collective-permute-start.3 = (bf16[4,2,128,128]{3,2,1,0:T(8,128)(2,1)S(1)}, bf16[4,2,128,128]{3,2,1,0:T(8,128)(2,1)S(1)}, u32[]{:S(2)}, u32[]{:S(2)}) collective-permute-start(bf16[4,2,128,128]{3,2,1,0:T(8,128)(2,1)S(1)} %get-tuple-element.18), channel_id=1, source_target_pairs={{0,1},{1,0},{2,3},{3,2},{4,5},{5,4},{6,7},{7,6},{8,9},{9,8},{10,11... | collective-permute-start | bytes 786440 | tf_op jit(solution)/shard_map/ppermute | solution.py:30
  9.9 10.4 %collective-permute-start.6 = (bf16[256,256]{1,0:T(8,128)(2,1)S(1)}, bf16[256,256]{1,0:T(8,128)(2,1)S(1)}, u32[]{:S(2)}, u32[]{:S(2)}) collective-permute-start(bf16[256,256]{1,0:T(8,128)(2,1)S(1)} %shard_map.58.refs_0_), channel_id=1, source_target_pairs={{0,4},{2,6},{4,0},{6,2},{8,12},{10,14},{12,8},{14,10},{1,5},{3,7},... | collective-permute-start | bytes 393224 | tf_op jit(solution)/shard_map/ppermute | solution.py:26
  11.5 9.0 %collective-permute-start.4 = (bf16[2,4,128,128]{3,2,1,0:T(8,128)(2,1)S(1)}, bf16[2,4,128,128]{3,2,1,0:T(8,128)(2,1)S(1)}, u32[]{:S(2)}, u32[]{:S(2)}) collective-permute-start(bf16[2,4,128,128]{3,2,1,0:T(8,128)(2,1)S(1)} %shard_map.57), channel_id=1, source_target_pairs={{0,2},{2,0},{4,6},{6,4},{8,10},{10,8},{12,14},{14,12},{1,3},{3,1},... | collective-permute-start | bytes 786440 | tf_op jit(solution)/shard_map/ppermute | solution.py:26
  20.3 1.6 %collective-permute-start.7 = (bf16[512,256]{1,0:T(8,128)(2,1)S(1)}, bf16[512,256]{1,0:T(8,128)(2,1)S(1)}, u32[]{:S(2)}, u32[]{:S(2)}) collective-permute-start(bf16[512,256]{1,0:T(8,128)(2,1)S(1)} %shard_map.59.refs_9_), channel_id=1, source_target_pairs={{0,1},{1,0},{2,3},{3,2},{4,5},{5,4},{6,7},{7,6},{8,9},{9,8},{10,11... | collective-permute-start | bytes 786440 | tf_op jit(solution)/shard_map/ppermute | solution.py:30
  22.2 4.4 %collective-permute-start.8 = (bf16[144,256]{1,0:T(8,128)(2,1)S(1)}, bf16[144,256]{1,0:T(8,128)(2,1)S(1)}, u32[]{:S(2)}, u32[]{:S(2)}) collective-permute-start(bf16[144,256]{1,0:T(8,128)(2,1)S(1)} %shard_map.63), channel_id=1, source_target_pairs={{0,2},{2,0},{4,6},{6,4},{8,10},{10,8},{12,14},{14,12},{1,3},{3,1},... | collective-permute-start | bytes 221192 | tf_op jit(solution)/shard_map/ppermute | solution.py:26
  23.8 0.7 %copy-start.3 = (s32[128]{0:T(128)S(1)}, s32[128]{0:T(128)}, u32[]{:S(2)}) copy-start(s32[128]{0:T(128)} %param.8) | copy-start | bytes 1540
  23.8 0.7 %copy-start.4 = (s32[128]{0:T(128)S(1)}, s32[128]{0:T(128)}, u32[]{:S(2)}) copy-start(s32[128]{0:T(128)} %param.9) | copy-start | bytes 1540
  26.8 6.5 %collective-permute-start.9 = (bf16[128,256]{1,0:T(8,128)(2,1)S(1)}, bf16[128,256]{1,0:T(8,128)(2,1)S(1)}, u32[]{:S(2)}, u32[]{:S(2)}) collective-permute-start(bf16[128,256]{1,0:T(8,128)(2,1)S(1)} %fusion.5.refs_0_), channel_id=1, source_target_pairs={{0,12},{2,14},{4,8},{6,10},{8,4},{10,6},{12,0},{14,2},{1,13},{3,15... | collective-permute-start | bytes 196616 | tf_op jit(solution)/shard_map/ppermute | solution.py:26
  28.3 5.0 %collective-permute-start.10 = (bf16[128,256]{1,0:T(8,128)(2,1)S(1)}, bf16[128,256]{1,0:T(8,128)(2,1)S(1)}, u32[]{:S(2)}, u32[]{:S(2)}) collective-permute-start(bf16[128,256]{1,0:T(8,128)(2,1)S(1)} %fusion.5.refs_0_), channel_id=1, source_target_pairs={{0,4},{2,6},{4,0},{6,2},{8,12},{10,14},{12,8},{14,10},{1,5},{3,7},... | collective-permute-start | bytes 196616 | tf_op jit(solution)/shard_map/ppermute | solution.py:26
  28.7 6.4 %collective-permute-start.11 = (bf16[128,256]{1,0:T(8,128)(2,1)S(1)}, bf16[128,256]{1,0:T(8,128)(2,1)S(1)}, u32[]{:S(2)}, u32[]{:S(2)}) collective-permute-start(bf16[128,256]{1,0:T(8,128)(2,1)S(1)} %fusion.5.refs_0_), channel_id=1, source_target_pairs={{0,8},{2,10},{4,12},{6,14},{8,0},{10,2},{12,4},{14,6},{1,9},{3,11}... | collective-permute-start | bytes 196616 | tf_op jit(solution)/shard_map/ppermute | solution.py:26
  35.2 1.6 %collective-permute-start.12 = (bf16[512,256]{1,0:T(8,128)(2,1)S(1)}, bf16[512,256]{1,0:T(8,128)(2,1)S(1)}, u32[]{:S(2)}, u32[]{:S(2)}) collective-permute-start(bf16[512,256]{1,0:T(8,128)(2,1)S(1)} %shard_map.65.refs_9_), channel_id=1, source_target_pairs={{0,1},{1,0},{2,3},{3,2},{4,5},{5,4},{6,7},{7,6},{8,9},{9,8},{10,11... | collective-permute-start | bytes 786440 | tf_op jit(solution)/shard_map/ppermute | solution.py:30
  37.0 4.3 %collective-permute-start.13 = (bf16[128,256]{1,0:T(8,128)(2,1)S(1)}, bf16[128,256]{1,0:T(8,128)(2,1)S(1)}, u32[]{:S(2)}, u32[]{:S(2)}) collective-permute-start(bf16[128,256]{1,0:T(8,128)(2,1)S(1)} %shard_map.68), channel_id=1, source_target_pairs={{0,2},{2,0},{4,6},{6,4},{8,10},{10,8},{12,14},{14,12},{1,3},{3,1},... | collective-permute-start | bytes 196616 | tf_op jit(solution)/shard_map/ppermute | solution.py:26

commit v15 on v14

--- a/solution.py
+++ b/solution.py
@@ -13,6 +13,7 @@
 PAIR_FLOPS = 4_000_000_000
 STRIPS_FLOPS = 3_000_000_000
 OURS_FLOPS = 3_000_000_000
+LAST_FLOPS = 2_000_000_000
 MIB = 1024 * 1024
 
 
@@ -49,11 +50,11 @@
 
 def others_late(count):
     half = count // 2
-    return list(range(half + 1, count)) + list(range(1, half)) + [half]
+    return list(range(1, half)) + list(range(half + 1, count)) + [half]
 
 
 def prepare_kernel(z_count, y_count, live, tile, lead, *outs):
-    strips, other = outs[:z_count], outs[z_count]
+    strips = outs
     row, col = lax.axis_index("row"), lax.axis_index("col")
     z, y = lax.div(row, y_count), lax.rem(row, y_count)
     width = tile.shape[1]
@@ -61,12 +62,16 @@
         for j in range(y_count):
             block = lax.bitwise_xor(z, k) * y_count + lax.bitwise_xor(y, j)
             rows = tile.at[pl.ds(pl.multiple_of(block * 2 * width, 2 * width), 2 * width)]
-            pair = []
             for side in range(2):
                 piece = rows[pl.ds(side, width, stride=2), :]
-                pair.append(jnp.where(live[side, 0, block] == 1, piece, jnp.zeros_like(piece)))
-                strips[k][lax.bitwise_xor(col, side), j] = pair[-1]
-            other[k, j] = jnp.where(col == 0, pair[1], pair[0])
+                keep = live[side, 0, block] == 1
+                strips[k][lax.bitwise_xor(col, side), j] = jnp.where(keep, piece, jnp.zeros_like(piece))
+
+
+def other_kernel(*refs):
+    strips, out = refs[:-1], refs[-1]
+    for k, strip in enumerate(strips):
+        out[k] = strip[1]
 
 
 def halves_kernel(z_count, *refs):
@@ -176,15 +181,16 @@
 
     strip = jax.ShapeDtypeStruct((2, y_count, width, width), jnp.bfloat16)
     half = jax.ShapeDtypeStruct((2, z_count, width, width), jnp.bfloat16)
-    *sent, other = call(
+    sent = call(
         lambda *refs: prepare_kernel(z_count, y_count, *refs),
-        [strip] * z_count + [jax.ShapeDtypeStruct((z_count, y_count, width, width), jnp.bfloat16)],
+        [strip] * z_count,
         block_live.transpose(1, 2, 0),
         affinity.reshape(stripe * sides, width),
         call(lead_kernel, jax.ShapeDtypeStruct((SUBLANES, width), jnp.float32), flops=LEAD_FLOPS),
         smem=1,
     )
-    from_core = swap_cores(other)
+    other = jax.ShapeDtypeStruct((z_count, y_count, width, width), jnp.bfloat16)
+    from_core = swap_cores(call(other_kernel, other, *sent))
     halves = call(lambda *refs: halves_kernel(z_count, *refs), [half] * (y_count - 1), *sent, from_core)
     halves = [swap_rows(x, j + 1) for j, x in enumerate(halves)]
     arrived = {k: swap_rows(sent[k], k * y_count) for k in others(z_count)}
@@ -211,7 +217,7 @@
             order = [0] + others_late(z_count)
             have = [current] + [swap_rows(current, k * y_count) for k in order[1:]]
         first = step == 0
-        have = [join(have)]
+        have = [join(have)] if first else [join(have[:-1]), join(have[-1:], LAST_FLOPS)]
         extra = SUBLANES if first else 0
         part = jax.ShapeDtypeStruct((width + extra, classes), jnp.float32)
         send = jax.ShapeDtypeStruct((width + 2 * extra, classes), jnp.bfloat16)

time: 42.2 us -> 41.9 us (level)
  waiting for transfers between devices: 18.5 us -> 17.3 us
  local copies, waits for them, and re-layouts: 1.35 us -> 2.08 us
    ppermute x3 -> x4, waiting for transfers between devices: 2.97 us -> 1.96 us  [swap_cores(): return lax.ppermute(value, 'col', [(0, 1), (1, 0)])]
    unnamed x10, local copies, waits for them, and re-layouts: 1.35 us -> 2.08 us
    pallas_call x14 -> x16, Pallas kernels: 2.71 us -> 2.69 us  [call(): pl.pallas_call(kernel, out_shape=out_shape, in_specs=[pl.BlockSpec(memory...]
  transfers between devices with their start and end apart: 14 -> 15, of which waited for: 10 -> 9; matrix products, arithmetic and copies ran while one was open for 0% -> 0% of each run, Pallas kernels for 5% -> 5%
where the time goes in v15:
time: 41.9 us; the launch traced here: 41.7 us
  starting transfers between devices  18.7 us (45%)
  waiting for transfers between devices  17.3 us (41%)
  Pallas kernels  2.69 us (6%)
  local copies, waits for them, and re-layouts  2.08 us (5%)
  other arithmetic  0.86 us (2%)
    ppermute x11, starting transfers between devices, swap_rows(): return lax.ppermute(value, 'row', [(i, i ^ shift) for i in range(count)])  18.4 us
    ppermute x11, waiting for transfers between devices, swap_rows(): return lax.ppermute(value, 'row', [(i, i ^ shift) for i in range(count)])  15.3 us
    pallas_call x16, Pallas kernels, call(): pl.pallas_call(kernel, out_shape=out_shape, in_specs=[pl.BlockSpec(memory...  2.69 us
    unnamed x10, local copies, waits for them, and re-layouts  2.08 us
    ppermute x4, waiting for transfers between devices, swap_cores(): return lax.ppermute(value, 'col', [(0, 1), (1, 0)])  1.96 us
  transfers between devices with their start and end apart: 15, of which 9 were waited for; matrix products, arithmetic and copies ran while one was open for 0% of the time, Pallas kernels for 5%

profile of v15, /device:TPU:0, one launch (start us, length us, event | category | flops | bytes accessed | tf_op | source)
XLA Modules:
  0.0 41.7 jit_solution(13047160583221203927)
XLA Ops:
  0.0 0.0 copy-start
  0.0 4.0 %collective-permute-start.5 = (bf16[128,256]{1,0:T(8,128)(2,1)}, bf16[128,256]{1,0:T(8,128)(2,1)S(1)}, u32[]{:S(2)}, u32[]{:S(2)}) collective-permute-start(bf16[128,256]{1,0:T(8,128)(2,1)} %refs_0_.1), channel_id=1, source_target_pairs={{0,8},{2,10},{4,12},{6,14},{8,0},{10,2},{12,4},{14,6},{1,9},{3,11}... | collective-permute-start | bytes 196616 | tf_op jit(solution)/shard_map/ppermute | solution.py:27
  4.0 0.0 copy-start.2
  4.0 0.0 copy-done
  4.0 0.7 %copy-done.2 = s32[8,2,1]{0,2,1:T(1,128)S(1)} copy-done((s32[8,2,1]{0,2,1:T(1,128)S(1)}, s32[8,2,1]{0,2,1:T(1,128)}, u32[]{:S(2)}) %copy-start.2) | copy-done | bytes 88
  4.7 0.7 %shard_map.56 = (bf16[2,2,128,128]{3,2,1,0:T(8,128)(2,1)S(1)}, bf16[2,2,128,128]{3,2,1,0:T(8,128)(2,1)S(1)}, bf16[2,2,128,128]{3,2,1,0:T(8,128)(2,1)S(1)}, bf16[2,2,128,128]{3,2,1,0:T(8,128)(2,1)S(1)}) custom-call(s32[2,1,8]{2,1,0:T(1,128)S(1)} %bitcast.13, bf16[2048,128]{1,0:T(8,128)(2,1)S(1)} %bitcast.12, f32[8,128]{1,0:T(8,128)S(1)} %shard_map.55.refs_2_), custom_call_target="tpu_custom_call" | custom-call | bytes 1052736 | tf_op jit(solution)/shard_map/pallas_call | solution.py:37
  5.4 1.6 %collective-permute-start = (bf16[2,2,128,128]{3,2,1,0:T(8,128)(2,1)S(1)}, bf16[2,2,128,128]{3,2,1,0:T(8,128)(2,1)S(1)}, u32[]{:S(2)}, u32[]{:S(2)}) collective-permute-start(bf16[2,2,128,128]{3,2,1,0:T(8,128)(2,1)S(1)} %get-tuple-element.14.refs_1_), channel_id=1, source_target_pairs={{0,4},{2,6},{4,0},{6,2},{8,12},{10,14},{12,8},{14,10},{1,5},{3,7},... | collective-permute-start | bytes 393224 | tf_op jit(solution)/shard_map/ppermute | solution.py:27
  7.0 0.4 collective-permute-start.1
  7.4 2.4 %collective-permute-start.2 = (bf16[2,2,128,128]{3,2,1,0:T(8,128)(2,1)S(1)}, bf16[2,2,128,128]{3,2,1,0:T(8,128)(2,1)S(1)}, u32[]{:S(2)}, u32[]{:S(2)}) collective-permute-start(bf16[2,2,128,128]{3,2,1,0:T(8,128)(2,1)S(1)} %get-tuple-element.16.refs_3_), channel_id=1, source_target_pairs={{0,12},{2,14},{4,8},{6,10},{8,4},{10,6},{12,0},{14,2},{1,13},{3,15... | collective-permute-start | bytes 393224 | tf_op jit(solution)/shard_map/ppermute | solution.py:27
  9.9 0.0 copy-start.1
  9.9 0.1 collective-permute-start.3
  10.0 0.0 collective-permute-done.5.refs_1_
  10.0 0.7 %copy-done.1 = bf16[128,256]{1,0:T(8,128)(2,1)S(1)} copy-done((bf16[128,256]{1,0:T(8,128)(2,1)S(1)}, bf16[128,256]{1,0:T(8,128)(2,1)}, u32[]{:S(2)}) %copy-start.1) | copy-done | bytes 65560
  10.7 0.7 %collective-permute-start.6 = (bf16[256,256]{1,0:T(8,128)(2,1)S(1)}, bf16[256,256]{1,0:T(8,128)(2,1)S(1)}, u32[]{:S(2)}, u32[]{:S(2)}) collective-permute-start(bf16[256,256]{1,0:T(8,128)(2,1)S(1)} %shard_map.59.refs_0_), channel_id=1, source_target_pairs={{0,4},{2,6},{4,0},{6,2},{8,12},{10,14},{12,8},{14,10},{1,5},{3,7},... | collective-permute-start | bytes 393224 | tf_op jit(solution)/shard_map/ppermute | solution.py:27
  11.5 0.0 collective-permute-done.3.refs_4_.refs_7_
  11.5 1.6 %collective-permute-start.4 = (bf16[2,4,128,128]{3,2,1,0:T(8,128)(2,1)S(1)}, bf16[2,4,128,128]{3,2,1,0:T(8,128)(2,1)S(1)}, u32[]{:S(2)}, u32[]{:S(2)}) collective-permute-start(bf16[2,4,128,128]{3,2,1,0:T(8,128)(2,1)S(1)} %shard_map.58), channel_id=1, source_target_pairs={{0,2},{2,0},{4,6},{6,4},{8,10},{10,8},{12,14},{14,12},{1,3},{3,1},... | collective-permute-start | bytes 786440 | tf_op jit(solution)/shard_map/ppermute | solution.py:27
  13.1 0.0 collective-permute-done.refs_0_.refs_4_
  13.1 6.0 %collective-permute-done.1.refs_1_.refs_5_ = bf16[2,2,128,128]{3,2,1,0:T(8,128)(2,1)S(1)} collective-permute-done((bf16[2,2,128,128]{3,2,1,0:T(8,128)(2,1)S(1)}, bf16[2,2,128,128]{3,2,1,0:T(8,128)(2,1)S(1)}, u32[]{:S(2)}, u32[]{:S(2)}) %collective-permute-start.1) | collective-permute-done | bytes 131104 | tf_op jit(solution)/shard_map/ppermute | solution.py:27
  19.1 0.0 collective-permute-done.2.refs_2_.refs_6_
  19.1 1.2 %collective-permute-done.6.refs_1_ = bf16[256,256]{1,0:T(8,128)(2,1)S(1)} collective-permute-done((bf16[256,256]{1,0:T(8,128)(2,1)S(1)}, bf16[256,256]{1,0:T(8,128)(2,1)S(1)}, u32[]{:S(2)}, u32[]{:S(2)}) %collective-permute-start.6) | collective-permute-done | bytes 131104 | tf_op jit(solution)/shard_map/ppermute | solution.py:27
  20.3 0.1 collective-permute-start.7
  20.4 0.0 collective-permute-done.4.refs_8_
  20.4 0.5 %shard_map.62 = (f32[136,256]{1,0:T(8,128)S(1)}, f32[136,256]{1,0:T(8,128)S(1)}) custom-call(bf16[2,2,128,128]{3,2,1,0:T(8,128)(2,1)S(1)} %get-tuple-element.13.refs_0_, bf16[2,2,128,128]{3,2,1,0:T(8,128)(2,1)S(1)} %get-tuple-element.14.refs_1_, bf16[2,2,128,128]{3,2,1,0:T(8,128)(2,1)S(1)} %get-tuple-element.15.refs_2_, ...), custom_call_target="tpu_custom_call" | custom-call | flops 3000000000 | bytes 1986560 | tf_op jit(solution)/shard_map/pallas_call | solution.py:37
  20.9 1.0 %collective-permute-done.7.refs_9_ = bf16[512,256]{1,0:T(8,128)(2,1)S(1)} collective-permute-done((bf16[512,256]{1,0:T(8,128)(2,1)S(1)}, bf16[512,256]{1,0:T(8,128)(2,1)S(1)}, u32[]{:S(2)}, u32[]{:S(2)}) %collective-permute-start.7) | collective-permute-done | bytes 262176 | tf_op jit(solution)/shard_map/ppermute | solution.py:31
  21.9 0.3 shard_map.64
  22.2 1.6 %collective-permute-start.8 = (bf16[144,256]{1,0:T(8,128)(2,1)S(1)}, bf16[144,256]{1,0:T(8,128)(2,1)S(1)}, u32[]{:S(2)}, u32[]{:S(2)}) collective-permute-start(bf16[144,256]{1,0:T(8,128)(2,1)S(1)} %shard_map.64), channel_id=1, source_target_pairs={{0,2},{2,0},{4,6},{6,4},{8,10},{10,8},{12,14},{14,12},{1,3},{3,1},... | collective-permute-start | bytes 221192 | tf_op jit(solution)/shard_map/ppermute | solution.py:27
  23.8 0.0 copy-start.3
  23.8 0.0 copy-start.4
  23.8 0.7 %copy-done.3 = s32[128]{0:T(128)S(1)} copy-done((s32[128]{0:T(128)S(1)}, s32[128]{0:T(128)}, u32[]{:S(2)}) %copy-start.3) | copy-done | bytes 536
  24.4 0.0 copy-done.4
  24.4 0.1 shard_map.65
  24.5 0.3 shard_map.63
  24.8 1.8 %collective-permute-done.8 = bf16[144,256]{1,0:T(8,128)(2,1)S(1)} collective-permute-done((bf16[144,256]{1,0:T(8,128)(2,1)S(1)}, bf16[144,256]{1,0:T(8,128)(2,1)S(1)}, u32[]{:S(2)}, u32[]{:S(2)}) %collective-permute-start.8) | collective-permute-done | bytes 73760 | tf_op jit(solution)/shard_map/ppermute | solution.py:27
  26.6 0.1 fusion.5.refs_0_
  26.7 1.6 %collective-permute-start.10 = (bf16[128,256]{1,0:T(8,128)(2,1)S(1)}, bf16[128,256]{1,0:T(8,128)(2,1)S(1)}, u32[]{:S(2)}, u32[]{:S(2)}) collective-permute-start(bf16[128,256]{1,0:T(8,128)(2,1)S(1)} %fusion.5.refs_0_), channel_id=1, source_target_pairs={{0,12},{2,14},{4,8},{6,10},{8,4},{10,6},{12,0},{14,2},{1,13},{3,15... | collective-permute-start | bytes 196616 | tf_op jit(solution)/shard_map/ppermute | solution.py:27
  28.3 0.4 collective-permute-start.9
  28.7 2.4 %collective-permute-start.12 = (bf16[128,256]{1,0:T(8,128)(2,1)S(1)}, bf16[128,256]{1,0:T(8,128)(2,1)S(1)}, u32[]{:S(2)}, u32[]{:S(2)}) collective-permute-start(bf16[128,256]{1,0:T(8,128)(2,1)S(1)} %fusion.5.refs_0_), channel_id=1, source_target_pairs={{0,8},{2,10},{4,12},{6,14},{8,0},{10,2},{12,4},{14,6},{1,9},{3,11}... | collective-permute-start | bytes 196616 | tf_op jit(solution)/shard_map/ppermute | solution.py:27
  31.2 2.1 %collective-permute-done.10.refs_2_ = bf16[128,256]{1,0:T(8,128)(2,1)S(1)} collective-permute-done((bf16[128,256]{1,0:T(8,128)(2,1)S(1)}, bf16[128,256]{1,0:T(8,128)(2,1)S(1)}, u32[]{:S(2)}, u32[]{:S(2)}) %collective-permute-start.10) | collective-permute-done | bytes 65568 | tf_op jit(solution)/shard_map/ppermute | solution.py:27
  33.3 0.1 collective-permute-done.9.refs_1_
  33.4 0.1 collective-permute-start.11
  33.5 1.6 %collective-permute-done.12.refs_0_ = bf16[128,256]{1,0:T(8,128)(2,1)S(1)} collective-permute-done((bf16[128,256]{1,0:T(8,128)(2,1)S(1)}, bf16[128,256]{1,0:T(8,128)(2,1)S(1)}, u32[]{:S(2)}, u32[]{:S(2)}) %collective-permute-start.12) | collective-permute-done | bytes 65568 | tf_op jit(solution)/shard_map/ppermute | solution.py:27
  35.1 0.0 collective-permute-start.13
  35.1 0.3 shard_map.68
  35.5 0.9 %collective-permute-done.13.refs_10_ = bf16[128,256]{1,0:T(8,128)(2,1)S(1)} collective-permute-done((bf16[128,256]{1,0:T(8,128)(2,1)S(1)}, bf16[128,256]{1,0:T(8,128)(2,1)S(1)}, u32[]{:S(2)}, u32[]{:S(2)}) %collective-permute-start.13) | collective-permute-done | bytes 65568 | tf_op jit(solution)/shard_map/ppermute | solution.py:31
  36.4 0.0 collective-permute-done.11.refs_9_
  36.4 0.3 shard_map.70
  36.6 1.6 %collective-permute-start.14 = (bf16[128,256]{1,0:T(8,128)(2,1)S(1)}, bf16[128,256]{1,0:T(8,128)(2,1)S(1)}, u32[]{:S(2)}, u32[]{:S(2)}) collective-permute-start(bf16[128,256]{1,0:T(8,128)(2,1)S(1)} %shard_map.70), channel_id=1, source_target_pairs={{0,2},{2,0},{4,6},{6,4},{8,10},{10,8},{12,14},{14,12},{1,3},{3,1},... | collective-permute-start | bytes 196616 | tf_op jit(solution)/shard_map/ppermute | solution.py:27
  38.2 0.3 shard_map.69
  38.5 2.5 %collective-permute-done.14 = bf16[128,256]{1,0:T(8,128)(2,1)S(1)} collective-permute-done((bf16[128,256]{1,0:T(8,128)(2,1)S(1)}, bf16[128,256]{1,0:T(8,128)(2,1)S(1)}, u32[]{:S(2)}, u32[]{:S(2)}) %collective-permute-start.14) | collective-permute-done | bytes 65568 | tf_op jit(solution)/shard_map/ppermute | solution.py:27
  41.0 0.7 %add_convert_fusion = bf16[128,256]{1,0:T(8,128)(2,1)} fusion(f32[128,256]{1,0:T(8,128)S(1)} %shard_map.65, bf16[128,256]{1,0:T(8,128)(2,1)S(1)} %fusion.5.refs_0_, f32[128,256]{1,0:T(8,128)S(1)} %shard_map.69, bf16[128,256]{1,0:T(8,128)(2,1)S(1)} %collective-permute-done.14, f32[128]{0:T(128)S(1)} %fusion.8), kind=kLoop, calls=%fused_computation.6 | loop fusion | flops 294912 | bytes 459264 | tf_op jit(solution)/shard_map/convert_element_type | solution.py:244
  (11 shorter events, 0.1 us)
Async XLA Ops:
  0.0 4.0 %copy-start = (bf16[1024,2,128]{2,1,0:T(2,128)(2,1)S(1)}, bf16[1024,2,128]{2,1,0:T(2,128)(2,1)}, u32[]{:S(2)}) copy-start(bf16[1024,2,128]{2,1,0:T(2,128)(2,1)} %param.5) | copy-start | bytes 1572868
  0.0 10.0 %collective-permute-start.5 = (bf16[128,256]{1,0:T(8,128)(2,1)}, bf16[128,256]{1,0:T(8,128)(2,1)S(1)}, u32[]{:S(2)}, u32[]{:S(2)}) collective-permute-start(bf16[128,256]{1,0:T(8,128)(2,1)} %refs_0_.1), channel_id=1, source_target_pairs={{0,8},{2,10},{4,12},{6,14},{8,0},{10,2},{12,4},{14,6},{1,9},{3,11}... | collective-permute-start | bytes 196616 | tf_op jit(solution)/shard_map/ppermute | solution.py:27
  4.0 0.7 %copy-start.2 = (s32[8,2,1]{0,2,1:T(1,128)S(1)}, s32[8,2,1]{0,2,1:T(1,128)}, u32[]{:S(2)}) copy-start(s32[8,2,1]{0,2,1:T(1,128)} %param.6) | copy-start | bytes 196
  5.4 7.7 %collective-permute-start = (bf16[2,2,128,128]{3,2,1,0:T(8,128)(2,1)S(1)}, bf16[2,2,128,128]{3,2,1,0:T(8,128)(2,1)S(1)}, u32[]{:S(2)}, u32[]{:S(2)}) collective-permute-start(bf16[2,2,128,128]{3,2,1,0:T(8,128)(2,1)S(1)} %get-tuple-element.14.refs_1_), channel_id=1, source_target_pairs={{0,4},{2,6},{4,0},{6,2},{8,12},{10,14},{12,8},{14,10},{1,5},{3,7},... | collective-permute-start | bytes 393224 | tf_op jit(solution)/shard_map/ppermute | solution.py:27
  7.0 12.1 %collective-permute-start.1 = (bf16[2,2,128,128]{3,2,1,0:T(8,128)(2,1)S(1)}, bf16[2,2,128,128]{3,2,1,0:T(8,128)(2,1)S(1)}, u32[]{:S(2)}, u32[]{:S(2)}) collective-permute-start(bf16[2,2,128,128]{3,2,1,0:T(8,128)(2,1)S(1)} %get-tuple-element.15.refs_2_), channel_id=1, source_target_pairs={{0,8},{2,10},{4,12},{6,14},{8,0},{10,2},{12,4},{14,6},{1,9},{3,11}... | collective-permute-start | bytes 393224 | tf_op jit(solution)/shard_map/ppermute | solution.py:27
  7.4 11.7 %collective-permute-start.2 = (bf16[2,2,128,128]{3,2,1,0:T(8,128)(2,1)S(1)}, bf16[2,2,128,128]{3,2,1,0:T(8,128)(2,1)S(1)}, u32[]{:S(2)}, u32[]{:S(2)}) collective-permute-start(bf16[2,2,128,128]{3,2,1,0:T(8,128)(2,1)S(1)} %get-tuple-element.16.refs_3_), channel_id=1, source_target_pairs={{0,12},{2,14},{4,8},{6,10},{8,4},{10,6},{12,0},{14,2},{1,13},{3,15... | collective-permute-start | bytes 393224 | tf_op jit(solution)/shard_map/ppermute | solution.py:27
  9.9 0.8 %copy-start.1 = (bf16[128,256]{1,0:T(8,128)(2,1)S(1)}, bf16[128,256]{1,0:T(8,128)(2,1)}, u32[]{:S(2)}) copy-start(bf16[128,256]{1,0:T(8,128)(2,1)} %refs_0_.1) | copy-start | bytes 196612
  9.9 1.6 %collective-permute-start.3 = (bf16[4,2,128,128]{3,2,1,0:T(8,128)(2,1)S(1)}, bf16[4,2,128,128]{3,2,1,0:T(8,128)(2,1)S(1)}, u32[]{:S(2)}, u32[]{:S(2)}) collective-permute-start(bf16[4,2,128,128]{3,2,1,0:T(8,128)(2,1)S(1)} %shard_map.57), channel_id=1, source_target_pairs={{0,1},{1,0},{2,3},{3,2},{4,5},{5,4},{6,7},{7,6},{8,9},{9,8},{10,11... | collective-permute-start | bytes 786440 | tf_op jit(solution)/shard_map/ppermute | solution.py:31
  10.7 9.6 %collective-permute-start.6 = (bf16[256,256]{1,0:T(8,128)(2,1)S(1)}, bf16[256,256]{1,0:T(8,128)(2,1)S(1)}, u32[]{:S(2)}, u32[]{:S(2)}) collective-permute-start(bf16[256,256]{1,0:T(8,128)(2,1)S(1)} %shard_map.59.refs_0_), channel_id=1, source_target_pairs={{0,4},{2,6},{4,0},{6,2},{8,12},{10,14},{12,8},{14,10},{1,5},{3,7},... | collective-permute-start | bytes 393224 | tf_op jit(solution)/shard_map/ppermute | solution.py:27
  11.5 8.9 %collective-permute-start.4 = (bf16[2,4,128,128]{3,2,1,0:T(8,128)(2,1)S(1)}, bf16[2,4,128,128]{3,2,1,0:T(8,128)(2,1)S(1)}, u32[]{:S(2)}, u32[]{:S(2)}) collective-permute-start(bf16[2,4,128,128]{3,2,1,0:T(8,128)(2,1)S(1)} %shard_map.58), channel_id=1, source_target_pairs={{0,2},{2,0},{4,6},{6,4},{8,10},{10,8},{12,14},{14,12},{1,3},{3,1},... | collective-permute-start | bytes 786440 | tf_op jit(solution)/shard_map/ppermute | solution.py:27
  20.3 1.6 %collective-permute-start.7 = (bf16[512,256]{1,0:T(8,128)(2,1)S(1)}, bf16[512,256]{1,0:T(8,128)(2,1)S(1)}, u32[]{:S(2)}, u32[]{:S(2)}) collective-permute-start(bf16[512,256]{1,0:T(8,128)(2,1)S(1)} %shard_map.60.refs_9_), channel_id=1, source_target_pairs={{0,1},{1,0},{2,3},{3,2},{4,5},{5,4},{6,7},{7,6},{8,9},{9,8},{10,11... | collective-permute-start | bytes 786440 | tf_op jit(solution)/shard_map/ppermute | solution.py:31
  22.2 4.4 %collective-permute-start.8 = (bf16[144,256]{1,0:T(8,128)(2,1)S(1)}, bf16[144,256]{1,0:T(8,128)(2,1)S(1)}, u32[]{:S(2)}, u32[]{:S(2)}) collective-permute-start(bf16[144,256]{1,0:T(8,128)(2,1)S(1)} %shard_map.64), channel_id=1, source_target_pairs={{0,2},{2,0},{4,6},{6,4},{8,10},{10,8},{12,14},{14,12},{1,3},{3,1},... | collective-permute-start | bytes 221192 | tf_op jit(solution)/shard_map/ppermute | solution.py:27
  23.8 0.7 %copy-start.3 = (s32[128]{0:T(128)S(1)}, s32[128]{0:T(128)}, u32[]{:S(2)}) copy-start(s32[128]{0:T(128)} %param.8) | copy-start | bytes 1540
  23.8 0.7 %copy-start.4 = (s32[128]{0:T(128)S(1)}, s32[128]{0:T(128)}, u32[]{:S(2)}) copy-start(s32[128]{0:T(128)} %param.9) | copy-start | bytes 1540
  26.7 6.5 %collective-permute-start.10 = (bf16[128,256]{1,0:T(8,128)(2,1)S(1)}, bf16[128,256]{1,0:T(8,128)(2,1)S(1)}, u32[]{:S(2)}, u32[]{:S(2)}) collective-permute-start(bf16[128,256]{1,0:T(8,128)(2,1)S(1)} %fusion.5.refs_0_), channel_id=1, source_target_pairs={{0,12},{2,14},{4,8},{6,10},{8,4},{10,6},{12,0},{14,2},{1,13},{3,15... | collective-permute-start | bytes 196616 | tf_op jit(solution)/shard_map/ppermute | solution.py:27
  28.3 5.0 %collective-permute-start.9 = (bf16[128,256]{1,0:T(8,128)(2,1)S(1)}, bf16[128,256]{1,0:T(8,128)(2,1)S(1)}, u32[]{:S(2)}, u32[]{:S(2)}) collective-permute-start(bf16[128,256]{1,0:T(8,128)(2,1)S(1)} %fusion.5.refs_0_), channel_id=1, source_target_pairs={{0,4},{2,6},{4,0},{6,2},{8,12},{10,14},{12,8},{14,10},{1,5},{3,7},... | collective-permute-start | bytes 196616 | tf_op jit(solution)/shard_map/ppermute | solution.py:27
  28.7 6.4 %collective-permute-start.12 = (bf16[128,256]{1,0:T(8,128)(2,1)S(1)}, bf16[128,256]{1,0:T(8,128)(2,1)S(1)}, u32[]{:S(2)}, u32[]{:S(2)}) collective-permute-start(bf16[128,256]{1,0:T(8,128)(2,1)S(1)} %fusion.5.refs_0_), channel_id=1, source_target_pairs={{0,8},{2,10},{4,12},{6,14},{8,0},{10,2},{12,4},{14,6},{1,9},{3,11}... | collective-permute-start | bytes 196616 | tf_op jit(solution)/shard_map/ppermute | solution.py:27
  33.4 3.0 %collective-permute-start.11 = (bf16[384,256]{1,0:T(8,128)(2,1)S(1)}, bf16[384,256]{1,0:T(8,128)(2,1)S(1)}, u32[]{:S(2)}, u32[]{:S(2)}) collective-permute-start(bf16[384,256]{1,0:T(8,128)(2,1)S(1)} %shard_map.66.refs_9_), channel_id=1, source_target_pairs={{0,1},{1,0},{2,3},{3,2},{4,5},{5,4},{6,7},{7,6},{8,9},{9,8},{10,11... | collective-permute-start | bytes 589832 | tf_op jit(solution)/shard_map/ppermute | solution.py:31
  35.1 1.3 %collective-permute-start.13 = (bf16[128,256]{1,0:T(8,128)(2,1)S(1)}, bf16[128,256]{1,0:T(8,128)(2,1)S(1)}, u32[]{:S(2)}, u32[]{:S(2)}) collective-permute-start(bf16[128,256]{1,0:T(8,128)(2,1)S(1)} %shard_map.67.refs_10_), channel_id=1, source_target_pairs={{0,1},{1,0},{2,3},{3,2},{4,5},{5,4},{6,7},{7,6},{8,9},{9,8},{10,11... | collective-permute-start | bytes 196616 | tf_op jit(solution)/shard_map/ppermute | solution.py:31
  36.6 4.3 %collective-permute-start.14 = (bf16[128,256]{1,0:T(8,128)(2,1)S(1)}, bf16[128,256]{1,0:T(8,128)(2,1)S(1)}, u32[]{:S(2)}, u32[]{:S(2)}) collective-permute-start(bf16[128,256]{1,0:T(8,128)(2,1)S(1)} %shard_map.70), channel_id=1, source_target_pairs={{0,2},{2,0},{4,6},{6,4},{8,10},{10,8},{12,14},{14,12},{1,3},{3,1},... | collective-permute-start | bytes 196616 | tf_op jit(solution)/shard_map/ppermute | solution.py:27

commit v16 on v15

--- a/solution.py
+++ b/solution.py
@@ -53,7 +53,7 @@
     return list(range(1, half)) + list(range(half + 1, count)) + [half]
 
 
-def prepare_kernel(z_count, y_count, live, tile, lead, *outs):
+def prepare_kernel(z_count, y_count, live, tile, labels, lead, *outs):
     strips = outs
     row, col = lax.axis_index("row"), lax.axis_index("col")
     z, y = lax.div(row, y_count), lax.rem(row, y_count)
@@ -120,8 +120,7 @@
     return lax.dot_general(left, right, ((contract[:1], contract[1:]), ((), ())), preferred_element_type=jnp.float32)
 
 
-def blocks_of(order, y_count, refs, i, j):
-    z_count = len(order)
+def blocks_of(z_count, y_count, refs, i, j, order):
     sent, refs = refs[:z_count], refs[z_count:]
     strips = dict(zip([0] + others(z_count), sent[:1] + refs))
     from_core, halves = refs[z_count - 1], refs[z_count:]
@@ -135,31 +134,31 @@
     return back, jnp.concatenate([strips[k][i, j] for k in order], axis=1)
 
 
-def ours_kernel(order, y_count, first, *refs):
-    count = 2 * len(order) + y_count - 1
+def ours_kernel(z_count, y_count, order, first, *refs):
+    count = 2 * z_count + y_count - 1
     blocks, pieces, outs = refs[:count], refs[count:-y_count], refs[-y_count:]
     pieces = pieces[:-1] if first else pieces
     values = jnp.concatenate([piece[...] for piece in pieces], axis=0)
     depth, classes = values.shape
-    width = depth // len(order)
+    width = depth // z_count
     ones = jnp.ones((SUBLANES, depth), jnp.bfloat16)
     for j, out in enumerate(outs):
-        back, ahead = blocks_of(order, y_count, blocks, 0, j)
+        back, ahead = blocks_of(z_count, y_count, blocks, 0, j, order)
         out[:width, :] = product(back, values, (0, 0)) + product(ahead, values, (1, 0))
         if first:
             sums = product(ones, back, (1, 0)) + product(ones, ahead, (1, 1))
-            back, ahead = blocks_of(order, y_count, blocks, 1, j)
+            back, ahead = blocks_of(z_count, y_count, blocks, 1, j, order)
             sums += product(ones, back, (1, 0)) + product(ones, ahead, (1, 1))
             out[width:, :] = jnp.concatenate([sums] * (classes // width), axis=1)
 
 
-def theirs_kernel(order, y_count, wanted, first, *refs):
-    count = 2 * len(order) + y_count - 1
-    blocks, pieces, refs = refs[:count], refs[count : -2 * len(wanted)], refs[-2 * len(wanted) :]
-    values = jnp.concatenate([piece[...] for piece in pieces], axis=0)
+def theirs_kernel(z_count, y_count, order, wanted, first, *refs):
+    count = 2 * z_count + y_count - 1
+    blocks, piece, parts, outs = refs[:count], refs[count], refs[count + 1 : -len(wanted)], refs[-len(wanted) :]
+    values = piece[...]
     width = values.shape[0] // len(order)
-    for j, part, out in zip(wanted, refs[: len(wanted)], refs[len(wanted) :]):
-        back, ahead = blocks_of(order, y_count, blocks, 1, j)
+    for j, part, out in zip(wanted, parts, outs):
+        back, ahead = blocks_of(z_count, y_count, blocks, 1, j, order)
         total = part[:width, :] + product(back, values, (0, 0)) + product(ahead, values, (1, 0))
         out[:width, :] = total.astype(out.dtype)
         if first:
@@ -186,6 +185,7 @@
         [strip] * z_count,
         block_live.transpose(1, 2, 0),
         affinity.reshape(stripe * sides, width),
+        labels,
         call(lead_kernel, jax.ShapeDtypeStruct((SUBLANES, width), jnp.float32), flops=LEAD_FLOPS),
         smem=1,
     )
@@ -222,19 +222,29 @@
         part = jax.ShapeDtypeStruct((width + extra, classes), jnp.float32)
         send = jax.ShapeDtypeStruct((width + 2 * extra, classes), jnp.bfloat16)
         parts = call(
-            lambda *refs: ours_kernel(order, y_count, first, *refs),
+            lambda *refs: ours_kernel(z_count, y_count, order, first, *refs),
             [part] * y_count,
             *blocks,
             *have,
             *([mark] if first else []),
             flops=OURS_FLOPS if first else 0,
         )
-        have = [swap_cores(x) for x in have]
-        wanted = range(1, y_count)
-        sends = call(
-            lambda *refs: theirs_kernel(order, y_count, wanted, first, *refs), [send] * (y_count - 1), *blocks, *have, *parts[1:]
-        )
-        (total,) = call(lambda *refs: theirs_kernel(order, y_count, [0], first, *refs), [part], *blocks, *have, parts[0])
+
+        def add_theirs(values, order, wanted, shape):
+            return call(
+                lambda *refs: theirs_kernel(z_count, y_count, order, wanted, first, *refs),
+                [shape] * len(wanted),
+                *blocks,
+                values,
+                *[parts[j] for j in wanted],
+            )
+
+        *early, last = [swap_cores(x) for x in have]
+        if early:
+            parts = add_theirs(early[0], order[:-1], range(y_count), part)
+        ending = order[-1:] if early else order
+        sends = add_theirs(last, ending, range(1, y_count), send)
+        (total,) = add_theirs(last, ending, range(1), part)
         sends = [swap_rows(x, j + 1).astype(jnp.float32) for j, x in enumerate(sends)]
         spread = sum((x[:width] for x in sends), total[:width])
         if first:

time: 41.9 us -> 41.8 us (level)
  local copies, waits for them, and re-layouts: 2.08 us -> 1.35 us
    unnamed x10, local copies, waits for them, and re-layouts: 2.08 us -> 1.35 us
    pallas_call x16 -> x17, Pallas kernels: 2.69 us -> 2.94 us  [call(): pl.pallas_call(kernel, out_shape=out_shape, in_specs=[pl.BlockSpec(memory...]
  transfers between devices with their start and end apart: 15 -> 15, of which waited for: 9 -> 10; matrix products, arithmetic and copies ran while one was open for 0% -> 0% of each run, Pallas kernels for 5% -> 6%
where the time goes in v16:
time: 41.8 us; the launch traced here: 41.6 us
  starting transfers between devices  18.7 us (45%)
  waiting for transfers between devices  17.7 us (42%)
  Pallas kernels  2.94 us (7%)
  local copies, waits for them, and re-layouts  1.35 us (3%)
  other arithmetic  0.86 us (2%)
    ppermute x11, starting transfers between devices, swap_rows(): return lax.ppermute(value, 'row', [(i, i ^ shift) for i in range(count)])  18.4 us
    ppermute x11, waiting for transfers between devices, swap_rows(): return lax.ppermute(value, 'row', [(i, i ^ shift) for i in range(count)])  15.3 us
    pallas_call x17, Pallas kernels, call(): pl.pallas_call(kernel, out_shape=out_shape, in_specs=[pl.BlockSpec(memory...  2.94 us
    ppermute x4, waiting for transfers between devices, swap_cores(): return lax.ppermute(value, 'col', [(0, 1), (1, 0)])  2.32 us
    unnamed x10, local copies, waits for them, and re-layouts  1.35 us
  transfers between devices with their start and end apart: 15, of which 10 were waited for; matrix products, arithmetic and copies ran while one was open for 0% of the time, Pallas kernels for 6%

profile of v16, /device:TPU:0, one launch (start us, length us, event | category | flops | bytes accessed | tf_op | source)
XLA Modules:
  0.0 41.6 jit_solution(8688230975378803301)
XLA Ops:
  0.0 0.0 copy-start.1
  0.0 0.0 copy-start
  0.0 4.0 %collective-permute-start.5 = (bf16[128,256]{1,0:T(8,128)(2,1)}, bf16[128,256]{1,0:T(8,128)(2,1)S(1)}, u32[]{:S(2)}, u32[]{:S(2)}) collective-permute-start(bf16[128,256]{1,0:T(8,128)(2,1)} %refs_0_.1), channel_id=1, source_target_pairs={{0,8},{2,10},{4,12},{6,14},{8,0},{10,2},{12,4},{14,6},{1,9},{3,11}... | collective-permute-start | bytes 196616 | tf_op jit(solution)/shard_map/ppermute | solution.py:27
  4.0 0.0 copy-start.2
  4.0 0.0 copy-done.1
  4.0 0.0 copy-done
  4.1 0.7 %copy-done.2 = s32[8,2,1]{0,2,1:T(1,128)S(1)} copy-done((s32[8,2,1]{0,2,1:T(1,128)S(1)}, s32[8,2,1]{0,2,1:T(1,128)}, u32[]{:S(2)}) %copy-start.2) | copy-done | bytes 88
  4.7 0.7 %shard_map.56 = (bf16[2,2,128,128]{3,2,1,0:T(8,128)(2,1)S(1)}, bf16[2,2,128,128]{3,2,1,0:T(8,128)(2,1)S(1)}, bf16[2,2,128,128]{3,2,1,0:T(8,128)(2,1)S(1)}, bf16[2,2,128,128]{3,2,1,0:T(8,128)(2,1)S(1)}) custom-call(s32[2,1,8]{2,1,0:T(1,128)S(1)} %bitcast.13, bf16[2048,128]{1,0:T(8,128)(2,1)S(1)} %bitcast.12, bf16[128,256]{1,0:T(8,128)(2,1)S(1)} %copy-done.1, ...), custom_call_target="tpu_custom_call" | custom-call | bytes 1118272 | tf_op jit(solution)/shard_map/pallas_call | solution.py:37
  5.4 1.6 %collective-permute-start = (bf16[2,2,128,128]{3,2,1,0:T(8,128)(2,1)S(1)}, bf16[2,2,128,128]{3,2,1,0:T(8,128)(2,1)S(1)}, u32[]{:S(2)}, u32[]{:S(2)}) collective-permute-start(bf16[2,2,128,128]{3,2,1,0:T(8,128)(2,1)S(1)} %get-tuple-element.16.refs_1_), channel_id=1, source_target_pairs={{0,4},{2,6},{4,0},{6,2},{8,12},{10,14},{12,8},{14,10},{1,5},{3,7},... | collective-permute-start | bytes 393224 | tf_op jit(solution)/shard_map/ppermute | solution.py:27
  7.0 0.4 collective-permute-start.1
  7.4 2.4 %collective-permute-start.2 = (bf16[2,2,128,128]{3,2,1,0:T(8,128)(2,1)S(1)}, bf16[2,2,128,128]{3,2,1,0:T(8,128)(2,1)S(1)}, u32[]{:S(2)}, u32[]{:S(2)}) collective-permute-start(bf16[2,2,128,128]{3,2,1,0:T(8,128)(2,1)S(1)} %get-tuple-element.18.refs_3_), channel_id=1, source_target_pairs={{0,12},{2,14},{4,8},{6,10},{8,4},{10,6},{12,0},{14,2},{1,13},{3,15... | collective-permute-start | bytes 393224 | tf_op jit(solution)/shard_map/ppermute | solution.py:27
  9.9 0.1 collective-permute-start.3
  10.0 0.0 collective-permute-done.5.refs_1_
  10.0 0.7 %collective-permute-start.6 = (bf16[256,256]{1,0:T(8,128)(2,1)S(1)}, bf16[256,256]{1,0:T(8,128)(2,1)S(1)}, u32[]{:S(2)}, u32[]{:S(2)}) collective-permute-start(bf16[256,256]{1,0:T(8,128)(2,1)S(1)} %shard_map.59.refs_0_), channel_id=1, source_target_pairs={{0,4},{2,6},{4,0},{6,2},{8,12},{10,14},{12,8},{14,10},{1,5},{3,7},... | collective-permute-start | bytes 393224 | tf_op jit(solution)/shard_map/ppermute | solution.py:27
  10.7 0.7 %collective-permute-done.3.refs_4_.refs_7_ = bf16[4,2,128,128]{3,2,1,0:T(8,128)(2,1)S(1)} collective-permute-done((bf16[4,2,128,128]{3,2,1,0:T(8,128)(2,1)S(1)}, bf16[4,2,128,128]{3,2,1,0:T(8,128)(2,1)S(1)}, u32[]{:S(2)}, u32[]{:S(2)}) %collective-permute-start.3) | collective-permute-done | bytes 262176 | tf_op jit(solution)/shard_map/ppermute | solution.py:31
  11.5 1.6 %collective-permute-start.4 = (bf16[2,4,128,128]{3,2,1,0:T(8,128)(2,1)S(1)}, bf16[2,4,128,128]{3,2,1,0:T(8,128)(2,1)S(1)}, u32[]{:S(2)}, u32[]{:S(2)}) collective-permute-start(bf16[2,4,128,128]{3,2,1,0:T(8,128)(2,1)S(1)} %shard_map.58), channel_id=1, source_target_pairs={{0,2},{2,0},{4,6},{6,4},{8,10},{10,8},{12,14},{14,12},{1,3},{3,1},... | collective-permute-start | bytes 786440 | tf_op jit(solution)/shard_map/ppermute | solution.py:27
  13.1 0.0 collective-permute-done.refs_0_.refs_4_
  13.1 6.0 %collective-permute-done.1.refs_1_.refs_5_ = bf16[2,2,128,128]{3,2,1,0:T(8,128)(2,1)S(1)} collective-permute-done((bf16[2,2,128,128]{3,2,1,0:T(8,128)(2,1)S(1)}, bf16[2,2,128,128]{3,2,1,0:T(8,128)(2,1)S(1)}, u32[]{:S(2)}, u32[]{:S(2)}) %collective-permute-start.1) | collective-permute-done | bytes 131104 | tf_op jit(solution)/shard_map/ppermute | solution.py:27
  19.1 0.0 collective-permute-done.2.refs_2_.refs_6_
  19.1 1.1 %collective-permute-done.6.refs_1_ = bf16[256,256]{1,0:T(8,128)(2,1)S(1)} collective-permute-done((bf16[256,256]{1,0:T(8,128)(2,1)S(1)}, bf16[256,256]{1,0:T(8,128)(2,1)S(1)}, u32[]{:S(2)}, u32[]{:S(2)}) %collective-permute-start.6) | collective-permute-done | bytes 131104 | tf_op jit(solution)/shard_map/ppermute | solution.py:27
  20.3 0.1 collective-permute-start.7
  20.4 0.0 collective-permute-done.4.refs_8_
  20.4 0.5 %shard_map.62 = (f32[136,256]{1,0:T(8,128)S(1)}, f32[136,256]{1,0:T(8,128)S(1)}) custom-call(bf16[2,2,128,128]{3,2,1,0:T(8,128)(2,1)S(1)} %get-tuple-element.15.refs_0_, bf16[2,2,128,128]{3,2,1,0:T(8,128)(2,1)S(1)} %get-tuple-element.16.refs_1_, bf16[2,2,128,128]{3,2,1,0:T(8,128)(2,1)S(1)} %get-tuple-element.17.refs_2_, ...), custom_call_target="tpu_custom_call" | custom-call | flops 3000000000 | bytes 1986560 | tf_op jit(solution)/shard_map/pallas_call | solution.py:37
  20.9 1.0 %collective-permute-done.7.refs_9_ = bf16[512,256]{1,0:T(8,128)(2,1)S(1)} collective-permute-done((bf16[512,256]{1,0:T(8,128)(2,1)S(1)}, bf16[512,256]{1,0:T(8,128)(2,1)S(1)}, u32[]{:S(2)}, u32[]{:S(2)}) %collective-permute-start.7) | collective-permute-done | bytes 262176 | tf_op jit(solution)/shard_map/ppermute | solution.py:31
  21.9 0.3 shard_map.64
  22.2 1.6 %collective-permute-start.8 = (bf16[144,256]{1,0:T(8,128)(2,1)S(1)}, bf16[144,256]{1,0:T(8,128)(2,1)S(1)}, u32[]{:S(2)}, u32[]{:S(2)}) collective-permute-start(bf16[144,256]{1,0:T(8,128)(2,1)S(1)} %shard_map.64), channel_id=1, source_target_pairs={{0,2},{2,0},{4,6},{6,4},{8,10},{10,8},{12,14},{14,12},{1,3},{3,1},... | collective-permute-start | bytes 221192 | tf_op jit(solution)/shard_map/ppermute | solution.py:27
  23.8 0.0 copy-start.3
  23.8 0.0 copy-start.4
  23.8 0.7 %copy-done.3 = s32[128]{0:T(128)S(1)} copy-done((s32[128]{0:T(128)S(1)}, s32[128]{0:T(128)}, u32[]{:S(2)}) %copy-start.3) | copy-done | bytes 536
  24.4 0.0 copy-done.4
  24.4 0.1 shard_map.65
  24.5 0.3 shard_map.63
  24.8 1.8 %collective-permute-done.8 = bf16[144,256]{1,0:T(8,128)(2,1)S(1)} collective-permute-done((bf16[144,256]{1,0:T(8,128)(2,1)S(1)}, bf16[144,256]{1,0:T(8,128)(2,1)S(1)}, u32[]{:S(2)}, u32[]{:S(2)}) %collective-permute-start.8) | collective-permute-done | bytes 73760 | tf_op jit(solution)/shard_map/ppermute | solution.py:27
  26.6 0.1 fusion.5.refs_0_
  26.7 1.6 %collective-permute-start.12 = (bf16[128,256]{1,0:T(8,128)(2,1)S(1)}, bf16[128,256]{1,0:T(8,128)(2,1)S(1)}, u32[]{:S(2)}, u32[]{:S(2)}) collective-permute-start(bf16[128,256]{1,0:T(8,128)(2,1)S(1)} %fusion.5.refs_0_), channel_id=1, source_target_pairs={{0,12},{2,14},{4,8},{6,10},{8,4},{10,6},{12,0},{14,2},{1,13},{3,15... | collective-permute-start | bytes 196616 | tf_op jit(solution)/shard_map/ppermute | solution.py:27
  28.3 0.4 %collective-permute-start.11 = (bf16[128,256]{1,0:T(8,128)(2,1)S(1)}, bf16[128,256]{1,0:T(8,128)(2,1)S(1)}, u32[]{:S(2)}, u32[]{:S(2)}) collective-permute-start(bf16[128,256]{1,0:T(8,128)(2,1)S(1)} %fusion.5.refs_0_), channel_id=1, source_target_pairs={{0,4},{2,6},{4,0},{6,2},{8,12},{10,14},{12,8},{14,10},{1,5},{3,7},... | collective-permute-start | bytes 196616 | tf_op jit(solution)/shard_map/ppermute | solution.py:27
  28.8 2.4 %collective-permute-start.9 = (bf16[128,256]{1,0:T(8,128)(2,1)S(1)}, bf16[128,256]{1,0:T(8,128)(2,1)S(1)}, u32[]{:S(2)}, u32[]{:S(2)}) collective-permute-start(bf16[128,256]{1,0:T(8,128)(2,1)S(1)} %fusion.5.refs_0_), channel_id=1, source_target_pairs={{0,8},{2,10},{4,12},{6,14},{8,0},{10,2},{12,4},{14,6},{1,9},{3,11}... | collective-permute-start | bytes 196616 | tf_op jit(solution)/shard_map/ppermute | solution.py:27
  31.2 2.1 %collective-permute-done.12.refs_2_ = bf16[128,256]{1,0:T(8,128)(2,1)S(1)} collective-permute-done((bf16[128,256]{1,0:T(8,128)(2,1)S(1)}, bf16[128,256]{1,0:T(8,128)(2,1)S(1)}, u32[]{:S(2)}, u32[]{:S(2)}) %collective-permute-start.12) | collective-permute-done | bytes 65568 | tf_op jit(solution)/shard_map/ppermute | solution.py:27
  33.3 0.1 collective-permute-done.11.refs_1_
  33.4 0.1 collective-permute-start.13
  33.5 1.6 %collective-permute-done.9.refs_0_ = bf16[128,256]{1,0:T(8,128)(2,1)S(1)} collective-permute-done((bf16[128,256]{1,0:T(8,128)(2,1)S(1)}, bf16[128,256]{1,0:T(8,128)(2,1)S(1)}, u32[]{:S(2)}, u32[]{:S(2)}) %collective-permute-start.9) | collective-permute-done | bytes 65568 | tf_op jit(solution)/shard_map/ppermute | solution.py:27
  35.1 0.0 collective-permute-start.10
  35.1 0.3 shard_map.68
  35.5 0.0 collective-permute-done.13.refs_9_
  35.5 0.3 shard_map.69
  35.8 0.5 %collective-permute-done.10.refs_9_ = bf16[128,256]{1,0:T(8,128)(2,1)S(1)} collective-permute-done((bf16[128,256]{1,0:T(8,128)(2,1)S(1)}, bf16[128,256]{1,0:T(8,128)(2,1)S(1)}, u32[]{:S(2)}, u32[]{:S(2)}) %collective-permute-start.10) | collective-permute-done | bytes 65568 | tf_op jit(solution)/shard_map/ppermute | solution.py:31
  36.4 0.2 shard_map.71
  36.6 1.6 %collective-permute-start.14 = (bf16[128,256]{1,0:T(8,128)(2,1)S(1)}, bf16[128,256]{1,0:T(8,128)(2,1)S(1)}, u32[]{:S(2)}, u32[]{:S(2)}) collective-permute-start(bf16[128,256]{1,0:T(8,128)(2,1)S(1)} %shard_map.71), channel_id=1, source_target_pairs={{0,2},{2,0},{4,6},{6,4},{8,10},{10,8},{12,14},{14,12},{1,3},{3,1},... | collective-permute-start | bytes 196616 | tf_op jit(solution)/shard_map/ppermute | solution.py:27
  38.2 0.2 shard_map.70
  38.4 2.5 %collective-permute-done.14 = bf16[128,256]{1,0:T(8,128)(2,1)S(1)} collective-permute-done((bf16[128,256]{1,0:T(8,128)(2,1)S(1)}, bf16[128,256]{1,0:T(8,128)(2,1)S(1)}, u32[]{:S(2)}, u32[]{:S(2)}) %collective-permute-start.14) | collective-permute-done | bytes 65568 | tf_op jit(solution)/shard_map/ppermute | solution.py:27
  40.9 0.7 %add_convert_fusion = bf16[128,256]{1,0:T(8,128)(2,1)} fusion(f32[128,256]{1,0:T(8,128)S(1)} %shard_map.65, bf16[128,256]{1,0:T(8,128)(2,1)S(1)} %fusion.5.refs_0_, f32[128,256]{1,0:T(8,128)S(1)} %shard_map.70, bf16[128,256]{1,0:T(8,128)(2,1)S(1)} %collective-permute-done.14, f32[128]{0:T(128)S(1)} %fusion.8), kind=kLoop, calls=%fused_computation.6 | loop fusion | flops 294912 | bytes 459264 | tf_op jit(solution)/shard_map/convert_element_type | solution.py:254
  (11 shorter events, 0.1 us)
Async XLA Ops:
  0.0 4.0 %copy-start.1 = (bf16[128,256]{1,0:T(8,128)(2,1)S(1)}, bf16[128,256]{1,0:T(8,128)(2,1)}, u32[]{:S(2)}) copy-start(bf16[128,256]{1,0:T(8,128)(2,1)} %refs_0_.1) | copy-start | bytes 196612
  0.0 4.0 %copy-start = (bf16[1024,2,128]{2,1,0:T(2,128)(2,1)S(1)}, bf16[1024,2,128]{2,1,0:T(2,128)(2,1)}, u32[]{:S(2)}) copy-start(bf16[1024,2,128]{2,1,0:T(2,128)(2,1)} %param.5) | copy-start | bytes 1572868
  0.0 10.0 %collective-permute-start.5 = (bf16[128,256]{1,0:T(8,128)(2,1)}, bf16[128,256]{1,0:T(8,128)(2,1)S(1)}, u32[]{:S(2)}, u32[]{:S(2)}) collective-permute-start(bf16[128,256]{1,0:T(8,128)(2,1)} %refs_0_.1), channel_id=1, source_target_pairs={{0,8},{2,10},{4,12},{6,14},{8,0},{10,2},{12,4},{14,6},{1,9},{3,11}... | collective-permute-start | bytes 196616 | tf_op jit(solution)/shard_map/ppermute | solution.py:27
  4.0 0.7 %copy-start.2 = (s32[8,2,1]{0,2,1:T(1,128)S(1)}, s32[8,2,1]{0,2,1:T(1,128)}, u32[]{:S(2)}) copy-start(s32[8,2,1]{0,2,1:T(1,128)} %param.6) | copy-start | bytes 196
  5.4 7.7 %collective-permute-start = (bf16[2,2,128,128]{3,2,1,0:T(8,128)(2,1)S(1)}, bf16[2,2,128,128]{3,2,1,0:T(8,128)(2,1)S(1)}, u32[]{:S(2)}, u32[]{:S(2)}) collective-permute-start(bf16[2,2,128,128]{3,2,1,0:T(8,128)(2,1)S(1)} %get-tuple-element.16.refs_1_), channel_id=1, source_target_pairs={{0,4},{2,6},{4,0},{6,2},{8,12},{10,14},{12,8},{14,10},{1,5},{3,7},... | collective-permute-start | bytes 393224 | tf_op jit(solution)/shard_map/ppermute | solution.py:27
  7.0 12.1 %collective-permute-start.1 = (bf16[2,2,128,128]{3,2,1,0:T(8,128)(2,1)S(1)}, bf16[2,2,128,128]{3,2,1,0:T(8,128)(2,1)S(1)}, u32[]{:S(2)}, u32[]{:S(2)}) collective-permute-start(bf16[2,2,128,128]{3,2,1,0:T(8,128)(2,1)S(1)} %get-tuple-element.17.refs_2_), channel_id=1, source_target_pairs={{0,8},{2,10},{4,12},{6,14},{8,0},{10,2},{12,4},{14,6},{1,9},{3,11}... | collective-permute-start | bytes 393224 | tf_op jit(solution)/shard_map/ppermute | solution.py:27
  7.4 11.7 %collective-permute-start.2 = (bf16[2,2,128,128]{3,2,1,0:T(8,128)(2,1)S(1)}, bf16[2,2,128,128]{3,2,1,0:T(8,128)(2,1)S(1)}, u32[]{:S(2)}, u32[]{:S(2)}) collective-permute-start(bf16[2,2,128,128]{3,2,1,0:T(8,128)(2,1)S(1)} %get-tuple-element.18.refs_3_), channel_id=1, source_target_pairs={{0,12},{2,14},{4,8},{6,10},{8,4},{10,6},{12,0},{14,2},{1,13},{3,15... | collective-permute-start | bytes 393224 | tf_op jit(solution)/shard_map/ppermute | solution.py:27
  9.9 1.6 %collective-permute-start.3 = (bf16[4,2,128,128]{3,2,1,0:T(8,128)(2,1)S(1)}, bf16[4,2,128,128]{3,2,1,0:T(8,128)(2,1)S(1)}, u32[]{:S(2)}, u32[]{:S(2)}) collective-permute-start(bf16[4,2,128,128]{3,2,1,0:T(8,128)(2,1)S(1)} %shard_map.57), channel_id=1, source_target_pairs={{0,1},{1,0},{2,3},{3,2},{4,5},{5,4},{6,7},{7,6},{8,9},{9,8},{10,11... | collective-permute-start | bytes 786440 | tf_op jit(solution)/shard_map/ppermute | solution.py:31
  10.0 10.3 %collective-permute-start.6 = (bf16[256,256]{1,0:T(8,128)(2,1)S(1)}, bf16[256,256]{1,0:T(8,128)(2,1)S(1)}, u32[]{:S(2)}, u32[]{:S(2)}) collective-permute-start(bf16[256,256]{1,0:T(8,128)(2,1)S(1)} %shard_map.59.refs_0_), channel_id=1, source_target_pairs={{0,4},{2,6},{4,0},{6,2},{8,12},{10,14},{12,8},{14,10},{1,5},{3,7},... | collective-permute-start | bytes 393224 | tf_op jit(solution)/shard_map/ppermute | solution.py:27
  11.5 8.9 %collective-permute-start.4 = (bf16[2,4,128,128]{3,2,1,0:T(8,128)(2,1)S(1)}, bf16[2,4,128,128]{3,2,1,0:T(8,128)(2,1)S(1)}, u32[]{:S(2)}, u32[]{:S(2)}) collective-permute-start(bf16[2,4,128,128]{3,2,1,0:T(8,128)(2,1)S(1)} %shard_map.58), channel_id=1, source_target_pairs={{0,2},{2,0},{4,6},{6,4},{8,10},{10,8},{12,14},{14,12},{1,3},{3,1},... | collective-permute-start | bytes 786440 | tf_op jit(solution)/shard_map/ppermute | solution.py:27
  20.3 1.6 %collective-permute-start.7 = (bf16[512,256]{1,0:T(8,128)(2,1)S(1)}, bf16[512,256]{1,0:T(8,128)(2,1)S(1)}, u32[]{:S(2)}, u32[]{:S(2)}) collective-permute-start(bf16[512,256]{1,0:T(8,128)(2,1)S(1)} %shard_map.60.refs_9_), channel_id=1, source_target_pairs={{0,1},{1,0},{2,3},{3,2},{4,5},{5,4},{6,7},{7,6},{8,9},{9,8},{10,11... | collective-permute-start | bytes 786440 | tf_op jit(solution)/shard_map/ppermute | solution.py:31
  22.2 4.4 %collective-permute-start.8 = (bf16[144,256]{1,0:T(8,128)(2,1)S(1)}, bf16[144,256]{1,0:T(8,128)(2,1)S(1)}, u32[]{:S(2)}, u32[]{:S(2)}) collective-permute-start(bf16[144,256]{1,0:T(8,128)(2,1)S(1)} %shard_map.64), channel_id=1, source_target_pairs={{0,2},{2,0},{4,6},{6,4},{8,10},{10,8},{12,14},{14,12},{1,3},{3,1},... | collective-permute-start | bytes 221192 | tf_op jit(solution)/shard_map/ppermute | solution.py:27
  23.8 0.7 %copy-start.3 = (s32[128]{0:T(128)S(1)}, s32[128]{0:T(128)}, u32[]{:S(2)}) copy-start(s32[128]{0:T(128)} %param.8) | copy-start | bytes 1540
  23.8 0.7 %copy-start.4 = (s32[128]{0:T(128)S(1)}, s32[128]{0:T(128)}, u32[]{:S(2)}) copy-start(s32[128]{0:T(128)} %param.9) | copy-start | bytes 1540
  26.7 6.5 %collective-permute-start.12 = (bf16[128,256]{1,0:T(8,128)(2,1)S(1)}, bf16[128,256]{1,0:T(8,128)(2,1)S(1)}, u32[]{:S(2)}, u32[]{:S(2)}) collective-permute-start(bf16[128,256]{1,0:T(8,128)(2,1)S(1)} %fusion.5.refs_0_), channel_id=1, source_target_pairs={{0,12},{2,14},{4,8},{6,10},{8,4},{10,6},{12,0},{14,2},{1,13},{3,15... | collective-permute-start | bytes 196616 | tf_op jit(solution)/shard_map/ppermute | solution.py:27
  28.3 5.0 %collective-permute-start.11 = (bf16[128,256]{1,0:T(8,128)(2,1)S(1)}, bf16[128,256]{1,0:T(8,128)(2,1)S(1)}, u32[]{:S(2)}, u32[]{:S(2)}) collective-permute-start(bf16[128,256]{1,0:T(8,128)(2,1)S(1)} %fusion.5.refs_0_), channel_id=1, source_target_pairs={{0,4},{2,6},{4,0},{6,2},{8,12},{10,14},{12,8},{14,10},{1,5},{3,7},... | collective-permute-start | bytes 196616 | tf_op jit(solution)/shard_map/ppermute | solution.py:27
  28.8 6.4 %collective-permute-start.9 = (bf16[128,256]{1,0:T(8,128)(2,1)S(1)}, bf16[128,256]{1,0:T(8,128)(2,1)S(1)}, u32[]{:S(2)}, u32[]{:S(2)}) collective-permute-start(bf16[128,256]{1,0:T(8,128)(2,1)S(1)} %fusion.5.refs_0_), channel_id=1, source_target_pairs={{0,8},{2,10},{4,12},{6,14},{8,0},{10,2},{12,4},{14,6},{1,9},{3,11}... | collective-permute-start | bytes 196616 | tf_op jit(solution)/shard_map/ppermute | solution.py:27
  33.4 2.1 %collective-permute-start.13 = (bf16[384,256]{1,0:T(8,128)(2,1)S(1)}, bf16[384,256]{1,0:T(8,128)(2,1)S(1)}, u32[]{:S(2)}, u32[]{:S(2)}) collective-permute-start(bf16[384,256]{1,0:T(8,128)(2,1)S(1)} %shard_map.67.refs_9_), channel_id=1, source_target_pairs={{0,1},{1,0},{2,3},{3,2},{4,5},{5,4},{6,7},{7,6},{8,9},{9,8},{10,11... | collective-permute-start | bytes 589832 | tf_op jit(solution)/shard_map/ppermute | solution.py:31
  35.1 1.3 %collective-permute-start.10 = (bf16[128,256]{1,0:T(8,128)(2,1)S(1)}, bf16[128,256]{1,0:T(8,128)(2,1)S(1)}, u32[]{:S(2)}, u32[]{:S(2)}) collective-permute-start(bf16[128,256]{1,0:T(8,128)(2,1)S(1)} %shard_map.66.refs_10_), channel_id=1, source_target_pairs={{0,1},{1,0},{2,3},{3,2},{4,5},{5,4},{6,7},{7,6},{8,9},{9,8},{10,11... | collective-permute-start | bytes 196616 | tf_op jit(solution)/shard_map/ppermute | solution.py:31
  36.6 4.3 %collective-permute-start.14 = (bf16[128,256]{1,0:T(8,128)(2,1)S(1)}, bf16[128,256]{1,0:T(8,128)(2,1)S(1)}, u32[]{:S(2)}, u32[]{:S(2)}) collective-permute-start(bf16[128,256]{1,0:T(8,128)(2,1)S(1)} %shard_map.71), channel_id=1, source_target_pairs={{0,2},{2,0},{4,6},{6,4},{8,10},{10,8},{12,14},{14,12},{1,3},{3,1},... | collective-permute-start | bytes 196616 | tf_op jit(solution)/shard_map/ppermute | solution.py:27

commit v17 on v15

--- a/solution.py
+++ b/solution.py
@@ -53,7 +53,7 @@
     return list(range(1, half)) + list(range(half + 1, count)) + [half]
 
 
-def prepare_kernel(z_count, y_count, live, tile, lead, *outs):
+def prepare_kernel(z_count, y_count, live, tile, labels, lead, *outs):
     strips = outs
     row, col = lax.axis_index("row"), lax.axis_index("col")
     z, y = lax.div(row, y_count), lax.rem(row, y_count)
@@ -150,7 +150,14 @@
             sums = product(ones, back, (1, 0)) + product(ones, ahead, (1, 1))
             back, ahead = blocks_of(order, y_count, blocks, 1, j)
             sums += product(ones, back, (1, 0)) + product(ones, ahead, (1, 1))
-            out[width:, :] = jnp.concatenate([sums] * (classes // width), axis=1)
+            sums = jnp.concatenate([sums] * (classes // width), axis=1)
+            if j > 0:
+                sums = jnp.concatenate([sums] * 2, axis=0)
+                high = sums.astype(jnp.bfloat16).astype(jnp.float32)
+                middle = (sums - high).astype(jnp.bfloat16).astype(jnp.float32)
+                row = lax.broadcasted_iota(jnp.int32, sums.shape, 0)
+                sums = jnp.where(row == 0, high, jnp.where(row == 1, middle, sums - high - middle))
+            out[width:, :] = sums
 
 
 def theirs_kernel(order, y_count, wanted, first, *refs):
@@ -163,14 +170,7 @@
         total = part[:width, :] + product(back, values, (0, 0)) + product(ahead, values, (1, 0))
         out[:width, :] = total.astype(out.dtype)
         if first:
-            sums = part[width:, :]
-            if j > 0:
-                sums = jnp.concatenate([sums] * 2, axis=0)
-                high = sums.astype(jnp.bfloat16).astype(jnp.float32)
-                middle = (sums - high).astype(jnp.bfloat16).astype(jnp.float32)
-                row = lax.broadcasted_iota(jnp.int32, sums.shape, 0)
-                sums = jnp.where(row == 0, high, jnp.where(row == 1, middle, sums - high - middle))
-            out[width:, :] = sums.astype(out.dtype)
+            out[width:, :] = part[width:, :].astype(out.dtype)
 
 
 def on_device(affinity, block_live, labels, seed_class, seed_mask):
@@ -186,6 +186,7 @@
         [strip] * z_count,
         block_live.transpose(1, 2, 0),
         affinity.reshape(stripe * sides, width),
+        labels,
         call(lead_kernel, jax.ShapeDtypeStruct((SUBLANES, width), jnp.float32), flops=LEAD_FLOPS),
         smem=1,
     )
@@ -223,7 +224,7 @@
         send = jax.ShapeDtypeStruct((width + 2 * extra, classes), jnp.bfloat16)
         parts = call(
             lambda *refs: ours_kernel(order, y_count, first, *refs),
-            [part] * y_count,
+            [part] + [jax.ShapeDtypeStruct(send.shape, jnp.float32)] * (y_count - 1),
             *blocks,
             *have,
             *([mark] if first else []),

time: 41.9 us -> 41.8 us (level)
  local copies, waits for them, and re-layouts: 2.08 us -> 1.35 us
  waiting for transfers between devices: 17.3 us -> 18 us
    unnamed x10, local copies, waits for them, and re-layouts: 2.08 us -> 1.35 us
    ppermute x4, waiting for transfers between devices: 1.96 us -> 2.67 us  [swap_cores(): return lax.ppermute(value, 'col', [(0, 1), (1, 0)])]
  transfers between devices with their start and end apart: 15 -> 15, of which waited for: 9 -> 10; matrix products, arithmetic and copies ran while one was open for 0% -> 0% of each run, Pallas kernels for 5% -> 5%
where the time goes in v17:
time: 41.8 us; the launch traced here: 41.7 us
  starting transfers between devices  18.7 us (45%)
  waiting for transfers between devices  18 us (43%)
  Pallas kernels  2.7 us (6%)
  local copies, waits for them, and re-layouts  1.35 us (3%)
  other arithmetic  0.86 us (2%)
    ppermute x11, starting transfers between devices, swap_rows(): return lax.ppermute(value, 'row', [(i, i ^ shift) for i in range(count)])  18.4 us
    ppermute x11, waiting for transfers between devices, swap_rows(): return lax.ppermute(value, 'row', [(i, i ^ shift) for i in range(count)])  15.3 us
    pallas_call x16, Pallas kernels, call(): pl.pallas_call(kernel, out_shape=out_shape, in_specs=[pl.BlockSpec(memory...  2.7 us
    ppermute x4, waiting for transfers between devices, swap_cores(): return lax.ppermute(value, 'col', [(0, 1), (1, 0)])  2.67 us
    unnamed x10, local copies, waits for them, and re-layouts  1.35 us
  transfers between devices with their start and end apart: 15, of which 10 were waited for; matrix products, arithmetic and copies ran while one was open for 0% of the time, Pallas kernels for 5%

profile of v17, /device:TPU:0, one launch (start us, length us, event | category | flops | bytes accessed | tf_op | source)
XLA Modules:
  0.0 41.7 jit_solution(9100642403674064079)
XLA Ops:
  0.0 0.0 copy-start.1
  0.0 0.0 copy-start
  0.0 4.0 %collective-permute-start.5 = (bf16[128,256]{1,0:T(8,128)(2,1)}, bf16[128,256]{1,0:T(8,128)(2,1)S(1)}, u32[]{:S(2)}, u32[]{:S(2)}) collective-permute-start(bf16[128,256]{1,0:T(8,128)(2,1)} %refs_0_.1), channel_id=1, source_target_pairs={{0,8},{2,10},{4,12},{6,14},{8,0},{10,2},{12,4},{14,6},{1,9},{3,11}... | collective-permute-start | bytes 196616 | tf_op jit(solution)/shard_map/ppermute | solution.py:27
  4.0 0.0 copy-start.2
  4.0 0.0 copy-done.1
  4.0 0.0 copy-done
  4.1 0.7 %copy-done.2 = s32[8,2,1]{0,2,1:T(1,128)S(1)} copy-done((s32[8,2,1]{0,2,1:T(1,128)S(1)}, s32[8,2,1]{0,2,1:T(1,128)}, u32[]{:S(2)}) %copy-start.2) | copy-done | bytes 88
  4.7 0.7 %shard_map.56 = (bf16[2,2,128,128]{3,2,1,0:T(8,128)(2,1)S(1)}, bf16[2,2,128,128]{3,2,1,0:T(8,128)(2,1)S(1)}, bf16[2,2,128,128]{3,2,1,0:T(8,128)(2,1)S(1)}, bf16[2,2,128,128]{3,2,1,0:T(8,128)(2,1)S(1)}) custom-call(s32[2,1,8]{2,1,0:T(1,128)S(1)} %bitcast.13, bf16[2048,128]{1,0:T(8,128)(2,1)S(1)} %bitcast.12, bf16[128,256]{1,0:T(8,128)(2,1)S(1)} %copy-done.1, ...), custom_call_target="tpu_custom_call" | custom-call | bytes 1118272 | tf_op jit(solution)/shard_map/pallas_call | solution.py:37
  5.4 1.6 %collective-permute-start = (bf16[2,2,128,128]{3,2,1,0:T(8,128)(2,1)S(1)}, bf16[2,2,128,128]{3,2,1,0:T(8,128)(2,1)S(1)}, u32[]{:S(2)}, u32[]{:S(2)}) collective-permute-start(bf16[2,2,128,128]{3,2,1,0:T(8,128)(2,1)S(1)} %get-tuple-element.14.refs_1_), channel_id=1, source_target_pairs={{0,4},{2,6},{4,0},{6,2},{8,12},{10,14},{12,8},{14,10},{1,5},{3,7},... | collective-permute-start | bytes 393224 | tf_op jit(solution)/shard_map/ppermute | solution.py:27
  7.0 0.4 collective-permute-start.1
  7.4 2.4 %collective-permute-start.2 = (bf16[2,2,128,128]{3,2,1,0:T(8,128)(2,1)S(1)}, bf16[2,2,128,128]{3,2,1,0:T(8,128)(2,1)S(1)}, u32[]{:S(2)}, u32[]{:S(2)}) collective-permute-start(bf16[2,2,128,128]{3,2,1,0:T(8,128)(2,1)S(1)} %get-tuple-element.16.refs_3_), channel_id=1, source_target_pairs={{0,12},{2,14},{4,8},{6,10},{8,4},{10,6},{12,0},{14,2},{1,13},{3,15... | collective-permute-start | bytes 393224 | tf_op jit(solution)/shard_map/ppermute | solution.py:27
  9.9 0.1 collective-permute-start.3
  10.0 0.0 collective-permute-done.5.refs_1_
  10.0 0.7 %collective-permute-start.6 = (bf16[256,256]{1,0:T(8,128)(2,1)S(1)}, bf16[256,256]{1,0:T(8,128)(2,1)S(1)}, u32[]{:S(2)}, u32[]{:S(2)}) collective-permute-start(bf16[256,256]{1,0:T(8,128)(2,1)S(1)} %shard_map.59.refs_0_), channel_id=1, source_target_pairs={{0,4},{2,6},{4,0},{6,2},{8,12},{10,14},{12,8},{14,10},{1,5},{3,7},... | collective-permute-start | bytes 393224 | tf_op jit(solution)/shard_map/ppermute | solution.py:27
  10.7 0.7 %collective-permute-done.3.refs_4_.refs_7_ = bf16[4,2,128,128]{3,2,1,0:T(8,128)(2,1)S(1)} collective-permute-done((bf16[4,2,128,128]{3,2,1,0:T(8,128)(2,1)S(1)}, bf16[4,2,128,128]{3,2,1,0:T(8,128)(2,1)S(1)}, u32[]{:S(2)}, u32[]{:S(2)}) %collective-permute-start.3) | collective-permute-done | bytes 262176 | tf_op jit(solution)/shard_map/ppermute | solution.py:31
  11.5 1.6 %collective-permute-start.4 = (bf16[2,4,128,128]{3,2,1,0:T(8,128)(2,1)S(1)}, bf16[2,4,128,128]{3,2,1,0:T(8,128)(2,1)S(1)}, u32[]{:S(2)}, u32[]{:S(2)}) collective-permute-start(bf16[2,4,128,128]{3,2,1,0:T(8,128)(2,1)S(1)} %shard_map.58), channel_id=1, source_target_pairs={{0,2},{2,0},{4,6},{6,4},{8,10},{10,8},{12,14},{14,12},{1,3},{3,1},... | collective-permute-start | bytes 786440 | tf_op jit(solution)/shard_map/ppermute | solution.py:27
  13.1 0.0 collective-permute-done.refs_0_.refs_4_
  13.1 6.0 %collective-permute-done.1.refs_1_.refs_5_ = bf16[2,2,128,128]{3,2,1,0:T(8,128)(2,1)S(1)} collective-permute-done((bf16[2,2,128,128]{3,2,1,0:T(8,128)(2,1)S(1)}, bf16[2,2,128,128]{3,2,1,0:T(8,128)(2,1)S(1)}, u32[]{:S(2)}, u32[]{:S(2)}) %collective-permute-start.1) | collective-permute-done | bytes 131104 | tf_op jit(solution)/shard_map/ppermute | solution.py:27
  19.1 0.0 collective-permute-done.2.refs_2_.refs_6_
  19.1 1.1 %collective-permute-done.6.refs_1_ = bf16[256,256]{1,0:T(8,128)(2,1)S(1)} collective-permute-done((bf16[256,256]{1,0:T(8,128)(2,1)S(1)}, bf16[256,256]{1,0:T(8,128)(2,1)S(1)}, u32[]{:S(2)}, u32[]{:S(2)}) %collective-permute-start.6) | collective-permute-done | bytes 131104 | tf_op jit(solution)/shard_map/ppermute | solution.py:27
  20.3 0.1 collective-permute-start.7
  20.4 0.0 collective-permute-done.4.refs_8_
  20.4 0.5 %shard_map.62 = (f32[136,256]{1,0:T(8,128)S(1)}, f32[144,256]{1,0:T(8,128)S(1)}) custom-call(bf16[2,2,128,128]{3,2,1,0:T(8,128)(2,1)S(1)} %get-tuple-element.13.refs_0_, bf16[2,2,128,128]{3,2,1,0:T(8,128)(2,1)S(1)} %get-tuple-element.14.refs_1_, bf16[2,2,128,128]{3,2,1,0:T(8,128)(2,1)S(1)} %get-tuple-element.15.refs_2_, ...), custom_call_target="tpu_custom_call" | custom-call | flops 3000000000 | bytes 1994752 | tf_op jit(solution)/shard_map/pallas_call | solution.py:37
  20.9 1.0 %collective-permute-done.7.refs_9_ = bf16[512,256]{1,0:T(8,128)(2,1)S(1)} collective-permute-done((bf16[512,256]{1,0:T(8,128)(2,1)S(1)}, bf16[512,256]{1,0:T(8,128)(2,1)S(1)}, u32[]{:S(2)}, u32[]{:S(2)}) %collective-permute-start.7) | collective-permute-done | bytes 262176 | tf_op jit(solution)/shard_map/ppermute | solution.py:31
  21.9 0.3 shard_map.64
  22.2 1.6 %collective-permute-start.8 = (bf16[144,256]{1,0:T(8,128)(2,1)S(1)}, bf16[144,256]{1,0:T(8,128)(2,1)S(1)}, u32[]{:S(2)}, u32[]{:S(2)}) collective-permute-start(bf16[144,256]{1,0:T(8,128)(2,1)S(1)} %shard_map.64), channel_id=1, source_target_pairs={{0,2},{2,0},{4,6},{6,4},{8,10},{10,8},{12,14},{14,12},{1,3},{3,1},... | collective-permute-start | bytes 221192 | tf_op jit(solution)/shard_map/ppermute | solution.py:27
  23.8 0.0 copy-start.3
  23.8 0.0 copy-start.4
  23.8 0.7 %copy-done.3 = s32[128]{0:T(128)S(1)} copy-done((s32[128]{0:T(128)S(1)}, s32[128]{0:T(128)}, u32[]{:S(2)}) %copy-start.3) | copy-done | bytes 536
  24.4 0.0 copy-done.4
  24.4 0.1 shard_map.65
  24.5 0.3 shard_map.63
  24.8 1.8 %collective-permute-done.8 = bf16[144,256]{1,0:T(8,128)(2,1)S(1)} collective-permute-done((bf16[144,256]{1,0:T(8,128)(2,1)S(1)}, bf16[144,256]{1,0:T(8,128)(2,1)S(1)}, u32[]{:S(2)}, u32[]{:S(2)}) %collective-permute-start.8) | collective-permute-done | bytes 73760 | tf_op jit(solution)/shard_map/ppermute | solution.py:27
  26.6 0.1 fusion.5.refs_0_
  26.7 1.6 %collective-permute-start.10 = (bf16[128,256]{1,0:T(8,128)(2,1)S(1)}, bf16[128,256]{1,0:T(8,128)(2,1)S(1)}, u32[]{:S(2)}, u32[]{:S(2)}) collective-permute-start(bf16[128,256]{1,0:T(8,128)(2,1)S(1)} %fusion.5.refs_0_), channel_id=1, source_target_pairs={{0,12},{2,14},{4,8},{6,10},{8,4},{10,6},{12,0},{14,2},{1,13},{3,15... | collective-permute-start | bytes 196616 | tf_op jit(solution)/shard_map/ppermute | solution.py:27
  28.3 0.4 collective-permute-start.9
  28.8 2.4 %collective-permute-start.12 = (bf16[128,256]{1,0:T(8,128)(2,1)S(1)}, bf16[128,256]{1,0:T(8,128)(2,1)S(1)}, u32[]{:S(2)}, u32[]{:S(2)}) collective-permute-start(bf16[128,256]{1,0:T(8,128)(2,1)S(1)} %fusion.5.refs_0_), channel_id=1, source_target_pairs={{0,8},{2,10},{4,12},{6,14},{8,0},{10,2},{12,4},{14,6},{1,9},{3,11}... | collective-permute-start | bytes 196616 | tf_op jit(solution)/shard_map/ppermute | solution.py:27
  31.2 2.1 %collective-permute-done.10.refs_2_ = bf16[128,256]{1,0:T(8,128)(2,1)S(1)} collective-permute-done((bf16[128,256]{1,0:T(8,128)(2,1)S(1)}, bf16[128,256]{1,0:T(8,128)(2,1)S(1)}, u32[]{:S(2)}, u32[]{:S(2)}) %collective-permute-start.10) | collective-permute-done | bytes 65568 | tf_op jit(solution)/shard_map/ppermute | solution.py:27
  33.3 0.1 collective-permute-done.9.refs_1_
  33.4 0.1 collective-permute-start.11
  33.5 1.6 %collective-permute-done.12.refs_0_ = bf16[128,256]{1,0:T(8,128)(2,1)S(1)} collective-permute-done((bf16[128,256]{1,0:T(8,128)(2,1)S(1)}, bf16[128,256]{1,0:T(8,128)(2,1)S(1)}, u32[]{:S(2)}, u32[]{:S(2)}) %collective-permute-start.12) | collective-permute-done | bytes 65568 | tf_op jit(solution)/shard_map/ppermute | solution.py:27
  35.1 0.0 collective-permute-start.13
  35.1 0.3 shard_map.68
  35.5 0.9 %collective-permute-done.13.refs_10_ = bf16[128,256]{1,0:T(8,128)(2,1)S(1)} collective-permute-done((bf16[128,256]{1,0:T(8,128)(2,1)S(1)}, bf16[128,256]{1,0:T(8,128)(2,1)S(1)}, u32[]{:S(2)}, u32[]{:S(2)}) %collective-permute-start.13) | collective-permute-done | bytes 65568 | tf_op jit(solution)/shard_map/ppermute | solution.py:31
  36.4 0.0 collective-permute-done.11.refs_9_
  36.4 0.3 shard_map.70
  36.6 1.6 %collective-permute-start.14 = (bf16[128,256]{1,0:T(8,128)(2,1)S(1)}, bf16[128,256]{1,0:T(8,128)(2,1)S(1)}, u32[]{:S(2)}, u32[]{:S(2)}) collective-permute-start(bf16[128,256]{1,0:T(8,128)(2,1)S(1)} %shard_map.70), channel_id=1, source_target_pairs={{0,2},{2,0},{4,6},{6,4},{8,10},{10,8},{12,14},{14,12},{1,3},{3,1},... | collective-permute-start | bytes 196616 | tf_op jit(solution)/shard_map/ppermute | solution.py:27
  38.2 0.3 shard_map.69
  38.5 2.5 %collective-permute-done.14 = bf16[128,256]{1,0:T(8,128)(2,1)S(1)} collective-permute-done((bf16[128,256]{1,0:T(8,128)(2,1)S(1)}, bf16[128,256]{1,0:T(8,128)(2,1)S(1)}, u32[]{:S(2)}, u32[]{:S(2)}) %collective-permute-start.14) | collective-permute-done | bytes 65568 | tf_op jit(solution)/shard_map/ppermute | solution.py:27
  41.0 0.7 %add_convert_fusion = bf16[128,256]{1,0:T(8,128)(2,1)} fusion(f32[128,256]{1,0:T(8,128)S(1)} %shard_map.65, bf16[128,256]{1,0:T(8,128)(2,1)S(1)} %fusion.5.refs_0_, f32[128,256]{1,0:T(8,128)S(1)} %shard_map.69, bf16[128,256]{1,0:T(8,128)(2,1)S(1)} %collective-permute-done.14, f32[128]{0:T(128)S(1)} %fusion.8), kind=kLoop, calls=%fused_computation.6 | loop fusion | flops 294912 | bytes 459264 | tf_op jit(solution)/shard_map/convert_element_type | solution.py:245
  (11 shorter events, 0.1 us)
Async XLA Ops:
  0.0 4.0 %copy-start.1 = (bf16[128,256]{1,0:T(8,128)(2,1)S(1)}, bf16[128,256]{1,0:T(8,128)(2,1)}, u32[]{:S(2)}) copy-start(bf16[128,256]{1,0:T(8,128)(2,1)} %refs_0_.1) | copy-start | bytes 196612
  0.0 4.0 %copy-start = (bf16[1024,2,128]{2,1,0:T(2,128)(2,1)S(1)}, bf16[1024,2,128]{2,1,0:T(2,128)(2,1)}, u32[]{:S(2)}) copy-start(bf16[1024,2,128]{2,1,0:T(2,128)(2,1)} %param.5) | copy-start | bytes 1572868
  0.0 10.0 %collective-permute-start.5 = (bf16[128,256]{1,0:T(8,128)(2,1)}, bf16[128,256]{1,0:T(8,128)(2,1)S(1)}, u32[]{:S(2)}, u32[]{:S(2)}) collective-permute-start(bf16[128,256]{1,0:T(8,128)(2,1)} %refs_0_.1), channel_id=1, source_target_pairs={{0,8},{2,10},{4,12},{6,14},{8,0},{10,2},{12,4},{14,6},{1,9},{3,11}... | collective-permute-start | bytes 196616 | tf_op jit(solution)/shard_map/ppermute | solution.py:27
  4.0 0.7 %copy-start.2 = (s32[8,2,1]{0,2,1:T(1,128)S(1)}, s32[8,2,1]{0,2,1:T(1,128)}, u32[]{:S(2)}) copy-start(s32[8,2,1]{0,2,1:T(1,128)} %param.6) | copy-start | bytes 196
  5.4 7.7 %collective-permute-start = (bf16[2,2,128,128]{3,2,1,0:T(8,128)(2,1)S(1)}, bf16[2,2,128,128]{3,2,1,0:T(8,128)(2,1)S(1)}, u32[]{:S(2)}, u32[]{:S(2)}) collective-permute-start(bf16[2,2,128,128]{3,2,1,0:T(8,128)(2,1)S(1)} %get-tuple-element.14.refs_1_), channel_id=1, source_target_pairs={{0,4},{2,6},{4,0},{6,2},{8,12},{10,14},{12,8},{14,10},{1,5},{3,7},... | collective-permute-start | bytes 393224 | tf_op jit(solution)/shard_map/ppermute | solution.py:27
  7.0 12.1 %collective-permute-start.1 = (bf16[2,2,128,128]{3,2,1,0:T(8,128)(2,1)S(1)}, bf16[2,2,128,128]{3,2,1,0:T(8,128)(2,1)S(1)}, u32[]{:S(2)}, u32[]{:S(2)}) collective-permute-start(bf16[2,2,128,128]{3,2,1,0:T(8,128)(2,1)S(1)} %get-tuple-element.15.refs_2_), channel_id=1, source_target_pairs={{0,8},{2,10},{4,12},{6,14},{8,0},{10,2},{12,4},{14,6},{1,9},{3,11}... | collective-permute-start | bytes 393224 | tf_op jit(solution)/shard_map/ppermute | solution.py:27
  7.4 11.7 %collective-permute-start.2 = (bf16[2,2,128,128]{3,2,1,0:T(8,128)(2,1)S(1)}, bf16[2,2,128,128]{3,2,1,0:T(8,128)(2,1)S(1)}, u32[]{:S(2)}, u32[]{:S(2)}) collective-permute-start(bf16[2,2,128,128]{3,2,1,0:T(8,128)(2,1)S(1)} %get-tuple-element.16.refs_3_), channel_id=1, source_target_pairs={{0,12},{2,14},{4,8},{6,10},{8,4},{10,6},{12,0},{14,2},{1,13},{3,15... | collective-permute-start | bytes 393224 | tf_op jit(solution)/shard_map/ppermute | solution.py:27
  9.9 1.6 %collective-permute-start.3 = (bf16[4,2,128,128]{3,2,1,0:T(8,128)(2,1)S(1)}, bf16[4,2,128,128]{3,2,1,0:T(8,128)(2,1)S(1)}, u32[]{:S(2)}, u32[]{:S(2)}) collective-permute-start(bf16[4,2,128,128]{3,2,1,0:T(8,128)(2,1)S(1)} %shard_map.57), channel_id=1, source_target_pairs={{0,1},{1,0},{2,3},{3,2},{4,5},{5,4},{6,7},{7,6},{8,9},{9,8},{10,11... | collective-permute-start | bytes 786440 | tf_op jit(solution)/shard_map/ppermute | solution.py:31
  10.0 10.3 %collective-permute-start.6 = (bf16[256,256]{1,0:T(8,128)(2,1)S(1)}, bf16[256,256]{1,0:T(8,128)(2,1)S(1)}, u32[]{:S(2)}, u32[]{:S(2)}) collective-permute-start(bf16[256,256]{1,0:T(8,128)(2,1)S(1)} %shard_map.59.refs_0_), channel_id=1, source_target_pairs={{0,4},{2,6},{4,0},{6,2},{8,12},{10,14},{12,8},{14,10},{1,5},{3,7},... | collective-permute-start | bytes 393224 | tf_op jit(solution)/shard_map/ppermute | solution.py:27
  11.5 8.9 %collective-permute-start.4 = (bf16[2,4,128,128]{3,2,1,0:T(8,128)(2,1)S(1)}, bf16[2,4,128,128]{3,2,1,0:T(8,128)(2,1)S(1)}, u32[]{:S(2)}, u32[]{:S(2)}) collective-permute-start(bf16[2,4,128,128]{3,2,1,0:T(8,128)(2,1)S(1)} %shard_map.58), channel_id=1, source_target_pairs={{0,2},{2,0},{4,6},{6,4},{8,10},{10,8},{12,14},{14,12},{1,3},{3,1},... | collective-permute-start | bytes 786440 | tf_op jit(solution)/shard_map/ppermute | solution.py:27
  20.3 1.6 %collective-permute-start.7 = (bf16[512,256]{1,0:T(8,128)(2,1)S(1)}, bf16[512,256]{1,0:T(8,128)(2,1)S(1)}, u32[]{:S(2)}, u32[]{:S(2)}) collective-permute-start(bf16[512,256]{1,0:T(8,128)(2,1)S(1)} %shard_map.60.refs_9_), channel_id=1, source_target_pairs={{0,1},{1,0},{2,3},{3,2},{4,5},{5,4},{6,7},{7,6},{8,9},{9,8},{10,11... | collective-permute-start | bytes 786440 | tf_op jit(solution)/shard_map/ppermute | solution.py:31
  22.2 4.4 %collective-permute-start.8 = (bf16[144,256]{1,0:T(8,128)(2,1)S(1)}, bf16[144,256]{1,0:T(8,128)(2,1)S(1)}, u32[]{:S(2)}, u32[]{:S(2)}) collective-permute-start(bf16[144,256]{1,0:T(8,128)(2,1)S(1)} %shard_map.64), channel_id=1, source_target_pairs={{0,2},{2,0},{4,6},{6,4},{8,10},{10,8},{12,14},{14,12},{1,3},{3,1},... | collective-permute-start | bytes 221192 | tf_op jit(solution)/shard_map/ppermute | solution.py:27
  23.8 0.7 %copy-start.3 = (s32[128]{0:T(128)S(1)}, s32[128]{0:T(128)}, u32[]{:S(2)}) copy-start(s32[128]{0:T(128)} %param.8) | copy-start | bytes 1540
  23.8 0.7 %copy-start.4 = (s32[128]{0:T(128)S(1)}, s32[128]{0:T(128)}, u32[]{:S(2)}) copy-start(s32[128]{0:T(128)} %param.9) | copy-start | bytes 1540
  26.7 6.5 %collective-permute-start.10 = (bf16[128,256]{1,0:T(8,128)(2,1)S(1)}, bf16[128,256]{1,0:T(8,128)(2,1)S(1)}, u32[]{:S(2)}, u32[]{:S(2)}) collective-permute-start(bf16[128,256]{1,0:T(8,128)(2,1)S(1)} %fusion.5.refs_0_), channel_id=1, source_target_pairs={{0,12},{2,14},{4,8},{6,10},{8,4},{10,6},{12,0},{14,2},{1,13},{3,15... | collective-permute-start | bytes 196616 | tf_op jit(solution)/shard_map/ppermute | solution.py:27
  28.3 5.0 %collective-permute-start.9 = (bf16[128,256]{1,0:T(8,128)(2,1)S(1)}, bf16[128,256]{1,0:T(8,128)(2,1)S(1)}, u32[]{:S(2)}, u32[]{:S(2)}) collective-permute-start(bf16[128,256]{1,0:T(8,128)(2,1)S(1)} %fusion.5.refs_0_), channel_id=1, source_target_pairs={{0,4},{2,6},{4,0},{6,2},{8,12},{10,14},{12,8},{14,10},{1,5},{3,7},... | collective-permute-start | bytes 196616 | tf_op jit(solution)/shard_map/ppermute | solution.py:27
  28.8 6.4 %collective-permute-start.12 = (bf16[128,256]{1,0:T(8,128)(2,1)S(1)}, bf16[128,256]{1,0:T(8,128)(2,1)S(1)}, u32[]{:S(2)}, u32[]{:S(2)}) collective-permute-start(bf16[128,256]{1,0:T(8,128)(2,1)S(1)} %fusion.5.refs_0_), channel_id=1, source_target_pairs={{0,8},{2,10},{4,12},{6,14},{8,0},{10,2},{12,4},{14,6},{1,9},{3,11}... | collective-permute-start | bytes 196616 | tf_op jit(solution)/shard_map/ppermute | solution.py:27
  33.4 3.0 %collective-permute-start.11 = (bf16[384,256]{1,0:T(8,128)(2,1)S(1)}, bf16[384,256]{1,0:T(8,128)(2,1)S(1)}, u32[]{:S(2)}, u32[]{:S(2)}) collective-permute-start(bf16[384,256]{1,0:T(8,128)(2,1)S(1)} %shard_map.66.refs_9_), channel_id=1, source_target_pairs={{0,1},{1,0},{2,3},{3,2},{4,5},{5,4},{6,7},{7,6},{8,9},{9,8},{10,11... | collective-permute-start | bytes 589832 | tf_op jit(solution)/shard_map/ppermute | solution.py:31
  35.1 1.3 %collective-permute-start.13 = (bf16[128,256]{1,0:T(8,128)(2,1)S(1)}, bf16[128,256]{1,0:T(8,128)(2,1)S(1)}, u32[]{:S(2)}, u32[]{:S(2)}) collective-permute-start(bf16[128,256]{1,0:T(8,128)(2,1)S(1)} %shard_map.67.refs_10_), channel_id=1, source_target_pairs={{0,1},{1,0},{2,3},{3,2},{4,5},{5,4},{6,7},{7,6},{8,9},{9,8},{10,11... | collective-permute-start | bytes 196616 | tf_op jit(solution)/shard_map/ppermute | solution.py:31
  36.6 4.3 %collective-permute-start.14 = (bf16[128,256]{1,0:T(8,128)(2,1)S(1)}, bf16[128,256]{1,0:T(8,128)(2,1)S(1)}, u32[]{:S(2)}, u32[]{:S(2)}) collective-permute-start(bf16[128,256]{1,0:T(8,128)(2,1)S(1)} %shard_map.70), channel_id=1, source_target_pairs={{0,2},{2,0},{4,6},{6,4},{8,10},{10,8},{12,14},{14,12},{1,3},{3,1},... | collective-permute-start | bytes 196616 | tf_op jit(solution)/shard_map/ppermute | solution.py:27

commit v18 on v16

--- a/solution.py
+++ b/solution.py
@@ -13,6 +13,7 @@
 PAIR_FLOPS = 4_000_000_000
 STRIPS_FLOPS = 3_000_000_000
 OURS_FLOPS = 3_000_000_000
+EARLY_FLOPS = 3_000_000_000
 LAST_FLOPS = 2_000_000_000
 MIB = 1024 * 1024
 
@@ -95,6 +96,10 @@
     return call(join_kernel, jax.ShapeDtypeStruct((rows,) + parts[0].shape[1:], parts[0].dtype), *parts, flops=flops)
 
 
+def behind_kernel(value, *refs):
+    refs[-1][...] = value[...]
+
+
 def guard_kernel(*refs):
     refs[-1][...] = jnp.zeros_like(refs[-1])
 
@@ -152,7 +157,7 @@
             out[width:, :] = jnp.concatenate([sums] * (classes // width), axis=1)
 
 
-def theirs_kernel(z_count, y_count, order, wanted, first, *refs):
+def theirs_kernel(z_count, y_count, order, wanted, first, last, *refs):
     count = 2 * z_count + y_count - 1
     blocks, piece, parts, outs = refs[:count], refs[count], refs[count + 1 : -len(wanted)], refs[-len(wanted) :]
     values = piece[...]
@@ -163,7 +168,7 @@
         out[:width, :] = total.astype(out.dtype)
         if first:
             sums = part[width:, :]
-            if j > 0:
+            if j > 0 and last:
                 sums = jnp.concatenate([sums] * 2, axis=0)
                 high = sums.astype(jnp.bfloat16).astype(jnp.float32)
                 middle = (sums - high).astype(jnp.bfloat16).astype(jnp.float32)
@@ -192,6 +197,7 @@
     other = jax.ShapeDtypeStruct((z_count, y_count, width, width), jnp.bfloat16)
     from_core = swap_cores(call(other_kernel, other, *sent))
     halves = call(lambda *refs: halves_kernel(z_count, *refs), [half] * (y_count - 1), *sent, from_core)
+    ready = halves
     halves = [swap_rows(x, j + 1) for j, x in enumerate(halves)]
     arrived = {k: swap_rows(sent[k], k * y_count) for k in others(z_count)}
     strips = [arrived[k] for k in others(z_count)]
@@ -217,7 +223,7 @@
             order = [0] + others_late(z_count)
             have = [current] + [swap_rows(current, k * y_count) for k in order[1:]]
         first = step == 0
-        have = [join(have)] if first else [join(have[:-1]), join(have[-1:], LAST_FLOPS)]
+        have = have if first else [join(have[:-1]), join(have[-1:], LAST_FLOPS)]
         extra = SUBLANES if first else 0
         part = jax.ShapeDtypeStruct((width + extra, classes), jnp.float32)
         send = jax.ShapeDtypeStruct((width + 2 * extra, classes), jnp.bfloat16)
@@ -230,21 +236,24 @@
             flops=OURS_FLOPS if first else 0,
         )
 
-        def add_theirs(values, order, wanted, shape):
+        def add_theirs(values, order, wanted, last, shape, flops=0):
             return call(
-                lambda *refs: theirs_kernel(z_count, y_count, order, wanted, first, *refs),
+                lambda *refs: theirs_kernel(z_count, y_count, order, wanted, first, last, *refs),
                 [shape] * len(wanted),
                 *blocks,
                 values,
                 *[parts[j] for j in wanted],
+                flops=flops,
             )
 
-        *early, last = [swap_cores(x) for x in have]
-        if early:
-            parts = add_theirs(early[0], order[:-1], range(y_count), part)
-        ending = order[-1:] if early else order
-        sends = add_theirs(last, ending, range(1, y_count), send)
-        (total,) = add_theirs(last, ending, range(1), part)
+        early = have[0]
+        if first:
+            early = call(behind_kernel, jax.ShapeDtypeStruct(early.shape, early.dtype), early, arrived[1], *ready)
+        early, last = swap_cores(early), swap_cores(have[1])
+        cut = early.shape[0] // width
+        parts = add_theirs(early, order[:cut], range(y_count), False, part, EARLY_FLOPS if first else 0)
+        sends = add_theirs(last, order[cut:], range(1, y_count), True, send)
+        (total,) = add_theirs(last, order[cut:], range(1), True, part)
         sends = [swap_rows(x, j + 1).astype(jnp.float32) for j, x in enumerate(sends)]
         spread = sum((x[:width] for x in sends), total[:width])
         if first:

time: 41.8 us -> 42.7 us (1.022)
  starting transfers between devices: 18.7 us -> 19.2 us
    ppermute x11, waiting for transfers between devices: 15.3 us -> 16.1 us  [swap_rows(): return lax.ppermute(value, 'row', [(i, i ^ shift) for i in range(count)])]
    ppermute x4 -> x5, waiting for transfers between devices: 2.32 us -> 1.8 us  [swap_cores(): return lax.ppermute(value, 'col', [(0, 1), (1, 0)])]
    ppermute x4 -> x5, starting transfers between devices: 0.22 us -> 0.72 us  [swap_cores(): return lax.ppermute(value, 'col', [(0, 1), (1, 0)])]
    pallas_call x17 -> x18, Pallas kernels: 2.94 us -> 3.1 us  [call(): pl.pallas_call(kernel, out_shape=out_shape, in_specs=[pl.BlockSpec(memory...]
  transfers between devices with their start and end apart: 15 -> 16, of which waited for: 10 -> 9; matrix products, arithmetic and copies ran while one was open for 0% -> 0% of each run, Pallas kernels for 6% -> 6%
where the time goes in v18:
time: 42.7 us; the launch traced here: 42.6 us
  starting transfers between devices  19.2 us (45%)
  waiting for transfers between devices  17.9 us (42%)
  Pallas kernels  3.1 us (7%)
  local copies, waits for them, and re-layouts  1.35 us (3%)
  other arithmetic  0.86 us (2%)
    ppermute x11, starting transfers between devices, swap_rows(): return lax.ppermute(value, 'row', [(i, i ^ shift) for i in range(count)])  18.5 us
    ppermute x11, waiting for transfers between devices, swap_rows(): return lax.ppermute(value, 'row', [(i, i ^ shift) for i in range(count)])  16.1 us
    pallas_call x18, Pallas kernels, call(): pl.pallas_call(kernel, out_shape=out_shape, in_specs=[pl.BlockSpec(memory...  3.1 us
    ppermute x5, waiting for transfers between devices, swap_cores(): return lax.ppermute(value, 'col', [(0, 1), (1, 0)])  1.8 us
    unnamed x10, local copies, waits for them, and re-layouts  1.35 us
  transfers between devices with their start and end apart: 16, of which 9 were waited for; matrix products, arithmetic and copies ran while one was open for 0% of the time, Pallas kernels for 6%

profile of v18, /device:TPU:0, one launch (start us, length us, event | category | flops | bytes accessed | tf_op | source)
XLA Modules:
  0.0 42.6 jit_solution(14386499923410315294)
XLA Ops:
  0.0 0.0 copy-start.1
  0.0 0.0 copy-start
  0.0 4.0 %collective-permute-start.5 = (bf16[128,256]{1,0:T(8,128)(2,1)}, bf16[128,256]{1,0:T(8,128)(2,1)S(1)}, u32[]{:S(2)}, u32[]{:S(2)}) collective-permute-start(bf16[128,256]{1,0:T(8,128)(2,1)} %refs_0_.1), channel_id=1, source_target_pairs={{0,8},{2,10},{4,12},{6,14},{8,0},{10,2},{12,4},{14,6},{1,9},{3,11}... | collective-permute-start | bytes 196616 | tf_op jit(solution)/shard_map/ppermute | solution.py:28
  4.0 0.0 copy-start.2
  4.0 0.0 copy-done.1
  4.0 0.0 copy-done
  4.1 0.7 %copy-done.2 = s32[8,2,1]{0,2,1:T(1,128)S(1)} copy-done((s32[8,2,1]{0,2,1:T(1,128)S(1)}, s32[8,2,1]{0,2,1:T(1,128)}, u32[]{:S(2)}) %copy-start.2) | copy-done | bytes 88
  4.7 0.7 %shard_map.56 = (bf16[2,2,128,128]{3,2,1,0:T(8,128)(2,1)S(1)}, bf16[2,2,128,128]{3,2,1,0:T(8,128)(2,1)S(1)}, bf16[2,2,128,128]{3,2,1,0:T(8,128)(2,1)S(1)}, bf16[2,2,128,128]{3,2,1,0:T(8,128)(2,1)S(1)}) custom-call(s32[2,1,8]{2,1,0:T(1,128)S(1)} %bitcast.13, bf16[2048,128]{1,0:T(8,128)(2,1)S(1)} %bitcast.12, bf16[128,256]{1,0:T(8,128)(2,1)S(1)} %copy-done.1, ...), custom_call_target="tpu_custom_call" | custom-call | bytes 1118272 | tf_op jit(solution)/shard_map/pallas_call | solution.py:38
  5.4 1.6 %collective-permute-start = (bf16[2,2,128,128]{3,2,1,0:T(8,128)(2,1)S(1)}, bf16[2,2,128,128]{3,2,1,0:T(8,128)(2,1)S(1)}, u32[]{:S(2)}, u32[]{:S(2)}) collective-permute-start(bf16[2,2,128,128]{3,2,1,0:T(8,128)(2,1)S(1)} %get-tuple-element.18.refs_1_), channel_id=1, source_target_pairs={{0,4},{2,6},{4,0},{6,2},{8,12},{10,14},{12,8},{14,10},{1,5},{3,7},... | collective-permute-start | bytes 393224 | tf_op jit(solution)/shard_map/ppermute | solution.py:28
  7.0 0.4 collective-permute-start.1
  7.4 2.4 %collective-permute-start.2 = (bf16[2,2,128,128]{3,2,1,0:T(8,128)(2,1)S(1)}, bf16[2,2,128,128]{3,2,1,0:T(8,128)(2,1)S(1)}, u32[]{:S(2)}, u32[]{:S(2)}) collective-permute-start(bf16[2,2,128,128]{3,2,1,0:T(8,128)(2,1)S(1)} %get-tuple-element.20.refs_3_), channel_id=1, source_target_pairs={{0,12},{2,14},{4,8},{6,10},{8,4},{10,6},{12,0},{14,2},{1,13},{3,15... | collective-permute-start | bytes 393224 | tf_op jit(solution)/shard_map/ppermute | solution.py:28
  9.9 0.1 collective-permute-start.3
  10.0 0.0 collective-permute-done.5.refs_1_
  10.0 0.7 %collective-permute-start.6 = (bf16[256,256]{1,0:T(8,128)(2,1)S(1)}, bf16[256,256]{1,0:T(8,128)(2,1)S(1)}, u32[]{:S(2)}, u32[]{:S(2)}) collective-permute-start(bf16[256,256]{1,0:T(8,128)(2,1)S(1)} %shard_map.59.value.refs_9_), channel_id=1, source_target_pairs={{0,4},{2,6},{4,0},{6,2},{8,12},{10,14},{12,8},{14,10},{1,5},{3,7},... | collective-permute-start | bytes 393224 | tf_op jit(solution)/shard_map/ppermute | solution.py:28
  10.7 0.7 %collective-permute-done.3.refs_4_.refs_7_ = bf16[4,2,128,128]{3,2,1,0:T(8,128)(2,1)S(1)} collective-permute-done((bf16[4,2,128,128]{3,2,1,0:T(8,128)(2,1)S(1)}, bf16[4,2,128,128]{3,2,1,0:T(8,128)(2,1)S(1)}, u32[]{:S(2)}, u32[]{:S(2)}) %collective-permute-start.3) | collective-permute-done | bytes 262176 | tf_op jit(solution)/shard_map/ppermute | solution.py:32
  11.5 1.6 %collective-permute-start.4 = (bf16[2,4,128,128]{3,2,1,0:T(8,128)(2,1)S(1)}, bf16[2,4,128,128]{3,2,1,0:T(8,128)(2,1)S(1)}, u32[]{:S(2)}, u32[]{:S(2)}) collective-permute-start(bf16[2,4,128,128]{3,2,1,0:T(8,128)(2,1)S(1)} %shard_map.58.refs_1_), channel_id=1, source_target_pairs={{0,2},{2,0},{4,6},{6,4},{8,10},{10,8},{12,14},{14,12},{1,3},{3,1},... | collective-permute-start | bytes 786440 | tf_op jit(solution)/shard_map/ppermute | solution.py:28
  13.1 0.0 collective-permute-done.refs_0_.refs_4_
  13.1 6.0 %collective-permute-done.1.refs_1_.refs_5_ = bf16[2,2,128,128]{3,2,1,0:T(8,128)(2,1)S(1)} collective-permute-done((bf16[2,2,128,128]{3,2,1,0:T(8,128)(2,1)S(1)}, bf16[2,2,128,128]{3,2,1,0:T(8,128)(2,1)S(1)}, u32[]{:S(2)}, u32[]{:S(2)}) %collective-permute-start.1) | collective-permute-done | bytes 131104 | tf_op jit(solution)/shard_map/ppermute | solution.py:28
  19.1 0.0 collective-permute-done.2.refs_2_.refs_6_
  19.1 1.1 %collective-permute-done.6.refs_10_ = bf16[256,256]{1,0:T(8,128)(2,1)S(1)} collective-permute-done((bf16[256,256]{1,0:T(8,128)(2,1)S(1)}, bf16[256,256]{1,0:T(8,128)(2,1)S(1)}, u32[]{:S(2)}, u32[]{:S(2)}) %collective-permute-start.6) | collective-permute-done | bytes 131104 | tf_op jit(solution)/shard_map/ppermute | solution.py:28
  20.3 0.0 collective-permute-start.7
  20.3 0.6 %collective-permute-start.8 = (bf16[256,256]{1,0:T(8,128)(2,1)S(1)}, bf16[256,256]{1,0:T(8,128)(2,1)S(1)}, u32[]{:S(2)}, u32[]{:S(2)}) collective-permute-start(bf16[256,256]{1,0:T(8,128)(2,1)S(1)} %shard_map.60), channel_id=1, source_target_pairs={{0,1},{1,0},{2,3},{3,2},{4,5},{5,4},{6,7},{7,6},{8,9},{9,8},{10,11... | collective-permute-start | bytes 393224 | tf_op jit(solution)/shard_map/ppermute | solution.py:32
  20.9 0.0 collective-permute-done.4.refs_8_
  20.9 0.5 %shard_map.62 = (f32[136,256]{1,0:T(8,128)S(1)}, f32[136,256]{1,0:T(8,128)S(1)}) custom-call(bf16[2,2,128,128]{3,2,1,0:T(8,128)(2,1)S(1)} %get-tuple-element.17.refs_0_, bf16[2,2,128,128]{3,2,1,0:T(8,128)(2,1)S(1)} %get-tuple-element.18.refs_1_, bf16[2,2,128,128]{3,2,1,0:T(8,128)(2,1)S(1)} %get-tuple-element.19.refs_2_, ...), custom_call_target="tpu_custom_call" | custom-call | flops 3000000000 | bytes 1986560 | tf_op jit(solution)/shard_map/pallas_call | solution.py:38
  21.4 0.5 %collective-permute-done.8.refs_9_ = bf16[256,256]{1,0:T(8,128)(2,1)S(1)} collective-permute-done((bf16[256,256]{1,0:T(8,128)(2,1)S(1)}, bf16[256,256]{1,0:T(8,128)(2,1)S(1)}, u32[]{:S(2)}, u32[]{:S(2)}) %collective-permute-start.8) | collective-permute-done | bytes 131104 | tf_op jit(solution)/shard_map/ppermute | solution.py:32
  21.9 0.3 shard_map.63
  22.1 0.0 collective-permute-done.7.refs_9_
  22.1 0.2 shard_map.65
  22.4 1.6 %collective-permute-start.9 = (bf16[144,256]{1,0:T(8,128)(2,1)S(1)}, bf16[144,256]{1,0:T(8,128)(2,1)S(1)}, u32[]{:S(2)}, u32[]{:S(2)}) collective-permute-start(bf16[144,256]{1,0:T(8,128)(2,1)S(1)} %shard_map.65), channel_id=1, source_target_pairs={{0,2},{2,0},{4,6},{6,4},{8,10},{10,8},{12,14},{14,12},{1,3},{3,1},... | collective-permute-start | bytes 221192 | tf_op jit(solution)/shard_map/ppermute | solution.py:28
  24.0 0.0 copy-start.3
  24.0 0.0 copy-start.4
  24.0 0.7 %copy-done.3 = s32[128]{0:T(128)S(1)} copy-done((s32[128]{0:T(128)S(1)}, s32[128]{0:T(128)}, u32[]{:S(2)}) %copy-start.3) | copy-done | bytes 536
  24.6 0.0 copy-done.4
  24.6 0.1 shard_map.66
  24.7 0.2 shard_map.64
  25.0 2.0 %collective-permute-done.9 = bf16[144,256]{1,0:T(8,128)(2,1)S(1)} collective-permute-done((bf16[144,256]{1,0:T(8,128)(2,1)S(1)}, bf16[144,256]{1,0:T(8,128)(2,1)S(1)}, u32[]{:S(2)}, u32[]{:S(2)}) %collective-permute-start.9) | collective-permute-done | bytes 73760 | tf_op jit(solution)/shard_map/ppermute | solution.py:28
  27.0 0.1 fusion.5.refs_0_
  27.1 1.6 %collective-permute-start.13 = (bf16[128,256]{1,0:T(8,128)(2,1)S(1)}, bf16[128,256]{1,0:T(8,128)(2,1)S(1)}, u32[]{:S(2)}, u32[]{:S(2)}) collective-permute-start(bf16[128,256]{1,0:T(8,128)(2,1)S(1)} %fusion.5.refs_0_), channel_id=1, source_target_pairs={{0,12},{2,14},{4,8},{6,10},{8,4},{10,6},{12,0},{14,2},{1,13},{3,15... | collective-permute-start | bytes 196616 | tf_op jit(solution)/shard_map/ppermute | solution.py:28
  28.7 0.4 collective-permute-start.12
  29.1 2.4 %collective-permute-start.10 = (bf16[128,256]{1,0:T(8,128)(2,1)S(1)}, bf16[128,256]{1,0:T(8,128)(2,1)S(1)}, u32[]{:S(2)}, u32[]{:S(2)}) collective-permute-start(bf16[128,256]{1,0:T(8,128)(2,1)S(1)} %fusion.5.refs_0_), channel_id=1, source_target_pairs={{0,8},{2,10},{4,12},{6,14},{8,0},{10,2},{12,4},{14,6},{1,9},{3,11}... | collective-permute-start | bytes 196616 | tf_op jit(solution)/shard_map/ppermute | solution.py:28
  31.6 2.4 %collective-permute-done.13.refs_2_ = bf16[128,256]{1,0:T(8,128)(2,1)S(1)} collective-permute-done((bf16[128,256]{1,0:T(8,128)(2,1)S(1)}, bf16[128,256]{1,0:T(8,128)(2,1)S(1)}, u32[]{:S(2)}, u32[]{:S(2)}) %collective-permute-start.13) | collective-permute-done | bytes 65568 | tf_op jit(solution)/shard_map/ppermute | solution.py:28
  33.9 0.0 collective-permute-done.12.refs_1_
  33.9 0.1 collective-permute-start.14
  34.0 2.0 %collective-permute-done.10.refs_0_ = bf16[128,256]{1,0:T(8,128)(2,1)S(1)} collective-permute-done((bf16[128,256]{1,0:T(8,128)(2,1)S(1)}, bf16[128,256]{1,0:T(8,128)(2,1)S(1)}, u32[]{:S(2)}, u32[]{:S(2)}) %collective-permute-start.10) | collective-permute-done | bytes 65568 | tf_op jit(solution)/shard_map/ppermute | solution.py:28
  36.0 0.0 collective-permute-start.11
  36.0 0.3 shard_map.69
  36.4 0.0 collective-permute-done.14.refs_9_
  36.4 0.3 shard_map.70
  36.7 0.5 %collective-permute-done.11.refs_9_ = bf16[128,256]{1,0:T(8,128)(2,1)S(1)} collective-permute-done((bf16[128,256]{1,0:T(8,128)(2,1)S(1)}, bf16[128,256]{1,0:T(8,128)(2,1)S(1)}, u32[]{:S(2)}, u32[]{:S(2)}) %collective-permute-start.11) | collective-permute-done | bytes 65568 | tf_op jit(solution)/shard_map/ppermute | solution.py:32
  37.3 0.2 shard_map.72
  37.5 1.6 %collective-permute-start.15 = (bf16[128,256]{1,0:T(8,128)(2,1)S(1)}, bf16[128,256]{1,0:T(8,128)(2,1)S(1)}, u32[]{:S(2)}, u32[]{:S(2)}) collective-permute-start(bf16[128,256]{1,0:T(8,128)(2,1)S(1)} %shard_map.72), channel_id=1, source_target_pairs={{0,2},{2,0},{4,6},{6,4},{8,10},{10,8},{12,14},{14,12},{1,3},{3,1},... | collective-permute-start | bytes 196616 | tf_op jit(solution)/shard_map/ppermute | solution.py:28
  39.1 0.2 shard_map.71
  39.3 2.5 %collective-permute-done.15 = bf16[128,256]{1,0:T(8,128)(2,1)S(1)} collective-permute-done((bf16[128,256]{1,0:T(8,128)(2,1)S(1)}, bf16[128,256]{1,0:T(8,128)(2,1)S(1)}, u32[]{:S(2)}, u32[]{:S(2)}) %collective-permute-start.15) | collective-permute-done | bytes 65568 | tf_op jit(solution)/shard_map/ppermute | solution.py:28
  41.8 0.7 %add_convert_fusion = bf16[128,256]{1,0:T(8,128)(2,1)} fusion(f32[128,256]{1,0:T(8,128)S(1)} %shard_map.66, bf16[128,256]{1,0:T(8,128)(2,1)S(1)} %fusion.5.refs_0_, f32[128,256]{1,0:T(8,128)S(1)} %shard_map.71, bf16[128,256]{1,0:T(8,128)(2,1)S(1)} %collective-permute-done.15, f32[128]{0:T(128)S(1)} %fusion.8), kind=kLoop, calls=%fused_computation.6 | loop fusion | flops 294912 | bytes 459264 | tf_op jit(solution)/shard_map/convert_element_type | solution.py:263
  (11 shorter events, 0.1 us)
Async XLA Ops:
  0.0 4.0 %copy-start.1 = (bf16[128,256]{1,0:T(8,128)(2,1)S(1)}, bf16[128,256]{1,0:T(8,128)(2,1)}, u32[]{:S(2)}) copy-start(bf16[128,256]{1,0:T(8,128)(2,1)} %refs_0_.1) | copy-start | bytes 196612
  0.0 4.0 %copy-start = (bf16[1024,2,128]{2,1,0:T(2,128)(2,1)S(1)}, bf16[1024,2,128]{2,1,0:T(2,128)(2,1)}, u32[]{:S(2)}) copy-start(bf16[1024,2,128]{2,1,0:T(2,128)(2,1)} %param.5) | copy-start | bytes 1572868
  0.0 10.0 %collective-permute-start.5 = (bf16[128,256]{1,0:T(8,128)(2,1)}, bf16[128,256]{1,0:T(8,128)(2,1)S(1)}, u32[]{:S(2)}, u32[]{:S(2)}) collective-permute-start(bf16[128,256]{1,0:T(8,128)(2,1)} %refs_0_.1), channel_id=1, source_target_pairs={{0,8},{2,10},{4,12},{6,14},{8,0},{10,2},{12,4},{14,6},{1,9},{3,11}... | collective-permute-start | bytes 196616 | tf_op jit(solution)/shard_map/ppermute | solution.py:28
  4.0 0.7 %copy-start.2 = (s32[8,2,1]{0,2,1:T(1,128)S(1)}, s32[8,2,1]{0,2,1:T(1,128)}, u32[]{:S(2)}) copy-start(s32[8,2,1]{0,2,1:T(1,128)} %param.6) | copy-start | bytes 196
  5.4 7.7 %collective-permute-start = (bf16[2,2,128,128]{3,2,1,0:T(8,128)(2,1)S(1)}, bf16[2,2,128,128]{3,2,1,0:T(8,128)(2,1)S(1)}, u32[]{:S(2)}, u32[]{:S(2)}) collective-permute-start(bf16[2,2,128,128]{3,2,1,0:T(8,128)(2,1)S(1)} %get-tuple-element.18.refs_1_), channel_id=1, source_target_pairs={{0,4},{2,6},{4,0},{6,2},{8,12},{10,14},{12,8},{14,10},{1,5},{3,7},... | collective-permute-start | bytes 393224 | tf_op jit(solution)/shard_map/ppermute | solution.py:28
  7.0 12.1 %collective-permute-start.1 = (bf16[2,2,128,128]{3,2,1,0:T(8,128)(2,1)S(1)}, bf16[2,2,128,128]{3,2,1,0:T(8,128)(2,1)S(1)}, u32[]{:S(2)}, u32[]{:S(2)}) collective-permute-start(bf16[2,2,128,128]{3,2,1,0:T(8,128)(2,1)S(1)} %get-tuple-element.19.refs_2_), channel_id=1, source_target_pairs={{0,8},{2,10},{4,12},{6,14},{8,0},{10,2},{12,4},{14,6},{1,9},{3,11}... | collective-permute-start | bytes 393224 | tf_op jit(solution)/shard_map/ppermute | solution.py:28
  7.4 11.7 %collective-permute-start.2 = (bf16[2,2,128,128]{3,2,1,0:T(8,128)(2,1)S(1)}, bf16[2,2,128,128]{3,2,1,0:T(8,128)(2,1)S(1)}, u32[]{:S(2)}, u32[]{:S(2)}) collective-permute-start(bf16[2,2,128,128]{3,2,1,0:T(8,128)(2,1)S(1)} %get-tuple-element.20.refs_3_), channel_id=1, source_target_pairs={{0,12},{2,14},{4,8},{6,10},{8,4},{10,6},{12,0},{14,2},{1,13},{3,15... | collective-permute-start | bytes 393224 | tf_op jit(solution)/shard_map/ppermute | solution.py:28
  9.9 1.6 %collective-permute-start.3 = (bf16[4,2,128,128]{3,2,1,0:T(8,128)(2,1)S(1)}, bf16[4,2,128,128]{3,2,1,0:T(8,128)(2,1)S(1)}, u32[]{:S(2)}, u32[]{:S(2)}) collective-permute-start(bf16[4,2,128,128]{3,2,1,0:T(8,128)(2,1)S(1)} %shard_map.57), channel_id=1, source_target_pairs={{0,1},{1,0},{2,3},{3,2},{4,5},{5,4},{6,7},{7,6},{8,9},{9,8},{10,11... | collective-permute-start | bytes 786440 | tf_op jit(solution)/shard_map/ppermute | solution.py:32
  10.0 10.3 %collective-permute-start.6 = (bf16[256,256]{1,0:T(8,128)(2,1)S(1)}, bf16[256,256]{1,0:T(8,128)(2,1)S(1)}, u32[]{:S(2)}, u32[]{:S(2)}) collective-permute-start(bf16[256,256]{1,0:T(8,128)(2,1)S(1)} %shard_map.59.value.refs_9_), channel_id=1, source_target_pairs={{0,4},{2,6},{4,0},{6,2},{8,12},{10,14},{12,8},{14,10},{1,5},{3,7},... | collective-permute-start | bytes 393224 | tf_op jit(solution)/shard_map/ppermute | solution.py:28
  11.5 9.4 %collective-permute-start.4 = (bf16[2,4,128,128]{3,2,1,0:T(8,128)(2,1)S(1)}, bf16[2,4,128,128]{3,2,1,0:T(8,128)(2,1)S(1)}, u32[]{:S(2)}, u32[]{:S(2)}) collective-permute-start(bf16[2,4,128,128]{3,2,1,0:T(8,128)(2,1)S(1)} %shard_map.58.refs_1_), channel_id=1, source_target_pairs={{0,2},{2,0},{4,6},{6,4},{8,10},{10,8},{12,14},{14,12},{1,3},{3,1},... | collective-permute-start | bytes 786440 | tf_op jit(solution)/shard_map/ppermute | solution.py:28
  20.3 1.9 %collective-permute-start.7 = (bf16[256,256]{1,0:T(8,128)(2,1)S(1)}, bf16[256,256]{1,0:T(8,128)(2,1)S(1)}, u32[]{:S(2)}, u32[]{:S(2)}) collective-permute-start(bf16[256,256]{1,0:T(8,128)(2,1)S(1)} %collective-permute-done.6.refs_10_), channel_id=1, source_target_pairs={{0,1},{1,0},{2,3},{3,2},{4,5},{5,4},{6,7},{7,6},{8,9},{9,8},{10,11... | collective-permute-start | bytes 393224 | tf_op jit(solution)/shard_map/ppermute | solution.py:32
  20.3 1.6 %collective-permute-start.8 = (bf16[256,256]{1,0:T(8,128)(2,1)S(1)}, bf16[256,256]{1,0:T(8,128)(2,1)S(1)}, u32[]{:S(2)}, u32[]{:S(2)}) collective-permute-start(bf16[256,256]{1,0:T(8,128)(2,1)S(1)} %shard_map.60), channel_id=1, source_target_pairs={{0,1},{1,0},{2,3},{3,2},{4,5},{5,4},{6,7},{7,6},{8,9},{9,8},{10,11... | collective-permute-start | bytes 393224 | tf_op jit(solution)/shard_map/ppermute | solution.py:32
  22.4 4.6 %collective-permute-start.9 = (bf16[144,256]{1,0:T(8,128)(2,1)S(1)}, bf16[144,256]{1,0:T(8,128)(2,1)S(1)}, u32[]{:S(2)}, u32[]{:S(2)}) collective-permute-start(bf16[144,256]{1,0:T(8,128)(2,1)S(1)} %shard_map.65), channel_id=1, source_target_pairs={{0,2},{2,0},{4,6},{6,4},{8,10},{10,8},{12,14},{14,12},{1,3},{3,1},... | collective-permute-start | bytes 221192 | tf_op jit(solution)/shard_map/ppermute | solution.py:28
  24.0 0.7 %copy-start.3 = (s32[128]{0:T(128)S(1)}, s32[128]{0:T(128)}, u32[]{:S(2)}) copy-start(s32[128]{0:T(128)} %param.8) | copy-start | bytes 1540
  24.0 0.7 %copy-start.4 = (s32[128]{0:T(128)S(1)}, s32[128]{0:T(128)}, u32[]{:S(2)}) copy-start(s32[128]{0:T(128)} %param.9) | copy-start | bytes 1540
  27.1 6.8 %collective-permute-start.13 = (bf16[128,256]{1,0:T(8,128)(2,1)S(1)}, bf16[128,256]{1,0:T(8,128)(2,1)S(1)}, u32[]{:S(2)}, u32[]{:S(2)}) collective-permute-start(bf16[128,256]{1,0:T(8,128)(2,1)S(1)} %fusion.5.refs_0_), channel_id=1, source_target_pairs={{0,12},{2,14},{4,8},{6,10},{8,4},{10,6},{12,0},{14,2},{1,13},{3,15... | collective-permute-start | bytes 196616 | tf_op jit(solution)/shard_map/ppermute | solution.py:28
  28.7 5.2 %collective-permute-start.12 = (bf16[128,256]{1,0:T(8,128)(2,1)S(1)}, bf16[128,256]{1,0:T(8,128)(2,1)S(1)}, u32[]{:S(2)}, u32[]{:S(2)}) collective-permute-start(bf16[128,256]{1,0:T(8,128)(2,1)S(1)} %fusion.5.refs_0_), channel_id=1, source_target_pairs={{0,4},{2,6},{4,0},{6,2},{8,12},{10,14},{12,8},{14,10},{1,5},{3,7},... | collective-permute-start | bytes 196616 | tf_op jit(solution)/shard_map/ppermute | solution.py:28
  29.1 6.9 %collective-permute-start.10 = (bf16[128,256]{1,0:T(8,128)(2,1)S(1)}, bf16[128,256]{1,0:T(8,128)(2,1)S(1)}, u32[]{:S(2)}, u32[]{:S(2)}) collective-permute-start(bf16[128,256]{1,0:T(8,128)(2,1)S(1)} %fusion.5.refs_0_), channel_id=1, source_target_pairs={{0,8},{2,10},{4,12},{6,14},{8,0},{10,2},{12,4},{14,6},{1,9},{3,11}... | collective-permute-start | bytes 196616 | tf_op jit(solution)/shard_map/ppermute | solution.py:28
  33.9 2.4 %collective-permute-start.14 = (bf16[384,256]{1,0:T(8,128)(2,1)S(1)}, bf16[384,256]{1,0:T(8,128)(2,1)S(1)}, u32[]{:S(2)}, u32[]{:S(2)}) collective-permute-start(bf16[384,256]{1,0:T(8,128)(2,1)S(1)} %shard_map.68.refs_9_), channel_id=1, source_target_pairs={{0,1},{1,0},{2,3},{3,2},{4,5},{5,4},{6,7},{7,6},{8,9},{9,8},{10,11... | collective-permute-start | bytes 589832 | tf_op jit(solution)/shard_map/ppermute | solution.py:32
  36.0 1.3 %collective-permute-start.11 = (bf16[128,256]{1,0:T(8,128)(2,1)S(1)}, bf16[128,256]{1,0:T(8,128)(2,1)S(1)}, u32[]{:S(2)}, u32[]{:S(2)}) collective-permute-start(bf16[128,256]{1,0:T(8,128)(2,1)S(1)} %shard_map.67.refs_10_), channel_id=1, source_target_pairs={{0,1},{1,0},{2,3},{3,2},{4,5},{5,4},{6,7},{7,6},{8,9},{9,8},{10,11... | collective-permute-start | bytes 196616 | tf_op jit(solution)/shard_map/ppermute | solution.py:32
  37.5 4.3 %collective-permute-start.15 = (bf16[128,256]{1,0:T(8,128)(2,1)S(1)}, bf16[128,256]{1,0:T(8,128)(2,1)S(1)}, u32[]{:S(2)}, u32[]{:S(2)}) collective-permute-start(bf16[128,256]{1,0:T(8,128)(2,1)S(1)} %shard_map.72), channel_id=1, source_target_pairs={{0,2},{2,0},{4,6},{6,4},{8,10},{10,8},{12,14},{14,12},{1,3},{3,1},... | collective-permute-start | bytes 196616 | tf_op jit(solution)/shard_map/ppermute | solution.py:28

commit v19 on v15

--- a/solution.py
+++ b/solution.py
@@ -211,7 +211,7 @@
         seed_mask.reshape(1, width),
     )
 
-    current, degree = labels, None
+    current, scale = labels, None
     for step in range(ITERS):
         if step > 0:
             order = [0] + others_late(z_count)
@@ -239,8 +239,8 @@
         spread = sum((x[:width] for x in sends), total[:width])
         if first:
             sums = sum((x[width : width + 3, :width].sum(axis=0) for x in sends), total[width, :width])
-            degree = 1.0 + 0.5 * sums[:, None]
-        mixed = CARRY * (0.5 * spread + current.astype(jnp.float32)) / degree
+            scale = (CARRY / (1.0 + 0.5 * sums))[:, None]
+        mixed = (0.5 * spread + current.astype(jnp.float32)) * scale
         current = (mixed + base).astype(jnp.bfloat16)
     return current
 

time: 41.9 us -> 41.9 us (level)
  no operation moved by 1% of the time
where the time goes in v19:
time: 41.9 us; the launch traced here: 41.7 us
  starting transfers between devices  18.7 us (45%)
  waiting for transfers between devices  17.3 us (41%)
  Pallas kernels  2.69 us (6%)
  local copies, waits for them, and re-layouts  2.08 us (5%)
  other arithmetic  0.85 us (2%)
    ppermute x11, starting transfers between devices, swap_rows(): return lax.ppermute(value, 'row', [(i, i ^ shift) for i in range(count)])  18.4 us
    ppermute x11, waiting for transfers between devices, swap_rows(): return lax.ppermute(value, 'row', [(i, i ^ shift) for i in range(count)])  15.3 us
    pallas_call x16, Pallas kernels, call(): pl.pallas_call(kernel, out_shape=out_shape, in_specs=[pl.BlockSpec(memory...  2.69 us
    unnamed x10, local copies, waits for them, and re-layouts  2.08 us
    ppermute x4, waiting for transfers between devices, swap_cores(): return lax.ppermute(value, 'col', [(0, 1), (1, 0)])  1.96 us
  transfers between devices with their start and end apart: 15, of which 9 were waited for; matrix products, arithmetic and copies ran while one was open for 0% of the time, Pallas kernels for 5%

profile of v19, /device:TPU:0, one launch (start us, length us, event | category | flops | bytes accessed | tf_op | source)
XLA Modules:
  0.0 41.7 jit_solution(16711211195867521748)
XLA Ops:
  0.0 0.0 copy-start
  0.0 4.0 %collective-permute-start.5 = (bf16[128,256]{1,0:T(8,128)(2,1)}, bf16[128,256]{1,0:T(8,128)(2,1)S(1)}, u32[]{:S(2)}, u32[]{:S(2)}) collective-permute-start(bf16[128,256]{1,0:T(8,128)(2,1)} %refs_0_.1), channel_id=1, source_target_pairs={{0,8},{2,10},{4,12},{6,14},{8,0},{10,2},{12,4},{14,6},{1,9},{3,11}... | collective-permute-start | bytes 196616 | tf_op jit(solution)/shard_map/ppermute | solution.py:27
  4.0 0.0 copy-start.2
  4.0 0.0 copy-done
  4.0 0.7 %copy-done.2 = s32[8,2,1]{0,2,1:T(1,128)S(1)} copy-done((s32[8,2,1]{0,2,1:T(1,128)S(1)}, s32[8,2,1]{0,2,1:T(1,128)}, u32[]{:S(2)}) %copy-start.2) | copy-done | bytes 88
  4.7 0.7 %shard_map.56 = (bf16[2,2,128,128]{3,2,1,0:T(8,128)(2,1)S(1)}, bf16[2,2,128,128]{3,2,1,0:T(8,128)(2,1)S(1)}, bf16[2,2,128,128]{3,2,1,0:T(8,128)(2,1)S(1)}, bf16[2,2,128,128]{3,2,1,0:T(8,128)(2,1)S(1)}) custom-call(s32[2,1,8]{2,1,0:T(1,128)S(1)} %bitcast.13, bf16[2048,128]{1,0:T(8,128)(2,1)S(1)} %bitcast.12, f32[8,128]{1,0:T(8,128)S(1)} %shard_map.55.refs_2_), custom_call_target="tpu_custom_call" | custom-call | bytes 1052736 | tf_op jit(solution)/shard_map/pallas_call | solution.py:37
  5.4 1.6 %collective-permute-start = (bf16[2,2,128,128]{3,2,1,0:T(8,128)(2,1)S(1)}, bf16[2,2,128,128]{3,2,1,0:T(8,128)(2,1)S(1)}, u32[]{:S(2)}, u32[]{:S(2)}) collective-permute-start(bf16[2,2,128,128]{3,2,1,0:T(8,128)(2,1)S(1)} %get-tuple-element.14.refs_1_), channel_id=1, source_target_pairs={{0,4},{2,6},{4,0},{6,2},{8,12},{10,14},{12,8},{14,10},{1,5},{3,7},... | collective-permute-start | bytes 393224 | tf_op jit(solution)/shard_map/ppermute | solution.py:27
  7.0 0.4 collective-permute-start.1
  7.4 2.4 %collective-permute-start.2 = (bf16[2,2,128,128]{3,2,1,0:T(8,128)(2,1)S(1)}, bf16[2,2,128,128]{3,2,1,0:T(8,128)(2,1)S(1)}, u32[]{:S(2)}, u32[]{:S(2)}) collective-permute-start(bf16[2,2,128,128]{3,2,1,0:T(8,128)(2,1)S(1)} %get-tuple-element.16.refs_3_), channel_id=1, source_target_pairs={{0,12},{2,14},{4,8},{6,10},{8,4},{10,6},{12,0},{14,2},{1,13},{3,15... | collective-permute-start | bytes 393224 | tf_op jit(solution)/shard_map/ppermute | solution.py:27
  9.9 0.0 copy-start.1
  9.9 0.1 collective-permute-start.3
  10.0 0.0 collective-permute-done.5.refs_1_
  10.0 0.7 %copy-done.1 = bf16[128,256]{1,0:T(8,128)(2,1)S(1)} copy-done((bf16[128,256]{1,0:T(8,128)(2,1)S(1)}, bf16[128,256]{1,0:T(8,128)(2,1)}, u32[]{:S(2)}) %copy-start.1) | copy-done | bytes 65560
  10.7 0.7 %collective-permute-start.6 = (bf16[256,256]{1,0:T(8,128)(2,1)S(1)}, bf16[256,256]{1,0:T(8,128)(2,1)S(1)}, u32[]{:S(2)}, u32[]{:S(2)}) collective-permute-start(bf16[256,256]{1,0:T(8,128)(2,1)S(1)} %shard_map.59.refs_0_), channel_id=1, source_target_pairs={{0,4},{2,6},{4,0},{6,2},{8,12},{10,14},{12,8},{14,10},{1,5},{3,7},... | collective-permute-start | bytes 393224 | tf_op jit(solution)/shard_map/ppermute | solution.py:27
  11.5 0.0 collective-permute-done.3.refs_4_.refs_7_
  11.5 1.6 %collective-permute-start.4 = (bf16[2,4,128,128]{3,2,1,0:T(8,128)(2,1)S(1)}, bf16[2,4,128,128]{3,2,1,0:T(8,128)(2,1)S(1)}, u32[]{:S(2)}, u32[]{:S(2)}) collective-permute-start(bf16[2,4,128,128]{3,2,1,0:T(8,128)(2,1)S(1)} %shard_map.58), channel_id=1, source_target_pairs={{0,2},{2,0},{4,6},{6,4},{8,10},{10,8},{12,14},{14,12},{1,3},{3,1},... | collective-permute-start | bytes 786440 | tf_op jit(solution)/shard_map/ppermute | solution.py:27
  13.1 0.0 collective-permute-done.refs_0_.refs_4_
  13.1 6.0 %collective-permute-done.1.refs_1_.refs_5_ = bf16[2,2,128,128]{3,2,1,0:T(8,128)(2,1)S(1)} collective-permute-done((bf16[2,2,128,128]{3,2,1,0:T(8,128)(2,1)S(1)}, bf16[2,2,128,128]{3,2,1,0:T(8,128)(2,1)S(1)}, u32[]{:S(2)}, u32[]{:S(2)}) %collective-permute-start.1) | collective-permute-done | bytes 131104 | tf_op jit(solution)/shard_map/ppermute | solution.py:27
  19.1 0.0 collective-permute-done.2.refs_2_.refs_6_
  19.1 1.2 %collective-permute-done.6.refs_1_ = bf16[256,256]{1,0:T(8,128)(2,1)S(1)} collective-permute-done((bf16[256,256]{1,0:T(8,128)(2,1)S(1)}, bf16[256,256]{1,0:T(8,128)(2,1)S(1)}, u32[]{:S(2)}, u32[]{:S(2)}) %collective-permute-start.6) | collective-permute-done | bytes 131104 | tf_op jit(solution)/shard_map/ppermute | solution.py:27
  20.3 0.1 collective-permute-start.7
  20.4 0.0 collective-permute-done.4.refs_8_
  20.4 0.5 %shard_map.62 = (f32[136,256]{1,0:T(8,128)S(1)}, f32[136,256]{1,0:T(8,128)S(1)}) custom-call(bf16[2,2,128,128]{3,2,1,0:T(8,128)(2,1)S(1)} %get-tuple-element.13.refs_0_, bf16[2,2,128,128]{3,2,1,0:T(8,128)(2,1)S(1)} %get-tuple-element.14.refs_1_, bf16[2,2,128,128]{3,2,1,0:T(8,128)(2,1)S(1)} %get-tuple-element.15.refs_2_, ...), custom_call_target="tpu_custom_call" | custom-call | flops 3000000000 | bytes 1986560 | tf_op jit(solution)/shard_map/pallas_call | solution.py:37
  20.9 1.0 %collective-permute-done.7.refs_9_ = bf16[512,256]{1,0:T(8,128)(2,1)S(1)} collective-permute-done((bf16[512,256]{1,0:T(8,128)(2,1)S(1)}, bf16[512,256]{1,0:T(8,128)(2,1)S(1)}, u32[]{:S(2)}, u32[]{:S(2)}) %collective-permute-start.7) | collective-permute-done | bytes 262176 | tf_op jit(solution)/shard_map/ppermute | solution.py:31
  21.9 0.3 shard_map.64
  22.2 1.6 %collective-permute-start.8 = (bf16[144,256]{1,0:T(8,128)(2,1)S(1)}, bf16[144,256]{1,0:T(8,128)(2,1)S(1)}, u32[]{:S(2)}, u32[]{:S(2)}) collective-permute-start(bf16[144,256]{1,0:T(8,128)(2,1)S(1)} %shard_map.64), channel_id=1, source_target_pairs={{0,2},{2,0},{4,6},{6,4},{8,10},{10,8},{12,14},{14,12},{1,3},{3,1},... | collective-permute-start | bytes 221192 | tf_op jit(solution)/shard_map/ppermute | solution.py:27
  23.8 0.0 copy-start.3
  23.8 0.0 copy-start.4
  23.8 0.7 %copy-done.3 = s32[128]{0:T(128)S(1)} copy-done((s32[128]{0:T(128)S(1)}, s32[128]{0:T(128)}, u32[]{:S(2)}) %copy-start.3) | copy-done | bytes 536
  24.4 0.0 copy-done.4
  24.4 0.1 shard_map.65
  24.5 0.3 shard_map.63
  24.8 1.8 %collective-permute-done.8 = bf16[144,256]{1,0:T(8,128)(2,1)S(1)} collective-permute-done((bf16[144,256]{1,0:T(8,128)(2,1)S(1)}, bf16[144,256]{1,0:T(8,128)(2,1)S(1)}, u32[]{:S(2)}, u32[]{:S(2)}) %collective-permute-start.8) | collective-permute-done | bytes 73760 | tf_op jit(solution)/shard_map/ppermute | solution.py:27
  26.6 0.1 fusion.4.refs_0_
  26.7 1.6 %collective-permute-start.10 = (bf16[128,256]{1,0:T(8,128)(2,1)S(1)}, bf16[128,256]{1,0:T(8,128)(2,1)S(1)}, u32[]{:S(2)}, u32[]{:S(2)}) collective-permute-start(bf16[128,256]{1,0:T(8,128)(2,1)S(1)} %fusion.4.refs_0_), channel_id=1, source_target_pairs={{0,12},{2,14},{4,8},{6,10},{8,4},{10,6},{12,0},{14,2},{1,13},{3,15... | collective-permute-start | bytes 196616 | tf_op jit(solution)/shard_map/ppermute | solution.py:27
  28.3 0.4 collective-permute-start.9
  28.7 2.4 %collective-permute-start.12 = (bf16[128,256]{1,0:T(8,128)(2,1)S(1)}, bf16[128,256]{1,0:T(8,128)(2,1)S(1)}, u32[]{:S(2)}, u32[]{:S(2)}) collective-permute-start(bf16[128,256]{1,0:T(8,128)(2,1)S(1)} %fusion.4.refs_0_), channel_id=1, source_target_pairs={{0,8},{2,10},{4,12},{6,14},{8,0},{10,2},{12,4},{14,6},{1,9},{3,11}... | collective-permute-start | bytes 196616 | tf_op jit(solution)/shard_map/ppermute | solution.py:27
  31.2 2.1 %collective-permute-done.10.refs_2_ = bf16[128,256]{1,0:T(8,128)(2,1)S(1)} collective-permute-done((bf16[128,256]{1,0:T(8,128)(2,1)S(1)}, bf16[128,256]{1,0:T(8,128)(2,1)S(1)}, u32[]{:S(2)}, u32[]{:S(2)}) %collective-permute-start.10) | collective-permute-done | bytes 65568 | tf_op jit(solution)/shard_map/ppermute | solution.py:27
  33.3 0.1 collective-permute-done.9.refs_1_
  33.4 0.1 collective-permute-start.11
  33.5 1.6 %collective-permute-done.12.refs_0_ = bf16[128,256]{1,0:T(8,128)(2,1)S(1)} collective-permute-done((bf16[128,256]{1,0:T(8,128)(2,1)S(1)}, bf16[128,256]{1,0:T(8,128)(2,1)S(1)}, u32[]{:S(2)}, u32[]{:S(2)}) %collective-permute-start.12) | collective-permute-done | bytes 65568 | tf_op jit(solution)/shard_map/ppermute | solution.py:27
  35.1 0.0 collective-permute-start.13
  35.1 0.3 shard_map.68
  35.5 0.9 %collective-permute-done.13.refs_10_ = bf16[128,256]{1,0:T(8,128)(2,1)S(1)} collective-permute-done((bf16[128,256]{1,0:T(8,128)(2,1)S(1)}, bf16[128,256]{1,0:T(8,128)(2,1)S(1)}, u32[]{:S(2)}, u32[]{:S(2)}) %collective-permute-start.13) | collective-permute-done | bytes 65568 | tf_op jit(solution)/shard_map/ppermute | solution.py:31
  36.4 0.0 collective-permute-done.11.refs_9_
  36.4 0.3 shard_map.70
  36.6 1.6 %collective-permute-start.14 = (bf16[128,256]{1,0:T(8,128)(2,1)S(1)}, bf16[128,256]{1,0:T(8,128)(2,1)S(1)}, u32[]{:S(2)}, u32[]{:S(2)}) collective-permute-start(bf16[128,256]{1,0:T(8,128)(2,1)S(1)} %shard_map.70), channel_id=1, source_target_pairs={{0,2},{2,0},{4,6},{6,4},{8,10},{10,8},{12,14},{14,12},{1,3},{3,1},... | collective-permute-start | bytes 196616 | tf_op jit(solution)/shard_map/ppermute | solution.py:27
  38.2 0.3 shard_map.69
  38.5 2.5 %collective-permute-done.14 = bf16[128,256]{1,0:T(8,128)(2,1)S(1)} collective-permute-done((bf16[128,256]{1,0:T(8,128)(2,1)S(1)}, bf16[128,256]{1,0:T(8,128)(2,1)S(1)}, u32[]{:S(2)}, u32[]{:S(2)}) %collective-permute-start.14) | collective-permute-done | bytes 65568 | tf_op jit(solution)/shard_map/ppermute | solution.py:27
  41.0 0.7 %add_convert_fusion = bf16[128,256]{1,0:T(8,128)(2,1)} fusion(f32[128,256]{1,0:T(8,128)S(1)} %shard_map.65, bf16[128,256]{1,0:T(8,128)(2,1)S(1)} %fusion.4.refs_0_, f32[128,256]{1,0:T(8,128)S(1)} %shard_map.69, bf16[128,256]{1,0:T(8,128)(2,1)S(1)} %collective-permute-done.14, f32[128]{0:T(128)S(1)} %add_divide_fusion), kind=kLoop, calls=%fused_computation.6 | loop fusion | flops 262144 | bytes 459264 | tf_op jit(solution)/shard_map/convert_element_type | solution.py:244
  (11 shorter events, 0.1 us)
Async XLA Ops:
  0.0 4.0 %copy-start = (bf16[1024,2,128]{2,1,0:T(2,128)(2,1)S(1)}, bf16[1024,2,128]{2,1,0:T(2,128)(2,1)}, u32[]{:S(2)}) copy-start(bf16[1024,2,128]{2,1,0:T(2,128)(2,1)} %param.5) | copy-start | bytes 1572868
  0.0 10.0 %collective-permute-start.5 = (bf16[128,256]{1,0:T(8,128)(2,1)}, bf16[128,256]{1,0:T(8,128)(2,1)S(1)}, u32[]{:S(2)}, u32[]{:S(2)}) collective-permute-start(bf16[128,256]{1,0:T(8,128)(2,1)} %refs_0_.1), channel_id=1, source_target_pairs={{0,8},{2,10},{4,12},{6,14},{8,0},{10,2},{12,4},{14,6},{1,9},{3,11}... | collective-permute-start | bytes 196616 | tf_op jit(solution)/shard_map/ppermute | solution.py:27
  4.0 0.7 %copy-start.2 = (s32[8,2,1]{0,2,1:T(1,128)S(1)}, s32[8,2,1]{0,2,1:T(1,128)}, u32[]{:S(2)}) copy-start(s32[8,2,1]{0,2,1:T(1,128)} %param.6) | copy-start | bytes 196
  5.4 7.7 %collective-permute-start = (bf16[2,2,128,128]{3,2,1,0:T(8,128)(2,1)S(1)}, bf16[2,2,128,128]{3,2,1,0:T(8,128)(2,1)S(1)}, u32[]{:S(2)}, u32[]{:S(2)}) collective-permute-start(bf16[2,2,128,128]{3,2,1,0:T(8,128)(2,1)S(1)} %get-tuple-element.14.refs_1_), channel_id=1, source_target_pairs={{0,4},{2,6},{4,0},{6,2},{8,12},{10,14},{12,8},{14,10},{1,5},{3,7},... | collective-permute-start | bytes 393224 | tf_op jit(solution)/shard_map/ppermute | solution.py:27
  7.0 12.1 %collective-permute-start.1 = (bf16[2,2,128,128]{3,2,1,0:T(8,128)(2,1)S(1)}, bf16[2,2,128,128]{3,2,1,0:T(8,128)(2,1)S(1)}, u32[]{:S(2)}, u32[]{:S(2)}) collective-permute-start(bf16[2,2,128,128]{3,2,1,0:T(8,128)(2,1)S(1)} %get-tuple-element.15.refs_2_), channel_id=1, source_target_pairs={{0,8},{2,10},{4,12},{6,14},{8,0},{10,2},{12,4},{14,6},{1,9},{3,11}... | collective-permute-start | bytes 393224 | tf_op jit(solution)/shard_map/ppermute | solution.py:27
  7.4 11.7 %collective-permute-start.2 = (bf16[2,2,128,128]{3,2,1,0:T(8,128)(2,1)S(1)}, bf16[2,2,128,128]{3,2,1,0:T(8,128)(2,1)S(1)}, u32[]{:S(2)}, u32[]{:S(2)}) collective-permute-start(bf16[2,2,128,128]{3,2,1,0:T(8,128)(2,1)S(1)} %get-tuple-element.16.refs_3_), channel_id=1, source_target_pairs={{0,12},{2,14},{4,8},{6,10},{8,4},{10,6},{12,0},{14,2},{1,13},{3,15... | collective-permute-start | bytes 393224 | tf_op jit(solution)/shard_map/ppermute | solution.py:27
  9.9 0.8 %copy-start.1 = (bf16[128,256]{1,0:T(8,128)(2,1)S(1)}, bf16[128,256]{1,0:T(8,128)(2,1)}, u32[]{:S(2)}) copy-start(bf16[128,256]{1,0:T(8,128)(2,1)} %refs_0_.1) | copy-start | bytes 196612
  9.9 1.6 %collective-permute-start.3 = (bf16[4,2,128,128]{3,2,1,0:T(8,128)(2,1)S(1)}, bf16[4,2,128,128]{3,2,1,0:T(8,128)(2,1)S(1)}, u32[]{:S(2)}, u32[]{:S(2)}) collective-permute-start(bf16[4,2,128,128]{3,2,1,0:T(8,128)(2,1)S(1)} %shard_map.57), channel_id=1, source_target_pairs={{0,1},{1,0},{2,3},{3,2},{4,5},{5,4},{6,7},{7,6},{8,9},{9,8},{10,11... | collective-permute-start | bytes 786440 | tf_op jit(solution)/shard_map/ppermute | solution.py:31
  10.7 9.6 %collective-permute-start.6 = (bf16[256,256]{1,0:T(8,128)(2,1)S(1)}, bf16[256,256]{1,0:T(8,128)(2,1)S(1)}, u32[]{:S(2)}, u32[]{:S(2)}) collective-permute-start(bf16[256,256]{1,0:T(8,128)(2,1)S(1)} %shard_map.59.refs_0_), channel_id=1, source_target_pairs={{0,4},{2,6},{4,0},{6,2},{8,12},{10,14},{12,8},{14,10},{1,5},{3,7},... | collective-permute-start | bytes 393224 | tf_op jit(solution)/shard_map/ppermute | solution.py:27
  11.5 8.9 %collective-permute-start.4 = (bf16[2,4,128,128]{3,2,1,0:T(8,128)(2,1)S(1)}, bf16[2,4,128,128]{3,2,1,0:T(8,128)(2,1)S(1)}, u32[]{:S(2)}, u32[]{:S(2)}) collective-permute-start(bf16[2,4,128,128]{3,2,1,0:T(8,128)(2,1)S(1)} %shard_map.58), channel_id=1, source_target_pairs={{0,2},{2,0},{4,6},{6,4},{8,10},{10,8},{12,14},{14,12},{1,3},{3,1},... | collective-permute-start | bytes 786440 | tf_op jit(solution)/shard_map/ppermute | solution.py:27
  20.3 1.6 %collective-permute-start.7 = (bf16[512,256]{1,0:T(8,128)(2,1)S(1)}, bf16[512,256]{1,0:T(8,128)(2,1)S(1)}, u32[]{:S(2)}, u32[]{:S(2)}) collective-permute-start(bf16[512,256]{1,0:T(8,128)(2,1)S(1)} %shard_map.60.refs_9_), channel_id=1, source_target_pairs={{0,1},{1,0},{2,3},{3,2},{4,5},{5,4},{6,7},{7,6},{8,9},{9,8},{10,11... | collective-permute-start | bytes 786440 | tf_op jit(solution)/shard_map/ppermute | solution.py:31
  22.2 4.4 %collective-permute-start.8 = (bf16[144,256]{1,0:T(8,128)(2,1)S(1)}, bf16[144,256]{1,0:T(8,128)(2,1)S(1)}, u32[]{:S(2)}, u32[]{:S(2)}) collective-permute-start(bf16[144,256]{1,0:T(8,128)(2,1)S(1)} %shard_map.64), channel_id=1, source_target_pairs={{0,2},{2,0},{4,6},{6,4},{8,10},{10,8},{12,14},{14,12},{1,3},{3,1},... | collective-permute-start | bytes 221192 | tf_op jit(solution)/shard_map/ppermute | solution.py:27
  23.8 0.7 %copy-start.3 = (s32[128]{0:T(128)S(1)}, s32[128]{0:T(128)}, u32[]{:S(2)}) copy-start(s32[128]{0:T(128)} %param.8) | copy-start | bytes 1540
  23.8 0.7 %copy-start.4 = (s32[128]{0:T(128)S(1)}, s32[128]{0:T(128)}, u32[]{:S(2)}) copy-start(s32[128]{0:T(128)} %param.9) | copy-start | bytes 1540
  26.7 6.5 %collective-permute-start.10 = (bf16[128,256]{1,0:T(8,128)(2,1)S(1)}, bf16[128,256]{1,0:T(8,128)(2,1)S(1)}, u32[]{:S(2)}, u32[]{:S(2)}) collective-permute-start(bf16[128,256]{1,0:T(8,128)(2,1)S(1)} %fusion.4.refs_0_), channel_id=1, source_target_pairs={{0,12},{2,14},{4,8},{6,10},{8,4},{10,6},{12,0},{14,2},{1,13},{3,15... | collective-permute-start | bytes 196616 | tf_op jit(solution)/shard_map/ppermute | solution.py:27
  28.3 5.0 %collective-permute-start.9 = (bf16[128,256]{1,0:T(8,128)(2,1)S(1)}, bf16[128,256]{1,0:T(8,128)(2,1)S(1)}, u32[]{:S(2)}, u32[]{:S(2)}) collective-permute-start(bf16[128,256]{1,0:T(8,128)(2,1)S(1)} %fusion.4.refs_0_), channel_id=1, source_target_pairs={{0,4},{2,6},{4,0},{6,2},{8,12},{10,14},{12,8},{14,10},{1,5},{3,7},... | collective-permute-start | bytes 196616 | tf_op jit(solution)/shard_map/ppermute | solution.py:27
  28.7 6.4 %collective-permute-start.12 = (bf16[128,256]{1,0:T(8,128)(2,1)S(1)}, bf16[128,256]{1,0:T(8,128)(2,1)S(1)}, u32[]{:S(2)}, u32[]{:S(2)}) collective-permute-start(bf16[128,256]{1,0:T(8,128)(2,1)S(1)} %fusion.4.refs_0_), channel_id=1, source_target_pairs={{0,8},{2,10},{4,12},{6,14},{8,0},{10,2},{12,4},{14,6},{1,9},{3,11}... | collective-permute-start | bytes 196616 | tf_op jit(solution)/shard_map/ppermute | solution.py:27
  33.4 3.0 %collective-permute-start.11 = (bf16[384,256]{1,0:T(8,128)(2,1)S(1)}, bf16[384,256]{1,0:T(8,128)(2,1)S(1)}, u32[]{:S(2)}, u32[]{:S(2)}) collective-permute-start(bf16[384,256]{1,0:T(8,128)(2,1)S(1)} %shard_map.66.refs_9_), channel_id=1, source_target_pairs={{0,1},{1,0},{2,3},{3,2},{4,5},{5,4},{6,7},{7,6},{8,9},{9,8},{10,11... | collective-permute-start | bytes 589832 | tf_op jit(solution)/shard_map/ppermute | solution.py:31
  35.1 1.3 %collective-permute-start.13 = (bf16[128,256]{1,0:T(8,128)(2,1)S(1)}, bf16[128,256]{1,0:T(8,128)(2,1)S(1)}, u32[]{:S(2)}, u32[]{:S(2)}) collective-permute-start(bf16[128,256]{1,0:T(8,128)(2,1)S(1)} %shard_map.67.refs_10_), channel_id=1, source_target_pairs={{0,1},{1,0},{2,3},{3,2},{4,5},{5,4},{6,7},{7,6},{8,9},{9,8},{10,11... | collective-permute-start | bytes 196616 | tf_op jit(solution)/shard_map/ppermute | solution.py:31
  36.6 4.3 %collective-permute-start.14 = (bf16[128,256]{1,0:T(8,128)(2,1)S(1)}, bf16[128,256]{1,0:T(8,128)(2,1)S(1)}, u32[]{:S(2)}, u32[]{:S(2)}) collective-permute-start(bf16[128,256]{1,0:T(8,128)(2,1)S(1)} %shard_map.70), channel_id=1, source_target_pairs={{0,2},{2,0},{4,6},{6,4},{8,10},{10,8},{12,14},{14,12},{1,3},{3,1},... | collective-permute-start | bytes 196616 | tf_op jit(solution)/shard_map/ppermute | solution.py:27
